TPU v7x, 32 devices: a whole 2x2x4 slice. The times are simulated.
32 devices in a mesh: dp: 8 (over y, x, core), fsdp: 4 (over z).
Axes of the slice: x: 2, y: 2, z: 4, core: 2. Of those that a mesh axis runs over, the one named last changes fastest.
Arguments:
- hidden: bfloat16 [16, 1024, 768], P('dp', 'fsdp'), may hold values from -6 to 6
- skip_tokens: bfloat16 [16, 1024, 768], P('dp', 'fsdp'), may hold values from -6 to 6
- backbone_cotangent: bfloat16 [16, 1024, 768], P('dp', 'fsdp'), may hold values from -6 to 6
- head_cotangent: bfloat16 [16, 1024, 768], P('dp', 'fsdp'), may hold values from -6 to 6
- starts: int32 [16, 8], P('dp'), may hold values from 0 to 1023, as said below
- positives: int32 [128], replicated, may hold values from 0 to 127, as said below
- qkv_weight: bfloat16 [2, 768, 2304], P(None, ('dp', 'fsdp')), may hold values from -0.3125 to 0.3125
- qv_bias: bfloat16 [2, 1536], P(None, ('dp', 'fsdp')), may hold values from -3 to 3
- attn_weight: bfloat16 [2, 768, 768], P(None, ('dp', 'fsdp')), may hold values from -1.25 to 1.25
- attn_bias: bfloat16 [2, 768], P(None, ('dp', 'fsdp')), may hold values from -2 to 2
- attn_gain: bfloat16 [2, 768], P(None, ('dp', 'fsdp')), may hold values from 0.5 to 1.5
- attn_shift: bfloat16 [2, 768], P(None, ('dp', 'fsdp')), may hold values from -2 to 2
- inner_weight: bfloat16 [2, 768, 3072], P(None, ('dp', 'fsdp')), may hold values from -0.21875 to 0.21875
- inner_bias: bfloat16 [2, 3072], P(None, ('dp', 'fsdp')), may hold values from -3 to 3
- outer_weight: bfloat16 [2, 3072, 768], P(None, ('dp', 'fsdp')), may hold values from -0.21875 to 0.21875
- outer_bias: bfloat16 [2, 768], P(None, ('dp', 'fsdp')), may hold values from -2 to 2
- ffn_gain: bfloat16 [2, 768], P(None, ('dp', 'fsdp')), may hold values from 0.5 to 1.5
- ffn_shift: bfloat16 [2, 768], P(None, ('dp', 'fsdp')), may hold values from -2 to 2
Outputs:
- contrast_loss: float32 [], replicated
- backbone_out: bfloat16 [16, 1024, 768], P('dp', 'fsdp')
- head_out: bfloat16 [16, 1024, 768], P('dp', 'fsdp')
- grad_hidden: float32 [16, 1024, 768], P('dp', 'fsdp')
- grad_skip_tokens: float32 [16, 1024, 768], P('dp', 'fsdp')
- grad_qkv_weight: float32 [2, 768, 2304], P(None, ('dp', 'fsdp'))
- grad_qv_bias: float32 [2, 1536], P(None, ('dp', 'fsdp'))
- grad_attn_weight: float32 [2, 768, 768], P(None, ('dp', 'fsdp'))
- grad_attn_bias: float32 [2, 768], P(None, ('dp', 'fsdp'))
- grad_attn_gain: float32 [2, 768], P(None, ('dp', 'fsdp'))
- grad_attn_shift: float32 [2, 768], P(None, ('dp', 'fsdp'))
- grad_inner_weight: float32 [2, 768, 3072], P(None, ('dp', 'fsdp'))
- grad_inner_bias: float32 [2, 3072], P(None, ('dp', 'fsdp'))
- grad_outer_weight: float32 [2, 3072, 768], P(None, ('dp', 'fsdp'))
- grad_outer_bias: float32 [2, 768], P(None, ('dp', 'fsdp'))
- grad_ffn_gain: float32 [2, 768], P(None, ('dp', 'fsdp'))
- grad_ffn_shift: float32 [2, 768], P(None, ('dp', 'fsdp'))
Inputs may be any that keep to these rules, and one draw needn't show every extreme that they name: In each row the 8 starts rise strictly from 0. A passage covers the positions from its start up to the next start or the row's end; its first token is its CLS token. Passage p is segment p % 8 of row p // 8. positives is a permutation of the passages with positives[p] != p.
All inputs are finite; a program needn't handle non-finite values.
Results may differ from a plain program's by a relative error of at most 0.015.
The roundings to bfloat16 on the way count: a program that leaves them out, or rounds other values in their place, can miss the bound.
Values may be sent and summed in bfloat16 or wider, within the bound.
No kernel may reach another device: no remote copies, remote signals or barrier semaphores. Data moves between devices by JAX's collectives and lax.ppermute only.
A program may use at most 384 MiB of HBM per device.

v0:
```python
import jax
import jax.numpy as jnp
from jax import lax
from jax.sharding import PartitionSpec as P

HEADS = 12
HEAD_DIM = 64
SEGS = 8
CH_ROWS = 1


EPS = 1e-12
SOFTMAX_HEAT = 0.02
NEGATIVE = -1e30
FULL_PRECISION = lax.Precision.HIGHEST


def layer_norm(residual, norm_gain, norm_shift):
    average = jnp.mean(residual, axis=-1, keepdims=True)
    centred = residual - average
    inv_std = lax.rsqrt(jnp.mean(centred * centred, axis=-1, keepdims=True) + EPS)
    normed = centred * inv_std
    return (normed * norm_gain + norm_shift, normed, inv_std)


def norm_back(upstream, normed, inv_std, norm_gain):
    scaled = upstream * norm_gain
    return inv_std * (
        scaled
        - jnp.mean(scaled, axis=-1, keepdims=True)
        - normed * jnp.mean(scaled * normed, axis=-1, keepdims=True)
    )


def gelu_exact(inputs):
    return jax.nn.gelu(inputs, approximate=False)


def matrix_product(first_op, second_op):
    return jnp.dot(first_op, second_op, preferred_element_type=jnp.float32)


def left_t(first_op, second_op):
    return lax.dot_general(
        first_op, second_op, (((0,), (0,)), ((), ())), preferred_element_type=jnp.float32
    )


def right_t(first_op, second_op):
    return lax.dot_general(
        first_op, second_op, (((1,), (1,)), ((), ())), preferred_element_type=jnp.float32
    )


def column_sum(inputs):
    return jnp.sum(inputs.astype(jnp.float32), axis=0)


def segment_ids(row_starts, positions):
    return (
        jnp.sum((row_starts[:, :, None] <= positions[None, None, :]).astype(jnp.int32), axis=1) - 1
    )


def masked_scores(queries, key_rows, seg_query, seg_key):
    scores = jnp.einsum(
        "bqhd,bkhd->bhqk", queries, key_rows, preferred_element_type=jnp.float32
    ) * HEAD_DIM ** (-0.5)
    allowed = seg_query[:, None, :, None] == seg_key[:, None, None, :]
    return jnp.where(allowed, scores, NEGATIVE)


def attend(queries, key_rows, value_rows, seg_query, seg_key):
    scores = masked_scores(queries, key_rows, seg_query, seg_key)
    highest = jnp.max(scores, axis=-1, keepdims=True)
    powers = jnp.exp(scores - highest)
    loss_totals = jnp.sum(powers, axis=-1, keepdims=True)
    attn_probs = (powers / loss_totals).astype(jnp.bfloat16)
    mixture = jnp.einsum(
        "bhqk,bkhd->bqhd", attn_probs, value_rows, preferred_element_type=jnp.float32
    )
    return (mixture, highest + jnp.log(loss_totals))


def block_tail(residual, mixture_low, weights):
    (
        qkv_w,
        qv_b,
        attn_w,
        attn_b,
        attn_g,
        attn_s,
        inner_w,
        inner_b,
        outer_w,
        outer_b,
        ffn_g,
        ffn_s,
    ) = weights
    branch = matrix_product(mixture_low, attn_w) + attn_b.astype(jnp.float32)
    normed_out, normed_one, inv_one = layer_norm(
        residual + branch, attn_g.astype(jnp.float32), attn_s.astype(jnp.float32)
    )
    normed_low = normed_out.astype(jnp.bfloat16)
    inner = matrix_product(normed_low, inner_w) + inner_b.astype(jnp.float32)
    active_low = gelu_exact(inner).astype(jnp.bfloat16)
    outer = matrix_product(active_low, outer_w) + outer_b.astype(jnp.float32)
    output, normed_two, inv_two = layer_norm(
        normed_out + outer, ffn_g.astype(jnp.float32), ffn_s.astype(jnp.float32)
    )
    return (output, (normed_one, inv_one, normed_low, inner, active_low, normed_two, inv_two))


def encode_cls(hidden, starts, weights):
    qkv_w = weights[0]
    bias_full = weights[1].astype(jnp.float32)
    rows_dev, local, feature_width = hidden.shape
    flat_low = hidden.reshape(rows_dev * local, feature_width)
    key_value = matrix_product(flat_low, qkv_w[:, feature_width:])
    key_rows = (
        key_value[:, :feature_width].astype(jnp.bfloat16).reshape(rows_dev, local, feature_width)
    )
    value_rows = (
        (key_value[:, feature_width:] + bias_full[feature_width:])
        .astype(jnp.bfloat16)
        .reshape(rows_dev, local, feature_width)
    )
    key_all, value_all, token_all = (
        lax.all_gather(key_rows, "fsdp", axis=1, tiled=True),
        lax.all_gather(value_rows, "fsdp", axis=1, tiled=True),
        lax.all_gather(hidden, "fsdp", axis=1, tiled=True),
    )
    length = token_all.shape[1]
    share = rows_dev * SEGS // lax.axis_size("fsdp")
    passage = lax.axis_index("fsdp") * share + jnp.arange(share, dtype=jnp.int32)
    row_of = passage // SEGS
    seg_of = passage % SEGS
    picked_starts = starts[row_of]
    cls_pos = jnp.take_along_axis(picked_starts, seg_of[:, None], axis=1)[:, 0]
    tokens = token_all[row_of, cls_pos]
    key_sel = key_all[row_of].reshape(share, length, HEADS, HEAD_DIM)
    value_sel = value_all[row_of].reshape(share, length, HEADS, HEAD_DIM)
    seg_key = segment_ids(picked_starts, jnp.arange(length, dtype=jnp.int32))
    queries = (
        (matrix_product(tokens, qkv_w[:, :feature_width]) + bias_full[:feature_width])
        .astype(jnp.bfloat16)
        .reshape(share, 1, HEADS, HEAD_DIM)
    )
    mixture, _ = attend(queries, key_sel, value_sel, seg_of[:, None], seg_key)
    mixture_low = mixture.reshape(share, feature_width).astype(jnp.bfloat16)
    output, _ = block_tail(tokens.astype(jnp.float32), mixture_low, weights)
    return output


def layer_forward(inputs, weights, seg_query, seg_key):
    qkv_w = weights[0]
    bias_full = weights[1].astype(jnp.float32)
    rows, local, feature_width = inputs.shape
    flat = inputs.reshape(rows * local, feature_width)
    flat_low = flat.astype(jnp.bfloat16)
    qkv = matrix_product(flat_low, qkv_w)
    queries = (qkv[:, :feature_width] + bias_full[:feature_width]).astype(jnp.bfloat16)
    key_rows = (
        qkv[:, feature_width : 2 * feature_width]
        .astype(jnp.bfloat16)
        .reshape(rows, local, feature_width)
    )
    value_rows = (
        (qkv[:, 2 * feature_width :] + bias_full[feature_width:])
        .astype(jnp.bfloat16)
        .reshape(rows, local, feature_width)
    )
    key_all, value_all = (
        lax.all_gather(key_rows, "fsdp", axis=1, tiled=True),
        lax.all_gather(value_rows, "fsdp", axis=1, tiled=True),
    )
    length = key_all.shape[1]
    query_heads = queries.reshape(rows, local, HEADS, HEAD_DIM)
    key_heads = key_all.reshape(rows, length, HEADS, HEAD_DIM)
    value_heads = value_all.reshape(rows, length, HEADS, HEAD_DIM)
    mixture, lse_rows = attend(query_heads, key_heads, value_heads, seg_query, seg_key)
    mixture_low = mixture.reshape(rows * local, feature_width).astype(jnp.bfloat16)
    output, tail_saved = block_tail(flat, mixture_low, weights)
    saved = (flat_low, query_heads, key_heads, value_heads, lse_rows, mixture_low) + tail_saved
    return (output.reshape(rows, local, feature_width), saved)


def layer_backward(upstream, weights, saved, seg_query, seg_key):
    (
        qkv_w,
        qv_b,
        attn_w,
        attn_b,
        attn_g,
        attn_s,
        inner_w,
        inner_b,
        outer_w,
        outer_b,
        ffn_g,
        ffn_s,
    ) = weights
    (
        flat_low,
        query_heads,
        key_heads,
        value_heads,
        lse_rows,
        mixture_low,
        normed_one,
        inv_one,
        normed_low,
        inner,
        active_low,
        normed_two,
        inv_two,
    ) = saved
    rows, local = (query_heads.shape[0], query_heads.shape[1])
    length = key_heads.shape[1]
    feature_width = flat_low.shape[1]
    grad_ffn_g = jnp.sum(upstream * normed_two, axis=0)
    grad_ffn_s = jnp.sum(upstream, axis=0)
    d_second = norm_back(upstream, normed_two, inv_two, ffn_g.astype(jnp.float32))
    d_outer = d_second.astype(jnp.bfloat16)
    grad_outer_b = column_sum(d_outer)
    grad_outer_w = left_t(active_low, d_outer)
    d_active = right_t(d_outer, outer_w)
    _, gelu_pull = jax.vjp(gelu_exact, inner)
    d_inner = gelu_pull(d_active)[0].astype(jnp.bfloat16)
    grad_inner_b = column_sum(d_inner)
    grad_inner_w = left_t(normed_low, d_inner)
    d_normed = right_t(d_inner, inner_w) + d_second
    grad_attn_g = jnp.sum(d_normed * normed_one, axis=0)
    grad_attn_s = jnp.sum(d_normed, axis=0)
    d_first = norm_back(d_normed, normed_one, inv_one, attn_g.astype(jnp.float32))
    d_branch = d_first.astype(jnp.bfloat16)
    grad_attn_b = column_sum(d_branch)
    grad_attn_w = left_t(mixture_low, d_branch)
    d_mixture = right_t(d_branch, attn_w).astype(jnp.bfloat16).reshape(rows, local, HEADS, HEAD_DIM)
    scores = masked_scores(query_heads, key_heads, seg_query, seg_key)
    attn_probs = jnp.exp(scores - lse_rows)
    d_probs = jnp.einsum(
        "bqhd,bkhd->bhqk", d_mixture, value_heads, preferred_element_type=jnp.float32
    )
    offsets = jnp.sum(attn_probs * d_probs, axis=-1, keepdims=True)
    d_scores = (attn_probs * (d_probs - offsets)).astype(jnp.bfloat16)
    scaling = HEAD_DIM ** (-0.5)
    d_queries = (
        jnp.einsum("bhqk,bkhd->bqhd", d_scores, key_heads, preferred_element_type=jnp.float32)
        * scaling
    ).astype(jnp.bfloat16)
    d_key_terms = (
        jnp.einsum("bhqk,bqhd->bkhd", d_scores, query_heads, preferred_element_type=jnp.float32)
        * scaling
    )
    d_value_terms = jnp.einsum(
        "bhqk,bqhd->bkhd",
        attn_probs.astype(jnp.bfloat16),
        d_mixture,
        preferred_element_type=jnp.float32,
    )
    d_key_sum, d_value_sum = (
        lax.psum_scatter(
            d_key_terms.reshape(rows, length, feature_width).astype(jnp.bfloat16),
            "fsdp",
            scatter_dimension=1,
            tiled=True,
        ).astype(jnp.float32),
        lax.psum_scatter(
            d_value_terms.reshape(rows, length, feature_width).astype(jnp.bfloat16),
            "fsdp",
            scatter_dimension=1,
            tiled=True,
        ).astype(jnp.float32),
    )
    d_keys = d_key_sum.reshape(rows * local, feature_width).astype(jnp.bfloat16)
    d_values = d_value_sum.reshape(rows * local, feature_width).astype(jnp.bfloat16)
    d_query_flat = d_queries.reshape(rows * local, feature_width)
    d_qkv = jnp.concatenate([d_query_flat, d_keys, d_values], axis=1)
    grad_qv_b = jnp.concatenate([column_sum(d_query_flat), column_sum(d_values)])
    grad_qkv_w = left_t(flat_low, d_qkv)
    d_input = right_t(d_qkv, qkv_w) + d_first
    grads = (
        grad_qkv_w,
        grad_qv_b,
        grad_attn_w,
        grad_attn_b,
        grad_attn_g,
        grad_attn_s,
        grad_inner_w,
        grad_inner_b,
        grad_outer_w,
        grad_outer_b,
        grad_ffn_g,
        grad_ffn_s,
    )
    return (d_input, grads)


def contrastive(gathered_class_vectors):
    feature_width = gathered_class_vectors.shape[1]
    count = gathered_class_vectors.shape[0]
    similarity_scores = jnp.dot(
        gathered_class_vectors, gathered_class_vectors.T, precision=FULL_PRECISION
    ) / (feature_width * SOFTMAX_HEAT)
    diagonal = (
        jnp.arange(count, dtype=jnp.int32)[:, None] == jnp.arange(count, dtype=jnp.int32)[None, :]
    )
    similarity_scores = jnp.where(diagonal, NEGATIVE, similarity_scores)
    highest = jnp.max(similarity_scores, axis=1, keepdims=True)
    loss_totals = highest + jnp.log(
        jnp.sum(jnp.exp(similarity_scores - highest), axis=1, keepdims=True)
    )
    return (similarity_scores, loss_totals)


def body(
    hidden,
    skip_tokens,
    backbone_cotangent,
    head_cotangent,
    starts,
    positives,
    qkv_weight,
    qv_bias,
    attn_weight,
    attn_bias,
    attn_gain,
    attn_shift,
    inner_weight,
    inner_bias,
    outer_weight,
    outer_bias,
    ffn_gain,
    ffn_shift,
):
    rows_dev, local, feature_width = hidden.shape
    backbone = (
        lax.all_gather(qkv_weight[0], ("dp", "fsdp"), axis=0, tiled=True),
        lax.all_gather(qv_bias[0], ("dp", "fsdp"), axis=0, tiled=True),
        lax.all_gather(attn_weight[0], ("dp", "fsdp"), axis=0, tiled=True),
        lax.all_gather(attn_bias[0], ("dp", "fsdp"), axis=0, tiled=True),
        lax.all_gather(attn_gain[0], ("dp", "fsdp"), axis=0, tiled=True),
        lax.all_gather(attn_shift[0], ("dp", "fsdp"), axis=0, tiled=True),
        lax.all_gather(inner_weight[0], ("dp", "fsdp"), axis=0, tiled=True),
        lax.all_gather(inner_bias[0], ("dp", "fsdp"), axis=0, tiled=True),
        lax.all_gather(outer_weight[0], ("dp", "fsdp"), axis=0, tiled=True),
        lax.all_gather(outer_bias[0], ("dp", "fsdp"), axis=0, tiled=True),
        lax.all_gather(ffn_gain[0], ("dp", "fsdp"), axis=0, tiled=True),
        lax.all_gather(ffn_shift[0], ("dp", "fsdp"), axis=0, tiled=True),
    )
    cls_own = encode_cls(hidden, starts, backbone)
    gathered_class_vectors = lax.all_gather(cls_own, ("dp", "fsdp"), axis=0, tiled=True)
    similarity_scores, loss_totals = contrastive(gathered_class_vectors)
    count = gathered_class_vectors.shape[0]
    column_ids = jnp.arange(count, dtype=jnp.int32)
    picked = jnp.take_along_axis(similarity_scores, positives[:, None], axis=1)
    contrast_loss = jnp.sum(loss_totals - picked)
    positive_index = (positives[:, None] == column_ids[None, :]).astype(jnp.float32)
    similarity_gradient = (jnp.exp(similarity_scores - loss_totals) - positive_index) / (
        feature_width * SOFTMAX_HEAT
    )
    d_cls_all = jnp.dot(
        similarity_gradient + similarity_gradient.T,
        gathered_class_vectors,
        precision=FULL_PRECISION,
    )
    stacked = (
        lax.all_gather(qkv_weight, ("dp", "fsdp"), axis=1, tiled=True),
        lax.all_gather(qv_bias, ("dp", "fsdp"), axis=1, tiled=True),
        lax.all_gather(attn_weight, ("dp", "fsdp"), axis=1, tiled=True),
        lax.all_gather(attn_bias, ("dp", "fsdp"), axis=1, tiled=True),
        lax.all_gather(attn_gain, ("dp", "fsdp"), axis=1, tiled=True),
        lax.all_gather(attn_shift, ("dp", "fsdp"), axis=1, tiled=True),
        lax.all_gather(inner_weight, ("dp", "fsdp"), axis=1, tiled=True),
        lax.all_gather(inner_bias, ("dp", "fsdp"), axis=1, tiled=True),
        lax.all_gather(outer_weight, ("dp", "fsdp"), axis=1, tiled=True),
        lax.all_gather(outer_bias, ("dp", "fsdp"), axis=1, tiled=True),
        lax.all_gather(ffn_gain, ("dp", "fsdp"), axis=1, tiled=True),
        lax.all_gather(ffn_shift, ("dp", "fsdp"), axis=1, tiled=True),
    )
    backbone = tuple((weight[0] for weight in stacked))
    head = tuple((weight[1] for weight in stacked))
    d_cls_mine = lax.dynamic_slice_in_dim(
        d_cls_all.reshape(-1, SEGS, feature_width), lax.axis_index("dp") * rows_dev, rows_dev, 0
    )
    length = local * lax.axis_size("fsdp")
    positions_local = lax.axis_index("fsdp") * local + jnp.arange(local, dtype=jnp.int32)
    seg_query_all = segment_ids(starts, positions_local)
    seg_key_all = segment_ids(starts, jnp.arange(length, dtype=jnp.int32))
    cls_hot = (starts[:, :, None] == positions_local[None, None, :]).astype(jnp.float32)
    is_cls = jnp.any(starts[:, :, None] == positions_local[None, None, :], axis=1)[:, :, None]
    backbone_parts = []
    head_parts = []
    hidden_parts = []
    skip_parts = []
    totals_grad = None
    for block in range(rows_dev // CH_ROWS):
        lower = block * CH_ROWS
        upper = lower + CH_ROWS
        seg_query = seg_query_all[lower:upper]
        seg_key = seg_key_all[lower:upper]
        first, saved_one = layer_forward(
            hidden[lower:upper].astype(jnp.float32), backbone, seg_query, seg_key
        )
        head_in = jnp.where(
            is_cls[lower:upper], first, skip_tokens[lower:upper].astype(jnp.float32)
        )
        second, saved_two = layer_forward(head_in, head, seg_query, seg_key)
        backbone_parts.append(first.astype(jnp.bfloat16))
        head_parts.append(second.astype(jnp.bfloat16))
        upstream_two = (
            head_cotangent[lower:upper].astype(jnp.float32).reshape(CH_ROWS * local, feature_width)
        )
        d_head_in, grads_two = layer_backward(upstream_two, head, saved_two, seg_query, seg_key)
        d_head_in = d_head_in.reshape(CH_ROWS, local, feature_width)
        skip_parts.append(jnp.where(is_cls[lower:upper], 0.0, d_head_in))
        cls_term = jnp.einsum(
            "bsc,bsd->bcd", cls_hot[lower:upper], d_cls_mine[lower:upper], precision=FULL_PRECISION
        )
        upstream_one = (
            backbone_cotangent[lower:upper].astype(jnp.float32)
            + jnp.where(is_cls[lower:upper], d_head_in, 0.0)
            + cls_term
        )
        d_input, grads_one = layer_backward(
            upstream_one.reshape(CH_ROWS * local, feature_width),
            backbone,
            saved_one,
            seg_query,
            seg_key,
        )
        hidden_parts.append(d_input.reshape(CH_ROWS, local, feature_width))
        paired = tuple(
            (jnp.stack([one_grad, two_grad]) for one_grad, two_grad in zip(grads_one, grads_two))
        )
        if totals_grad is None:
            totals_grad = paired
        else:
            totals_grad = tuple((summed + extra for summed, extra in zip(totals_grad, paired)))
    totals_grad = (
        lax.psum_scatter(totals_grad[0], ("dp", "fsdp"), scatter_dimension=1, tiled=True),
        lax.psum_scatter(totals_grad[1], ("dp", "fsdp"), scatter_dimension=1, tiled=True),
        lax.psum_scatter(totals_grad[2], ("dp", "fsdp"), scatter_dimension=1, tiled=True),
        lax.psum_scatter(totals_grad[3], ("dp", "fsdp"), scatter_dimension=1, tiled=True),
        lax.psum_scatter(totals_grad[4], ("dp", "fsdp"), scatter_dimension=1, tiled=True),
        lax.psum_scatter(totals_grad[5], ("dp", "fsdp"), scatter_dimension=1, tiled=True),
        lax.psum_scatter(totals_grad[6], ("dp", "fsdp"), scatter_dimension=1, tiled=True),
        lax.psum_scatter(totals_grad[7], ("dp", "fsdp"), scatter_dimension=1, tiled=True),
        lax.psum_scatter(totals_grad[8], ("dp", "fsdp"), scatter_dimension=1, tiled=True),
        lax.psum_scatter(totals_grad[9], ("dp", "fsdp"), scatter_dimension=1, tiled=True),
        lax.psum_scatter(totals_grad[10], ("dp", "fsdp"), scatter_dimension=1, tiled=True),
        lax.psum_scatter(totals_grad[11], ("dp", "fsdp"), scatter_dimension=1, tiled=True),
    )
    backbone_out = jnp.concatenate(backbone_parts, axis=0)
    head_out = jnp.concatenate(head_parts, axis=0)
    grad_hidden = jnp.concatenate(hidden_parts, axis=0)
    grad_skip_tokens = jnp.concatenate(skip_parts, axis=0)
    return (
        contrast_loss,
        backbone_out,
        head_out,
        grad_hidden,
        grad_skip_tokens,
        totals_grad[0],
        totals_grad[1],
        totals_grad[2],
        totals_grad[3],
        totals_grad[4],
        totals_grad[5],
        totals_grad[6],
        totals_grad[7],
        totals_grad[8],
        totals_grad[9],
        totals_grad[10],
        totals_grad[11],
    )


def solution(mesh):
    return jax.shard_map(
        body,
        mesh=mesh,
        in_specs=(
            P("dp", "fsdp", None),
            P("dp", "fsdp", None),
            P("dp", "fsdp", None),
            P("dp", "fsdp", None),
            P("dp", None),
            P(),
            P(None, ("dp", "fsdp"), None),
            P(None, ("dp", "fsdp")),
            P(None, ("dp", "fsdp"), None),
            P(None, ("dp", "fsdp")),
            P(None, ("dp", "fsdp")),
            P(None, ("dp", "fsdp")),
            P(None, ("dp", "fsdp"), None),
            P(None, ("dp", "fsdp")),
            P(None, ("dp", "fsdp"), None),
            P(None, ("dp", "fsdp")),
            P(None, ("dp", "fsdp")),
            P(None, ("dp", "fsdp")),
        ),
        out_specs=(
            P(),
            P("dp", "fsdp", None),
            P("dp", "fsdp", None),
            P("dp", "fsdp", None),
            P("dp", "fsdp", None),
            P(None, ("dp", "fsdp"), None),
            P(None, ("dp", "fsdp")),
            P(None, ("dp", "fsdp"), None),
            P(None, ("dp", "fsdp")),
            P(None, ("dp", "fsdp")),
            P(None, ("dp", "fsdp")),
            P(None, ("dp", "fsdp"), None),
            P(None, ("dp", "fsdp")),
            P(None, ("dp", "fsdp"), None),
            P(None, ("dp", "fsdp")),
            P(None, ("dp", "fsdp")),
            P(None, ("dp", "fsdp")),
        ),
        check_vma=False,
    )
```

profile of v0, /device:TPU:0, one launch (start us, length us, event | category | flops | bytes accessed | tf_op | source)
XLA Modules:
  0.0 2431.3 jit_solution(5170081798279463252)
XLA Ops:
  9.6 76.8 %all-gather.55.cloned.1.call-done = bf16[2,768,2304]{2,1,0:T(8,128)(2,1)} async-done(((bf16[2,24,2304]{2,1,0:T(8,128)(2,1)}), bf16[2,768,2304]{2,1,0:T(8,128)(2,1)}) %all-gather.55.cloned.1.call-update) | async-done | bytes 7077904 | tf_op jit(solution)/shard_map/all_gather | solution.py:369
  90.6 65.6 %all-gather.21 = bf16[32,48,2]{1,2,0:T(2,128)(2,1)S(1)} all-gather(bf16[1,48,2]{1,2,0:T(2,128)(2,1)S(1)} %bitcast.809), channel_id=1, replica_groups=mesh['dp'=8,'fsdp'=4] {'dp','fsdp'}, dimensions={0}, use_global_device_ids=true | all-gather | bytes 6336 | tf_op jit(solution)/shard_map/all_gather | solution.py:370
  166.9 63.9 %all-gather.26 = bf16[32,24,2]{1,2,0:T(2,128)(2,1)S(1)} all-gather(bf16[1,24,2]{1,2,0:T(2,128)(2,1)S(1)} %bitcast.804), channel_id=1, replica_groups=mesh['dp'=8,'fsdp'=4] {'dp','fsdp'}, dimensions={0}, use_global_device_ids=true | all-gather | bytes 3168 | tf_op jit(solution)/shard_map/all_gather | solution.py:378
  230.9 65.2 %all-gather.25 = bf16[32,96,2]{1,2,0:T(2,128)(2,1)S(1)} all-gather(bf16[1,96,2]{1,2,0:T(2,128)(2,1)S(1)} %bitcast.810), channel_id=1, replica_groups=mesh['dp'=8,'fsdp'=4] {'dp','fsdp'}, dimensions={0}, use_global_device_ids=true | all-gather | bytes 12672 | tf_op jit(solution)/shard_map/all_gather | solution.py:376
  296.3 64.1 %all-gather.22 = bf16[32,24,2]{1,2,0:T(2,128)(2,1)S(1)} all-gather(bf16[1,24,2]{1,2,0:T(2,128)(2,1)S(1)} %bitcast.803), channel_id=1, replica_groups=mesh['dp'=8,'fsdp'=4] {'dp','fsdp'}, dimensions={0}, use_global_device_ids=true | all-gather | bytes 3168 | tf_op jit(solution)/shard_map/all_gather | solution.py:372
  360.5 65.5 %all-gather.24 = bf16[32,24,2]{1,2,0:T(2,128)(2,1)S(1)} all-gather(bf16[1,24,2]{1,2,0:T(2,128)(2,1)S(1)} %bitcast.805), channel_id=1, replica_groups=mesh['dp'=8,'fsdp'=4] {'dp','fsdp'}, dimensions={0}, use_global_device_ids=true | all-gather | bytes 3168 | tf_op jit(solution)/shard_map/all_gather | solution.py:374
  426.1 63.2 %all-gather.23 = bf16[32,24,2]{1,2,0:T(2,128)(2,1)S(1)} all-gather(bf16[1,24,2]{1,2,0:T(2,128)(2,1)S(1)} %bitcast.806), channel_id=1, replica_groups=mesh['dp'=8,'fsdp'=4] {'dp','fsdp'}, dimensions={0}, use_global_device_ids=true | all-gather | bytes 3168 | tf_op jit(solution)/shard_map/all_gather | solution.py:373
  489.4 65.7 %all-gather.28 = bf16[32,24,2]{1,2,0:T(2,128)(2,1)S(1)} all-gather(bf16[1,24,2]{1,2,0:T(2,128)(2,1)S(1)} %bitcast.807), channel_id=1, replica_groups=mesh['dp'=8,'fsdp'=4] {'dp','fsdp'}, dimensions={0}, use_global_device_ids=true | all-gather | bytes 3168 | tf_op jit(solution)/shard_map/all_gather | solution.py:380
  555.2 63.8 %all-gather.27 = bf16[32,24,2]{1,2,0:T(2,128)(2,1)S(1)} all-gather(bf16[1,24,2]{1,2,0:T(2,128)(2,1)S(1)} %bitcast.808), channel_id=1, replica_groups=mesh['dp'=8,'fsdp'=4] {'dp','fsdp'}, dimensions={0}, use_global_device_ids=true | all-gather | bytes 3168 | tf_op jit(solution)/shard_map/all_gather | solution.py:379
  645.4 7.8 fusion.126
  669.5 7.7 fusion.127
  678.5 11.6 multiply_convert_fusion.11
  700.3 11.5 multiply_convert_fusion.10
  726.5 40.8 %all-reduce.16 = (bf16[1536]{0:T(1024)(128)(2,1)S(1)}, bf16[3072]{0:T(1024)(128)(2,1)S(1)}, bf16[768]{0:T(1024)(128)(2,1)S(1)}, bf16[768]{0:T(1024)(128)(2,1)S(1...) all-reduce(bf16[1536]{0:T(1024)(128)(2,1)S(1)} %dynamic-update-slic, ...), channel_id=3, replica_groups=mesh['dp'=8,'fsdp'=4] {'dp','fsdp'}, use_global_device_ids=true, to_apply=%add | all-reduce | flops 9216 | bytes 36864
  782.0 5.7 gather_fusion.3
  787.6 8.9 copy.165
  811.6 7.1 fusion.125
  832.7 17.4 all-gather.83.cloned.1.call-done
  851.9 7.1 fusion.124
  861.0 11.7 multiply_convert_fusion.9
  872.7 10.2 multiply_convert_fusion.8
  890.1 5.5 convert_reduce_fusion.2
  897.8 5.1 convert_reduce_fusion
  910.3 9.0 fusion.92
  923.8 5.5 gather_fusion.2
  929.3 8.7 copy.164
  939.3 8.0 multiply_reduce_fusion.1
  947.3 6.8 multiply_convert_fusion.1
  962.4 7.6 all-gather.65.cloned.1.call-done
  971.9 63.9 %all-gather.69.cloned.1.call-done = bf16[1,3072,768]{2,1,0:T(8,128)(2,1)} async-done(((bf16[1,96,768]{2,1,0:T(8,128)(2,1)}), bf16[1,3072,768]{2,1,0:T(8,128)(2,1)}) %all-gather.69.cloned.1.call-update) | async-done | bytes 4718608 | tf_op jit(solution)/shard_map/all_gather | solution.py:347
  1035.8 65.2 %all-gather.67.cloned.1.call-done = bf16[1,768,3072]{2,1,0:T(8,128)(2,1)} async-done(((bf16[1,24,3072]{2,1,0:T(8,128)(2,1)}), bf16[1,768,3072]{2,1,0:T(8,128)(2,1)}) %all-gather.67.cloned.1.call-update) | async-done | bytes 4718608 | tf_op jit(solution)/shard_map/all_gather | solution.py:345
  1101.0 5.4 fusion.406
  1108.4 8.0 fusion.86
  1116.7 11.6 multiply_reduce_fusion.3
  1129.4 6.8 multiply_convert_fusion.3
  1139.6 79.7 %all-gather.20 = f32[32,4,768]{2,1,0:T(4,128)} all-gather(f32[1,4,768]{2,1,0:T(4,128)S(1)} %add_bitcast_fusion), channel_id=1, replica_groups=mesh['dp'=8,'fsdp'=4] {'dp','fsdp'}, dimensions={0}, use_global_device_ids=true | all-gather | bytes 405504 | tf_op jit(solution)/shard_map/all_gather | solution.py:353
  1230.3 6.2 convert_reduce_fusion.15
  1244.9 8.8 reduce-scatter.24.cloned.1.call-done
  1262.7 6.9 convert_reduce_fusion.3
  1281.5 7.8 fusion.83
  1294.4 8.0 fusion.89
  1302.4 8.3 multiply_reduce_fusion.2
  1310.8 6.9 multiply_convert_fusion.2
  1320.9 7.9 multiply_reduce_fusion
  1328.8 6.9 multiply_convert_fusion
  1340.9 5.7 convert_reduce_fusion.21
  1350.4 5.7 convert_reduce_fusion.17
  1358.0 5.5 convolution_bitcast_fusion.1
  1363.6 4.8 convolution_bitcast_fusion
  1372.2 25.2 %reduce-scatter.28.cloned.1.call-done = bf16[1,256,768]{1,2,0:T(8,128)(2,1)} async-done(((bf16[1,1024,768]{1,2,0:T(8,128)(2,1)}), bf16[1,256,768]{1,2,0:T(8,128)(2,1)}) %reduce-scatter.28.cloned.1.call-update) | async-done | bytes 393232 | tf_op jit(solution)/shard_map/reduce_scatter | solution.py:263
  1397.4 5.4 convolution_bitcast_fusion.11
  1402.8 31.1 %reduce-scatter.36.cloned.1.call-done = bf16[1,256,768]{1,2,0:T(8,128)(2,1)} async-done(((bf16[1,1024,768]{1,2,0:T(8,128)(2,1)}), bf16[1,256,768]{1,2,0:T(8,128)(2,1)}) %reduce-scatter.36.cloned.1.call-update) | async-done | bytes 393232 | tf_op jit(solution)/shard_map/reduce_scatter | solution.py:263
  1436.5 10.6 maximum_add_fusion.2
  1447.1 21.8 copy.194
  1483.2 5.3 convolution_bitcast_fusion.7
  1488.5 11.5 maximum_add_fusion
  1507.5 5.0 convolution_bitcast_fusion.3
  1512.5 11.4 maximum_add_fusion.1
  1554.2 39.9 %all-reduce.15 = (f32[2,768]{1,0:T(2,128)S(1)}, f32[2,768]{1,0:T(2,128)S(1)}, f32[2,768]{1,0:T(2,128)S(1)}, f32[2,768]{1,0:T(2,128)S(1)}, f32[2,768]{1,0:T(2,128)S(1)}, /*index=5*/f32[2,768]{1,0:T(2,128)S(1)}) all-reduce(f32[2,768]{1,0:T(2,128)S(1)} %maximum_add_fusion.6, ...), channel_id=33, replica_groups=mesh['dp'=8,'fsdp'=4] {'dp','fsdp'}, use_global_device_ids=true, to_apply=%region_80.81.clone | all-reduce | flops 9216 | bytes 73728
  1611.6 23.1 reduce-scatter.46.cloned.1.call-done
  1636.1 250.5 %all-reduce.19.cloned.1.call-done = f32[2,768,2304]{2,0,1:T(2,128)} async-done(((f32[2,768,2304]{2,0,1:T(2,128)}), f32[2,768,2304]{2,0,1:T(2,128)}) %all-reduce.19.cloned.1.call-update) | async-done | bytes 14155792
  1888.4 111.2 %reduce-scatter.40.cloned.1.call-done = f32[2,24,768]{2,1,0:T(8,128)} async-done(((f32[2,768,768]{2,1,0:T(8,128)}), f32[2,24,768]{2,1,0:T(8,128)}) %reduce-scatter.40.cloned.1.call-update) | async-done | bytes 147472 | tf_op jit(solution)/shard_map/reduce_scatter | solution.py:444
  1999.7 212.3 %reduce-scatter.42.cloned.1.call-done = f32[2,24,3072]{2,1,0:T(8,128)} async-done(((f32[2,768,3072]{2,1,0:T(8,128)}), f32[2,24,3072]{2,1,0:T(8,128)}) %reduce-scatter.42.cloned.1.call-update) | async-done | bytes 589840 | tf_op jit(solution)/shard_map/reduce_scatter | solution.py:448
  2212.0 212.0 %reduce-scatter.44.cloned.1.call-done = f32[2,96,768]{2,1,0:T(8,128)} async-done(((f32[2,3072,768]{2,1,0:T(8,128)}), f32[2,96,768]{2,1,0:T(8,128)}) %reduce-scatter.44.cloned.1.call-update) | async-done | bytes 589840 | tf_op jit(solution)/shard_map/reduce_scatter | solution.py:450
  (880 shorter events, 309.0 us)
Async XLA Ops:
  7.2 79.3 %all-gather.55.cloned.1.call-start = ((), (), s32[]{:S(2)}) async-start(), calls=%async_computation.16 | async-start | bytes 7299072 | tf_op jit(solution)/shard_map/all_gather | solution.py:369
  7.9 616.3 %all-gather.63.cloned.1.call-start = ((), (), s32[]{:S(2)}) async-start(), calls=%async_computation.31 | async-start | bytes 3649536 | tf_op jit(solution)/shard_map/all_gather | solution.py:339
  9.5 81.0 %copy-start.216 = (bf16[2,48]{1,0:T(2,128)(2,1)S(1)}, bf16[2,48]{1,0:T(2,128)(2,1)}, u32[]{:S(2)}) copy-start(bf16[2,48]{1,0:T(2,128)(2,1)} %param.25) | copy-start | bytes 580
  9.6 146.8 %copy-start.54 = (bf16[2,256,768]{2,1,0:T(8,128)(2,1)S(1)}, bf16[2,256,768]{2,1,0:T(8,128)(2,1)}, u32[]{:S(2)}) copy-start(bf16[2,256,768]{2,1,0:T(8,128)(2,1)} %param.18) | copy-start | bytes 2359300
  9.6 621.8 %all-gather.77.cloned.1.call-start = ((), (), s32[]{:S(2)}) async-start(), calls=%async_computation.38 | async-start | bytes 1966080 | tf_op jit(solution)/shard_map/all_gather | solution.py:174
  90.5 553.1 %all-gather.75.cloned.1.call-start = ((), (), s32[]{:S(2)}) async-start(), calls=%async_computation.37 | async-start | bytes 1966080 | tf_op jit(solution)/shard_map/all_gather | solution.py:175
  159.6 136.6 %copy-start.205 = (bf16[2,24]{1,0:T(2,128)(2,1)S(1)}, bf16[2,24]{1,0:T(2,128)(2,1)}, u32[]{:S(2)}) copy-start(bf16[2,24]{1,0:T(2,128)(2,1)} %param.27) | copy-start | bytes 292
  161.4 199.1 %copy-start.208 = (bf16[2,24]{1,0:T(2,128)(2,1)S(1)}, bf16[2,24]{1,0:T(2,128)(2,1)}, u32[]{:S(2)}) copy-start(bf16[2,24]{1,0:T(2,128)(2,1)} %param.29) | copy-start | bytes 292
  161.4 264.7 %copy-start.210 = (bf16[2,24]{1,0:T(2,128)(2,1)S(1)}, bf16[2,24]{1,0:T(2,128)(2,1)}, u32[]{:S(2)}) copy-start(bf16[2,24]{1,0:T(2,128)(2,1)} %param.28) | copy-start | bytes 292
  161.4 328.0 %copy-start.212 = (bf16[2,24]{1,0:T(2,128)(2,1)S(1)}, bf16[2,24]{1,0:T(2,128)(2,1)}, u32[]{:S(2)}) copy-start(bf16[2,24]{1,0:T(2,128)(2,1)} %param.35) | copy-start | bytes 292
  161.4 393.8 %copy-start.214 = (bf16[2,24]{1,0:T(2,128)(2,1)S(1)}, bf16[2,24]{1,0:T(2,128)(2,1)}, u32[]{:S(2)}) copy-start(bf16[2,24]{1,0:T(2,128)(2,1)} %param.34) | copy-start | bytes 292
  161.4 457.7 %copy-start.128 = (s32[2,8]{1,0:T(2,128)S(1)}, s32[2,8]{1,0:T(2,128)}, u32[]{:S(2)}) copy-start(s32[2,8]{1,0:T(2,128)} %param.22) | copy-start | bytes 196
  161.4 462.8 %copy-start.55 = (bf16[2,256,768]{2,1,0:T(8,128)(2,1)S(1)}, bf16[2,256,768]{2,1,0:T(8,128)(2,1)}, u32[]{:S(2)}) copy-start(bf16[2,256,768]{2,1,0:T(8,128)(2,1)} %param.18) | copy-start | bytes 2359300
  161.5 491.7 %all-gather.57.cloned.1.call-start = ((), (), s32[]{:S(2)}) async-start(), calls=%async_computation.17 | async-start | bytes 2433024 | tf_op jit(solution)/shard_map/all_gather | solution.py:371
  162.1 493.3 %all-gather.73.cloned.1.call-start = ((), (), s32[]{:S(2)}) async-start(), calls=%async_computation.36 | async-start | bytes 1966080 | tf_op jit(solution)/shard_map/all_gather | solution.py:174
  164.0 503.7 %all-gather.71.cloned.1.call-start = ((), (), s32[]{:S(2)}) async-start(), calls=%async_computation.35 | async-start | bytes 1966080 | tf_op jit(solution)/shard_map/all_gather | solution.py:175
  164.8 513.7 %all-gather.59.cloned.1.call-start = ((), (), s32[]{:S(2)}) async-start(), calls=%async_computation.18 | async-start | bytes 9732096 | tf_op jit(solution)/shard_map/all_gather | solution.py:375
  165.6 524.5 %all-gather.61.cloned.1.call-start = ((), (), s32[]{:S(2)}) async-start(), calls=%async_computation.19 | async-start | bytes 9732096 | tf_op jit(solution)/shard_map/all_gather | solution.py:377
  166.3 612.5 %all-gather.49.cloned.1.call-start = ((), (), s32[]{:S(2)}) async-start(), calls=%async_computation.13 | async-start | bytes 3932160 | tf_op jit(solution)/shard_map/all_gather | solution.py:131
  166.9 615.1 %all-gather.53.cloned.1.call-start = ((), (), s32[]{:S(2)}) async-start(), calls=%async_computation.15 | async-start | bytes 3932160 | tf_op jit(solution)/shard_map/all_gather | solution.py:129
  620.4 198.3 %copy-start.197 = (pred[256]{0:T(512)(128)(4,1)}, pred[256]{0:T(512)(128)(4,1)S(1)}, u32[]{:S(2)}) copy-start(pred[256]{0:T(512)(128)(4,1)S(1)} %get-tuple-element.152) | copy-start | bytes 772
  622.5 89.4 %copy-start.115 = (f32[768]{0:T(1024)}, f32[768]{0:T(1024)S(1)}, u32[]{:S(2)}) copy-start(f32[768]{0:T(1024)S(1)} %get-tuple-element.302) | copy-start | bytes 9220
  622.5 89.4 %copy-start.129 = (f32[768]{0:T(1024)}, f32[768]{0:T(1024)S(1)}, u32[]{:S(2)}) copy-start(f32[768]{0:T(1024)S(1)} %get-tuple-element.149) | copy-start | bytes 9220
  623.1 236.0 %copy-start.137 = (f32[768]{0:T(1024)}, f32[768]{0:T(1024)S(1)}, u32[]{:S(2)}) copy-start(f32[768]{0:T(1024)S(1)} %get-tuple-element.304) | copy-start | bytes 9220
  623.1 236.0 %copy-start.142 = (f32[768]{0:T(1024)}, f32[768]{0:T(1024)S(1)}, u32[]{:S(2)}) copy-start(f32[768]{0:T(1024)S(1)} %get-tuple-element.143) | copy-start | bytes 9220
  630.0 167.7 %all-gather.81.cloned.1.call-start = ((), (), s32[]{:S(2)}) async-start(), calls=%async_computation.40 | async-start | bytes 1966080 | tf_op jit(solution)/shard_map/all_gather | solution.py:174
  694.4 124.3 %copy-start.15 = (f32[256,768]{1,0:T(8,128)}, f32[256,768]{1,0:T(8,128)S(1)}, u32[]{:S(2)}) copy-start(f32[256,768]{1,0:T(8,128)S(1)} %get-tuple-element.256) | copy-start | bytes 2359300
  694.5 124.3 %copy-start.150 = (f32[256]{0:T(256)}, f32[256]{0:T(256)S(1)}, u32[]{:S(2)}) copy-start(f32[256]{0:T(256)S(1)} %broadcast_multiply_fusion.22) | copy-start | bytes 3076
  694.7 124.0 %copy-start.175 = (f32[256]{0:T(256)}, f32[256]{0:T(256)S(1)}, u32[]{:S(2)}) copy-start(f32[256]{0:T(256)S(1)} %add_rsqrt_fusion.6) | copy-start | bytes 3076
  700.3 109.6 %all-gather.79.cloned.1.call-start = ((), (), s32[]{:S(2)}) async-start(), calls=%async_computation.39 | async-start | bytes 1966080 | tf_op jit(solution)/shard_map/all_gather | solution.py:175
  716.3 142.8 %copy-start.152 = (f32[256]{0:T(256)}, f32[256]{0:T(256)S(1)}, u32[]{:S(2)}) copy-start(f32[256]{0:T(256)S(1)} %broadcast_multiply_fusion.20) | copy-start | bytes 3076
  716.6 142.5 %copy-start.177 = (f32[256]{0:T(256)}, f32[256]{0:T(256)S(1)}, u32[]{:S(2)}) copy-start(f32[256]{0:T(256)S(1)} %add_rsqrt_fusion.4) | copy-start | bytes 3076
  721.8 98.8 %all-gather.85.cloned.1.call-start = ((), (), s32[]{:S(2)}) async-start(), calls=%async_computation.42 | async-start | bytes 1966080 | tf_op jit(solution)/shard_map/all_gather | solution.py:174
  723.8 126.3 %all-gather.83.cloned.1.call-start = ((), (), s32[]{:S(2)}) async-start(), calls=%async_computation.41 | async-start | bytes 1966080 | tf_op jit(solution)/shard_map/all_gather | solution.py:175
  724.4 199.4 %all-gather.51.cloned.1.call-start = ((), (), s32[]{:S(2)}) async-start(), calls=%async_computation.14 | async-start | bytes 3932160 | tf_op jit(solution)/shard_map/all_gather | solution.py:130
  769.7 200.3 %all-gather.65.cloned.1.call-start = ((), (), s32[]{:S(2)}) async-start(), calls=%async_computation.32 | async-start | bytes 1216512 | tf_op jit(solution)/shard_map/all_gather | solution.py:341
  770.4 265.3 %all-gather.69.cloned.1.call-start = ((), (), s32[]{:S(2)}) async-start(), calls=%async_computation.34 | async-start | bytes 4866048 | tf_op jit(solution)/shard_map/all_gather | solution.py:347
  771.2 329.8 %all-gather.67.cloned.1.call-start = ((), (), s32[]{:S(2)}) async-start(), calls=%async_computation.33 | async-start | bytes 4866048 | tf_op jit(solution)/shard_map/all_gather | solution.py:345
  772.0 467.3 %reduce-scatter.34.cloned.1.call-start = ((), (), s32[]{:S(2)}) async-start(), calls=%async_computation.25 | async-start | bytes 1966080 | tf_op jit(solution)/shard_map/reduce_scatter | solution.py:269
  819.5 83.4 %copy-start.180 = (f32[256]{0:T(256)}, f32[256]{0:T(256)S(1)}, u32[]{:S(2)}) copy-start(f32[256]{0:T(256)S(1)} %broadcast_multiply_fusion.19) | copy-start | bytes 3076
  820.6 82.3 %copy-start.192 = (f32[256]{0:T(256)}, f32[256]{0:T(256)S(1)}, u32[]{:S(2)}) copy-start(f32[256]{0:T(256)S(1)} %add_rsqrt_fusion.3) | copy-start | bytes 3076
  907.1 332.2 %copy-start.29 = (f32[256,768]{1,0:T(8,128)}, f32[256,768]{1,0:T(8,128)S(1)}, u32[]{:S(2)}) copy-start(f32[256,768]{1,0:T(8,128)S(1)} %get-tuple-element.179) | copy-start | bytes 2359300
  919.3 319.9 %reduce-scatter.32.cloned.1.call-start = ((), (), s32[]{:S(2)}) async-start(), calls=%async_computation.24 | async-start | bytes 1966080 | tf_op jit(solution)/shard_map/reduce_scatter | solution.py:263
  957.3 287.7 %reduce-scatter.26.cloned.1.call-start = ((), (), s32[]{:S(2)}) async-start(), calls=%async_computation.21 | async-start | bytes 1966080 | tf_op jit(solution)/shard_map/reduce_scatter | solution.py:269
  957.8 143.2 %copy-start.146 = (f32[3072]{0:T(1024)S(1)}, f32[3072]{0:T(1024)}, u32[]{:S(2)}) copy-start(f32[3072]{0:T(1024)} %convert_element_type.885) | copy-start | bytes 36868
  957.8 143.2 %copy-start.159 = (f32[768]{0:T(1024)S(1)}, f32[768]{0:T(1024)}, u32[]{:S(2)}) copy-start(f32[768]{0:T(1024)} %convert_element_type.886) | copy-start | bytes 9220
  957.8 143.2 %copy-start.160 = (f32[768]{0:T(1024)S(1)}, f32[768]{0:T(1024)}, u32[]{:S(2)}) copy-start(f32[768]{0:T(1024)} %convert_element_type.884) | copy-start | bytes 9220
  957.8 143.2 %copy-start.161 = (f32[768]{0:T(1024)S(1)}, f32[768]{0:T(1024)}, u32[]{:S(2)}) copy-start(f32[768]{0:T(1024)} %convert_element_type.883) | copy-start | bytes 9220
  971.9 134.5 %copy-start.63 = (f32[256,768]{1,0:T(8,128)S(1)}, f32[256,768]{1,0:T(8,128)}, u32[]{:S(2)}) copy-start(f32[256,768]{1,0:T(8,128)} %get-tuple-element.183) | copy-start | bytes 2359300
  1116.4 137.3 %reduce-scatter.24.cloned.1.call-start = ((), (), s32[]{:S(2)}) async-start(), calls=%async_computation.20 | async-start | bytes 1966080 | tf_op jit(solution)/shard_map/reduce_scatter | solution.py:263
  1139.4 84.6 %copy-start.26 = (s32[128]{0:T(128)S(1)}, s32[128]{0:T(128)}, u32[]{:S(2)}) copy-start(s32[128]{0:T(128)} %or_bitcast_fusion) | copy-start | bytes 1540
  1139.4 86.5 %copy-start.201 = (s32[128]{0:T(128)S(1)}, s32[128]{0:T(128)}, u32[]{:S(2)}) copy-start(s32[128]{0:T(128)} %param.23) | copy-start | bytes 1540
  1139.4 229.0 %reduce-scatter.30.cloned.1.call-start = ((), (), s32[]{:S(2)}) async-start(), calls=%async_computation.23 | async-start | bytes 1966080 | tf_op jit(solution)/shard_map/reduce_scatter | solution.py:269
  1289.4 80.3 %reduce-scatter.38.cloned.1.call-start = ((), (), s32[]{:S(2)}) async-start(), calls=%async_computation.27 | async-start | bytes 1966080 | tf_op jit(solution)/shard_map/reduce_scatter | solution.py:269
  1302.4 95.1 %reduce-scatter.28.cloned.1.call-start = ((), (), s32[]{:S(2)}) async-start(), calls=%async_computation.22 | async-start | bytes 1966080 | tf_op jit(solution)/shard_map/reduce_scatter | solution.py:263
  1320.8 113.0 %reduce-scatter.36.cloned.1.call-start = ((), (), s32[]{:S(2)}) async-start(), calls=%async_computation.26 | async-start | bytes 1966080 | tf_op jit(solution)/shard_map/reduce_scatter | solution.py:263
  1339.1 263.1 %reduce-scatter.48.cloned.1.call-start = ((), (), s32[]{:S(2)}) async-start(), calls=%async_computation.44 | async-start | bytes 1622016
  1368.4 266.4 %reduce-scatter.46.cloned.1.call-start = ((), (), s32[]{:S(2)}) async-start(), calls=%async_computation.43 | async-start | bytes 811008
  1372.2 514.4 %all-reduce.19.cloned.1.call-start = ((), (), s32[]{:S(2)}) async-start(), calls=%async_computation.45 | async-start | bytes 28311552
  1468.9 530.8 %reduce-scatter.40.cloned.1.call-start = ((), (), s32[]{:S(2)}) async-start(), calls=%async_computation.28 | async-start | bytes 4866048 | tf_op jit(solution)/shard_map/reduce_scatter | solution.py:444
  1475.6 736.4 %reduce-scatter.42.cloned.1.call-start = ((), (), s32[]{:S(2)}) async-start(), calls=%async_computation.29 | async-start | bytes 19464192 | tf_op jit(solution)/shard_map/reduce_scatter | solution.py:448
  1500.0 924.0 %reduce-scatter.44.cloned.1.call-start = ((), (), s32[]{:S(2)}) async-start(), calls=%async_computation.30 | async-start | bytes 19464192 | tf_op jit(solution)/shard_map/reduce_scatter | solution.py:450
  1523.9 76.2 %copy-start.62 = (f32[256,768]{1,0:T(8,128)S(1)}, f32[256,768]{1,0:T(8,128)}, u32[]{:S(2)}) copy-start(f32[256,768]{1,0:T(8,128)} %copy-done.61) | copy-start | bytes 2359300
  1525.1 75.8 %copy-start.73 = (f32[256,768]{1,0:T(8,128)S(1)}, f32[256,768]{1,0:T(8,128)}, u32[]{:S(2)}) copy-start(f32[256,768]{1,0:T(8,128)} %copy-done.72) | copy-start | bytes 2359300
  (210 other events, 1723.1 us)
Sparse Core Ops, SparseCore 0:
  11.1 75.3 all-gather.54
  89.8 58.7 all-gather.62
  150.8 36.0 all-gather.76
  188.9 36.0 all-gather.74
  227.9 56.2 all-gather.56
  286.2 36.1 all-gather.72
  324.5 36.0 all-gather.70
  363.6 80.7 all-gather.58
  447.6 80.6 all-gather.60
  529.6 62.2 all-gather.48
  630.1 61.5 all-gather.52
  700.4 35.2 all-gather.80
  737.8 36.4 all-gather.78
  775.8 36.3 all-gather.84
  814.2 35.9 all-gather.82
  852.1 62.3 all-gather.50
  917.2 52.7 all-gather.64
  973.3 62.4 all-gather.68
  1038.6 62.3 all-gather.66
  1103.7 34.0 reduce-scatter.33
  1140.2 37.7 reduce-scatter.31
  1180.2 37.2 reduce-scatter.25
  1219.8 33.9 reduce-scatter.23
  1289.5 34.2 reduce-scatter.29
  1326.7 34.2 reduce-scatter.37
  1363.1 34.2 reduce-scatter.27
  1399.6 34.2 reduce-scatter.35
  1439.1 95.9 reduce-scatter.47
  1540.2 94.4 reduce-scatter.45
  1640.9 245.6 all-reduce.18
  1892.7 106.9 reduce-scatter.39
  2007.8 204.1 reduce-scatter.41
  2220.0 203.9 reduce-scatter.43
where the time goes:
time: 2440 us; the launch traced here: 2430 us
  waiting for transfers between devices  1110 us (45%)
  blocking collectives  677 us (28%)
  matrix products  337 us (14%)
  local copies, waits for them, and re-layouts  162 us (7%)
  other arithmetic  123 us (5%)
    unnamed x36, waiting for transfers between devices  278 us
    reduce_scatter x1, waiting for transfers between devices, body(): lax.psum_scatter(totals_grad[6], ('dp', 'fsdp'), scatter_dimension=1, til...  212 us
    reduce_scatter x1, waiting for transfers between devices, body(): lax.psum_scatter(totals_grad[8], ('dp', 'fsdp'), scatter_dimension=1, til...  212 us
    reduce_scatter x1, waiting for transfers between devices, body(): lax.psum_scatter(totals_grad[2], ('dp', 'fsdp'), scatter_dimension=1, til...  111 us
    dot_general x20, matrix products, matrix_product(): return jnp.dot(first_op, second_op, preferred_element_type=jnp.float32)  86.6 us
    unnamed x2, blocking collectives  80.7 us
    all_gather x1, blocking collectives, body(): lax.all_gather(cls_own, ('dp', 'fsdp'), axis=0, tiled=True)  79.7 us
    all_gather x1, waiting for transfers between devices, body(): lax.all_gather(qkv_weight, ('dp', 'fsdp'), axis=1, tiled=True)  76.8 us
  transfers between devices with their start and end apart: 33, of which 13 were waited for; matrix products, arithmetic and copies ran while one was open for 23% of the time, Pallas kernels for 0%

commit v1 on v0

v1 whole, which is shorter than its diff:
```python
import functools

import jax
import jax.numpy as jnp
from jax import lax
from jax.experimental import pallas as pl
from jax.experimental.pallas import tpu as pltpu
from jax.sharding import PartitionSpec as P

HEADS = 12
HEAD_DIM = 64
SEGS = 8
CORES = 2

EPS = 1e-12
SOFTMAX_HEAT = 0.02
NEGATIVE = -1e30
FULL_PRECISION = lax.Precision.HIGHEST
SCALING = HEAD_DIM ** (-0.5)
PAIR = 2 * HEAD_DIM
BF = jnp.bfloat16
F32 = jnp.float32


def layer_norm(residual, norm_gain, norm_shift):
    average = jnp.mean(residual, axis=-1, keepdims=True)
    centred = residual - average
    inv_std = lax.rsqrt(jnp.mean(centred * centred, axis=-1, keepdims=True) + EPS)
    normed = centred * inv_std
    return (normed * norm_gain + norm_shift, normed, inv_std)


def norm_back(upstream, normed, inv_std, norm_gain):
    scaled = upstream * norm_gain
    return inv_std * (
        scaled
        - jnp.mean(scaled, axis=-1, keepdims=True)
        - normed * jnp.mean(scaled * normed, axis=-1, keepdims=True)
    )


def gelu_both(v):
    phi_cdf = 0.5 * (1.0 + lax.erf(v * 0.7071067811865476))
    phi_pdf = jnp.exp(-0.5 * v * v) * 0.3989422804014327
    return v * phi_cdf, phi_cdf + v * phi_pdf


def matrix_product(first_op, second_op):
    return jnp.dot(first_op, second_op, preferred_element_type=F32)


def left_t(first_op, second_op):
    return lax.dot_general(
        first_op, second_op, (((0,), (0,)), ((), ())), preferred_element_type=F32
    )


def right_t(first_op, second_op):
    return lax.dot_general(
        first_op, second_op, (((1,), (1,)), ((), ())), preferred_element_type=F32
    )


def column_sum(inputs):
    return jnp.sum(inputs.astype(F32), axis=0)


def n_bits(count):
    return count.bit_length() - 1


class Grid:
    def __init__(self, rows_dev):
        self.n_dp = lax.axis_size("dp")
        self.n_f = lax.axis_size("fsdp")
        self.f_bits = n_bits(self.n_f)
        self.d_bits = n_bits(self.n_dp)
        self.dp = lax.axis_index("dp")
        self.f = lax.axis_index("fsdp")
        self.rows_dev = rows_dev
        self.chips_per_row = self.n_f // (CORES * rows_dev)
        self.members = CORES * self.chips_per_row
        self.core = self.dp % CORES
        self.row_in_group = self.f // self.chips_per_row
        self.member = (self.f % self.chips_per_row) * CORES + self.core

    def my_bit(self, bit):
        if bit < self.f_bits:
            return (self.f >> bit) & 1
        return (self.dp >> (bit - self.f_bits)) & 1

    def swap(self, x, bit):
        if bit < self.f_bits:
            return lax.ppermute(x, "fsdp", [(i, i ^ (1 << bit)) for i in range(self.n_f)])
        flip = 1 << (bit - self.f_bits)
        return lax.ppermute(x, "dp", [(i, i ^ flip) for i in range(self.n_dp)])

    def gather_order(self, turned):
        upper = list(range(self.f_bits + 1, self.f_bits + self.d_bits))
        if not turned:
            upper = upper[::-1]
        return list(range(self.f_bits)) + upper + [self.f_bits]

    def gather(self, x, order):
        have, out = [], x
        for bit in order:
            other = self.swap(out, bit)
            mine = self.my_bit(bit) == 0
            place = sum(1 for b in have if b > bit)
            low = jnp.where(mine, out, other)
            high = jnp.where(mine, other, out)
            out = jnp.stack([low, high], axis=place)
            have.append(bit)
        return out.reshape((-1,) + x.shape[1:])

    def scatter(self, x, order, wire=BF):
        left = sorted(order, reverse=True)
        tail = (x.shape[0] >> len(order),) + x.shape[1:]
        out = x.reshape((2,) * len(order) + tail)
        for bit in reversed(order):
            place = left.index(bit)
            low = lax.index_in_dim(out, 0, place, keepdims=False)
            high = lax.index_in_dim(out, 1, place, keepdims=False)
            mine = self.my_bit(bit) == 0
            kept = jnp.where(mine, low, high)
            sent = jnp.where(mine, high, low).astype(wire)
            got = self.swap(sent, bit)
            out = kept.astype(F32) + got.astype(F32)
            left.remove(bit)
            if left:
                out = out.astype(wire)
        return out

    def source(self, k):
        pairs = []
        for d in range(self.n_dp):
            for f in range(self.n_f):
                base, c = d // CORES * CORES, d % CORES
                b = (f + k) % self.rows_dev
                g = f // self.rows_dev
                row = self.rows_dev * c + b
                target_f = row * self.chips_per_row + g // CORES
                target_d = base + g % CORES
                pairs.append((d * self.n_f + f, target_d * self.n_f + target_f))
        return pairs

    def to_rows(self, x):
        got = []
        for k in range(self.rows_dev):
            block = lax.dynamic_index_in_dim(x, (self.f + k) % self.rows_dev, 0, keepdims=False)
            got.append(lax.ppermute(block, ("dp", "fsdp"), self.source(k)))
        got = jnp.stack(got)
        b = self.row_in_group % self.rows_dev
        return jnp.concatenate(
            [
                lax.dynamic_index_in_dim(got, (b - p) % self.rows_dev, 0, keepdims=False)
                for p in range(self.rows_dev)
            ]
        )

    def from_rows(self, y):
        parts = y.reshape((self.rows_dev, -1) + y.shape[1:])
        b = self.row_in_group % self.rows_dev
        got = []
        for k in range(self.rows_dev):
            block = lax.dynamic_index_in_dim(parts, (b - k) % self.rows_dev, 0, keepdims=False)
            back = [(t, s) for s, t in self.source(k)]
            got.append(lax.ppermute(block, ("dp", "fsdp"), back))
        got = jnp.stack(got)
        return jnp.stack(
            [
                lax.dynamic_index_in_dim(got, (row - self.f) % self.rows_dev, 0, keepdims=False)
                for row in range(self.rows_dev)
            ]
        )

    def shift_pairs(self, shift):
        pairs = []
        for d in range(self.n_dp):
            for f in range(self.n_f):
                g = (f % self.chips_per_row) * CORES + d % CORES
                t = (g + shift) % self.members
                td = d // CORES * CORES + t % CORES
                tf = f // self.chips_per_row * self.chips_per_row + t // CORES
                pairs.append((d * self.n_f + f, td * self.n_f + tf))
        return pairs

    def to_member(self, x, shift):
        return lax.ppermute(x, ("dp", "fsdp"), self.shift_pairs(shift))


def dot_nt(a, b):
    return lax.dot_general(a, b, (((1,), (1,)), ((), ())), preferred_element_type=F32)


def dot_nn(a, b):
    return lax.dot_general(a, b, (((1,), (0,)), ((), ())), preferred_element_type=F32)


def dot_tn(a, b):
    return lax.dot_general(a, b, (((0,), (0,)), ((), ())), preferred_element_type=F32)


def head_only(x, head):
    lane = lax.broadcasted_iota(jnp.int32, x.shape, 1)
    keep = (lane >= HEAD_DIM) if head else (lane < HEAD_DIM)
    return jnp.where(keep, x, jnp.zeros_like(x))


def attend_kernel(chunks, q_step, *refs):
    q_ref = refs[0]
    k_refs = refs[1 : 1 + chunks]
    v_refs = refs[1 + chunks : 1 + 2 * chunks]
    seg_q_ref, seg_k_ref, o_ref, lse_ref = refs[1 + 2 * chunks :]
    tokens = q_ref.shape[0]
    for q0 in range(0, tokens, q_step):
        q = q_ref[q0 : q0 + q_step, :]
        seg_q = seg_q_ref[:, q0 : q0 + q_step]
        halves = []
        for head in range(2):
            q_head = head_only(q, head)
            scores = []
            for c in range(chunks):
                s = dot_nt(k_refs[c][...], q_head) * SCALING
                seg_k = seg_k_ref[c * tokens : (c + 1) * tokens, :]
                scores.append(jnp.where(seg_k == seg_q, s, NEGATIVE))
            highest = functools.reduce(
                jnp.maximum, [jnp.max(s, axis=0, keepdims=True) for s in scores]
            )
            powers = [jnp.exp(s - highest) for s in scores]
            total = functools.reduce(
                jnp.add, [jnp.sum(p, axis=0, keepdims=True) for p in powers]
            )
            inverse = 1.0 / total
            mixed = functools.reduce(
                jnp.add,
                [dot_tn(v_refs[c][...], (powers[c] * inverse).astype(BF)) for c in range(chunks)],
            )
            halves.append(mixed[head * HEAD_DIM : (head + 1) * HEAD_DIM, :])
            lse_ref[0, head : head + 1, q0 : q0 + q_step] = highest + jnp.log(total)
        both = jnp.concatenate(halves, axis=0)
        o_ref[q0 : q0 + q_step, :] = both.T.astype(BF)


def attend_back_kernel(chunks, q_step, *refs):
    q_ref = refs[0]
    k_refs = refs[1 : 1 + chunks]
    v_refs = refs[1 + chunks : 1 + 2 * chunks]
    do_ref, lse_ref, seg_q_ref, seg_k_ref = refs[1 + 2 * chunks : 5 + 2 * chunks]
    dq_ref, own_ref = refs[5 + 2 * chunks : 7 + 2 * chunks]
    other_refs = refs[7 + 2 * chunks : 6 + 3 * chunks]
    acc_ref = refs[6 + 3 * chunks]
    tokens = q_ref.shape[0]
    first = True
    for q0 in range(0, tokens, q_step):
        q = q_ref[q0 : q0 + q_step, :]
        do = do_ref[q0 : q0 + q_step, :]
        seg_q = seg_q_ref[:, q0 : q0 + q_step]
        halves = []
        for head in range(2):
            q_head = head_only(q, head)
            do_head = head_only(do, head)
            lse = lse_ref[0, head : head + 1, q0 : q0 + q_step]
            probs, d_probs = [], []
            for c in range(chunks):
                s = dot_nt(k_refs[c][...], q_head) * SCALING
                seg_k = seg_k_ref[c * tokens : (c + 1) * tokens, :]
                s = jnp.where(seg_k == seg_q, s, NEGATIVE)
                probs.append(jnp.exp(s - lse))
                d_probs.append(dot_nt(v_refs[c][...], do_head))
            offset = functools.reduce(
                jnp.add,
                [jnp.sum(p * d, axis=0, keepdims=True) for p, d in zip(probs, d_probs)],
            )
            dq_t = None
            for c in range(chunks):
                ds = (probs[c] * (d_probs[c] - offset)).astype(BF)
                dk = dot_nn(ds, q_head) * SCALING
                dv = dot_nn(probs[c].astype(BF), do_head)
                term = dot_tn(k_refs[c][...], ds)
                dq_t = term if dq_t is None else dq_t + term
                if first:
                    acc_ref[c, 0] = dk
                    acc_ref[c, 1] = dv
                else:
                    acc_ref[c, 0] += dk
                    acc_ref[c, 1] += dv
            first = False
            halves.append(dq_t[head * HEAD_DIM : (head + 1) * HEAD_DIM, :])
        both = jnp.concatenate(halves, axis=0) * SCALING
        dq_ref[q0 : q0 + q_step, :] = both.T.astype(BF)
    own_ref[...] = acc_ref[0]
    for c in range(1, chunks):
        other_refs[c - 1][...] = acc_ref[c].astype(BF)


def attention_specs(qkv, others):
    tokens = qkv.shape[0]
    pairs = HEADS // 2
    block = (tokens, PAIR)
    at = lambda offset: pl.BlockSpec(block, lambda i, offset=offset: (0, offset + i))
    operands = [qkv, qkv] + others + [qkv] + others
    specs = (
        [at(0), at(pairs)]
        + [at(0) for _ in others]
        + [at(2 * pairs)]
        + [at(pairs) for _ in others]
    )
    return operands, specs, tokens, pairs


def attend(qkv, others, seg_q, seg_k):
    operands, specs, tokens, pairs = attention_specs(qkv, others)
    chunks = 1 + len(others)
    length = tokens * chunks
    whole = lambda shape: pl.BlockSpec(shape, lambda i: (0,) * len(shape))
    return pl.pallas_call(
        functools.partial(attend_kernel, chunks, min(256, tokens)),
        grid=(pairs,),
        in_specs=specs + [whole((1, tokens)), whole((length, 1))],
        out_specs=[
            pl.BlockSpec((tokens, PAIR), lambda i: (0, i)),
            pl.BlockSpec((1, 2, tokens), lambda i: (i, 0, 0)),
        ],
        out_shape=[
            jax.ShapeDtypeStruct((tokens, HEADS * HEAD_DIM), BF),
            jax.ShapeDtypeStruct((pairs, 2, tokens), F32),
        ],
        compiler_params=pltpu.CompilerParams(vmem_limit_bytes=40 * 2**20),
        cost_estimate=pl.CostEstimate(
            flops=16 * tokens * length * HEADS * HEAD_DIM,
            bytes_accessed=8 * length * HEADS * HEAD_DIM,
            transcendentals=tokens * length * HEADS,
        ),
        name="attend",
    )(*operands, seg_q, seg_k)


def attend_back(qkv, others, d_mixture, lse, seg_q, seg_k):
    operands, specs, tokens, pairs = attention_specs(qkv, others)
    chunks = 1 + len(others)
    length = tokens * chunks
    width = HEADS * HEAD_DIM
    whole = lambda shape: pl.BlockSpec(shape, lambda i: (0,) * len(shape))
    stacked = pl.BlockSpec((2, tokens, PAIR), lambda i: (0, 0, i))
    out = pl.pallas_call(
        functools.partial(attend_back_kernel, chunks, min(256, tokens)),
        grid=(pairs,),
        in_specs=specs
        + [
            pl.BlockSpec((tokens, PAIR), lambda i: (0, i)),
            pl.BlockSpec((1, 2, tokens), lambda i: (i, 0, 0)),
            whole((1, tokens)),
            whole((length, 1)),
        ],
        out_specs=[pl.BlockSpec((tokens, PAIR), lambda i: (0, i)), stacked]
        + [stacked for _ in others],
        out_shape=[
            jax.ShapeDtypeStruct((tokens, width), BF),
            jax.ShapeDtypeStruct((2, tokens, width), F32),
        ]
        + [jax.ShapeDtypeStruct((2, tokens, width), BF) for _ in others],
        scratch_shapes=[pltpu.VMEM((chunks, 2, tokens, PAIR), F32)],
        compiler_params=pltpu.CompilerParams(vmem_limit_bytes=40 * 2**20),
        cost_estimate=pl.CostEstimate(
            flops=40 * tokens * length * width,
            bytes_accessed=20 * length * width,
            transcendentals=tokens * length * HEADS,
        ),
        name="attend_back",
    )(*operands, d_mixture, lse, seg_q, seg_k)
    return out[0], out[1], out[2:]


def split_small(small, sizes):
    vectors, at = [], 0
    for size in sizes:
        vectors.append(small[:, at : at + size].reshape(-1).astype(F32))
        at += size
    return vectors


def layer_forward(grid, inputs, weights, seg_q, seg_k):
    (qkv_w, attn_w, inner_w, outer_w, qv_b, attn_b, attn_g, attn_s, inner_b, outer_b, ffn_g, ffn_s) = weights
    width = inputs.shape[1]
    x_low = inputs.astype(BF)
    bias = jnp.concatenate([qv_b[:width], jnp.zeros((width,), F32), qv_b[width:]])
    qkv = (matrix_product(x_low, qkv_w) + bias).astype(BF)
    key_value = qkv[:, width:]
    others = [grid.to_member(key_value, shift) for shift in range(1, grid.members)]
    mixture, lse = attend(qkv, others, seg_q, seg_k)
    branch = matrix_product(mixture, attn_w) + attn_b
    normed, normed_one, inv_one = layer_norm(inputs.astype(F32) + branch, attn_g, attn_s)
    normed_low = normed.astype(BF)
    inner = matrix_product(normed_low, inner_w) + inner_b
    active, slope = gelu_both(inner)
    active = active.astype(BF)
    outer = matrix_product(active, outer_w) + outer_b
    output, normed_two, inv_two = layer_norm(normed + outer, ffn_g, ffn_s)
    saved = (x_low, qkv, others, lse, mixture, normed_one, inv_one, normed_low, slope, active, normed_two, inv_two)
    return output, saved


def layer_backward(grid, upstream, weights, saved, seg_q, seg_k):
    (qkv_w, attn_w, inner_w, outer_w, qv_b, attn_b, attn_g, attn_s, inner_b, outer_b, ffn_g, ffn_s) = weights
    (x_low, qkv, others, lse, mixture, normed_one, inv_one, normed_low, slope, active, normed_two, inv_two) = saved
    grad_ffn_g = jnp.sum(upstream * normed_two, axis=0)
    grad_ffn_s = jnp.sum(upstream, axis=0)
    d_second = norm_back(upstream, normed_two, inv_two, ffn_g)
    d_outer = d_second.astype(BF)
    grad_outer_b = column_sum(d_outer)
    grad_outer_w = left_t(active, d_outer).astype(BF)
    d_inner = (right_t(d_outer, outer_w) * slope).astype(BF)
    grad_inner_b = column_sum(d_inner)
    grad_inner_w = left_t(normed_low, d_inner).astype(BF)
    d_normed = right_t(d_inner, inner_w) + d_second
    grad_attn_g = jnp.sum(d_normed * normed_one, axis=0)
    grad_attn_s = jnp.sum(d_normed, axis=0)
    d_first = norm_back(d_normed, normed_one, inv_one, attn_g)
    d_branch = d_first.astype(BF)
    grad_attn_b = column_sum(d_branch)
    grad_attn_w = left_t(mixture, d_branch).astype(BF)
    d_mixture = right_t(d_branch, attn_w).astype(BF)
    d_queries, own, for_others = attend_back(qkv, others, d_mixture, lse, seg_q, seg_k)
    for shift in range(1, grid.members):
        own = own + grid.to_member(for_others[shift - 1], -shift).astype(F32)
    own = own.astype(BF)
    d_qkv = jnp.concatenate([d_queries, own[0], own[1]], axis=1)
    grad_qv_b = jnp.concatenate([column_sum(d_queries), column_sum(own[1])])
    grad_qkv_w = left_t(x_low, d_qkv).astype(BF)
    d_input = right_t(d_qkv, qkv_w) + d_first
    grads = (grad_qkv_w, grad_attn_w, grad_inner_w, grad_outer_w)
    small = (grad_qv_b, grad_attn_b, grad_attn_g, grad_attn_s, grad_inner_b, grad_outer_b, grad_ffn_g, grad_ffn_s)
    return d_input, grads, small


def contrastive(vectors, positives):
    count, width = vectors.shape
    similarity = jnp.dot(vectors, vectors.T, precision=FULL_PRECISION) / (width * SOFTMAX_HEAT)
    ids = jnp.arange(count, dtype=jnp.int32)
    similarity = jnp.where(ids[:, None] == ids[None, :], NEGATIVE, similarity)
    highest = jnp.max(similarity, axis=1, keepdims=True)
    totals = highest + jnp.log(jnp.sum(jnp.exp(similarity - highest), axis=1, keepdims=True))
    positive = positives[:, None] == ids[None, :]
    loss = jnp.sum(totals) - jnp.sum(jnp.where(positive, similarity, 0.0))
    slope = (jnp.exp(similarity - totals) - positive.astype(F32)) / (width * SOFTMAX_HEAT)
    return loss, jnp.dot(slope + slope.T, vectors, precision=FULL_PRECISION)


def body(
    hidden,
    skip_tokens,
    backbone_cotangent,
    head_cotangent,
    starts,
    positives,
    qkv_weight,
    qv_bias,
    attn_weight,
    attn_bias,
    attn_gain,
    attn_shift,
    inner_weight,
    inner_bias,
    outer_weight,
    outer_bias,
    ffn_gain,
    ffn_shift,
):
    rows_dev, local, width = hidden.shape
    grid = Grid(rows_dev)
    tokens = rows_dev * local
    length = tokens * grid.members

    starts_both = jnp.stack([starts, grid.swap(starts, grid.f_bits)])
    from_other = jnp.where(grid.row_in_group // rows_dev == grid.core, 0, 1)
    my_starts = lax.dynamic_index_in_dim(starts_both, from_other, 0, keepdims=False)
    my_starts = lax.dynamic_index_in_dim(
        my_starts, grid.row_in_group % rows_dev, 0, keepdims=False
    )
    place = jnp.arange(tokens, dtype=jnp.int32)
    q_pos = grid.member * tokens + place
    k_pos = jnp.concatenate(
        [
            (grid.member - shift) % grid.members * tokens + place
            for shift in range(grid.members)
        ]
    )
    segment = lambda pos: jnp.sum((my_starts[:, None] <= pos[None, :]).astype(jnp.int32), axis=0) - 1
    seg_q = segment(q_pos)[None, :]
    seg_k = segment(k_pos)[:, None]
    cls_hot = (my_starts[:, None] == q_pos[None, :]).astype(F32)
    is_cls = jnp.any(my_starts[:, None] == q_pos[None, :], axis=0)[:, None]

    order, turned = grid.gather_order(False), grid.gather_order(True)
    x = grid.to_rows(hidden)
    vectors = (qv_bias, attn_bias, attn_gain, attn_shift, inner_bias, outer_bias, ffn_gain, ffn_shift)
    sizes = [v.shape[1] for v in vectors]
    small_own = jnp.concatenate(vectors, axis=1)
    small = grid.gather(small_own[None], order)
    layers = []
    for layer in range(2):
        qkv_w = grid.gather(qkv_weight[layer], order)
        mid = jnp.concatenate([attn_weight[layer], inner_weight[layer]], axis=1)
        mid = grid.gather(mid, turned)
        outer_w = grid.gather(outer_weight[layer], order)
        layers.append(
            (qkv_w, mid[:, :width], mid[:, width:], outer_w, *split_small(small[:, layer], sizes))
        )
    backbone, head = layers
    rest = grid.to_rows(jnp.concatenate([skip_tokens, head_cotangent, backbone_cotangent], axis=2))
    skip, head_cot, backbone_cot = rest[:, :width], rest[:, width : 2 * width], rest[:, 2 * width :]

    first, saved_one = layer_forward(grid, x, backbone, seg_q, seg_k)
    cls_own = jnp.dot(cls_hot, first, precision=FULL_PRECISION)[None]
    head_in = jnp.where(is_cls, first, skip.astype(F32))
    second, saved_two = layer_forward(grid, head_in, head, seg_q, seg_k)

    shared = n_bits(grid.chips_per_row)
    for bit in [grid.f_bits] + list(range(shared)):
        cls_own = cls_own + grid.swap(cls_own, bit)
    cls_order = list(range(shared, grid.f_bits)) + list(range(grid.f_bits + 1, grid.f_bits + grid.d_bits))
    cls_all = grid.gather(cls_own, cls_order).reshape(-1, width)
    contrast_loss, d_cls_all = contrastive(cls_all, positives)
    my_row = grid.dp // CORES * (CORES * rows_dev) + grid.row_in_group
    d_cls = lax.dynamic_slice_in_dim(d_cls_all, my_row * SEGS, SEGS, 0)

    d_head_in, grads_two, small_two = layer_backward(
        grid, head_cot.astype(F32), head, saved_two, seg_q, seg_k
    )
    upstream = (
        backbone_cot.astype(F32)
        + jnp.where(is_cls, d_head_in, 0.0)
        + lax.dot_general(cls_hot, d_cls, (((0,), (0,)), ((), ())), precision=FULL_PRECISION)
    )
    outs = jnp.concatenate(
        [first.astype(BF), second.astype(BF), jnp.where(is_cls, 0.0, d_head_in).astype(BF)], axis=1
    )
    outs = grid.from_rows(outs)
    d_input, grads_one, small_one = layer_backward(grid, upstream, backbone, saved_one, seg_q, seg_k)
    grad_hidden = grid.from_rows(d_input.astype(BF)).astype(F32)

    devices = grid.n_dp * grid.n_f
    scattered = []
    for grad_qkv, grad_attn, grad_inner, grad_outer in (grads_one, grads_two):
        outer_g = grid.scatter(grad_outer, order)
        mid = grid.scatter(jnp.concatenate([grad_attn, grad_inner], axis=1), turned)
        qkv_g = grid.scatter(grad_qkv, order)
        scattered.append((qkv_g, mid[:, :width], mid[:, width:], outer_g))
    small_g = jnp.stack(
        [
            jnp.concatenate([v.reshape(devices, -1) for v in small], axis=1)
            for small in (small_one, small_two)
        ],
        axis=1,
    )
    small_g = grid.scatter(small_g, order, F32)[0]
    cuts, at = [], 0
    for size in sizes:
        cuts.append(small_g[:, at : at + size])
        at += size
    qkv_g, attn_g, inner_g, outer_g = (jnp.stack(pair) for pair in zip(*scattered))
    return (
        contrast_loss,
        outs[:, :, :width],
        outs[:, :, width : 2 * width],
        grad_hidden,
        outs[:, :, 2 * width :].astype(F32),
        qkv_g,
        cuts[0],
        attn_g,
        cuts[1],
        cuts[2],
        cuts[3],
        inner_g,
        cuts[4],
        outer_g,
        cuts[5],
        cuts[6],
        cuts[7],
    )


def solution(mesh):
    rows = P("dp", "fsdp", None)
    matrix = P(None, ("dp", "fsdp"), None)
    vector = P(None, ("dp", "fsdp"))
    params = (
        matrix,
        vector,
        matrix,
        vector,
        vector,
        vector,
        matrix,
        vector,
        matrix,
        vector,
        vector,
        vector,
    )
    return jax.shard_map(
        body,
        mesh=mesh,
        in_specs=(rows, rows, rows, rows, P("dp", None), P()) + params,
        out_specs=(P(), rows, rows, rows, rows) + params,
        check_vma=False,
    )
```

time: 2440 us -> 829 us (0.34)
  waiting for transfers between devices: 1110 us -> 365 us
  blocking collectives: 677 us -> 0 us
  matrix products: 337 us -> 83.6 us
  starting transfers between devices: 2.6 us -> 107 us
  local copies, waits for them, and re-layouts: 162 us -> 69.9 us
  Pallas kernels: 0 us -> 88.6 us
    reduce_scatter x11 -> x0, waiting for transfers between devices: 601 us -> none  [the longest x1 212 us: body(): lax.psum_scatter(totals_grad[6], ('dp', 'fsdp'), scatter_dimension=1, til...]
    all_gather x9 -> x0, blocking collectives: 597 us -> none  [the longest x1 79.7 us: body(): lax.all_gather(cls_own, ('dp', 'fsdp'), axis=0, tiled=True)]
    ppermute x0 -> x88, waiting for transfers between devices: none -> 365 us  [the longest x30 219 us: swap(): return lax.ppermute(x, 'fsdp', [(i, i ^ 1 << bit) for i in range(self.n_f)])]
    unnamed x36 -> x0, waiting for transfers between devices: 278 us -> none
    all_gather x19 -> x0, waiting for transfers between devices: 231 us -> none  [the longest x1 76.8 us: body(): lax.all_gather(qkv_weight, ('dp', 'fsdp'), axis=1, tiled=True)]
    dot_general x50 -> x12, matrix products: 242 us -> 27.7 us  [the longest x8 21.3 us: matrix_product(): return jnp.dot(first_op, second_op, preferred_element_type=F32)]
    ppermute x0 -> x88, starting transfers between devices: none -> 107 us  [the longest x46 48.4 us: swap(): return lax.ppermute(x, 'dp', [(i, i ^ flip) for i in range(self.n_dp)])]
    pallas_call x0 -> x4, Pallas kernels: none -> 88.6 us  [the longest x2 50.7 us: attend_back(): pl.pallas_call(functools.partial(attend_back_kernel, chunks, min(256, tok...]
  transfers between devices with their start and end apart: 33 -> 88, of which waited for: 13 -> 38; matrix products, arithmetic and copies ran while one was open for 23% -> 24% of each run, Pallas kernels for 0% -> 5%
where the time goes in v1:
time: 829 us; the launch traced here: 824 us
  waiting for transfers between devices  365 us (44%)
  starting transfers between devices  107 us (13%)
  other arithmetic  104 us (13%)
  Pallas kernels  88.6 us (11%)
  matrix products  83.6 us (10%)
  local copies, waits for them, and re-layouts  69.9 us (8%)
    ppermute x30, waiting for transfers between devices, swap(): return lax.ppermute(x, 'fsdp', [(i, i ^ 1 << bit) for i in range(self.n_f)])  219 us
    ppermute x46, waiting for transfers between devices, swap(): return lax.ppermute(x, 'dp', [(i, i ^ flip) for i in range(self.n_dp)])  141 us
    pallas_call x2, Pallas kernels, attend_back(): pl.pallas_call(functools.partial(attend_back_kernel, chunks, min(256, tok...  50.7 us
    ppermute x46, starting transfers between devices, swap(): return lax.ppermute(x, 'dp', [(i, i ^ flip) for i in range(self.n_dp)])  48.4 us
    ppermute x30, starting transfers between devices, swap(): return lax.ppermute(x, 'fsdp', [(i, i ^ 1 << bit) for i in range(self.n_f)])  41.1 us
    pallas_call x2, Pallas kernels, attend(): pl.pallas_call(functools.partial(attend_kernel, chunks, min(256, tokens))...  37.8 us
    another operation x83, other arithmetic, gather(): out = jnp.stack([low, high], axis=place)  30.4 us
    dot_general x8, matrix products, left_t(): lax.dot_general(first_op, second_op, (((0,), (0,)), ((), ())), preferred_...  28.5 us
  transfers between devices with their start and end apart: 88, of which 38 were waited for; matrix products, arithmetic and copies ran while one was open for 24% of the time, Pallas kernels for 5%

profile of v1, /device:TPU:0, one launch (start us, length us, event | category | flops | bytes accessed | tf_op | source)
XLA Modules:
  0.0 824.0 jit_solution(17027867677963131817)
XLA Ops:
  20.1 3.4 collective-permute-start.9
  55.3 8.6 %collective-permute-start.4 = (bf16[2,24,2304]{2,1,0:T(8,128)(2,1)S(1)}, bf16[2,24,2304]{2,1,0:T(8,128)(2,1)S(1)}, u32[]{:S(2)}, u32[]{:S(2)}) collective-permute-start(bf16[2,24,2304]{2,1,0:T(8,128)(2,1)S(1)} %pad_maximum_fusion.46), channel_id=1, source_target_pairs={{0,2},{1,3},{2,0},{3,1},{4,6},{5,7},{6,4},{7,5},{8,10},{9,11},{10,... | collective-permute-start | bytes 663560 | tf_op jit(solution)/shard_map/ppermute | solution.py:94
  64.9 96.1 %collective-permute-done.4 = bf16[2,24,2304]{2,1,0:T(8,128)(2,1)S(1)} collective-permute-done((bf16[2,24,2304]{2,1,0:T(8,128)(2,1)S(1)}, bf16[2,24,2304]{2,1,0:T(8,128)(2,1)S(1)}, u32[]{:S(2)}, u32[]{:S(2)}) %collective-permute-start.4) | collective-permute-done | bytes 221216 | tf_op jit(solution)/shard_map/ppermute | solution.py:94
  161.1 8.8 %collective-permute-done.32 = bf16[2,24,2304]{2,1,0:T(8,128)(2,1)S(1)} collective-permute-done((bf16[2,24,2304]{2,1,0:T(8,128)(2,1)S(1)}, bf16[2,24,2304]{2,1,0:T(8,128)(2,1)S(1)}, u32[]{:S(2)}, u32[]{:S(2)}) %collective-permute-start.32) | collective-permute-done | bytes 221216 | tf_op jit(solution)/shard_map/ppermute | solution.py:94
  170.1 3.0 collective-permute-start.20
  173.5 11.8 %collective-permute-done.43 = bf16[2,96,768]{2,1,0:T(8,128)(2,1)S(1)} collective-permute-done((bf16[2,96,768]{2,1,0:T(8,128)(2,1)S(1)}, bf16[2,96,768]{2,1,0:T(8,128)(2,1)S(1)}, u32[]{:S(2)}, u32[]{:S(2)}) %collective-permute-start.43) | collective-permute-done | bytes 294944 | tf_op jit(solution)/shard_map/ppermute | solution.py:94
  185.4 3.0 collective-permute-done.20
  190.1 10.2 %collective-permute-done.38 = bf16[2,24,3840]{2,1,0:T(8,128)(2,1)S(1)} collective-permute-done((bf16[2,24,3840]{2,1,0:T(8,128)(2,1)S(1)}, bf16[2,24,3840]{2,1,0:T(8,128)(2,1)S(1)}, u32[]{:S(2)}, u32[]{:S(2)}) %collective-permute-start.38) | collective-permute-done | bytes 368672 | tf_op jit(solution)/shard_map/ppermute | solution.py:94
  204.3 9.1 %collective-permute-done.33 = bf16[2,2,24,2304]{3,2,1,0:T(8,128)(2,1)S(1)} collective-permute-done((bf16[2,2,24,2304]{3,2,1,0:T(8,128)(2,1)S(1)}, bf16[2,2,24,2304]{3,2,1,0:T(8,128)(2,1)S(1)}, u32[]{:S(2)}, u32[]{:S(2)}) %collective-permute-start.33) | collective-permute-done | bytes 442400 | tf_op jit(solution)/shard_map/ppermute | solution.py:96
  215.1 10.9 %collective-permute-done.21 = bf16[2,2,96,768]{3,2,1,0:T(8,128)(2,1)S(1)} collective-permute-done((bf16[2,2,96,768]{3,2,1,0:T(8,128)(2,1)S(1)}, bf16[2,2,96,768]{3,2,1,0:T(8,128)(2,1)S(1)}, u32[]{:S(2)}, u32[]{:S(2)}) %collective-permute-start.21) | collective-permute-done | bytes 589856 | tf_op jit(solution)/shard_map/ppermute | solution.py:96
  227.6 11.1 %collective-permute-done.44 = bf16[2,2,96,768]{3,2,1,0:T(8,128)(2,1)S(1)} collective-permute-done((bf16[2,2,96,768]{3,2,1,0:T(8,128)(2,1)S(1)}, bf16[2,2,96,768]{3,2,1,0:T(8,128)(2,1)S(1)}, u32[]{:S(2)}, u32[]{:S(2)}) %collective-permute-start.44) | collective-permute-done | bytes 589856 | tf_op jit(solution)/shard_map/ppermute | solution.py:96
  249.7 7.7 collective-permute-done.6
  259.2 7.7 collective-permute-done.34
  268.5 11.0 %collective-permute-done.22 = bf16[2,2,2,96,768]{4,3,2,1,0:T(8,128)(2,1)S(1)} collective-permute-done((bf16[2,2,2,96,768]{4,3,2,1,0:T(8,128)(2,1)S(1)}, bf16[2,2,2,96,768]{4,3,2,1,0:T(8,128)(2,1)S(1)}, u32[]{:S(2)}, u32[]{:S(2)}) %collective-permute-start.22) | collective-permute-done | bytes 1179680 | tf_op jit(solution)/shard_map/ppermute | solution.py:96
  279.9 12.2 %collective-permute-done.45 = bf16[2,2,2,96,768]{4,3,2,1,0:T(8,128)(2,1)S(1)} collective-permute-done((bf16[2,2,2,96,768]{4,3,2,1,0:T(8,128)(2,1)S(1)}, bf16[2,2,2,96,768]{4,3,2,1,0:T(8,128)(2,1)S(1)}, u32[]{:S(2)}, u32[]{:S(2)}) %collective-permute-start.45) | collective-permute-done | bytes 1179680 | tf_op jit(solution)/shard_map/ppermute | solution.py:96
  311.0 18.7 %attend.2 = (bf16[512,768]{1,0:T(8,128)(2,1)S(1)}, f32[6,2,512]{2,1,0:T(2,128)S(1)}) custom-call(bf16[512,2304]{1,0:T(8,128)(2,1)S(1)} %fusion.16.refs_0_.refs_1_.refs_3_, bf16[512,2304]{1,0:T(8,128)(2,1)S(1)} %fusion.16.refs_0_.refs_1_.refs_3_, bf16[512,1536]{1,0:T(8,128)(2,1)S(1)} %collective-permute-done.13.refs_2_.refs_4_, ...), custom_call_target="tpu_custom_call" | custom-call | flops 6442450944 | bytes 6291456 | tf_op jit(solution)/shard_map/attend/pallas_call | solution.py:317
  332.0 3.0 pad_maximum_fusion
  338.2 5.1 multiply_convert_fusion.1
  343.3 2.8 fusion.194
  351.2 2.8 copy.204
  354.1 3.5 collective-permute-start.26
  368.7 3.0 copy.202
  379.9 19.2 %attend.3 = (bf16[512,768]{1,0:T(8,128)(2,1)S(1)}, f32[6,2,512]{2,1,0:T(2,128)S(1)}) custom-call(bf16[512,2304]{1,0:T(8,128)(2,1)S(1)} %fusion.17.refs_0_.refs_1_.refs_3_, bf16[512,2304]{1,0:T(8,128)(2,1)S(1)} %fusion.17.refs_0_.refs_1_.refs_3_, bf16[512,1536]{1,0:T(8,128)(2,1)} %collective-permute-done.36.refs_2_.refs_4_, ...), custom_call_target="tpu_custom_call" | custom-call | flops 6442450944 | bytes 6291456 | tf_op jit(solution)/shard_map/attend/pallas_call | solution.py:317
  400.9 2.9 multiply_convert_fusion
  403.8 2.8 fusion.196
  409.4 4.4 convolution_convert_fusion
  413.8 5.9 convert_reduce_fusion
  419.7 5.1 multiply_reduce_fusion
  424.8 4.8 convolution_convert_fusion.2
  433.1 4.9 fusion.186
  443.6 25.8 %attend_back.2 = (bf16[512,768]{1,0:T(8,128)(2,1)S(1)}, f32[2,512,768]{2,1,0:T(8,128)S(1)}, bf16[2,512,768]{2,1,0:T(8,128)(2,1)S(1)}) custom-call(bf16[512,2304]{1,0:T(8,128)(2,1)S(1)} %copy-done.3, bf16[512,2304]{1,0:T(8,128)(2,1)S(1)} %copy-done.3, bf16[512,1536]{1,0:T(8,128)(2,1)} %collective-permute-done.36.refs_2_.refs_4_, ...), custom_call_target="tpu_custom_call" | custom-call | flops 16106127360 | bytes 15728640 | tf_op jit(solution)/shard_map/attend_back/pallas_call | solution.py:346
  471.8 4.1 select_bitcast_fusion.6
  485.4 2.9 select_convert_fusion
  488.3 4.2 convolution_convert_fusion.4
  496.7 4.4 convolution_convert_fusion.1
  501.2 4.9 convert_reduce_fusion.1
  506.1 3.1 multiply_reduce_fusion.2
  509.3 4.8 convolution_convert_fusion.3
  518.4 4.2 fusion.188
  525.0 10.4 %collective-permute-start.48 = (bf16[256,2304]{1,0:T(8,128)(2,1)}, bf16[256,2304]{1,0:T(8,128)(2,1)}, u32[]{:S(2)}, u32[]{:S(2)}) collective-permute-start(bf16[256,2304]{1,0:T(8,128)(2,1)} %get-tuple-element.96), channel_id=1, source_target_pairs={{0,0},{1,1},{4,2},{5,3},{2,4},{3,5},{6,6},{7,7},{8,8},{9,9},{12,10... | collective-permute-start | bytes 3538952 | tf_op jit(solution)/shard_map/ppermute | solution.py:168
  539.6 24.9 %attend_back.3 = (bf16[512,768]{1,0:T(8,128)(2,1)S(1)}, f32[2,512,768]{2,1,0:T(8,128)S(1)}, bf16[2,512,768]{2,1,0:T(8,128)(2,1)S(1)}) custom-call(bf16[512,2304]{1,0:T(8,128)(2,1)S(1)} %copy-done.1, bf16[512,2304]{1,0:T(8,128)(2,1)S(1)} %copy-done.1, bf16[512,1536]{1,0:T(8,128)(2,1)S(1)} %copy-done.14, bf16[512,2304]{1,0:T(8,128)(2,1)S(1)} %copy-done.1, ...), custom_call_target="tpu_custom_call" | custom-call | flops 16106127360 | bytes 15728640 | tf_op jit(solution)/shard_map/attend_back/pallas_call | solution.py:346
  569.5 5.7 pad_maximum_fusion.2
  577.6 4.8 select_bitcast_fusion.1
  596.6 2.9 fusion.12
  604.7 3.0 convolution_convert_fusion.5
  608.7 15.3 %collective-permute-done.64 = f32[2,2,2,1,2,288]{5,2,1,0,4,3:T(2,128)S(1)} collective-permute-done((f32[2,2,2,1,2,288]{5,2,1,0,4,3:T(2,128)S(1)}, f32[2,2,2,1,2,288]{5,2,1,0,4,3:T(2,128)S(1)}, u32[]{:S(2)}, u32[]{:S(2)}) %collective-permute-start.64) | collective-permute-done | bytes 18464 | tf_op jit(solution)/shard_map/ppermute | solution.py:96
  642.7 5.3 collective-permute-done.52
  649.6 5.6 collective-permute-start.53
  661.7 2.8 fusion.15
  664.7 28.7 %collective-permute-done.85 = bf16[2,2,96,768]{3,2,1,0:T(8,128)(2,1)S(1)} collective-permute-done((bf16[2,2,96,768]{3,2,1,0:T(8,128)(2,1)S(1)}, bf16[2,2,96,768]{3,2,1,0:T(8,128)(2,1)S(1)}, u32[]{:S(2)}, u32[]{:S(2)}) %collective-permute-start.85) | collective-permute-done | bytes 589856 | tf_op jit(solution)/shard_map/ppermute | solution.py:96
  695.8 13.5 %collective-permute-done.86 = bf16[2,96,768]{2,1,0:T(8,128)(2,1)S(1)} collective-permute-done((bf16[2,96,768]{2,1,0:T(8,128)(2,1)S(1)}, bf16[2,96,768]{2,1,0:T(8,128)(2,1)S(1)}, u32[]{:S(2)}, u32[]{:S(2)}) %collective-permute-start.86) | collective-permute-done | bytes 294944 | tf_op jit(solution)/shard_map/ppermute | solution.py:94
  712.4 2.9 fusion.13
  715.4 3.6 collective-permute-done.60
  721.8 9.3 %collective-permute-done.61 = bf16[2,24,2304]{2,1,0:T(8,128)(2,1)S(1)} collective-permute-done((bf16[2,24,2304]{2,1,0:T(8,128)(2,1)S(1)}, bf16[2,24,2304]{2,1,0:T(8,128)(2,1)S(1)}, u32[]{:S(2)}, u32[]{:S(2)}) %collective-permute-start.61) | collective-permute-done | bytes 221216 | tf_op jit(solution)/shard_map/ppermute | solution.py:94
  732.6 3.4 collective-permute-done.62
  739.3 13.9 %collective-permute-done.76 = bf16[2,24,3840]{2,1,0:T(8,128)(2,1)S(1)} collective-permute-done((bf16[2,24,3840]{2,1,0:T(8,128)(2,1)S(1)}, bf16[2,24,3840]{2,1,0:T(8,128)(2,1)S(1)}, u32[]{:S(2)}, u32[]{:S(2)}) %collective-permute-start.76) | collective-permute-done | bytes 368672 | tf_op jit(solution)/shard_map/ppermute | solution.py:94
  754.1 7.7 collective-permute-done.80
  764.4 11.8 %collective-permute-done.81 = bf16[2,96,768]{2,1,0:T(8,128)(2,1)S(1)} collective-permute-done((bf16[2,96,768]{2,1,0:T(8,128)(2,1)S(1)}, bf16[2,96,768]{2,1,0:T(8,128)(2,1)S(1)}, u32[]{:S(2)}, u32[]{:S(2)}) %collective-permute-start.81) | collective-permute-done | bytes 294944 | tf_op jit(solution)/shard_map/ppermute | solution.py:94
  778.5 3.4 collective-permute-start.56
  782.9 8.6 %collective-permute-done.56 = bf16[2,24,2304]{2,1,0:T(8,128)(2,1)S(1)} collective-permute-done((bf16[2,24,2304]{2,1,0:T(8,128)(2,1)S(1)}, bf16[2,24,2304]{2,1,0:T(8,128)(2,1)S(1)}, u32[]{:S(2)}, u32[]{:S(2)}) %collective-permute-start.56) | collective-permute-done | bytes 221216 | tf_op jit(solution)/shard_map/ppermute | solution.py:94
  791.7 3.0 collective-permute-done.70
  795.0 3.4 collective-permute-start.71
  798.5 15.5 %collective-permute-done.71 = bf16[2,24,3840]{2,1,0:T(8,128)(2,1)S(1)} collective-permute-done((bf16[2,24,3840]{2,1,0:T(8,128)(2,1)S(1)}, bf16[2,24,3840]{2,1,0:T(8,128)(2,1)S(1)}, u32[]{:S(2)}, u32[]{:S(2)}) %collective-permute-start.71) | collective-permute-done | bytes 368672 | tf_op jit(solution)/shard_map/ppermute | solution.py:94
  815.0 5.7 collective-permute-done.72
  (665 shorter events, 240.8 us)
Async XLA Ops:
  0.7 16.6 %collective-permute-start = (s32[2,8]{1,0:T(2,128)}, s32[2,8]{1,0:T(2,128)S(1)}, u32[]{:S(2)}, u32[]{:S(2)}) collective-permute-start(s32[2,8]{1,0:T(2,128)} %param.22), channel_id=1, source_target_pairs={{0,4},{4,0},{8,12},{12,8},{16,20},{20,16},{24,28},{28,24},{1,5},{5... | collective-permute-start | bytes 200 | tf_op jit(solution)/shard_map/ppermute | solution.py:96
  2.0 17.3 %collective-permute-start.8 = (bf16[1,2,288]{2,1,0:T(2,128)(2,1)S(1)}, bf16[1,2,288]{2,1,0:T(2,128)(2,1)}, u32[]{:S(2)}, u32[]{:S(2)}) collective-permute-start(bf16[1,2,288]{2,1,0:T(2,128)(2,1)S(1)} %bitcast.732), channel_id=1, source_target_pairs={{0,1},{1,0},{2,3},{3,2},{4,5},{5,4},{6,7},{7,6},{8,9},{9,8},{10,11... | collective-permute-start | bytes 3464 | tf_op jit(solution)/shard_map/ppermute | solution.py:94
  6.3 40.4 %collective-permute-start.31 = (bf16[24,2304]{1,0:T(8,128)(2,1)}, bf16[24,2304]{1,0:T(8,128)(2,1)}, u32[]{:S(2)}, u32[]{:S(2)}) collective-permute-start(bf16[24,2304]{1,0:T(8,128)(2,1)} %get-tuple-element.167), channel_id=1, source_target_pairs={{0,1},{1,0},{2,3},{3,2},{4,5},{5,4},{6,7},{7,6},{8,9},{9,8},{10,11... | collective-permute-start | bytes 331784 | tf_op jit(solution)/shard_map/ppermute | solution.py:94
  6.3 41.0 %collective-permute-start.3 = (bf16[24,2304]{1,0:T(8,128)(2,1)S(1)}, bf16[24,2304]{1,0:T(8,128)(2,1)}, u32[]{:S(2)}, u32[]{:S(2)}) collective-permute-start(bf16[24,2304]{1,0:T(8,128)(2,1)S(1)} %get-tuple-element.168), channel_id=1, source_target_pairs={{0,1},{1,0},{2,3},{3,2},{4,5},{5,4},{6,7},{7,6},{8,9},{9,8},{10,11... | collective-permute-start | bytes 331784 | tf_op jit(solution)/shard_map/ppermute | solution.py:94
  10.8 44.5 %collective-permute-start.14 = (bf16[24,3840]{1,0:T(8,128)(2,1)}, bf16[24,3840]{1,0:T(8,128)(2,1)}, u32[]{:S(2)}, u32[]{:S(2)}) collective-permute-start(bf16[24,3840]{1,0:T(8,128)(2,1)} %pad_maximum_fusion.49), channel_id=1, source_target_pairs={{0,1},{1,0},{2,3},{3,2},{4,5},{5,4},{6,7},{7,6},{8,9},{9,8},{10,11... | collective-permute-start | bytes 552968 | tf_op jit(solution)/shard_map/ppermute | solution.py:94
  17.2 37.0 %collective-permute-start.37 = (bf16[24,3840]{1,0:T(8,128)(2,1)}, bf16[24,3840]{1,0:T(8,128)(2,1)S(1)}, u32[]{:S(2)}, u32[]{:S(2)}) collective-permute-start(bf16[24,3840]{1,0:T(8,128)(2,1)} %pad_maximum_fusion.50), channel_id=1, source_target_pairs={{0,1},{1,0},{2,3},{3,2},{4,5},{5,4},{6,7},{7,6},{8,9},{9,8},{10,11... | collective-permute-start | bytes 552968 | tf_op jit(solution)/shard_map/ppermute | solution.py:94
  34.0 15.9 %collective-permute-start.42 = (bf16[96,768]{1,0:T(8,128)(2,1)}, bf16[96,768]{1,0:T(8,128)(2,1)}, u32[]{:S(2)}, u32[]{:S(2)}) collective-permute-start(bf16[96,768]{1,0:T(8,128)(2,1)} %get-tuple-element.161), channel_id=1, source_target_pairs={{0,1},{1,0},{2,3},{3,2},{4,5},{5,4},{6,7},{7,6},{8,9},{9,8},{10,11... | collective-permute-start | bytes 442376 | tf_op jit(solution)/shard_map/ppermute | solution.py:94
  47.3 122.8 %collective-permute-start.2 = (bf16[256,768]{1,0:T(8,128)(2,1)}, bf16[256,768]{1,0:T(8,128)(2,1)S(1)}, u32[]{:S(2)}, u32[]{:S(2)}) collective-permute-start(bf16[256,768]{1,0:T(8,128)(2,1)} %get-tuple-element.133), channel_id=1, source_target_pairs={{0,1},{1,0},{2,5},{3,4},{4,3},{5,2},{6,7},{7,6},{8,9},{9,8},{10,13... | collective-permute-start | bytes 1179656 | tf_op jit(solution)/shard_map/ppermute | solution.py:151
  49.8 123.2 %collective-permute-start.1 = (bf16[256,768]{1,0:T(8,128)(2,1)S(1)}, bf16[256,768]{1,0:T(8,128)(2,1)S(1)}, u32[]{:S(2)}, u32[]{:S(2)}) collective-permute-start(bf16[256,768]{1,0:T(8,128)(2,1)S(1)} %get-tuple-element.134), channel_id=1, source_target_pairs={{0,0},{1,1},{2,4},{3,5},{4,2},{5,3},{6,6},{7,7},{8,8},{9,9},{10,12... | collective-permute-start | bytes 1179656 | tf_op jit(solution)/shard_map/ppermute | solution.py:151
  52.6 187.9 %collective-permute-start.30 = (bf16[256,2304]{1,0:T(8,128)(2,1)S(1)}, bf16[256,2304]{1,0:T(8,128)(2,1)S(1)}, u32[]{:S(2)}, u32[]{:S(2)}) collective-permute-start(bf16[256,2304]{1,0:T(8,128)(2,1)S(1)} %copy-done.60), channel_id=1, source_target_pairs={{0,1},{1,0},{2,5},{3,4},{4,3},{5,2},{6,7},{7,6},{8,9},{9,8},{10,13... | collective-permute-start | bytes 3538952 | tf_op jit(solution)/shard_map/ppermute | solution.py:151
  54.3 186.9 %collective-permute-start.29 = (bf16[256,2304]{1,0:T(8,128)(2,1)S(1)}, bf16[256,2304]{1,0:T(8,128)(2,1)S(1)}, u32[]{:S(2)}, u32[]{:S(2)}) collective-permute-start(bf16[256,2304]{1,0:T(8,128)(2,1)S(1)} %copy-done.59), channel_id=1, source_target_pairs={{0,0},{1,1},{2,4},{3,5},{4,2},{5,3},{6,6},{7,7},{8,8},{9,9},{10,12... | collective-permute-start | bytes 3538952 | tf_op jit(solution)/shard_map/ppermute | solution.py:151
  55.3 105.7 %collective-permute-start.4 = (bf16[2,24,2304]{2,1,0:T(8,128)(2,1)S(1)}, bf16[2,24,2304]{2,1,0:T(8,128)(2,1)S(1)}, u32[]{:S(2)}, u32[]{:S(2)}) collective-permute-start(bf16[2,24,2304]{2,1,0:T(8,128)(2,1)S(1)} %pad_maximum_fusion.46), channel_id=1, source_target_pairs={{0,2},{1,3},{2,0},{3,1},{4,6},{5,7},{6,4},{7,5},{8,10},{9,11},{10,... | collective-permute-start | bytes 663560 | tf_op jit(solution)/shard_map/ppermute | solution.py:94
  169.9 15.3 %collective-permute-start.43 = (bf16[2,96,768]{2,1,0:T(8,128)(2,1)S(1)}, bf16[2,96,768]{2,1,0:T(8,128)(2,1)S(1)}, u32[]{:S(2)}, u32[]{:S(2)}) collective-permute-start(bf16[2,96,768]{2,1,0:T(8,128)(2,1)S(1)} %pad_maximum_fusion.43), channel_id=1, source_target_pairs={{0,2},{1,3},{2,0},{3,1},{4,6},{5,7},{6,4},{7,5},{8,10},{9,11},{10,... | collective-permute-start | bytes 884744 | tf_op jit(solution)/shard_map/ppermute | solution.py:94
  170.1 18.3 %collective-permute-start.20 = (bf16[2,96,768]{2,1,0:T(8,128)(2,1)S(1)}, bf16[2,96,768]{2,1,0:T(8,128)(2,1)S(1)}, u32[]{:S(2)}, u32[]{:S(2)}) collective-permute-start(bf16[2,96,768]{2,1,0:T(8,128)(2,1)S(1)} %pad_maximum_fusion.42), channel_id=1, source_target_pairs={{0,2},{1,3},{2,0},{3,1},{4,6},{5,7},{6,4},{7,5},{8,10},{9,11},{10,... | collective-permute-start | bytes 884744 | tf_op jit(solution)/shard_map/ppermute | solution.py:94
  173.1 28.9 %collective-permute-start.15 = (bf16[2,24,3840]{2,1,0:T(8,128)(2,1)S(1)}, bf16[2,24,3840]{2,1,0:T(8,128)(2,1)S(1)}, u32[]{:S(2)}, u32[]{:S(2)}) collective-permute-start(bf16[2,24,3840]{2,1,0:T(8,128)(2,1)S(1)} %pad_maximum_fusion.40), channel_id=1, source_target_pairs={{0,2},{1,3},{2,0},{3,1},{4,6},{5,7},{6,4},{7,5},{8,10},{9,11},{10,... | collective-permute-start | bytes 1105928 | tf_op jit(solution)/shard_map/ppermute | solution.py:94
  185.3 15.0 %collective-permute-start.38 = (bf16[2,24,3840]{2,1,0:T(8,128)(2,1)S(1)}, bf16[2,24,3840]{2,1,0:T(8,128)(2,1)S(1)}, u32[]{:S(2)}, u32[]{:S(2)}) collective-permute-start(bf16[2,24,3840]{2,1,0:T(8,128)(2,1)S(1)} %pad_maximum_fusion.41), channel_id=1, source_target_pairs={{0,2},{1,3},{2,0},{3,1},{4,6},{5,7},{6,4},{7,5},{8,10},{9,11},{10,... | collective-permute-start | bytes 1105928 | tf_op jit(solution)/shard_map/ppermute | solution.py:94
  188.4 14.2 %collective-permute-start.5 = (bf16[2,2,24,2304]{3,2,1,0:T(8,128)(2,1)S(1)}, bf16[2,2,24,2304]{3,2,1,0:T(8,128)(2,1)S(1)}, u32[]{:S(2)}, u32[]{:S(2)}) collective-permute-start(bf16[2,2,24,2304]{3,2,1,0:T(8,128)(2,1)S(1)} %pad_maximum_fusion.36), channel_id=1, source_target_pairs={{0,16},{4,20},{8,24},{12,28},{16,0},{20,4},{24,8},{28,12},{1,17},{... | collective-permute-start | bytes 1327112 | tf_op jit(solution)/shard_map/ppermute | solution.py:96
  200.3 13.1 %collective-permute-start.33 = (bf16[2,2,24,2304]{3,2,1,0:T(8,128)(2,1)S(1)}, bf16[2,2,24,2304]{3,2,1,0:T(8,128)(2,1)S(1)}, u32[]{:S(2)}, u32[]{:S(2)}) collective-permute-start(bf16[2,2,24,2304]{3,2,1,0:T(8,128)(2,1)S(1)} %pad_maximum_fusion.37), channel_id=1, source_target_pairs={{0,16},{4,20},{8,24},{12,28},{16,0},{20,4},{24,8},{28,12},{1,17},{... | collective-permute-start | bytes 1327112 | tf_op jit(solution)/shard_map/ppermute | solution.py:96
  202.0 24.1 %collective-permute-start.21 = (bf16[2,2,96,768]{3,2,1,0:T(8,128)(2,1)S(1)}, bf16[2,2,96,768]{3,2,1,0:T(8,128)(2,1)S(1)}, u32[]{:S(2)}, u32[]{:S(2)}) collective-permute-start(bf16[2,2,96,768]{3,2,1,0:T(8,128)(2,1)S(1)} %pad_maximum_fusion.32), channel_id=1, source_target_pairs={{0,16},{4,20},{8,24},{12,28},{16,0},{20,4},{24,8},{28,12},{1,17},{... | collective-permute-start | bytes 1769480 | tf_op jit(solution)/shard_map/ppermute | solution.py:96
  202.7 36.0 %collective-permute-start.44 = (bf16[2,2,96,768]{3,2,1,0:T(8,128)(2,1)S(1)}, bf16[2,2,96,768]{3,2,1,0:T(8,128)(2,1)S(1)}, u32[]{:S(2)}, u32[]{:S(2)}) collective-permute-start(bf16[2,2,96,768]{3,2,1,0:T(8,128)(2,1)S(1)} %pad_maximum_fusion.33), channel_id=1, source_target_pairs={{0,16},{4,20},{8,24},{12,28},{16,0},{20,4},{24,8},{28,12},{1,17},{... | collective-permute-start | bytes 1769480 | tf_op jit(solution)/shard_map/ppermute | solution.py:96
  213.4 31.1 %collective-permute-start.16 = (bf16[2,2,24,3840]{3,2,1,0:T(8,128)(2,1)S(1)}, bf16[2,2,24,3840]{3,2,1,0:T(8,128)(2,1)S(1)}, u32[]{:S(2)}, u32[]{:S(2)}) collective-permute-start(bf16[2,2,24,3840]{3,2,1,0:T(8,128)(2,1)S(1)} %pad_maximum_fusion.30), channel_id=1, source_target_pairs={{0,8},{4,12},{8,0},{12,4},{16,24},{20,28},{24,16},{28,20},{1,9},{5... | collective-permute-start | bytes 2211848 | tf_op jit(solution)/shard_map/ppermute | solution.py:96
  226.0 21.9 %collective-permute-start.39 = (bf16[2,2,24,3840]{3,2,1,0:T(8,128)(2,1)S(1)}, bf16[2,2,24,3840]{3,2,1,0:T(8,128)(2,1)S(1)}, u32[]{:S(2)}, u32[]{:S(2)}) collective-permute-start(bf16[2,2,24,3840]{3,2,1,0:T(8,128)(2,1)S(1)} %pad_maximum_fusion.31), channel_id=1, source_target_pairs={{0,8},{4,12},{8,0},{12,4},{16,24},{20,28},{24,16},{28,20},{1,9},{5... | collective-permute-start | bytes 2211848 | tf_op jit(solution)/shard_map/ppermute | solution.py:96
  238.7 18.7 %collective-permute-start.6 = (bf16[2,2,2,24,2304]{4,3,2,1,0:T(8,128)(2,1)S(1)}, bf16[2,2,2,24,2304]{4,3,2,1,0:T(8,128)(2,1)S(1)}, u32[]{:S(2)}, u32[]{:S(2)}) collective-permute-start(bf16[2,2,2,24,2304]{4,3,2,1,0:T(8,128)(2,1)S(1)} %pad_maximum_fusion.25), channel_id=1, source_target_pairs={{0,8},{4,12},{8,0},{12,4},{16,24},{20,28},{24,16},{28,20},{1,9},{5... | collective-permute-start | bytes 2654216 | tf_op jit(solution)/shard_map/ppermute | solution.py:96
  240.5 26.4 %collective-permute-start.34 = (bf16[2,2,2,24,2304]{4,3,2,1,0:T(8,128)(2,1)S(1)}, bf16[2,2,2,24,2304]{4,3,2,1,0:T(8,128)(2,1)S(1)}, u32[]{:S(2)}, u32[]{:S(2)}) collective-permute-start(bf16[2,2,2,24,2304]{4,3,2,1,0:T(8,128)(2,1)S(1)} %pad_maximum_fusion.26), channel_id=1, source_target_pairs={{0,8},{4,12},{8,0},{12,4},{16,24},{20,28},{24,16},{28,20},{1,9},{5... | collective-permute-start | bytes 2654216 | tf_op jit(solution)/shard_map/ppermute | solution.py:96
  241.1 38.4 %collective-permute-start.22 = (bf16[2,2,2,96,768]{4,3,2,1,0:T(8,128)(2,1)S(1)}, bf16[2,2,2,96,768]{4,3,2,1,0:T(8,128)(2,1)S(1)}, u32[]{:S(2)}, u32[]{:S(2)}) collective-permute-start(bf16[2,2,2,96,768]{4,3,2,1,0:T(8,128)(2,1)S(1)} %pad_maximum_fusion.19), channel_id=1, source_target_pairs={{0,8},{4,12},{8,0},{12,4},{16,24},{20,28},{24,16},{28,20},{1,9},{5... | collective-permute-start | bytes 3538952 | tf_op jit(solution)/shard_map/ppermute | solution.py:96
  244.5 47.7 %collective-permute-start.45 = (bf16[2,2,2,96,768]{4,3,2,1,0:T(8,128)(2,1)S(1)}, bf16[2,2,2,96,768]{4,3,2,1,0:T(8,128)(2,1)S(1)}, u32[]{:S(2)}, u32[]{:S(2)}) collective-permute-start(bf16[2,2,2,96,768]{4,3,2,1,0:T(8,128)(2,1)S(1)} %pad_maximum_fusion.20), channel_id=1, source_target_pairs={{0,8},{4,12},{8,0},{12,4},{16,24},{20,28},{24,16},{28,20},{1,9},{5... | collective-permute-start | bytes 3538952 | tf_op jit(solution)/shard_map/ppermute | solution.py:96
  247.9 46.1 %collective-permute-start.17 = (bf16[2,2,2,24,3840]{4,3,2,1,0:T(8,128)(2,1)S(1)}, bf16[2,2,2,24,3840]{4,3,2,1,0:T(8,128)(2,1)S(1)}, u32[]{:S(2)}, u32[]{:S(2)}) collective-permute-start(bf16[2,2,2,24,3840]{4,3,2,1,0:T(8,128)(2,1)S(1)} %pad_maximum_fusion.17), channel_id=1, source_target_pairs={{0,16},{4,20},{8,24},{12,28},{16,0},{20,4},{24,8},{28,12},{1,17},{... | collective-permute-start | bytes 4423688 | tf_op jit(solution)/shard_map/ppermute | solution.py:96
  257.4 39.2 %collective-permute-start.40 = (bf16[2,2,2,24,3840]{4,3,2,1,0:T(8,128)(2,1)S(1)}, bf16[2,2,2,24,3840]{4,3,2,1,0:T(8,128)(2,1)S(1)}, u32[]{:S(2)}, u32[]{:S(2)}) collective-permute-start(bf16[2,2,2,24,3840]{4,3,2,1,0:T(8,128)(2,1)S(1)} %pad_maximum_fusion.18), channel_id=1, source_target_pairs={{0,16},{4,20},{8,24},{12,28},{16,0},{20,4},{24,8},{28,12},{1,17},{... | collective-permute-start | bytes 4423688 | tf_op jit(solution)/shard_map/ppermute | solution.py:96
  266.9 31.8 %collective-permute-start.7 = (bf16[2,2,2,2,24,2304]{5,4,3,2,1,0:T(8,128)(2,1)S(1)}, bf16[2,2,2,2,24,2304]{5,4,3,2,1,0:T(8,128)(2,1)S(1)}, u32[]{:S(2)}, u32[]{:S(2)}) collective-permute-start(bf16[2,2,2,2,24,2304]{5,4,3,2,1,0:T(8,128)(2,1)S(1)} %pad_maximum_fusion.15), channel_id=1, source_target_pairs={{0,4},{4,0},{8,12},{12,8},{16,20},{20,16},{24,28},{28,24},{1,5},{5... | collective-permute-start | bytes 5308424 | tf_op jit(solution)/shard_map/ppermute | solution.py:96
  279.5 24.0 %collective-permute-start.35 = (bf16[2,2,2,2,24,2304]{5,4,3,2,1,0:T(8,128)(2,1)}, bf16[2,2,2,2,24,2304]{5,4,3,2,1,0:T(8,128)(2,1)S(1)}, u32[]{:S(2)}, u32[]{:S(2)}) collective-permute-start(bf16[2,2,2,2,24,2304]{5,4,3,2,1,0:T(8,128)(2,1)} %pad_maximum_fusion.16), channel_id=1, source_target_pairs={{0,4},{4,0},{8,12},{12,8},{16,20},{20,16},{24,28},{28,24},{1,5},{5... | collective-permute-start | bytes 5308424 | tf_op jit(solution)/shard_map/ppermute | solution.py:96
  292.2 14.0 %collective-permute-start.23 = (bf16[2,2,2,2,96,768]{5,4,3,2,1,0:T(8,128)(2,1)S(1)}, bf16[2,2,2,2,96,768]{5,4,3,2,1,0:T(8,128)(2,1)}, u32[]{:S(2)}, u32[]{:S(2)}) collective-permute-start(bf16[2,2,2,2,96,768]{5,4,3,2,1,0:T(8,128)(2,1)S(1)} %pad_maximum_fusion.10), channel_id=1, source_target_pairs={{0,4},{4,0},{8,12},{12,8},{16,20},{20,16},{24,28},{28,24},{1,5},{5... | collective-permute-start | bytes 7077896 | tf_op jit(solution)/shard_map/ppermute | solution.py:96
  294.0 53.8 %collective-permute-start.46 = (bf16[2,2,2,2,96,768]{5,4,3,2,1,0:T(8,128)(2,1)}, bf16[2,2,2,2,96,768]{5,4,3,2,1,0:T(8,128)(2,1)}, u32[]{:S(2)}, u32[]{:S(2)}) collective-permute-start(bf16[2,2,2,2,96,768]{5,4,3,2,1,0:T(8,128)(2,1)} %pad_maximum_fusion.11), channel_id=1, source_target_pairs={{0,4},{4,0},{8,12},{12,8},{16,20},{20,16},{24,28},{28,24},{1,5},{5... | collective-permute-start | bytes 7077896 | tf_op jit(solution)/shard_map/ppermute | solution.py:96
  296.6 33.1 %collective-permute-start.18 = (bf16[2,2,2,2,24,3840]{5,4,3,2,1,0:T(8,128)(2,1)}, bf16[2,2,2,2,24,3840]{5,4,3,2,1,0:T(8,128)(2,1)}, u32[]{:S(2)}, u32[]{:S(2)}) collective-permute-start(bf16[2,2,2,2,24,3840]{5,4,3,2,1,0:T(8,128)(2,1)} %pad_maximum_fusion.8), channel_id=1, source_target_pairs={{0,4},{4,0},{8,12},{12,8},{16,20},{20,16},{24,28},{28,24},{1,5},{5... | collective-permute-start | bytes 8847368 | tf_op jit(solution)/shard_map/ppermute | solution.py:96
  298.6 64.2 %collective-permute-start.41 = (bf16[2,2,2,2,24,3840]{5,4,3,2,1,0:T(8,128)(2,1)}, bf16[2,2,2,2,24,3840]{5,4,3,2,1,0:T(8,128)(2,1)}, u32[]{:S(2)}, u32[]{:S(2)}) collective-permute-start(bf16[2,2,2,2,24,3840]{5,4,3,2,1,0:T(8,128)(2,1)} %pad_maximum_fusion.9), channel_id=1, source_target_pairs={{0,4},{4,0},{8,12},{12,8},{16,20},{20,16},{24,28},{28,24},{1,5},{5... | collective-permute-start | bytes 8847368 | tf_op jit(solution)/shard_map/ppermute | solution.py:96
  361.2 18.6 %collective-permute-start.36 = (bf16[512,1536]{1,0:T(8,128)(2,1)}, bf16[512,1536]{1,0:T(8,128)(2,1)}, u32[]{:S(2)}, u32[]{:S(2)}) collective-permute-start(bf16[512,1536]{1,0:T(8,128)(2,1)} %slice.550), channel_id=1, source_target_pairs={{0,4},{1,5},{2,6},{3,7},{4,0},{5,1},{6,2},{7,3},{8,12},{9,13},{10,... | collective-permute-start | bytes 4718600 | tf_op jit(solution)/shard_map/ppermute | solution.py:189
  471.7 10.8 %collective-permute-start.47 = (bf16[2,512,768]{2,1,0:T(8,128)(2,1)}, bf16[2,512,768]{2,1,0:T(8,128)(2,1)S(1)}, u32[]{:S(2)}, u32[]{:S(2)}) collective-permute-start(bf16[2,512,768]{2,1,0:T(8,128)(2,1)} %copy-done.16), channel_id=1, source_target_pairs={{0,4},{1,5},{2,6},{3,7},{4,0},{5,1},{6,2},{7,3},{8,12},{9,13},{10,... | collective-permute-start | bytes 4718600 | tf_op jit(solution)/shard_map/ppermute | solution.py:189
  475.8 108.2 %collective-permute-start.83 = (bf16[2,2,2,2,96,768]{5,4,3,2,0,1:T(8,128)(2,1)}, bf16[2,2,2,2,96,768]{5,4,3,2,0,1:T(8,128)(2,1)}, u32[]{:S(2)}, u32[]{:S(2)}) collective-permute-start(bf16[2,2,2,2,96,768]{5,4,3,2,0,1:T(8,128)(2,1)} %select_bitcast_fusion.6), channel_id=1, source_target_pairs={{0,4},{4,0},{8,12},{12,8},{16,20},{20,16},{24,28},{28,24},{1,5},{5... | collective-permute-start | bytes 7077896 | tf_op jit(solution)/shard_map/ppermute | solution.py:96
  482.5 112.6 %collective-permute-start.73 = (bf16[2,2,2,2,24,3840]{5,4,3,2,1,0:T(8,128)(2,1)}, bf16[2,2,2,2,24,3840]{5,4,3,2,1,0:T(8,128)(2,1)}, u32[]{:S(2)}, u32[]{:S(2)}) collective-permute-start(bf16[2,2,2,2,24,3840]{5,4,3,2,1,0:T(8,128)(2,1)} %select_bitcast_fusion), channel_id=1, source_target_pairs={{0,4},{4,0},{8,12},{12,8},{16,20},{20,16},{24,28},{28,24},{1,5},{5... | collective-permute-start | bytes 8847368 | tf_op jit(solution)/shard_map/ppermute | solution.py:96
  524.4 65.7 %collective-permute-start.49 = (bf16[256,2304]{1,0:T(8,128)(2,1)}, bf16[256,2304]{1,0:T(8,128)(2,1)}, u32[]{:S(2)}, u32[]{:S(2)}) collective-permute-start(bf16[256,2304]{1,0:T(8,128)(2,1)} %get-tuple-element.95), channel_id=1, source_target_pairs={{1,0},{0,1},{5,2},{4,3},{3,4},{2,5},{7,6},{6,7},{9,8},{8,9},{13,10... | collective-permute-start | bytes 3538952 | tf_op jit(solution)/shard_map/ppermute | solution.py:168
  525.0 65.6 %collective-permute-start.48 = (bf16[256,2304]{1,0:T(8,128)(2,1)}, bf16[256,2304]{1,0:T(8,128)(2,1)}, u32[]{:S(2)}, u32[]{:S(2)}) collective-permute-start(bf16[256,2304]{1,0:T(8,128)(2,1)} %get-tuple-element.96), channel_id=1, source_target_pairs={{0,0},{1,1},{4,2},{5,3},{2,4},{3,5},{6,6},{7,7},{8,8},{9,9},{12,10... | collective-permute-start | bytes 3538952 | tf_op jit(solution)/shard_map/ppermute | solution.py:168
  569.4 32.1 %collective-permute-start.50 = (bf16[2,512,768]{2,1,0:T(8,128)(2,1)}, bf16[2,512,768]{2,1,0:T(8,128)(2,1)}, u32[]{:S(2)}, u32[]{:S(2)}) collective-permute-start(bf16[2,512,768]{2,1,0:T(8,128)(2,1)} %copy-done.15), channel_id=1, source_target_pairs={{0,4},{1,5},{2,6},{3,7},{4,0},{5,1},{6,2},{7,3},{8,12},{9,13},{10,... | collective-permute-start | bytes 4718600 | tf_op jit(solution)/shard_map/ppermute | solution.py:189
  584.0 55.5 %collective-permute-start.58 = (bf16[2,2,2,2,24,2304]{5,4,3,2,0,1:T(8,128)(2,1)}, bf16[2,2,2,2,24,2304]{5,4,3,2,0,1:T(8,128)(2,1)}, u32[]{:S(2)}, u32[]{:S(2)}) collective-permute-start(bf16[2,2,2,2,24,2304]{5,4,3,2,0,1:T(8,128)(2,1)} %select_bitcast_fusion.12), channel_id=1, source_target_pairs={{0,4},{4,0},{8,12},{12,8},{16,20},{20,16},{24,28},{28,24},{1,5},{5... | collective-permute-start | bytes 5308424 | tf_op jit(solution)/shard_map/ppermute | solution.py:96
  590.2 70.0 %collective-permute-start.78 = (bf16[2,2,2,2,96,768]{5,4,3,2,0,1:T(8,128)(2,1)}, bf16[2,2,2,2,96,768]{5,4,3,2,0,1:T(8,128)(2,1)}, u32[]{:S(2)}, u32[]{:S(2)}) collective-permute-start(bf16[2,2,2,2,96,768]{5,4,3,2,0,1:T(8,128)(2,1)} %select_bitcast_fusion.7), channel_id=1, source_target_pairs={{0,4},{4,0},{8,12},{12,8},{16,20},{20,16},{24,28},{28,24},{1,5},{5... | collective-permute-start | bytes 7077896 | tf_op jit(solution)/shard_map/ppermute | solution.py:96
  590.5 121.1 %collective-permute-start.68 = (bf16[2,2,2,2,24,3840]{5,4,3,2,1,0:T(8,128)(2,1)}, bf16[2,2,2,2,24,3840]{5,4,3,2,1,0:T(8,128)(2,1)}, u32[]{:S(2)}, u32[]{:S(2)}) collective-permute-start(bf16[2,2,2,2,24,3840]{5,4,3,2,1,0:T(8,128)(2,1)} %select_bitcast_fusion.1), channel_id=1, source_target_pairs={{0,4},{4,0},{8,12},{12,8},{16,20},{20,16},{24,28},{28,24},{1,5},{5... | collective-permute-start | bytes 8847368 | tf_op jit(solution)/shard_map/ppermute | solution.py:96
  595.1 61.6 %collective-permute-start.84 = (bf16[2,2,2,96,768]{4,3,2,1,0:T(8,128)(2,1)}, bf16[2,2,2,96,768]{4,3,2,1,0:T(8,128)(2,1)}, u32[]{:S(2)}, u32[]{:S(2)}) collective-permute-start(bf16[2,2,2,96,768]{4,3,2,1,0:T(8,128)(2,1)} %select_bitcast_fusion.24), channel_id=1, source_target_pairs={{0,8},{4,12},{8,0},{12,4},{16,24},{20,28},{24,16},{28,20},{1,9},{5... | collective-permute-start | bytes 3538952 | tf_op jit(solution)/shard_map/ppermute | solution.py:96
  607.9 16.2 %collective-permute-start.64 = (f32[2,2,2,1,2,288]{5,2,1,0,4,3:T(2,128)S(1)}, f32[2,2,2,1,2,288]{5,2,1,0,4,3:T(2,128)S(1)}, u32[]{:S(2)}, u32[]{:S(2)}) collective-permute-start(f32[2,2,2,1,2,288]{5,2,1,0,4,3:T(2,128)S(1)} %fusion.126), channel_id=1, source_target_pairs={{0,8},{4,12},{8,0},{12,4},{16,24},{20,28},{24,16},{28,20},{1,9},{5... | collective-permute-start | bytes 55304 | tf_op jit(solution)/shard_map/ppermute | solution.py:96
  636.2 11.9 %collective-permute-start.52 = (bf16[256,768]{1,0:T(8,128)(2,1)S(1)}, bf16[256,768]{1,0:T(8,128)(2,1)S(1)}, u32[]{:S(2)}, u32[]{:S(2)}) collective-permute-start(bf16[256,768]{1,0:T(8,128)(2,1)S(1)} %get-tuple-element.129), channel_id=1, source_target_pairs={{1,0},{0,1},{5,2},{4,3},{3,4},{2,5},{7,6},{6,7},{9,8},{8,9},{13,10... | collective-permute-start | bytes 1179656 | tf_op jit(solution)/shard_map/ppermute | solution.py:168
  648.0 62.9 %collective-permute-start.74 = (bf16[2,2,2,24,3840]{4,3,2,1,0:T(8,128)(2,1)S(1)}, bf16[2,2,2,24,3840]{4,3,2,1,0:T(8,128)(2,1)S(1)}, u32[]{:S(2)}, u32[]{:S(2)}) collective-permute-start(bf16[2,2,2,24,3840]{4,3,2,1,0:T(8,128)(2,1)S(1)} %copy-done.58), channel_id=1, source_target_pairs={{0,16},{4,20},{8,24},{12,28},{16,0},{20,4},{24,8},{28,12},{1,17},{... | collective-permute-start | bytes 4423688 | tf_op jit(solution)/shard_map/ppermute | solution.py:96
  649.6 81.7 %collective-permute-start.53 = (bf16[2,2,2,2,24,2304]{5,4,3,2,0,1:T(8,128)(2,1)S(1)}, bf16[2,2,2,2,24,2304]{5,4,3,2,0,1:T(8,128)(2,1)S(1)}, u32[]{:S(2)}, u32[]{:S(2)}) collective-permute-start(bf16[2,2,2,2,24,2304]{5,4,3,2,0,1:T(8,128)(2,1)S(1)} %select_bitcast_fusion.13), channel_id=1, source_target_pairs={{0,4},{4,0},{8,12},{12,8},{16,20},{20,16},{24,28},{28,24},{1,5},{5... | collective-permute-start | bytes 5308424 | tf_op jit(solution)/shard_map/ppermute | solution.py:96
  656.7 38.6 %collective-permute-start.59 = (bf16[2,2,2,24,2304]{4,3,2,1,0:T(8,128)(2,1)S(1)}, bf16[2,2,2,24,2304]{4,3,2,1,0:T(8,128)(2,1)S(1)}, u32[]{:S(2)}, u32[]{:S(2)}) collective-permute-start(bf16[2,2,2,24,2304]{4,3,2,1,0:T(8,128)(2,1)S(1)} %select_bitcast_fusion.30), channel_id=1, source_target_pairs={{0,8},{4,12},{8,0},{12,4},{16,24},{20,28},{24,16},{28,20},{1,9},{5... | collective-permute-start | bytes 2654216 | tf_op jit(solution)/shard_map/ppermute | solution.py:96
  660.2 33.3 %collective-permute-start.85 = (bf16[2,2,96,768]{3,2,1,0:T(8,128)(2,1)S(1)}, bf16[2,2,96,768]{3,2,1,0:T(8,128)(2,1)S(1)}, u32[]{:S(2)}, u32[]{:S(2)}) collective-permute-start(bf16[2,2,96,768]{3,2,1,0:T(8,128)(2,1)S(1)} %select_bitcast_fusion.42), channel_id=1, source_target_pairs={{0,16},{4,20},{8,24},{12,28},{16,0},{20,4},{24,8},{28,12},{1,17},{... | collective-permute-start | bytes 1769480 | tf_op jit(solution)/shard_map/ppermute | solution.py:96
  693.4 44.2 %collective-permute-start.79 = (bf16[2,2,2,96,768]{4,3,2,1,0:T(8,128)(2,1)S(1)}, bf16[2,2,2,96,768]{4,3,2,1,0:T(8,128)(2,1)S(1)}, u32[]{:S(2)}, u32[]{:S(2)}) collective-permute-start(bf16[2,2,2,96,768]{4,3,2,1,0:T(8,128)(2,1)S(1)} %select_bitcast_fusion.25), channel_id=1, source_target_pairs={{0,8},{4,12},{8,0},{12,4},{16,24},{20,28},{24,16},{28,20},{1,9},{5... | collective-permute-start | bytes 3538952 | tf_op jit(solution)/shard_map/ppermute | solution.py:96
  695.3 14.0 %collective-permute-start.86 = (bf16[2,96,768]{2,1,0:T(8,128)(2,1)S(1)}, bf16[2,96,768]{2,1,0:T(8,128)(2,1)S(1)}, u32[]{:S(2)}, u32[]{:S(2)}) collective-permute-start(bf16[2,96,768]{2,1,0:T(8,128)(2,1)S(1)} %select_bitcast_fusion.60), channel_id=1, source_target_pairs={{0,2},{1,3},{2,0},{3,1},{4,6},{5,7},{6,4},{7,5},{8,10},{9,11},{10,... | collective-permute-start | bytes 884744 | tf_op jit(solution)/shard_map/ppermute | solution.py:94
  710.9 10.7 %collective-permute-start.87 = (bf16[96,768]{1,0:T(8,128)(2,1)S(1)}, bf16[96,768]{1,0:T(8,128)(2,1)S(1)}, u32[]{:S(2)}, u32[]{:S(2)}) collective-permute-start(bf16[96,768]{1,0:T(8,128)(2,1)S(1)} %select_bitcast_fusion.79), channel_id=1, source_target_pairs={{0,1},{1,0},{2,3},{3,2},{4,5},{5,4},{6,7},{7,6},{8,9},{9,8},{10,11... | collective-permute-start | bytes 442376 | tf_op jit(solution)/shard_map/ppermute | solution.py:94
  711.7 24.3 %collective-permute-start.75 = (bf16[2,2,24,3840]{3,2,1,0:T(8,128)(2,1)S(1)}, bf16[2,2,24,3840]{3,2,1,0:T(8,128)(2,1)S(1)}, u32[]{:S(2)}, u32[]{:S(2)}) collective-permute-start(bf16[2,2,24,3840]{3,2,1,0:T(8,128)(2,1)S(1)} %select_bitcast_fusion.36), channel_id=1, source_target_pairs={{0,8},{4,12},{8,0},{12,4},{16,24},{20,28},{24,16},{28,20},{1,9},{5... | collective-permute-start | bytes 2211848 | tf_op jit(solution)/shard_map/ppermute | solution.py:96
  719.0 57.4 %collective-permute-start.69 = (bf16[2,2,2,24,3840]{4,3,2,1,0:T(8,128)(2,1)S(1)}, bf16[2,2,2,24,3840]{4,3,2,1,0:T(8,128)(2,1)S(1)}, u32[]{:S(2)}, u32[]{:S(2)}) collective-permute-start(bf16[2,2,2,24,3840]{4,3,2,1,0:T(8,128)(2,1)S(1)} %select_bitcast_fusion.19), channel_id=1, source_target_pairs={{0,16},{4,20},{8,24},{12,28},{16,0},{20,4},{24,8},{28,12},{1,17},{... | collective-permute-start | bytes 4423688 | tf_op jit(solution)/shard_map/ppermute | solution.py:96
  732.0 31.4 %collective-permute-start.54 = (bf16[2,2,2,24,2304]{4,3,2,1,0:T(8,128)(2,1)S(1)}, bf16[2,2,2,24,2304]{4,3,2,1,0:T(8,128)(2,1)S(1)}, u32[]{:S(2)}, u32[]{:S(2)}) collective-permute-start(bf16[2,2,2,24,2304]{4,3,2,1,0:T(8,128)(2,1)S(1)} %select_bitcast_fusion.31), channel_id=1, source_target_pairs={{0,8},{4,12},{8,0},{12,4},{16,24},{20,28},{24,16},{28,20},{1,9},{5... | collective-permute-start | bytes 2654216 | tf_op jit(solution)/shard_map/ppermute | solution.py:96
  736.4 16.8 %collective-permute-start.76 = (bf16[2,24,3840]{2,1,0:T(8,128)(2,1)S(1)}, bf16[2,24,3840]{2,1,0:T(8,128)(2,1)S(1)}, u32[]{:S(2)}, u32[]{:S(2)}) collective-permute-start(bf16[2,24,3840]{2,1,0:T(8,128)(2,1)S(1)} %select_bitcast_fusion.54), channel_id=1, source_target_pairs={{0,2},{1,3},{2,0},{3,1},{4,6},{5,7},{6,4},{7,5},{8,10},{9,11},{10,... | collective-permute-start | bytes 1105928 | tf_op jit(solution)/shard_map/ppermute | solution.py:94
  738.2 23.7 %collective-permute-start.80 = (bf16[2,2,96,768]{3,2,1,0:T(8,128)(2,1)S(1)}, bf16[2,2,96,768]{3,2,1,0:T(8,128)(2,1)S(1)}, u32[]{:S(2)}, u32[]{:S(2)}) collective-permute-start(bf16[2,2,96,768]{3,2,1,0:T(8,128)(2,1)S(1)} %select_bitcast_fusion.43), channel_id=1, source_target_pairs={{0,16},{4,20},{8,24},{12,28},{16,0},{20,4},{24,8},{28,12},{1,17},{... | collective-permute-start | bytes 1769480 | tf_op jit(solution)/shard_map/ppermute | solution.py:96
  762.1 14.1 %collective-permute-start.81 = (bf16[2,96,768]{2,1,0:T(8,128)(2,1)S(1)}, bf16[2,96,768]{2,1,0:T(8,128)(2,1)S(1)}, u32[]{:S(2)}, u32[]{:S(2)}) collective-permute-start(bf16[2,96,768]{2,1,0:T(8,128)(2,1)S(1)} %select_bitcast_fusion.61), channel_id=1, source_target_pairs={{0,2},{1,3},{2,0},{3,1},{4,6},{5,7},{6,4},{7,5},{8,10},{9,11},{10,... | collective-permute-start | bytes 884744 | tf_op jit(solution)/shard_map/ppermute | solution.py:94
  763.8 14.5 %collective-permute-start.55 = (bf16[2,2,24,2304]{3,2,1,0:T(8,128)(2,1)S(1)}, bf16[2,2,24,2304]{3,2,1,0:T(8,128)(2,1)S(1)}, u32[]{:S(2)}, u32[]{:S(2)}) collective-permute-start(bf16[2,2,24,2304]{3,2,1,0:T(8,128)(2,1)S(1)} %select_bitcast_fusion.49), channel_id=1, source_target_pairs={{0,16},{4,20},{8,24},{12,28},{16,0},{20,4},{24,8},{28,12},{1,17},{... | collective-permute-start | bytes 1327112 | tf_op jit(solution)/shard_map/ppermute | solution.py:96
  777.1 17.6 %collective-permute-start.70 = (bf16[2,2,24,3840]{3,2,1,0:T(8,128)(2,1)S(1)}, bf16[2,2,24,3840]{3,2,1,0:T(8,128)(2,1)S(1)}, u32[]{:S(2)}, u32[]{:S(2)}) collective-permute-start(bf16[2,2,24,3840]{3,2,1,0:T(8,128)(2,1)S(1)} %select_bitcast_fusion.37), channel_id=1, source_target_pairs={{0,8},{4,12},{8,0},{12,4},{16,24},{20,28},{24,16},{28,20},{1,9},{5... | collective-permute-start | bytes 2211848 | tf_op jit(solution)/shard_map/ppermute | solution.py:96
  778.5 13.0 %collective-permute-start.56 = (bf16[2,24,2304]{2,1,0:T(8,128)(2,1)S(1)}, bf16[2,24,2304]{2,1,0:T(8,128)(2,1)S(1)}, u32[]{:S(2)}, u32[]{:S(2)}) collective-permute-start(bf16[2,24,2304]{2,1,0:T(8,128)(2,1)S(1)} %select_bitcast_fusion.67), channel_id=1, source_target_pairs={{0,2},{1,3},{2,0},{3,1},{4,6},{5,7},{6,4},{7,5},{8,10},{9,11},{10,... | collective-permute-start | bytes 663560 | tf_op jit(solution)/shard_map/ppermute | solution.py:94
  795.0 19.0 %collective-permute-start.71 = (bf16[2,24,3840]{2,1,0:T(8,128)(2,1)S(1)}, bf16[2,24,3840]{2,1,0:T(8,128)(2,1)S(1)}, u32[]{:S(2)}, u32[]{:S(2)}) collective-permute-start(bf16[2,24,3840]{2,1,0:T(8,128)(2,1)S(1)} %select_bitcast_fusion.55), channel_id=1, source_target_pairs={{0,2},{1,3},{2,0},{3,1},{4,6},{5,7},{6,4},{7,5},{8,10},{9,11},{10,... | collective-permute-start | bytes 1105928 | tf_op jit(solution)/shard_map/ppermute | solution.py:94
  (130 other events, 1524.4 us)

commit v2 on v1

--- a/solution.py
+++ b/solution.py
@@ -20,6 +20,40 @@
 PAIR = 2 * HEAD_DIM
 BF = jnp.bfloat16
 F32 = jnp.float32
+
+GATHER_TICKS, HEAD_TICKS, TAIL_TICKS = 7, 2, 0
+PLAN = {
+    "g0": ["qkv_one"],
+    "g1": ["qkv_one", "ffn_one"],
+    "g2": ["qkv_one", "ffn_one"],
+    "g3": ["qkv_one", "hidden"],
+    "g4": ["qkv_one", "ffn_one"],
+    "g5": ["qkv_one", "hidden", "qkv_two"],
+    "f0.qkv": ["ffn_one", "qkv_two"],
+    "f0.attend": ["ffn_one", "qkv_two", "ffn_two"],
+    "f0.normed": ["ffn_one", "qkv_two", "ffn_two"],
+    "f0.active": ["skip"],
+    "f0.out": [],
+    "h0": ["qkv_two", "cls", "ffn_two"],
+    "h1": ["qkv_two", "cls", "skip", "cots"],
+    "f1.qkv": ["ffn_two", "cls"],
+    "f1.attend": ["ffn_two", "cls"],
+    "f1.normed": ["ffn_two", "cls"],
+    "f1.out": ["cls", "cots"],
+    "t": ["outs"],
+    "b1.d_outer": ["back_outer_two"],
+    "b1.d_inner": ["back_outer_two", "back_inner_two"],
+    "b1.d_mixture": ["back_inner_two"],
+    "b1.d_queries": ["back_outer_two", "back_inner_two"],
+    "b1.d_qkv": ["back_outer_two", "back_inner_two", "back_qkv_two", "outs"],
+    "u": ["back_z_two", "back_qkv_two", "skip_back"],
+    "b0.d_outer": ["back_outer_one"],
+    "b0.d_inner": ["back_z_two", "back_qkv_two", "back_outer_one", "back_inner_one"],
+    "b0.d_mixture": ["back_z_two", "back_inner_one"],
+    "b0.d_queries": ["back_outer_one", "back_inner_one", "back_qkv_two", "skip_back"],
+    "b0.d_qkv": ["back_outer_one", "back_inner_one", "back_qkv_one", "back_qkv_two"],
+    "b0.d_input": ["back_qkv_one", "back_qkv_two"],
+}
 
 
 def layer_norm(residual, norm_gain, norm_shift):
@@ -95,41 +129,88 @@
         flip = 1 << (bit - self.f_bits)
         return lax.ppermute(x, "dp", [(i, i ^ flip) for i in range(self.n_dp)])
 
-    def gather_order(self, turned):
-        upper = list(range(self.f_bits + 1, self.f_bits + self.d_bits))
-        if not turned:
-            upper = upper[::-1]
-        return list(range(self.f_bits)) + upper + [self.f_bits]
-
-    def gather(self, x, order):
-        have, out = [], x
-        for bit in order:
-            other = self.swap(out, bit)
-            mine = self.my_bit(bit) == 0
-            place = sum(1 for b in have if b > bit)
-            low = jnp.where(mine, out, other)
-            high = jnp.where(mine, other, out)
-            out = jnp.stack([low, high], axis=place)
-            have.append(bit)
+    def upper(self, turned):
+        bits = list(range(self.f_bits + 1, self.f_bits + self.d_bits))
+        return bits if turned else bits[::-1]
+
+    def join(self, own, other, bit, have):
+        mine = self.my_bit(bit) == 0
+        low = jnp.where(mine, own, other)
+        high = jnp.where(mine, other, own)
+        return jnp.stack([low, high], axis=sum(1 for b in have if b > bit))
+
+    def gather(self, x, bits):
+        out = x
+        for n, bit in enumerate(bits):
+            other = yield self.swap(out, bit)
+            out = self.join(out, other, bit, bits[:n])
         return out.reshape((-1,) + x.shape[1:])
 
-    def scatter(self, x, order, wire=BF):
-        left = sorted(order, reverse=True)
-        tail = (x.shape[0] >> len(order),) + x.shape[1:]
-        out = x.reshape((2,) * len(order) + tail)
-        for bit in reversed(order):
-            place = left.index(bit)
-            low = lax.index_in_dim(out, 0, place, keepdims=False)
-            high = lax.index_in_dim(out, 1, place, keepdims=False)
-            mine = self.my_bit(bit) == 0
-            kept = jnp.where(mine, low, high)
-            sent = jnp.where(mine, high, low).astype(wire)
-            got = self.swap(sent, bit)
-            out = kept.astype(F32) + got.astype(F32)
+    def gather_two(self, x, y):
+        outs = [x, y]
+        ways = [self.upper(False), self.upper(True)]
+        for n in range(self.d_bits - 1):
+            others = yield [self.swap(o, way[n]) for o, way in zip(outs, ways)]
+            outs = [
+                self.join(o, other, way[n], way[:n])
+                for o, other, way in zip(outs, others, ways)
+            ]
+        core = self.f_bits
+        others = yield [self.swap(o, core) for o in outs]
+        outs = [self.join(o, other, core, ways[0]) for o, other in zip(outs, others)]
+        return [o.reshape((-1,) + v.shape[1:]) for o, v in zip(outs, (x, y))]
+
+    def gather_split(self, x):
+        half = x.shape[0] // 2
+        outs = [x[:half], x[half:]]
+        ways = [self.upper(False), self.upper(True)]
+        for n in range(self.d_bits - 1):
+            others = yield [self.swap(o, way[n]) for o, way in zip(outs, ways)]
+            outs = [
+                self.join(o, other, way[n], way[:n])
+                for o, other, way in zip(outs, others, ways)
+            ]
+        out = jnp.concatenate(outs, axis=self.d_bits - 1)
+        core = self.f_bits
+        other = yield self.swap(out, core)
+        return self.join(out, other, core, ways[0]).reshape((-1,) + x.shape[1:])
+
+    def halves(self, x, bit, left):
+        place = left.index(bit)
+        mine = self.my_bit(bit)
+        pick = lambda at: lax.dynamic_index_in_dim(x, at, place, keepdims=False)
+        return pick(mine), pick(1 - mine)
+
+    def scatter(self, x, bits):
+        left = sorted(bits, reverse=True)
+        out = x.reshape((2,) * len(bits) + (-1,) + x.shape[1:])
+        for bit in bits:
+            kept, sent = self.halves(out, bit, left)
+            got = yield self.swap(sent, bit)
             left.remove(bit)
-            if left:
-                out = out.astype(wire)
+            out = (kept.astype(F32) + got.astype(F32)).astype(BF)
         return out
+
+    def scatter_split(self, x):
+        left = list(range(self.f_bits + self.d_bits - 1, self.f_bits - 1, -1))
+        out = x.reshape((2,) * self.d_bits + (2, -1) + x.shape[1:])
+        kept, sent = self.halves(out, self.f_bits, left)
+        got = yield self.swap(sent, self.f_bits)
+        out = (kept.astype(F32) + got.astype(F32)).astype(BF)
+        left.remove(self.f_bits)
+        outs = [lax.index_in_dim(out, h, len(left), keepdims=False) for h in range(2)]
+        ways = [self.upper(True), self.upper(False)]
+        lefts = [list(left), list(left)]
+        for n in range(self.d_bits - 1):
+            pairs = [self.halves(o, way[n], l) for o, way, l in zip(outs, ways, lefts)]
+            gots = yield [self.swap(sent, way[n]) for (_, sent), way in zip(pairs, ways)]
+            outs = [
+                (kept.astype(F32) + got.astype(F32)).astype(BF)
+                for (kept, _), got in zip(pairs, gots)
+            ]
+            for l, way in zip(lefts, ways):
+                l.remove(way[n])
+        return jnp.concatenate(outs, axis=0)
 
     def source(self, k):
         pairs = []
@@ -149,6 +230,7 @@
         for k in range(self.rows_dev):
             block = lax.dynamic_index_in_dim(x, (self.f + k) % self.rows_dev, 0, keepdims=False)
             got.append(lax.ppermute(block, ("dp", "fsdp"), self.source(k)))
+        got = yield got
         got = jnp.stack(got)
         b = self.row_in_group % self.rows_dev
         return jnp.concatenate(
@@ -166,6 +248,7 @@
             block = lax.dynamic_index_in_dim(parts, (b - k) % self.rows_dev, 0, keepdims=False)
             back = [(t, s) for s, t in self.source(k)]
             got.append(lax.ppermute(block, ("dp", "fsdp"), back))
+        got = yield got
         got = jnp.stack(got)
         return jnp.stack(
             [
@@ -187,6 +270,52 @@
 
     def to_member(self, x, shift):
         return lax.ppermute(x, ("dp", "fsdp"), self.shift_pairs(shift))
+
+
+class Schedule:
+    def __init__(self, plan):
+        self.plan = plan
+        self.makers, self.running, self.waiting, self.result = {}, {}, {}, {}
+
+    def add(self, name, maker, *operands):
+        self.makers[name] = (maker, operands)
+
+    def step(self, name, value):
+        try:
+            self.waiting[name] = (
+                next(self.running[name]) if value is None else self.running[name].send(value)
+            )
+        except StopIteration as end:
+            self.waiting.pop(name, None)
+            self.result[name] = end.value
+
+    def tick(self, point, value):
+        names = [n for n in self.plan.get(point, ()) if n not in self.result]
+        if not names:
+            return value
+        arrived = {n: self.waiting[n] for n in names if n in self.running}
+        fresh = {n: self.makers[n][1] for n in names if n not in self.running}
+        value, arrived, fresh = lax.optimization_barrier((value, arrived, fresh))
+        for name in names:
+            if name in arrived:
+                self.step(name, arrived[name])
+            else:
+                self.running[name] = self.makers[name][0](*fresh[name])
+                self.step(name, None)
+        return value
+
+    def get(self, name):
+        return self.finish(name)[0]
+
+    def finish(self, *names):
+        while any(n not in self.result for n in names):
+            for name in names:
+                if name not in self.running:
+                    self.running[name] = self.makers[name][0](*self.makers[name][1])
+                    self.step(name, None)
+                elif name not in self.result:
+                    self.step(name, self.waiting[name])
+        return [self.result[n] for n in names]
 
 
 def dot_nt(a, b):
@@ -380,29 +509,35 @@
     return vectors
 
 
-def layer_forward(grid, inputs, weights, seg_q, seg_k):
-    (qkv_w, attn_w, inner_w, outer_w, qv_b, attn_b, attn_g, attn_s, inner_b, outer_b, ffn_g, ffn_s) = weights
+def layer_forward(grid, tag, tick, inputs, weights, seg_q, seg_k):
     width = inputs.shape[1]
     x_low = inputs.astype(BF)
+    qkv_w, attn_w, qv_b, attn_b, attn_g, attn_s, inner_b, outer_b, ffn_g, ffn_s = weights("qkv")
     bias = jnp.concatenate([qv_b[:width], jnp.zeros((width,), F32), qv_b[width:]])
     qkv = (matrix_product(x_low, qkv_w) + bias).astype(BF)
+    qkv = tick(tag + "qkv", qkv)
     key_value = qkv[:, width:]
     others = [grid.to_member(key_value, shift) for shift in range(1, grid.members)]
     mixture, lse = attend(qkv, others, seg_q, seg_k)
+    mixture = tick(tag + "attend", mixture)
     branch = matrix_product(mixture, attn_w) + attn_b
     normed, normed_one, inv_one = layer_norm(inputs.astype(F32) + branch, attn_g, attn_s)
+    normed = tick(tag + "normed", normed)
+    inner_w, outer_w = weights("ffn")
     normed_low = normed.astype(BF)
     inner = matrix_product(normed_low, inner_w) + inner_b
     active, slope = gelu_both(inner)
-    active = active.astype(BF)
+    active = tick(tag + "active", active.astype(BF))
     outer = matrix_product(active, outer_w) + outer_b
     output, normed_two, inv_two = layer_norm(normed + outer, ffn_g, ffn_s)
+    output = tick(tag + "out", output)
     saved = (x_low, qkv, others, lse, mixture, normed_one, inv_one, normed_low, slope, active, normed_two, inv_two)
     return output, saved
 
 
-def layer_backward(grid, upstream, weights, saved, seg_q, seg_k):
-    (qkv_w, attn_w, inner_w, outer_w, qv_b, attn_b, attn_g, attn_s, inner_b, outer_b, ffn_g, ffn_s) = weights
+def layer_backward(grid, tag, tick, give, upstream, weights, saved, seg_q, seg_k):
+    qkv_w, attn_w, qv_b, attn_b, attn_g, attn_s, inner_b, outer_b, ffn_g, ffn_s = weights("qkv")
+    inner_w, outer_w = weights("ffn")
     (x_low, qkv, others, lse, mixture, normed_one, inv_one, normed_low, slope, active, normed_two, inv_two) = saved
     grad_ffn_g = jnp.sum(upstream * normed_two, axis=0)
     grad_ffn_s = jnp.sum(upstream, axis=0)
@@ -410,9 +545,15 @@
     d_outer = d_second.astype(BF)
     grad_outer_b = column_sum(d_outer)
     grad_outer_w = left_t(active, d_outer).astype(BF)
+    give("outer", grad_outer_w)
+    d_outer, grad_outer_w = lax.optimization_barrier((d_outer, grad_outer_w))
+    d_outer = tick(tag + "d_outer", d_outer)
     d_inner = (right_t(d_outer, outer_w) * slope).astype(BF)
     grad_inner_b = column_sum(d_inner)
     grad_inner_w = left_t(normed_low, d_inner).astype(BF)
+    give("inner", grad_inner_w)
+    d_inner, grad_inner_w = lax.optimization_barrier((d_inner, grad_inner_w))
+    d_inner = tick(tag + "d_inner", d_inner)
     d_normed = right_t(d_inner, inner_w) + d_second
     grad_attn_g = jnp.sum(d_normed * normed_one, axis=0)
     grad_attn_s = jnp.sum(d_normed, axis=0)
@@ -421,17 +562,21 @@
     grad_attn_b = column_sum(d_branch)
     grad_attn_w = left_t(mixture, d_branch).astype(BF)
     d_mixture = right_t(d_branch, attn_w).astype(BF)
+    d_mixture = tick(tag + "d_mixture", d_mixture)
     d_queries, own, for_others = attend_back(qkv, others, d_mixture, lse, seg_q, seg_k)
+    d_queries = tick(tag + "d_queries", d_queries)
     for shift in range(1, grid.members):
         own = own + grid.to_member(for_others[shift - 1], -shift).astype(F32)
     own = own.astype(BF)
     d_qkv = jnp.concatenate([d_queries, own[0], own[1]], axis=1)
     grad_qv_b = jnp.concatenate([column_sum(d_queries), column_sum(own[1])])
     grad_qkv_w = left_t(x_low, d_qkv).astype(BF)
+    small = (grad_qv_b, grad_attn_b, grad_attn_g, grad_attn_s, grad_inner_b, grad_outer_b, grad_ffn_g, grad_ffn_s)
+    give("qkv", grad_qkv_w, grad_attn_w, small)
+    d_qkv = tick(tag + "d_qkv", d_qkv)
     d_input = right_t(d_qkv, qkv_w) + d_first
-    grads = (grad_qkv_w, grad_attn_w, grad_inner_w, grad_outer_w)
-    small = (grad_qv_b, grad_attn_b, grad_attn_g, grad_attn_s, grad_inner_b, grad_outer_b, grad_ffn_g, grad_ffn_s)
-    return d_input, grads, small
+    d_input = tick(tag + "d_input", d_input)
+    return d_input
 
 
 def contrastive(vectors, positives):
@@ -492,89 +637,174 @@
     cls_hot = (my_starts[:, None] == q_pos[None, :]).astype(F32)
     is_cls = jnp.any(my_starts[:, None] == q_pos[None, :], axis=0)[:, None]
 
-    order, turned = grid.gather_order(False), grid.gather_order(True)
-    x = grid.to_rows(hidden)
+    devices = grid.n_dp * grid.n_f
+    z_up, z_down = list(range(grid.f_bits)), list(range(grid.f_bits))[::-1]
     vectors = (qv_bias, attn_bias, attn_gain, attn_shift, inner_bias, outer_bias, ffn_gain, ffn_shift)
     sizes = [v.shape[1] for v in vectors]
-    small_own = jnp.concatenate(vectors, axis=1)
-    small = grid.gather(small_own[None], order)
-    layers = []
-    for layer in range(2):
-        qkv_w = grid.gather(qkv_weight[layer], order)
-        mid = jnp.concatenate([attn_weight[layer], inner_weight[layer]], axis=1)
-        mid = grid.gather(mid, turned)
-        outer_w = grid.gather(outer_weight[layer], order)
-        layers.append(
-            (qkv_w, mid[:, :width], mid[:, width:], outer_w, *split_small(small[:, layer], sizes))
+    rows = qkv_weight.shape[1]
+    small_own = jnp.concatenate(vectors, axis=1).reshape(rows, -1)
+    small_cols = small_own.shape[1]
+    padded = -(-small_cols // 128) * 128
+    small_own = jnp.pad(small_own, ((0, 0), (0, padded - small_cols)))
+    schedule = Schedule(PLAN)
+    tick = schedule.tick
+
+    def gather_qkv(*parts):
+        out = jnp.concatenate(parts, axis=1)
+        out = yield from grid.gather(out, z_up)
+        return (yield from grid.gather_split(out))
+
+    def gather_ffn(inner, outer):
+        deep = outer.shape[0] // inner.shape[0]
+        out = jnp.concatenate([inner, outer.reshape(inner.shape[0], -1)], axis=1)
+        out = yield from grid.gather(out, z_up)
+        inner, outer = out[:, : inner.shape[1]], out[:, inner.shape[1] :]
+        return (yield from grid.gather_two(inner, outer.reshape(inner.shape[0] * deep, -1)))
+
+    for layer, tag in ((0, "one"), (1, "two")):
+        parts = [qkv_weight[layer], attn_weight[layer]] + ([small_own] if layer == 0 else [])
+        schedule.add("qkv_" + tag, gather_qkv, *parts)
+        schedule.add("ffn_" + tag, gather_ffn, inner_weight[layer], outer_weight[layer])
+    schedule.add("hidden", grid.to_rows, hidden)
+    schedule.add("skip", grid.to_rows, skip_tokens)
+    schedule.add("cots", grid.to_rows, jnp.concatenate([head_cotangent, backbone_cotangent], axis=2))
+
+    small = []
+
+    def weights_of(layer, tag):
+        def get(which):
+            if which == "ffn":
+                return schedule.get("ffn_" + tag)
+            if not small:
+                every = schedule.get("qkv_one")[:, -padded:][:, :small_cols]
+                small.append(every.reshape(devices, 2, -1))
+            pack = schedule.get("qkv_" + tag)
+            cut = qkv_weight.shape[2]
+            return (pack[:, :cut], pack[:, cut : cut + width], *split_small(small[0][:, layer], sizes))
+
+        return get
+
+    def scatter_qkv(*parts):
+        out = jnp.concatenate(parts, axis=1)
+        out = yield from grid.scatter_split(out)
+        return (yield from grid.scatter(out, z_down))
+
+    core_first = lambda turned: [grid.f_bits] + grid.upper(turned)
+
+    def scatter_z(inner, outer):
+        deep = outer.shape[0] // inner.shape[0]
+        out = jnp.concatenate([inner, outer.reshape(inner.shape[0], -1)], axis=1)
+        out = yield from grid.scatter(out, z_down)
+        return out[:, : inner.shape[1]], out[:, inner.shape[1] :].reshape(out.shape[0] * deep, -1)
+
+    kept_small = {}
+
+    def give_to(tag):
+        def give(which, *grads):
+            if which == "qkv":
+                *grads, vectors = grads
+                kept_small[tag] = vectors
+                if tag == "one":
+                    cut = [
+                        jnp.concatenate([v.reshape(devices, -1) for v in kept_small[t]], axis=1)
+                        for t in ("one", "two")
+                    ]
+                    flat = jnp.stack(cut, axis=1).reshape(devices * rows, small_cols).astype(BF)
+                    grads.append(jnp.pad(flat, ((0, 0), (0, padded - small_cols))))
+                schedule.add("back_qkv_" + tag, scatter_qkv, *grads)
+            else:
+                turned = which == "inner"
+                schedule.add(
+                    "back_" + which + "_" + tag,
+                    lambda g: grid.scatter(g, core_first(turned)),
+                    grads[0],
+                )
+
+        return give
+
+    def z_of(tag):
+        schedule.add(
+            "back_z_" + tag,
+            scatter_z,
+            schedule.get("back_inner_" + tag),
+            schedule.get("back_outer_" + tag),
         )
-    backbone, head = layers
-    rest = grid.to_rows(jnp.concatenate([skip_tokens, head_cotangent, backbone_cotangent], axis=2))
-    skip, head_cot, backbone_cot = rest[:, :width], rest[:, width : 2 * width], rest[:, 2 * width :]
-
-    first, saved_one = layer_forward(grid, x, backbone, seg_q, seg_k)
-    cls_own = jnp.dot(cls_hot, first, precision=FULL_PRECISION)[None]
-    head_in = jnp.where(is_cls, first, skip.astype(F32))
-    second, saved_two = layer_forward(grid, head_in, head, seg_q, seg_k)
+
+    mark = jnp.zeros((8, 128), F32) + my_starts[0].astype(F32)
+    for n in range(GATHER_TICKS):
+        mark = tick("g%d" % n, mark)
+    x = schedule.get("hidden")
+    first, saved_one = layer_forward(grid, "f0.", tick, x, weights_of(0, "one"), seg_q, seg_k)
 
     shared = n_bits(grid.chips_per_row)
-    for bit in [grid.f_bits] + list(range(shared)):
-        cls_own = cls_own + grid.swap(cls_own, bit)
-    cls_order = list(range(shared, grid.f_bits)) + list(range(grid.f_bits + 1, grid.f_bits + grid.d_bits))
-    cls_all = grid.gather(cls_own, cls_order).reshape(-1, width)
-    contrast_loss, d_cls_all = contrastive(cls_all, positives)
+    cls_bits = list(range(shared, grid.f_bits)) + grid.upper(True)
+
+    def gather_cls(own):
+        for bit in [grid.f_bits] + list(range(shared)):
+            got = yield grid.swap(own, bit)
+            own = own + got
+        return (yield from grid.gather(own, cls_bits))
+
+    schedule.add("cls", gather_cls, jnp.dot(cls_hot, first, precision=FULL_PRECISION)[None])
+    for n in range(HEAD_TICKS):
+        first = tick("h%d" % n, first)
+    head_in = jnp.where(is_cls, first, schedule.get("skip").astype(F32))
+    second, saved_two = layer_forward(grid, "f1.", tick, head_in, weights_of(1, "two"), seg_q, seg_k)
+
+    cots = schedule.get("cots")
+    schedule.add(
+        "outs", grid.from_rows, jnp.concatenate([first.astype(BF), second.astype(BF)], axis=1)
+    )
+    head_up = tick("t", cots[:, :width]).astype(F32)
+    d_head_in = layer_backward(
+        grid, "b1.", tick, give_to("two"), head_up, weights_of(1, "two"), saved_two, seg_q, seg_k
+    )
+    [cls_all] = schedule.finish("cls")
+    contrast_loss, d_cls_all = contrastive(cls_all.reshape(-1, width), positives)
     my_row = grid.dp // CORES * (CORES * rows_dev) + grid.row_in_group
     d_cls = lax.dynamic_slice_in_dim(d_cls_all, my_row * SEGS, SEGS, 0)
-
-    d_head_in, grads_two, small_two = layer_backward(
-        grid, head_cot.astype(F32), head, saved_two, seg_q, seg_k
-    )
     upstream = (
-        backbone_cot.astype(F32)
+        cots[:, width:].astype(F32)
         + jnp.where(is_cls, d_head_in, 0.0)
         + lax.dot_general(cls_hot, d_cls, (((0,), (0,)), ((), ())), precision=FULL_PRECISION)
     )
-    outs = jnp.concatenate(
-        [first.astype(BF), second.astype(BF), jnp.where(is_cls, 0.0, d_head_in).astype(BF)], axis=1
-    )
-    outs = grid.from_rows(outs)
-    d_input, grads_one, small_one = layer_backward(grid, upstream, backbone, saved_one, seg_q, seg_k)
-    grad_hidden = grid.from_rows(d_input.astype(BF)).astype(F32)
-
-    devices = grid.n_dp * grid.n_f
-    scattered = []
-    for grad_qkv, grad_attn, grad_inner, grad_outer in (grads_one, grads_two):
-        outer_g = grid.scatter(grad_outer, order)
-        mid = grid.scatter(jnp.concatenate([grad_attn, grad_inner], axis=1), turned)
-        qkv_g = grid.scatter(grad_qkv, order)
-        scattered.append((qkv_g, mid[:, :width], mid[:, width:], outer_g))
-    small_g = jnp.stack(
-        [
-            jnp.concatenate([v.reshape(devices, -1) for v in small], axis=1)
-            for small in (small_one, small_two)
-        ],
-        axis=1,
-    )
-    small_g = grid.scatter(small_g, order, F32)[0]
+    schedule.add("skip_back", grid.from_rows, jnp.where(is_cls, 0.0, d_head_in).astype(BF))
+    z_of("two")
+    upstream = tick("u", upstream)
+    d_input = layer_backward(
+        grid, "b0.", tick, give_to("one"), upstream, weights_of(0, "one"), saved_one, seg_q, seg_k
+    )
+    schedule.add("hidden_back", grid.from_rows, d_input.astype(BF))
+    schedule.finish("back_inner_one", "back_outer_one")
+    z_of("one")
+    mark = jnp.zeros((8, 128), F32)
+    for n in range(TAIL_TICKS):
+        mark = tick("e%d" % n, mark)
+    names = ["hidden_back", "skip_back", "outs", "back_z_one", "back_z_two", "back_qkv_one", "back_qkv_two"]
+    hidden_back, skip_back, outs, (inner_1, outer_1), (inner_2, outer_2), qkv_1, qkv_2 = schedule.finish(*names)
+
+    cut = qkv_weight.shape[2]
+    pair = lambda a, b: jnp.stack([a, b]).astype(F32)
+    small_g = qkv_1[:, -padded:][:, :small_cols].reshape(2, -1).astype(F32)
     cuts, at = [], 0
     for size in sizes:
         cuts.append(small_g[:, at : at + size])
         at += size
-    qkv_g, attn_g, inner_g, outer_g = (jnp.stack(pair) for pair in zip(*scattered))
     return (
         contrast_loss,
         outs[:, :, :width],
-        outs[:, :, width : 2 * width],
-        grad_hidden,
-        outs[:, :, 2 * width :].astype(F32),
-        qkv_g,
+        outs[:, :, width:],
+        hidden_back.astype(F32),
+        skip_back.astype(F32),
+        pair(qkv_1[:, :cut], qkv_2[:, :cut]),
         cuts[0],
-        attn_g,
+        pair(qkv_1[:, cut : cut + width], qkv_2[:, cut : cut + width]),
         cuts[1],
         cuts[2],
         cuts[3],
-        inner_g,
+        pair(inner_1, inner_2),
         cuts[4],
-        outer_g,
+        pair(outer_1, outer_2),
         cuts[5],
         cuts[6],
         cuts[7],

time: 829 us -> 659 us (0.79)
  waiting for transfers between devices: 365 us -> 155 us
  local copies, waits for them, and re-layouts: 69.9 us -> 92.9 us
  other arithmetic: 104 us -> 118 us
  starting transfers between devices: 107 us -> 96.7 us
    ppermute x30 -> x18, waiting for transfers between devices: 219 us -> 90.8 us  [swap(): return lax.ppermute(x, 'fsdp', [(i, i ^ 1 << bit) for i in range(self.n_f)])]
    ppermute x46 -> x48, waiting for transfers between devices: 141 us -> 56.3 us  [swap(): return lax.ppermute(x, 'dp', [(i, i ^ flip) for i in range(self.n_dp)])]
    squeeze x6 -> x32, local copies, waits for them, and re-layouts: 4.34 us -> 27.7 us  [the longest x28 22.8 us: halves(): pick = lambda at: lax.dynamic_index_in_dim(x, at, place, keepdims=False)]
    ppermute x30 -> x18, starting transfers between devices: 41.1 us -> 18.9 us  [swap(): return lax.ppermute(x, 'fsdp', [(i, i ^ 1 << bit) for i in range(self.n_f)])]
    convert_element_type x26 -> x39, other arithmetic: 23.3 us -> 42.4 us  [the longest x20 24.6 us: scatter(): out = (kept.astype(F32) + got.astype(F32)).astype(BF)]
    select_n x35 -> x2, other arithmetic: 18.1 us -> 0.83 us  [join(): high = jnp.where(mine, other, own)]
    unnamed x216 -> x328, local copies, waits for them, and re-layouts: 19.6 us -> 36.1 us
    ppermute x4 -> x6, starting transfers between devices: 13.4 us -> 24.5 us  [from_rows(): got.append(lax.ppermute(block, ('dp', 'fsdp'), back))]
  transfers between devices with their start and end apart: 88 -> 82, of which waited for: 38 -> 28; matrix products, arithmetic and copies ran while one was open for 24% -> 36% of each run, Pallas kernels for 5% -> 14%
where the time goes in v2:
time: 659 us; the launch traced here: 648 us
  waiting for transfers between devices  155 us (24%)
  other arithmetic  118 us (18%)
  starting transfers between devices  96.7 us (15%)
  local copies, waits for them, and re-layouts  92.9 us (14%)
  matrix products  89.5 us (14%)
  Pallas kernels  89.5 us (14%)
    ppermute x18, waiting for transfers between devices, swap(): return lax.ppermute(x, 'fsdp', [(i, i ^ 1 << bit) for i in range(self.n_f)])  90.8 us
    ppermute x48, waiting for transfers between devices, swap(): return lax.ppermute(x, 'dp', [(i, i ^ flip) for i in range(self.n_dp)])  56.3 us
    pallas_call x2, Pallas kernels, attend_back(): pl.pallas_call(functools.partial(attend_back_kernel, chunks, min(256, tok...  52.1 us
    ppermute x48, starting transfers between devices, swap(): return lax.ppermute(x, 'dp', [(i, i ^ flip) for i in range(self.n_dp)])  42.2 us
    another operation x63, other arithmetic, join(): return jnp.stack([low, high], axis=sum((1 for b in have if b > bit)))  39.5 us
    pallas_call x2, Pallas kernels, attend(): pl.pallas_call(functools.partial(attend_kernel, chunks, min(256, tokens))...  37.4 us
    unnamed x328, local copies, waits for them, and re-layouts  36.1 us
    dot_general x8, matrix products, right_t(): lax.dot_general(first_op, second_op, (((1,), (1,)), ((), ())), preferred_...  33.3 us
  transfers between devices with their start and end apart: 82, of which 28 were waited for; matrix products, arithmetic and copies ran while one was open for 36% of the time, Pallas kernels for 14%

profile of v2, /device:TPU:0, one launch (start us, length us, event | category | flops | bytes accessed | tf_op | source)
XLA Modules:
  0.0 647.8 jit_solution(6927641294568655701)
XLA Ops:
  4.2 3.1 collective-permute-start
  11.3 2.8 collective-permute-start.2
  16.1 13.5 %collective-permute-done.1 = bf16[24,6144]{1,0:T(8,128)(2,1)S(1)} collective-permute-done((bf16[24,6144]{1,0:T(8,128)(2,1)S(1)}, bf16[24,6144]{1,0:T(8,128)(2,1)S(1)}, u32[]{:S(2)}, u32[]{:S(2)}) %collective-permute-start.1) | collective-permute-done | bytes 294944 | tf_op jit(solution)/shard_map/ppermute | solution.py:128
  33.7 4.1 collective-permute-done.3
  45.2 4.5 collective-permute-start.5
  50.2 19.4 %collective-permute-done.7 = bf16[2,24,6144]{2,1,0:T(8,128)(2,1)} collective-permute-done((bf16[2,24,6144]{2,1,0:T(8,128)(2,1)}, bf16[2,24,6144]{2,1,0:T(8,128)(2,1)}, u32[]{:S(2)}, u32[]{:S(2)}) %collective-permute-start.7) | collective-permute-done | bytes 589856 | tf_op jit(solution)/shard_map/ppermute | solution.py:128
  78.7 2.5 select_bitcast_fusion.1
  81.8 2.2 copy-done.61
  87.2 4.3 fusion.18.refs_0_.refs_1_.refs_3_
  100.6 18.4 %attend.2 = (bf16[512,768]{1,0:T(8,128)(2,1)S(1)}, f32[6,2,512]{2,1,0:T(2,128)S(1)}) custom-call(bf16[512,2304]{1,0:T(8,128)(2,1)S(1)} %fusion.18.refs_0_.refs_1_.refs_3_, bf16[512,2304]{1,0:T(8,128)(2,1)S(1)} %fusion.18.refs_0_.refs_1_.refs_3_, bf16[512,1536]{1,0:T(8,128)(2,1)S(1)} %collective-permute-done.14.refs_2_.refs_4_, ...), custom_call_target="tpu_custom_call" | custom-call | flops 6442450944 | bytes 6291456 | tf_op jit(solution)/shard_map/attend/pallas_call | solution.py:446
  119.1 3.6 collective-permute-done.17
  122.6 3.1 collective-permute-done.16
  138.6 2.4 fusion.162
  142.1 4.0 collective-permute-done.21
  151.3 2.3 select_bitcast_fusion.9
  156.0 5.5 multiply_convert_fusion.1
  163.1 2.7 fusion.163
  166.9 4.5 collective-permute-start.29
  173.4 6.7 %collective-permute-done.24 = bf16[2,24,6144]{2,1,0:T(8,128)(2,1)S(1)} collective-permute-done((bf16[2,24,6144]{2,1,0:T(8,128)(2,1)S(1)}, bf16[2,24,6144]{2,1,0:T(8,128)(2,1)S(1)}, u32[]{:S(2)}, u32[]{:S(2)}) %collective-permute-start.24) | collective-permute-done | bytes 589856 | tf_op jit(solution)/shard_map/ppermute | solution.py:128
  184.7 2.6 reshape.533
  188.7 6.5 %collective-permute-start.32 = (bf16[96,3072]{1,0:T(8,128)(2,1)}, bf16[96,3072]{1,0:T(8,128)(2,1)S(1)}, u32[]{:S(2)}, u32[]{:S(2)}) collective-permute-start(bf16[96,3072]{1,0:T(8,128)(2,1)} %get-tuple-element.356), channel_id=1, source_target_pairs={{0,16},{4,20},{8,24},{12,28},{16,0},{20,4},{24,8},{28,12},{1,17},{... | collective-permute-start | bytes 1769480 | tf_op jit(solution)/shard_map/ppermute | solution.py:130
  195.3 2.5 select_bitcast_fusion.7
  203.7 4.8 collective-permute-done.32
  218.4 18.9 %attend.3 = (bf16[512,768]{1,0:T(8,128)(2,1)S(1)}, f32[6,2,512]{2,1,0:T(2,128)S(1)}) custom-call(bf16[512,2304]{1,0:T(8,128)(2,1)S(1)} %fusion.19.refs_0_.refs_1_.refs_3_, bf16[512,2304]{1,0:T(8,128)(2,1)S(1)} %fusion.19.refs_0_.refs_1_.refs_3_, bf16[512,1536]{1,0:T(8,128)(2,1)} %collective-permute-done.34.refs_2_.refs_4_, ...), custom_call_target="tpu_custom_call" | custom-call | flops 6442450944 | bytes 6291456 | tf_op jit(solution)/shard_map/attend/pallas_call | solution.py:446
  238.0 6.4 collective-permute-done.36
  255.8 2.2 fusion.164
  267.7 5.6 multiply_convert_fusion
  273.3 2.7 fusion.165
  276.7 7.3 %collective-permute-done.43 = bf16[256,1536]{1,0:T(8,128)(2,1)S(1)} collective-permute-done((bf16[256,1536]{1,0:T(8,128)(2,1)S(1)}, bf16[256,1536]{1,0:T(8,128)(2,1)S(1)}, u32[]{:S(2)}, u32[]{:S(2)}) %collective-permute-start.43) | collective-permute-done | bytes 786464 | tf_op jit(solution)/shard_map/ppermute | solution.py:232
  286.6 2.9 convolution_convert_fusion.5
  292.5 4.6 fusion.166
  297.1 4.4 convolution_convert_fusion.4
  302.7 7.8 %collective-permute-start.51 = (bf16[256,1536]{1,0:T(8,128)(2,1)}, bf16[256,1536]{1,0:T(8,128)(2,1)}, u32[]{:S(2)}, u32[]{:S(2)}) collective-permute-start(bf16[256,1536]{1,0:T(8,128)(2,1)} %get-tuple-element.344), channel_id=1, source_target_pairs={{0,0},{1,1},{4,2},{5,3},{2,4},{3,5},{6,6},{7,7},{8,8},{9,9},{12,10... | collective-permute-start | bytes 2359304 | tf_op jit(solution)/shard_map/ppermute | solution.py:250
  310.5 8.7 %collective-permute-start.52 = (bf16[256,1536]{1,0:T(8,128)(2,1)}, bf16[256,1536]{1,0:T(8,128)(2,1)}, u32[]{:S(2)}, u32[]{:S(2)}) collective-permute-start(bf16[256,1536]{1,0:T(8,128)(2,1)} %get-tuple-element.343), channel_id=1, source_target_pairs={{1,0},{0,1},{5,2},{4,3},{3,4},{2,5},{7,6},{6,7},{9,8},{8,9},{13,10... | collective-permute-start | bytes 2359304 | tf_op jit(solution)/shard_map/ppermute | solution.py:250
  327.4 2.4 fusion.16
  333.3 5.8 multiply_reduce_fusion
  339.7 2.7 convolution_convert_fusion.9.refs_5_
  346.3 26.7 %attend_back.2 = (bf16[512,768]{1,0:T(8,128)(2,1)S(1)}, f32[2,512,768]{2,1,0:T(8,128)S(1)}, bf16[2,512,768]{2,1,0:T(8,128)(2,1)}) custom-call(bf16[512,2304]{1,0:T(8,128)(2,1)S(1)} %copy-done.7, bf16[512,2304]{1,0:T(8,128)(2,1)S(1)} %copy-done.7, bf16[512,1536]{1,0:T(8,128)(2,1)} %collective-permute-done.34.refs_2_.refs_4_, bf16[512,2304]{1,0:T(8,128)(2,1)S(1)} %copy-done.7, ...), custom_call_target="tpu_custom_call" | custom-call | flops 16106127360 | bytes 15728640 | tf_op jit(solution)/shard_map/attend_back/pallas_call | solution.py:475
  375.3 2.1 fusion.28
  391.6 2.9 collective-permute-done.50
  394.6 3.7 collective-permute-done.49
  401.9 2.1 fusion.60
  407.4 5.0 select_convert_fusion
  417.0 3.3 fusion.15
  425.0 3.1 convolution_convert_fusion.2
  435.7 4.6 fusion.167
  440.4 4.4 convolution_convert_fusion.1
  445.7 4.5 collective-permute-start.64
  458.5 6.4 multiply_reduce_fusion.2
  465.8 3.2 fusion.13
  475.4 2.1 convolution_convert_fusion.8.refs_5_
  478.6 2.7 fusion.14
  484.3 25.4 %attend_back.3 = (bf16[512,768]{1,0:T(8,128)(2,1)S(1)}, f32[2,512,768]{2,1,0:T(8,128)S(1)}, bf16[2,512,768]{2,1,0:T(8,128)(2,1)S(1)}) custom-call(bf16[512,2304]{1,0:T(8,128)(2,1)S(1)} %copy-done.5, bf16[512,2304]{1,0:T(8,128)(2,1)S(1)} %copy-done.5, bf16[512,1536]{1,0:T(8,128)(2,1)S(1)} %copy-done.17, bf16[512,2304]{1,0:T(8,128)(2,1)S(1)} %copy-done.5, ...), custom_call_target="tpu_custom_call" | custom-call | flops 16106127360 | bytes 15728640 | tf_op jit(solution)/shard_map/attend_back/pallas_call | solution.py:475
  514.9 5.5 collective-permute-done.62
  525.2 2.2 collective-permute-start.69
  542.2 3.9 convolution_convert_fusion
  547.2 2.1 fusion.46
  559.2 18.7 %collective-permute-done.80 = bf16[2,24,6144]{2,1,0:T(8,128)(2,1)S(1)} collective-permute-done((bf16[2,24,6144]{2,1,0:T(8,128)(2,1)S(1)}, bf16[2,24,6144]{2,1,0:T(8,128)(2,1)S(1)}, u32[]{:S(2)}, u32[]{:S(2)}) %collective-permute-start.80) | collective-permute-done | bytes 589856 | tf_op jit(solution)/shard_map/ppermute | solution.py:128
  580.2 6.0 collective-permute-done.81
  588.1 3.0 fusion.12
  594.0 11.4 %collective-permute-done.74 = bf16[2,48,3200]{2,1,0:T(8,128)(2,1)S(1)} collective-permute-done((bf16[2,48,3200]{2,1,0:T(8,128)(2,1)S(1)}, bf16[2,48,3200]{2,1,0:T(8,128)(2,1)S(1)}, u32[]{:S(2)}, u32[]{:S(2)}) %collective-permute-start.74) | collective-permute-done | bytes 614432 | tf_op jit(solution)/shard_map/ppermute | solution.py:130
  608.7 3.8 collective-permute-done.75
  617.6 17.6 %collective-permute-done.78 = bf16[2,24,3200]{2,1,0:T(8,128)(2,1)S(1)} collective-permute-done((bf16[2,24,3200]{2,1,0:T(8,128)(2,1)S(1)}, bf16[2,24,3200]{2,1,0:T(8,128)(2,1)S(1)}, u32[]{:S(2)}, u32[]{:S(2)}) %collective-permute-start.78) | collective-permute-done | bytes 307232 | tf_op jit(solution)/shard_map/ppermute | solution.py:128
  638.0 4.7 collective-permute-done.79
  (770 shorter events, 251.9 us)
Async XLA Ops:
  11.3 18.2 %collective-permute-start.2 = (bf16[2,24,3200]{2,1,0:T(8,128)(2,1)S(1)}, bf16[2,24,3200]{2,1,0:T(8,128)(2,1)S(1)}, u32[]{:S(2)}, u32[]{:S(2)}) collective-permute-start(bf16[2,24,3200]{2,1,0:T(8,128)(2,1)S(1)} %pad_maximum_fusion.35), channel_id=1, source_target_pairs={{0,2},{1,3},{2,0},{3,1},{4,6},{5,7},{6,4},{7,5},{8,10},{9,11},{10,... | collective-permute-start | bytes 921608 | tf_op jit(solution)/shard_map/ppermute | solution.py:128
  14.3 15.3 %collective-permute-start.1 = (bf16[24,6144]{1,0:T(8,128)(2,1)S(1)}, bf16[24,6144]{1,0:T(8,128)(2,1)S(1)}, u32[]{:S(2)}, u32[]{:S(2)}) collective-permute-start(bf16[24,6144]{1,0:T(8,128)(2,1)S(1)} %constant_dynamic-update-slice_fusion.3), channel_id=1, source_target_pairs={{0,1},{1,0},{2,3},{3,2},{4,5},{5,4},{6,7},{7,6},{8,9},{9,8},{10,11... | collective-permute-start | bytes 884744 | tf_op jit(solution)/shard_map/ppermute | solution.py:128
  33.7 35.9 %collective-permute-start.7 = (bf16[2,24,6144]{2,1,0:T(8,128)(2,1)}, bf16[2,24,6144]{2,1,0:T(8,128)(2,1)}, u32[]{:S(2)}, u32[]{:S(2)}) collective-permute-start(bf16[2,24,6144]{2,1,0:T(8,128)(2,1)} %pad_maximum_fusion.29), channel_id=1, source_target_pairs={{0,2},{1,3},{2,0},{3,1},{4,6},{5,7},{6,4},{7,5},{8,10},{9,11},{10,... | collective-permute-start | bytes 1769480 | tf_op jit(solution)/shard_map/ppermute | solution.py:128
  40.0 29.6 %collective-permute-start.9 = (bf16[2,48,3200]{2,1,0:T(8,128)(2,1)}, bf16[2,48,3200]{2,1,0:T(8,128)(2,1)}, u32[]{:S(2)}, u32[]{:S(2)}) collective-permute-start(bf16[2,48,3200]{2,1,0:T(8,128)(2,1)} %pad_maximum_fusion.27), channel_id=1, source_target_pairs={{0,16},{4,20},{8,24},{12,28},{16,0},{20,4},{24,8},{28,12},{1,17},{... | collective-permute-start | bytes 1843208 | tf_op jit(solution)/shard_map/ppermute | solution.py:130
  41.5 28.1 %collective-permute-start.8 = (bf16[2,48,3200]{2,1,0:T(8,128)(2,1)}, bf16[2,48,3200]{2,1,0:T(8,128)(2,1)S(1)}, u32[]{:S(2)}, u32[]{:S(2)}) collective-permute-start(bf16[2,48,3200]{2,1,0:T(8,128)(2,1)} %pad_maximum_fusion.26), channel_id=1, source_target_pairs={{0,8},{4,12},{8,0},{12,4},{16,24},{20,28},{24,16},{28,20},{1,9},{5... | collective-permute-start | bytes 1843208 | tf_op jit(solution)/shard_map/ppermute | solution.py:130
  45.2 33.5 %collective-permute-start.5 = (bf16[256,768]{1,0:T(8,128)(2,1)}, bf16[256,768]{1,0:T(8,128)(2,1)}, u32[]{:S(2)}, u32[]{:S(2)}) collective-permute-start(bf16[256,768]{1,0:T(8,128)(2,1)} %get-tuple-element.385), channel_id=1, source_target_pairs={{0,0},{1,1},{2,4},{3,5},{4,2},{5,3},{6,6},{7,7},{8,8},{9,9},{10,12... | collective-permute-start | bytes 1179656 | tf_op jit(solution)/shard_map/ppermute | solution.py:232
  49.7 29.0 %collective-permute-start.6 = (bf16[256,768]{1,0:T(8,128)(2,1)}, bf16[256,768]{1,0:T(8,128)(2,1)}, u32[]{:S(2)}, u32[]{:S(2)}) collective-permute-start(bf16[256,768]{1,0:T(8,128)(2,1)} %get-tuple-element.384), channel_id=1, source_target_pairs={{0,1},{1,0},{2,5},{3,4},{4,3},{5,2},{6,7},{7,6},{8,9},{9,8},{10,13... | collective-permute-start | bytes 1179656 | tf_op jit(solution)/shard_map/ppermute | solution.py:232
  77.6 15.9 %collective-permute-start.12 = (bf16[384,768]{1,0:T(8,128)(2,1)S(1)}, bf16[384,768]{1,0:T(8,128)(2,1)}, u32[]{:S(2)}, u32[]{:S(2)}) collective-permute-start(bf16[384,768]{1,0:T(8,128)(2,1)S(1)} %reshape.527), channel_id=1, source_target_pairs={{0,8},{4,12},{8,0},{12,4},{16,24},{20,28},{24,16},{28,20},{1,9},{5... | collective-permute-start | bytes 1769480 | tf_op jit(solution)/shard_map/ppermute | solution.py:130
  78.2 15.8 %collective-permute-start.11 = (bf16[96,3072]{1,0:T(8,128)(2,1)}, bf16[96,3072]{1,0:T(8,128)(2,1)}, u32[]{:S(2)}, u32[]{:S(2)}) collective-permute-start(bf16[96,3072]{1,0:T(8,128)(2,1)} %get-tuple-element.366), channel_id=1, source_target_pairs={{0,16},{4,20},{8,24},{12,28},{16,0},{20,4},{24,8},{28,12},{1,17},{... | collective-permute-start | bytes 1769480 | tf_op jit(solution)/shard_map/ppermute | solution.py:130
  95.3 27.3 %collective-permute-start.17 = (bf16[2,384,768]{2,1,0:T(8,128)(2,1)S(1)}, bf16[2,384,768]{2,1,0:T(8,128)(2,1)S(1)}, u32[]{:S(2)}, u32[]{:S(2)}) collective-permute-start(bf16[2,384,768]{2,1,0:T(8,128)(2,1)S(1)} %pad_maximum_fusion.18), channel_id=1, source_target_pairs={{0,16},{4,20},{8,24},{12,28},{16,0},{20,4},{24,8},{28,12},{1,17},{... | collective-permute-start | bytes 3538952 | tf_op jit(solution)/shard_map/ppermute | solution.py:130
  97.8 27.9 %collective-permute-start.16 = (bf16[2,96,3072]{2,1,0:T(8,128)(2,1)S(1)}, bf16[2,96,3072]{2,1,0:T(8,128)(2,1)S(1)}, u32[]{:S(2)}, u32[]{:S(2)}) collective-permute-start(bf16[2,96,3072]{2,1,0:T(8,128)(2,1)S(1)} %pad_maximum_fusion.17), channel_id=1, source_target_pairs={{0,8},{4,12},{8,0},{12,4},{16,24},{20,28},{24,16},{28,20},{1,9},{5... | collective-permute-start | bytes 3538952 | tf_op jit(solution)/shard_map/ppermute | solution.py:130
  99.4 19.6 %collective-permute-start.18 = (bf16[2,24,3072]{2,1,0:T(8,128)(2,1)S(1)}, bf16[2,24,3072]{2,1,0:T(8,128)(2,1)S(1)}, u32[]{:S(2)}, u32[]{:S(2)}) collective-permute-start(bf16[2,24,3072]{2,1,0:T(8,128)(2,1)S(1)} %pad_maximum_fusion.36), channel_id=1, source_target_pairs={{0,2},{1,3},{2,0},{3,1},{4,6},{5,7},{6,4},{7,5},{8,10},{9,11},{10,... | collective-permute-start | bytes 884744 | tf_op jit(solution)/shard_map/ppermute | solution.py:128
  127.6 18.6 %collective-permute-start.20 = (bf16[2,2,384,768]{3,2,1,0:T(8,128)(2,1)}, bf16[2,2,384,768]{3,2,1,0:T(8,128)(2,1)}, u32[]{:S(2)}, u32[]{:S(2)}) collective-permute-start(bf16[2,2,384,768]{3,2,1,0:T(8,128)(2,1)} %pad_maximum_fusion.9), channel_id=1, source_target_pairs={{0,4},{4,0},{8,12},{12,8},{16,20},{20,16},{24,28},{28,24},{1,5},{5... | collective-permute-start | bytes 7077896 | tf_op jit(solution)/shard_map/ppermute | solution.py:130
  129.9 16.2 %collective-permute-start.19 = (bf16[2,2,96,3072]{3,2,1,0:T(8,128)(2,1)}, bf16[2,2,96,3072]{3,2,1,0:T(8,128)(2,1)}, u32[]{:S(2)}, u32[]{:S(2)}) collective-permute-start(bf16[2,2,96,3072]{3,2,1,0:T(8,128)(2,1)} %pad_maximum_fusion.8), channel_id=1, source_target_pairs={{0,4},{4,0},{8,12},{12,8},{16,20},{20,16},{24,28},{28,24},{1,5},{5... | collective-permute-start | bytes 7077896 | tf_op jit(solution)/shard_map/ppermute | solution.py:130
  147.3 26.1 %collective-permute-start.26 = (bf16[2,48,3072]{2,1,0:T(8,128)(2,1)S(1)}, bf16[2,48,3072]{2,1,0:T(8,128)(2,1)S(1)}, u32[]{:S(2)}, u32[]{:S(2)}) collective-permute-start(bf16[2,48,3072]{2,1,0:T(8,128)(2,1)S(1)} %pad_maximum_fusion.32), channel_id=1, source_target_pairs={{0,16},{4,20},{8,24},{12,28},{16,0},{20,4},{24,8},{28,12},{1,17},{... | collective-permute-start | bytes 1769480 | tf_op jit(solution)/shard_map/ppermute | solution.py:130
  149.0 24.4 %collective-permute-start.25 = (bf16[2,48,3072]{2,1,0:T(8,128)(2,1)S(1)}, bf16[2,48,3072]{2,1,0:T(8,128)(2,1)S(1)}, u32[]{:S(2)}, u32[]{:S(2)}) collective-permute-start(bf16[2,48,3072]{2,1,0:T(8,128)(2,1)S(1)} %pad_maximum_fusion.31), channel_id=1, source_target_pairs={{0,8},{4,12},{8,0},{12,4},{16,24},{20,28},{24,16},{28,20},{1,9},{5... | collective-permute-start | bytes 1769480 | tf_op jit(solution)/shard_map/ppermute | solution.py:130
  149.7 30.4 %collective-permute-start.24 = (bf16[2,24,6144]{2,1,0:T(8,128)(2,1)S(1)}, bf16[2,24,6144]{2,1,0:T(8,128)(2,1)S(1)}, u32[]{:S(2)}, u32[]{:S(2)}) collective-permute-start(bf16[2,24,6144]{2,1,0:T(8,128)(2,1)S(1)} %pad_maximum_fusion.30), channel_id=1, source_target_pairs={{0,2},{1,3},{2,0},{3,1},{4,6},{5,7},{6,4},{7,5},{8,10},{9,11},{10,... | collective-permute-start | bytes 1769480 | tf_op jit(solution)/shard_map/ppermute | solution.py:128
  166.9 21.7 %collective-permute-start.29 = (bf16[256,768]{1,0:T(8,128)(2,1)}, bf16[256,768]{1,0:T(8,128)(2,1)}, u32[]{:S(2)}, u32[]{:S(2)}) collective-permute-start(bf16[256,768]{1,0:T(8,128)(2,1)} %get-tuple-element.381), channel_id=1, source_target_pairs={{0,0},{1,1},{2,4},{3,5},{4,2},{5,3},{6,6},{7,7},{8,8},{9,9},{10,12... | collective-permute-start | bytes 1179656 | tf_op jit(solution)/shard_map/ppermute | solution.py:232
  171.4 23.8 %collective-permute-start.30 = (bf16[256,768]{1,0:T(8,128)(2,1)}, bf16[256,768]{1,0:T(8,128)(2,1)}, u32[]{:S(2)}, u32[]{:S(2)}) collective-permute-start(bf16[256,768]{1,0:T(8,128)(2,1)} %get-tuple-element.380), channel_id=1, source_target_pairs={{0,1},{1,0},{2,5},{3,4},{4,3},{5,2},{6,7},{7,6},{8,9},{9,8},{10,13... | collective-permute-start | bytes 1179656 | tf_op jit(solution)/shard_map/ppermute | solution.py:232
  181.8 13.3 %collective-permute-start.28 = (bf16[2,2,96,3072]{3,2,1,0:T(8,128)(2,1)}, bf16[2,2,96,3072]{3,2,1,0:T(8,128)(2,1)}, u32[]{:S(2)}, u32[]{:S(2)}) collective-permute-start(bf16[2,2,96,3072]{3,2,1,0:T(8,128)(2,1)} %maximum_maximum_fusion.1), channel_id=1, source_target_pairs={{0,4},{4,0},{8,12},{12,8},{16,20},{20,16},{24,28},{28,24},{1,5},{5... | collective-permute-start | bytes 7077896 | tf_op jit(solution)/shard_map/ppermute | solution.py:130
  181.8 13.3 %collective-permute-start.27 = (f32[1,8,768]{2,1,0:T(8,128)S(1)}, f32[1,8,768]{2,1,0:T(8,128)S(1)}, u32[]{:S(2)}, u32[]{:S(2)}) collective-permute-start(f32[1,8,768]{2,1,0:T(8,128)S(1)} %convolution_bitcast_fusion), channel_id=1, source_target_pairs={{0,4},{4,0},{8,12},{12,8},{16,20},{20,16},{24,28},{28,24},{1,5},{5... | collective-permute-start | bytes 73736 | tf_op jit(solution)/shard_map/ppermute | solution.py:130
  187.2 16.5 %collective-permute-start.33 = (bf16[384,768]{1,0:T(8,128)(2,1)}, bf16[384,768]{1,0:T(8,128)(2,1)S(1)}, u32[]{:S(2)}, u32[]{:S(2)}) collective-permute-start(bf16[384,768]{1,0:T(8,128)(2,1)} %reshape.533), channel_id=1, source_target_pairs={{0,8},{4,12},{8,0},{12,4},{16,24},{20,28},{24,16},{28,20},{1,9},{5... | collective-permute-start | bytes 1769480 | tf_op jit(solution)/shard_map/ppermute | solution.py:130
  188.7 19.9 %collective-permute-start.32 = (bf16[96,3072]{1,0:T(8,128)(2,1)}, bf16[96,3072]{1,0:T(8,128)(2,1)S(1)}, u32[]{:S(2)}, u32[]{:S(2)}) collective-permute-start(bf16[96,3072]{1,0:T(8,128)(2,1)} %get-tuple-element.356), channel_id=1, source_target_pairs={{0,16},{4,20},{8,24},{12,28},{16,0},{20,4},{24,8},{28,12},{1,17},{... | collective-permute-start | bytes 1769480 | tf_op jit(solution)/shard_map/ppermute | solution.py:130
  195.2 13.4 %collective-permute-start.31 = (f32[1,8,768]{2,1,0:T(8,128)S(1)}, f32[1,8,768]{2,1,0:T(8,128)S(1)}, u32[]{:S(2)}, u32[]{:S(2)}) collective-permute-start(f32[1,8,768]{2,1,0:T(8,128)S(1)} %add.582), channel_id=1, source_target_pairs={{0,1},{1,0},{2,3},{3,2},{4,5},{5,4},{6,7},{7,6},{8,9},{9,8},{10,11... | collective-permute-start | bytes 73736 | tf_op jit(solution)/shard_map/ppermute | solution.py:128
  210.6 27.3 %collective-permute-start.37 = (bf16[2,384,768]{2,1,0:T(8,128)(2,1)}, bf16[2,384,768]{2,1,0:T(8,128)(2,1)}, u32[]{:S(2)}, u32[]{:S(2)}) collective-permute-start(bf16[2,384,768]{2,1,0:T(8,128)(2,1)} %pad_maximum_fusion.21), channel_id=1, source_target_pairs={{0,16},{4,20},{8,24},{12,28},{16,0},{20,4},{24,8},{28,12},{1,17},{... | collective-permute-start | bytes 3538952 | tf_op jit(solution)/shard_map/ppermute | solution.py:130
  215.7 28.7 %collective-permute-start.36 = (bf16[2,96,3072]{2,1,0:T(8,128)(2,1)}, bf16[2,96,3072]{2,1,0:T(8,128)(2,1)}, u32[]{:S(2)}, u32[]{:S(2)}) collective-permute-start(bf16[2,96,3072]{2,1,0:T(8,128)(2,1)} %pad_maximum_fusion.20), channel_id=1, source_target_pairs={{0,8},{4,12},{8,0},{12,4},{16,24},{20,28},{24,16},{28,20},{1,9},{5... | collective-permute-start | bytes 3538952 | tf_op jit(solution)/shard_map/ppermute | solution.py:130
  216.6 20.8 %collective-permute-start.35 = (f32[2,1,8,768]{3,2,0,1:T(8,128)S(1)}, f32[2,1,8,768]{3,2,0,1:T(8,128)S(1)}, u32[]{:S(2)}, u32[]{:S(2)}) collective-permute-start(f32[2,1,8,768]{3,2,0,1:T(8,128)S(1)} %fusion.122), channel_id=1, source_target_pairs={{0,2},{1,3},{2,0},{3,1},{4,6},{5,7},{6,4},{7,5},{8,10},{9,11},{10,... | collective-permute-start | bytes 147464 | tf_op jit(solution)/shard_map/ppermute | solution.py:128
  248.1 12.5 %collective-permute-start.40 = (bf16[2,2,384,768]{3,2,1,0:T(8,128)(2,1)}, bf16[2,2,384,768]{3,2,1,0:T(8,128)(2,1)}, u32[]{:S(2)}, u32[]{:S(2)}) collective-permute-start(bf16[2,2,384,768]{3,2,1,0:T(8,128)(2,1)} %pad_maximum_fusion.11), channel_id=1, source_target_pairs={{0,4},{4,0},{8,12},{12,8},{16,20},{20,16},{24,28},{28,24},{1,5},{5... | collective-permute-start | bytes 7077896 | tf_op jit(solution)/shard_map/ppermute | solution.py:130
  254.2 22.5 %collective-permute-start.42 = (bf16[256,1536]{1,0:T(8,128)(2,1)S(1)}, bf16[256,1536]{1,0:T(8,128)(2,1)S(1)}, u32[]{:S(2)}, u32[]{:S(2)}) collective-permute-start(bf16[256,1536]{1,0:T(8,128)(2,1)S(1)} %get-tuple-element.348), channel_id=1, source_target_pairs={{0,0},{1,1},{2,4},{3,5},{4,2},{5,3},{6,6},{7,7},{8,8},{9,9},{10,12... | collective-permute-start | bytes 2359304 | tf_op jit(solution)/shard_map/ppermute | solution.py:232
  255.1 28.9 %collective-permute-start.43 = (bf16[256,1536]{1,0:T(8,128)(2,1)S(1)}, bf16[256,1536]{1,0:T(8,128)(2,1)S(1)}, u32[]{:S(2)}, u32[]{:S(2)}) collective-permute-start(bf16[256,1536]{1,0:T(8,128)(2,1)S(1)} %get-tuple-element.347), channel_id=1, source_target_pairs={{0,1},{1,0},{2,5},{3,4},{4,3},{5,2},{6,7},{7,6},{8,9},{9,8},{10,13... | collective-permute-start | bytes 2359304 | tf_op jit(solution)/shard_map/ppermute | solution.py:232
  260.8 23.2 %collective-permute-start.41 = (f32[2,2,2,1,8,768]{5,4,2,1,0,3:T(8,128)S(1)}, f32[2,2,2,1,8,768]{5,4,2,1,0,3:T(8,128)S(1)}, u32[]{:S(2)}, u32[]{:S(2)}) collective-permute-start(f32[2,2,2,1,8,768]{5,4,2,1,0,3:T(8,128)S(1)} %fusion.103), channel_id=1, source_target_pairs={{0,16},{4,20},{8,24},{12,28},{16,0},{20,4},{24,8},{28,12},{1,17},{... | collective-permute-start | bytes 589832 | tf_op jit(solution)/shard_map/ppermute | solution.py:130
  292.4 31.9 %collective-permute-start.44 = (bf16[2,2,384,768]{3,2,1,0:T(8,128)(2,1)}, bf16[2,2,384,768]{3,2,1,0:T(8,128)(2,1)}, u32[]{:S(2)}, u32[]{:S(2)}) collective-permute-start(bf16[2,2,384,768]{3,2,1,0:T(8,128)(2,1)} %dynamic-slice_bitcast_fusion.5), channel_id=1, source_target_pairs={{0,4},{4,0},{8,12},{12,8},{16,20},{20,16},{24,28},{28,24},{1,5},{5... | collective-permute-start | bytes 7077896 | tf_op jit(solution)/shard_map/ppermute | solution.py:130
  302.7 88.9 %collective-permute-start.51 = (bf16[256,1536]{1,0:T(8,128)(2,1)}, bf16[256,1536]{1,0:T(8,128)(2,1)}, u32[]{:S(2)}, u32[]{:S(2)}) collective-permute-start(bf16[256,1536]{1,0:T(8,128)(2,1)} %get-tuple-element.344), channel_id=1, source_target_pairs={{0,0},{1,1},{4,2},{5,3},{2,4},{3,5},{6,6},{7,7},{8,8},{9,9},{12,10... | collective-permute-start | bytes 2359304 | tf_op jit(solution)/shard_map/ppermute | solution.py:250
  310.5 81.1 %collective-permute-start.52 = (bf16[256,1536]{1,0:T(8,128)(2,1)}, bf16[256,1536]{1,0:T(8,128)(2,1)}, u32[]{:S(2)}, u32[]{:S(2)}) collective-permute-start(bf16[256,1536]{1,0:T(8,128)(2,1)} %get-tuple-element.343), channel_id=1, source_target_pairs={{1,0},{0,1},{5,2},{4,3},{3,4},{2,5},{7,6},{6,7},{9,8},{8,9},{13,10... | collective-permute-start | bytes 2359304 | tf_op jit(solution)/shard_map/ppermute | solution.py:250
  326.3 16.1 %collective-permute-start.45 = (bf16[2,2,96,3072]{3,2,1,0:T(8,128)(2,1)S(1)}, bf16[2,2,96,3072]{3,2,1,0:T(8,128)(2,1)S(1)}, u32[]{:S(2)}, u32[]{:S(2)}) collective-permute-start(bf16[2,2,96,3072]{3,2,1,0:T(8,128)(2,1)S(1)} %dynamic-slice_bitcast_fusion.4), channel_id=1, source_target_pairs={{0,4},{4,0},{8,12},{12,8},{16,20},{20,16},{24,28},{28,24},{1,5},{5... | collective-permute-start | bytes 7077896 | tf_op jit(solution)/shard_map/ppermute | solution.py:130
  332.4 42.9 %collective-permute-start.47 = (bf16[2,384,768]{2,1,0:T(8,128)(2,1)}, bf16[2,384,768]{2,1,0:T(8,128)(2,1)}, u32[]{:S(2)}, u32[]{:S(2)}) collective-permute-start(bf16[2,384,768]{2,1,0:T(8,128)(2,1)} %dynamic-slice_bitcast_fusion.8), channel_id=1, source_target_pairs={{0,16},{4,20},{8,24},{12,28},{16,0},{20,4},{24,8},{28,12},{1,17},{... | collective-permute-start | bytes 3538952 | tf_op jit(solution)/shard_map/ppermute | solution.py:130
  344.4 30.8 %collective-permute-start.46 = (bf16[2,96,3072]{2,1,0:T(8,128)(2,1)}, bf16[2,96,3072]{2,1,0:T(8,128)(2,1)}, u32[]{:S(2)}, u32[]{:S(2)}) collective-permute-start(bf16[2,96,3072]{2,1,0:T(8,128)(2,1)} %dynamic-slice_bitcast_fusion.9), channel_id=1, source_target_pairs={{0,8},{4,12},{8,0},{12,4},{16,24},{20,28},{24,16},{28,20},{1,9},{5... | collective-permute-start | bytes 3538952 | tf_op jit(solution)/shard_map/ppermute | solution.py:130
  373.0 11.9 %collective-permute-start.48 = (bf16[2,512,768]{2,1,0:T(8,128)(2,1)}, bf16[2,512,768]{2,1,0:T(8,128)(2,1)}, u32[]{:S(2)}, u32[]{:S(2)}) collective-permute-start(bf16[2,512,768]{2,1,0:T(8,128)(2,1)} %get-tuple-element.227), channel_id=1, source_target_pairs={{0,4},{1,5},{2,6},{3,7},{4,0},{5,1},{6,2},{7,3},{8,12},{9,13},{10,... | collective-permute-start | bytes 4718600 | tf_op jit(solution)/shard_map/ppermute | solution.py:272
  378.6 16.0 %collective-permute-start.50 = (bf16[384,768]{1,0:T(8,128)(2,1)}, bf16[384,768]{1,0:T(8,128)(2,1)}, u32[]{:S(2)}, u32[]{:S(2)}) collective-permute-start(bf16[384,768]{1,0:T(8,128)(2,1)} %dynamic-slice_bitcast_fusion.20), channel_id=1, source_target_pairs={{0,8},{4,12},{8,0},{12,4},{16,24},{20,28},{24,16},{28,20},{1,9},{5... | collective-permute-start | bytes 1769480 | tf_op jit(solution)/shard_map/ppermute | solution.py:130
  382.5 15.7 %collective-permute-start.49 = (bf16[96,3072]{1,0:T(8,128)(2,1)}, bf16[96,3072]{1,0:T(8,128)(2,1)}, u32[]{:S(2)}, u32[]{:S(2)}) collective-permute-start(bf16[96,3072]{1,0:T(8,128)(2,1)} %dynamic-slice_bitcast_fusion.21), channel_id=1, source_target_pairs={{0,16},{4,20},{8,24},{12,28},{16,0},{20,4},{24,8},{28,12},{1,17},{... | collective-permute-start | bytes 1769480 | tf_op jit(solution)/shard_map/ppermute | solution.py:130
  401.8 13.9 %collective-permute-start.53 = (bf16[2,2,2,48,3072]{4,3,2,1,0:T(8,128)(2,1)}, bf16[2,2,2,48,3072]{4,3,2,1,0:T(8,128)(2,1)}, u32[]{:S(2)}, u32[]{:S(2)}) collective-permute-start(bf16[2,2,2,48,3072]{4,3,2,1,0:T(8,128)(2,1)} %dynamic-slice_bitcast_fusion.3), channel_id=1, source_target_pairs={{0,4},{4,0},{8,12},{12,8},{16,20},{20,16},{24,28},{28,24},{1,5},{5... | collective-permute-start | bytes 7077896 | tf_op jit(solution)/shard_map/ppermute | solution.py:130
  416.9 33.6 %collective-permute-start.57 = (bf16[2,24,6144]{2,1,0:T(8,128)(2,1)}, bf16[2,24,6144]{2,1,0:T(8,128)(2,1)S(1)}, u32[]{:S(2)}, u32[]{:S(2)}) collective-permute-start(bf16[2,24,6144]{2,1,0:T(8,128)(2,1)} %fusion.76), channel_id=1, source_target_pairs={{0,2},{1,3},{2,0},{3,1},{4,6},{5,7},{6,4},{7,5},{8,10},{9,11},{10,... | collective-permute-start | bytes 1769480 | tf_op jit(solution)/shard_map/ppermute | solution.py:128
  430.9 21.0 %collective-permute-start.54 = (bf16[2,2,384,768]{3,2,1,0:T(8,128)(2,1)}, bf16[2,2,384,768]{3,2,1,0:T(8,128)(2,1)}, u32[]{:S(2)}, u32[]{:S(2)}) collective-permute-start(bf16[2,2,384,768]{3,2,1,0:T(8,128)(2,1)} %dynamic-slice_bitcast_fusion.2), channel_id=1, source_target_pairs={{0,4},{4,0},{8,12},{12,8},{16,20},{20,16},{24,28},{28,24},{1,5},{5... | collective-permute-start | bytes 7077896 | tf_op jit(solution)/shard_map/ppermute | solution.py:130
  432.3 19.7 %collective-permute-start.56 = (bf16[2,48,3072]{2,1,0:T(8,128)(2,1)}, bf16[2,48,3072]{2,1,0:T(8,128)(2,1)}, u32[]{:S(2)}, u32[]{:S(2)}) collective-permute-start(bf16[2,48,3072]{2,1,0:T(8,128)(2,1)} %dynamic-slice_bitcast_fusion.18), channel_id=1, source_target_pairs={{0,16},{4,20},{8,24},{12,28},{16,0},{20,4},{24,8},{28,12},{1,17},{... | collective-permute-start | bytes 1769480 | tf_op jit(solution)/shard_map/ppermute | solution.py:130
  434.1 17.8 %collective-permute-start.55 = (bf16[2,48,3072]{2,1,0:T(8,128)(2,1)}, bf16[2,48,3072]{2,1,0:T(8,128)(2,1)}, u32[]{:S(2)}, u32[]{:S(2)}) collective-permute-start(bf16[2,48,3072]{2,1,0:T(8,128)(2,1)} %dynamic-slice_bitcast_fusion.19), channel_id=1, source_target_pairs={{0,8},{4,12},{8,0},{12,4},{16,24},{20,28},{24,16},{28,20},{1,9},{5... | collective-permute-start | bytes 1769480 | tf_op jit(solution)/shard_map/ppermute | solution.py:130
  445.7 66.3 %collective-permute-start.64 = (bf16[256,768]{1,0:T(8,128)(2,1)}, bf16[256,768]{1,0:T(8,128)(2,1)}, u32[]{:S(2)}, u32[]{:S(2)}) collective-permute-start(bf16[256,768]{1,0:T(8,128)(2,1)} %get-tuple-element.377), channel_id=1, source_target_pairs={{0,0},{1,1},{4,2},{5,3},{2,4},{3,5},{6,6},{7,7},{8,8},{9,9},{12,10... | collective-permute-start | bytes 1179656 | tf_op jit(solution)/shard_map/ppermute | solution.py:250
  450.5 64.3 %collective-permute-start.65 = (bf16[256,768]{1,0:T(8,128)(2,1)}, bf16[256,768]{1,0:T(8,128)(2,1)}, u32[]{:S(2)}, u32[]{:S(2)}) collective-permute-start(bf16[256,768]{1,0:T(8,128)(2,1)} %get-tuple-element.376), channel_id=1, source_target_pairs={{1,0},{0,1},{5,2},{4,3},{3,4},{2,5},{7,6},{6,7},{9,8},{8,9},{13,10... | collective-permute-start | bytes 1179656 | tf_op jit(solution)/shard_map/ppermute | solution.py:250
  454.3 60.6 %collective-permute-start.63 = (bf16[48,3072]{1,0:T(8,128)(2,1)}, bf16[48,3072]{1,0:T(8,128)(2,1)}, u32[]{:S(2)}, u32[]{:S(2)}) collective-permute-start(bf16[48,3072]{1,0:T(8,128)(2,1)} %dynamic-slice_bitcast_fusion.35), channel_id=1, source_target_pairs={{0,8},{4,12},{8,0},{12,4},{16,24},{20,28},{24,16},{28,20},{1,9},{5... | collective-permute-start | bytes 884744 | tf_op jit(solution)/shard_map/ppermute | solution.py:130
  455.0 22.4 %collective-permute-start.59 = (bf16[24,6144]{1,0:T(8,128)(2,1)S(1)}, bf16[24,6144]{1,0:T(8,128)(2,1)S(1)}, u32[]{:S(2)}, u32[]{:S(2)}) collective-permute-start(bf16[24,6144]{1,0:T(8,128)(2,1)S(1)} %dynamic-slice_bitcast_fusion.37), channel_id=1, source_target_pairs={{0,1},{1,0},{2,3},{3,2},{4,5},{5,4},{6,7},{7,6},{8,9},{9,8},{10,11... | collective-permute-start | bytes 884744 | tf_op jit(solution)/shard_map/ppermute | solution.py:128
  457.4 21.2 %collective-permute-start.58 = (bf16[2,2,96,3072]{3,2,1,0:T(8,128)(2,1)}, bf16[2,2,96,3072]{3,2,1,0:T(8,128)(2,1)}, u32[]{:S(2)}, u32[]{:S(2)}) collective-permute-start(bf16[2,2,96,3072]{3,2,1,0:T(8,128)(2,1)} %dynamic-slice_bitcast_fusion.1), channel_id=1, source_target_pairs={{0,4},{4,0},{8,12},{12,8},{16,20},{20,16},{24,28},{28,24},{1,5},{5... | collective-permute-start | bytes 7077896 | tf_op jit(solution)/shard_map/ppermute | solution.py:130
  477.5 43.0 %collective-permute-start.61 = (bf16[2,384,768]{2,1,0:T(8,128)(2,1)}, bf16[2,384,768]{2,1,0:T(8,128)(2,1)}, u32[]{:S(2)}, u32[]{:S(2)}) collective-permute-start(bf16[2,384,768]{2,1,0:T(8,128)(2,1)} %dynamic-slice_bitcast_fusion.6), channel_id=1, source_target_pairs={{0,16},{4,20},{8,24},{12,28},{16,0},{20,4},{24,8},{28,12},{1,17},{... | collective-permute-start | bytes 3538952 | tf_op jit(solution)/shard_map/ppermute | solution.py:130
  482.5 38.0 %collective-permute-start.60 = (bf16[2,96,3072]{2,1,0:T(8,128)(2,1)}, bf16[2,96,3072]{2,1,0:T(8,128)(2,1)}, u32[]{:S(2)}, u32[]{:S(2)}) collective-permute-start(bf16[2,96,3072]{2,1,0:T(8,128)(2,1)} %dynamic-slice_bitcast_fusion.7), channel_id=1, source_target_pairs={{0,8},{4,12},{8,0},{12,4},{16,24},{20,28},{24,16},{28,20},{1,9},{5... | collective-permute-start | bytes 3538952 | tf_op jit(solution)/shard_map/ppermute | solution.py:130
  514.8 22.8 %collective-permute-start.66 = (bf16[2,512,768]{2,1,0:T(8,128)(2,1)}, bf16[2,512,768]{2,1,0:T(8,128)(2,1)}, u32[]{:S(2)}, u32[]{:S(2)}) collective-permute-start(bf16[2,512,768]{2,1,0:T(8,128)(2,1)} %copy-done.18), channel_id=1, source_target_pairs={{0,4},{1,5},{2,6},{3,7},{4,0},{5,1},{6,2},{7,3},{8,12},{9,13},{10,... | collective-permute-start | bytes 4718600 | tf_op jit(solution)/shard_map/ppermute | solution.py:272
  525.2 20.9 %collective-permute-start.69 = (bf16[2,24,3072]{2,1,0:T(8,128)(2,1)}, bf16[2,24,3072]{2,1,0:T(8,128)(2,1)}, u32[]{:S(2)}, u32[]{:S(2)}) collective-permute-start(bf16[2,24,3072]{2,1,0:T(8,128)(2,1)} %dynamic-slice_bitcast_fusion.34), channel_id=1, source_target_pairs={{0,2},{1,3},{2,0},{3,1},{4,6},{5,7},{6,4},{7,5},{8,10},{9,11},{10,... | collective-permute-start | bytes 884744 | tf_op jit(solution)/shard_map/ppermute | solution.py:128
  529.9 16.2 %collective-permute-start.68 = (bf16[384,768]{1,0:T(8,128)(2,1)}, bf16[384,768]{1,0:T(8,128)(2,1)}, u32[]{:S(2)}, u32[]{:S(2)}) collective-permute-start(bf16[384,768]{1,0:T(8,128)(2,1)} %dynamic-slice_bitcast_fusion.16), channel_id=1, source_target_pairs={{0,8},{4,12},{8,0},{12,4},{16,24},{20,28},{24,16},{28,20},{1,9},{5... | collective-permute-start | bytes 1769480 | tf_op jit(solution)/shard_map/ppermute | solution.py:130
  534.0 13.2 %collective-permute-start.67 = (bf16[96,3072]{1,0:T(8,128)(2,1)}, bf16[96,3072]{1,0:T(8,128)(2,1)}, u32[]{:S(2)}, u32[]{:S(2)}) collective-permute-start(bf16[96,3072]{1,0:T(8,128)(2,1)} %dynamic-slice_bitcast_fusion.17), channel_id=1, source_target_pairs={{0,16},{4,20},{8,24},{12,28},{16,0},{20,4},{24,8},{28,12},{1,17},{... | collective-permute-start | bytes 1769480 | tf_op jit(solution)/shard_map/ppermute | solution.py:130
  552.3 25.6 %collective-permute-start.80 = (bf16[2,24,6144]{2,1,0:T(8,128)(2,1)S(1)}, bf16[2,24,6144]{2,1,0:T(8,128)(2,1)S(1)}, u32[]{:S(2)}, u32[]{:S(2)}) collective-permute-start(bf16[2,24,6144]{2,1,0:T(8,128)(2,1)S(1)} %fusion.70), channel_id=1, source_target_pairs={{0,2},{1,3},{2,0},{3,1},{4,6},{5,7},{6,4},{7,5},{8,10},{9,11},{10,... | collective-permute-start | bytes 1769480 | tf_op jit(solution)/shard_map/ppermute | solution.py:128
  554.4 33.7 %collective-permute-start.71 = (bf16[24,3072]{1,0:T(8,128)(2,1)S(1)}, bf16[24,3072]{1,0:T(8,128)(2,1)}, u32[]{:S(2)}, u32[]{:S(2)}) collective-permute-start(bf16[24,3072]{1,0:T(8,128)(2,1)S(1)} %dynamic-slice_bitcast_fusion.39), channel_id=1, source_target_pairs={{0,1},{1,0},{2,3},{3,2},{4,5},{5,4},{6,7},{7,6},{8,9},{9,8},{10,11... | collective-permute-start | bytes 442376 | tf_op jit(solution)/shard_map/ppermute | solution.py:128
  559.2 28.9 %collective-permute-start.70 = (bf16[2,2,2,48,3200]{4,3,2,1,0:T(8,128)(2,1)}, bf16[2,2,2,48,3200]{4,3,2,1,0:T(8,128)(2,1)}, u32[]{:S(2)}, u32[]{:S(2)}) collective-permute-start(bf16[2,2,2,48,3200]{4,3,2,1,0:T(8,128)(2,1)} %dynamic-slice_bitcast_fusion), channel_id=1, source_target_pairs={{0,4},{4,0},{8,12},{12,8},{16,20},{20,16},{24,28},{28,24},{1,5},{5... | collective-permute-start | bytes 7372808 | tf_op jit(solution)/shard_map/ppermute | solution.py:130
  591.4 14.1 %collective-permute-start.74 = (bf16[2,48,3200]{2,1,0:T(8,128)(2,1)S(1)}, bf16[2,48,3200]{2,1,0:T(8,128)(2,1)S(1)}, u32[]{:S(2)}, u32[]{:S(2)}) collective-permute-start(bf16[2,48,3200]{2,1,0:T(8,128)(2,1)S(1)} %dynamic-slice_bitcast_fusion.15), channel_id=1, source_target_pairs={{0,8},{4,12},{8,0},{12,4},{16,24},{20,28},{24,16},{28,20},{1,9},{5... | collective-permute-start | bytes 1843208 | tf_op jit(solution)/shard_map/ppermute | solution.py:130
  592.0 14.6 %collective-permute-start.76 = (bf16[2,48,3200]{2,1,0:T(8,128)(2,1)S(1)}, bf16[2,48,3200]{2,1,0:T(8,128)(2,1)S(1)}, u32[]{:S(2)}, u32[]{:S(2)}) collective-permute-start(bf16[2,48,3200]{2,1,0:T(8,128)(2,1)S(1)} %dynamic-slice_bitcast_fusion.14), channel_id=1, source_target_pairs={{0,16},{4,20},{8,24},{12,28},{16,0},{20,4},{24,8},{28,12},{1,17},{... | collective-permute-start | bytes 1843208 | tf_op jit(solution)/shard_map/ppermute | solution.py:130
  613.9 21.3 %collective-permute-start.78 = (bf16[2,24,3200]{2,1,0:T(8,128)(2,1)S(1)}, bf16[2,24,3200]{2,1,0:T(8,128)(2,1)S(1)}, u32[]{:S(2)}, u32[]{:S(2)}) collective-permute-start(bf16[2,24,3200]{2,1,0:T(8,128)(2,1)S(1)} %dynamic-slice_bitcast_fusion.30), channel_id=1, source_target_pairs={{0,2},{1,3},{2,0},{3,1},{4,6},{5,7},{6,4},{7,5},{8,10},{9,11},{10,... | collective-permute-start | bytes 921608 | tf_op jit(solution)/shard_map/ppermute | solution.py:128
  615.4 21.0 %collective-permute-start.72 = (bf16[256,768]{1,0:T(8,128)(2,1)S(1)}, bf16[256,768]{1,0:T(8,128)(2,1)S(1)}, u32[]{:S(2)}, u32[]{:S(2)}) collective-permute-start(bf16[256,768]{1,0:T(8,128)(2,1)S(1)} %get-tuple-element.374), channel_id=1, source_target_pairs={{0,0},{1,1},{4,2},{5,3},{2,4},{3,5},{6,6},{7,7},{8,8},{9,9},{12,10... | collective-permute-start | bytes 1179656 | tf_op jit(solution)/shard_map/ppermute | solution.py:250
  616.1 20.3 %collective-permute-start.73 = (bf16[256,768]{1,0:T(8,128)(2,1)S(1)}, bf16[256,768]{1,0:T(8,128)(2,1)S(1)}, u32[]{:S(2)}, u32[]{:S(2)}) collective-permute-start(bf16[256,768]{1,0:T(8,128)(2,1)S(1)} %get-tuple-element.373), channel_id=1, source_target_pairs={{1,0},{0,1},{5,2},{4,3},{3,4},{2,5},{7,6},{6,7},{9,8},{8,9},{13,10... | collective-permute-start | bytes 1179656 | tf_op jit(solution)/shard_map/ppermute | solution.py:250
  (179 other events, 1233.7 us)

commit v3 on v2

--- a/solution.py
+++ b/solution.py
@@ -21,38 +21,52 @@
 BF = jnp.bfloat16
 F32 = jnp.float32
 
-GATHER_TICKS, HEAD_TICKS, TAIL_TICKS = 7, 2, 0
+(
+    QKV_1, FFN_1, QKV_2, FFN_2, HIDDEN, SKIP, COTS, CLS, OUTS, SKIP_BACK, HIDDEN_BACK,
+    OUTER_G1, INNER_G1, FFN_G1, QKV_G1, OUTER_G2, INNER_G2, FFN_G2, QKV_G2,
+) = range(19)
+START, F0, BETWEEN, F1, TURN, B1, UP, B0, END = range(9)
+AT_QKV, AT_HALF, AT_MIX, AT_NORM, AT_FFN, AT_ACTIVE, AT_OUT = range(7)
+AT_D_OUTER, AT_D_INNER, AT_D_NORM, AT_D_MIX, AT_D_HALF, AT_D_QUERY, AT_D_QKV, AT_D_INPUT = range(8)
+START_TICKS, BETWEEN_TICKS, END_TICKS = 7, 1, 4
+LATE = (FFN_G1, FFN_G2)
 PLAN = {
-    "g0": ["qkv_one"],
-    "g1": ["qkv_one", "ffn_one"],
-    "g2": ["qkv_one", "ffn_one"],
-    "g3": ["qkv_one", "hidden"],
-    "g4": ["qkv_one", "ffn_one"],
-    "g5": ["qkv_one", "hidden", "qkv_two"],
-    "f0.qkv": ["ffn_one", "qkv_two"],
-    "f0.attend": ["ffn_one", "qkv_two", "ffn_two"],
-    "f0.normed": ["ffn_one", "qkv_two", "ffn_two"],
-    "f0.active": ["skip"],
-    "f0.out": [],
-    "h0": ["qkv_two", "cls", "ffn_two"],
-    "h1": ["qkv_two", "cls", "skip", "cots"],
-    "f1.qkv": ["ffn_two", "cls"],
-    "f1.attend": ["ffn_two", "cls"],
-    "f1.normed": ["ffn_two", "cls"],
-    "f1.out": ["cls", "cots"],
-    "t": ["outs"],
-    "b1.d_outer": ["back_outer_two"],
-    "b1.d_inner": ["back_outer_two", "back_inner_two"],
-    "b1.d_mixture": ["back_inner_two"],
-    "b1.d_queries": ["back_outer_two", "back_inner_two"],
-    "b1.d_qkv": ["back_outer_two", "back_inner_two", "back_qkv_two", "outs"],
-    "u": ["back_z_two", "back_qkv_two", "skip_back"],
-    "b0.d_outer": ["back_outer_one"],
-    "b0.d_inner": ["back_z_two", "back_qkv_two", "back_outer_one", "back_inner_one"],
-    "b0.d_mixture": ["back_z_two", "back_inner_one"],
-    "b0.d_queries": ["back_outer_one", "back_inner_one", "back_qkv_two", "skip_back"],
-    "b0.d_qkv": ["back_outer_one", "back_inner_one", "back_qkv_one", "back_qkv_two"],
-    "b0.d_input": ["back_qkv_one", "back_qkv_two"],
+    (START, 0): [QKV_1],
+    (START, 1): [QKV_1, FFN_1],
+    (START, 2): [QKV_1, FFN_1],
+    (START, 3): [QKV_1, FFN_1],
+    (START, 4): [QKV_1, HIDDEN],
+    (START, 5): [QKV_1, FFN_1],
+    (START, 6): [QKV_1, HIDDEN, QKV_2],
+    (F0, AT_QKV): [FFN_1, QKV_2, FFN_2],
+    (F0, AT_HALF): [QKV_2, FFN_2],
+    (F0, AT_MIX): [FFN_1, QKV_2, FFN_2],
+    (F0, AT_NORM): [FFN_1, QKV_2, SKIP],
+    (F0, AT_OUT): [QKV_2, FFN_2, CLS],
+    (BETWEEN, 0): [QKV_2, SKIP, CLS],
+    (F1, AT_QKV): [FFN_2, CLS],
+    (F1, AT_HALF): [CLS],
+    (F1, AT_MIX): [FFN_2, CLS],
+    (F1, AT_NORM): [FFN_2, CLS],
+    (TURN, 0): [OUTS],
+    (B1, AT_D_OUTER): [OUTER_G2],
+    (B1, AT_D_INNER): [OUTER_G2, INNER_G2],
+    (B1, AT_D_MIX): [INNER_G2, OUTS],
+    (B1, AT_D_HALF): [OUTER_G2, COTS],
+    (B1, AT_D_QUERY): [INNER_G2],
+    (B1, AT_D_QKV): [OUTER_G2, INNER_G2, FFN_G2, QKV_G2, COTS],
+    (UP, 0): [FFN_G2, QKV_G2, SKIP_BACK],
+    (B0, AT_D_OUTER): [OUTER_G1],
+    (B0, AT_D_INNER): [FFN_G2, QKV_G2, OUTER_G1, INNER_G1],
+    (B0, AT_D_MIX): [FFN_G2, INNER_G1],
+    (B0, AT_D_HALF): [QKV_G2, OUTER_G1],
+    (B0, AT_D_QUERY): [INNER_G1, QKV_G2, SKIP_BACK],
+    (B0, AT_D_QKV): [OUTER_G1, INNER_G1, QKV_G1, FFN_G1, QKV_G2],
+    (B0, AT_D_INPUT): [QKV_G1, HIDDEN_BACK, FFN_G1, QKV_G2],
+    (END, 0): [QKV_G1, FFN_G1],
+    (END, 1): [QKV_G1],
+    (END, 2): [QKV_G1, HIDDEN_BACK, FFN_G1],
+    (END, 3): [QKV_G1],
 }
 
 
@@ -134,10 +148,11 @@
         return bits if turned else bits[::-1]
 
     def join(self, own, other, bit, have):
+        place = sum(1 for b in have if b > bit)
         mine = self.my_bit(bit) == 0
         low = jnp.where(mine, own, other)
         high = jnp.where(mine, other, own)
-        return jnp.stack([low, high], axis=sum(1 for b in have if b > bit))
+        return lax.optimization_barrier(jnp.stack([low, high], axis=place))
 
     def gather(self, x, bits):
         out = x
@@ -145,6 +160,30 @@
             other = yield self.swap(out, bit)
             out = self.join(out, other, bit, bits[:n])
         return out.reshape((-1,) + x.shape[1:])
+
+    def gather_z(self, x):
+        if self.n_f != 4:
+            return (yield from self.gather(x, list(range(self.f_bits))))
+        other = yield self.swap(x, 0)
+        pair = self.join(x, other, 0, [])
+        middle = yield lax.ppermute(pair, "fsdp", [(1, 2), (2, 1)])
+        outer = yield lax.ppermute(middle, "fsdp", [(1, 0), (2, 3)])
+        inside = (self.f == 1) | (self.f == 2)
+        out = self.join(pair, jnp.where(inside, middle, outer), 1, [0])
+        return out.reshape((-1,) + x.shape[1:])
+
+    def scatter_z(self, x):
+        if self.n_f != 4:
+            return (yield from self.scatter(x, list(range(self.f_bits))[::-1]))
+        out = x.reshape((2, 2, -1) + x.shape[1:])
+        kept, sent = self.halves(out, 1, [1, 0])
+        inward = yield lax.ppermute(sent, "fsdp", [(0, 1), (3, 2)])
+        summed = (sent.astype(F32) + inward.astype(F32)).astype(BF)
+        middle = yield lax.ppermute(summed, "fsdp", [(1, 2), (2, 1)])
+        out = (kept.astype(F32) + middle.astype(F32)).astype(BF)
+        kept, sent = self.halves(out, 0, [0])
+        got = yield self.swap(sent, 0)
+        return (kept.astype(F32) + got.astype(F32)).astype(BF)
 
     def gather_two(self, x, y):
         outs = [x, y]
@@ -277,31 +316,31 @@
         self.plan = plan
         self.makers, self.running, self.waiting, self.result = {}, {}, {}, {}
 
-    def add(self, name, maker, *operands):
+    def add(self, name, maker, operands):
         self.makers[name] = (maker, operands)
 
     def step(self, name, value):
         try:
-            self.waiting[name] = (
-                next(self.running[name]) if value is None else self.running[name].send(value)
-            )
+            chain = self.running[name]
+            self.waiting[name] = next(chain) if value is None else chain.send(value)
         except StopIteration as end:
             self.waiting.pop(name, None)
             self.result[name] = end.value
 
+    def start(self, name, operands):
+        self.running[name] = self.makers[name][0](*operands)
+        self.step(name, None)
+
     def tick(self, point, value):
         names = [n for n in self.plan.get(point, ()) if n not in self.result]
-        if not names:
-            return value
         arrived = {n: self.waiting[n] for n in names if n in self.running}
-        fresh = {n: self.makers[n][1] for n in names if n not in self.running}
-        value, arrived, fresh = lax.optimization_barrier((value, arrived, fresh))
-        for name in names:
-            if name in arrived:
-                self.step(name, arrived[name])
-            else:
-                self.running[name] = self.makers[name][0](*fresh[name])
-                self.step(name, None)
+        fresh = [n for n in names if n not in self.running]
+        ready = {n: self.makers[n][1]() for n in fresh if n not in LATE}
+        value, arrived, ready = lax.optimization_barrier((value, arrived, ready))
+        for name in arrived:
+            self.step(name, arrived[name])
+        for name in fresh:
+            self.start(name, ready[name] if name in ready else self.makers[name][1]())
         return value
 
     def get(self, name):
@@ -311,8 +350,7 @@
         while any(n not in self.result for n in names):
             for name in names:
                 if name not in self.running:
-                    self.running[name] = self.makers[name][0](*self.makers[name][1])
-                    self.step(name, None)
+                    self.start(name, self.makers[name][1]())
                 elif name not in self.result:
                     self.step(name, self.waiting[name])
         return [self.result[n] for n in names]
@@ -340,33 +378,32 @@
     q_ref = refs[0]
     k_refs = refs[1 : 1 + chunks]
     v_refs = refs[1 + chunks : 1 + 2 * chunks]
-    seg_q_ref, seg_k_ref, o_ref, lse_ref = refs[1 + 2 * chunks :]
+    seg_q_ref, seg_k_ref = refs[1 + 2 * chunks : 3 + 2 * chunks]
+    o_ref, lse_ref = refs[-2:]
     tokens = q_ref.shape[0]
     for q0 in range(0, tokens, q_step):
         q = q_ref[q0 : q0 + q_step, :]
         seg_q = seg_q_ref[:, q0 : q0 + q_step]
         halves = []
         for head in range(2):
-            q_head = head_only(q, head)
+            q_head = head_only(q, head) * SCALING
             scores = []
             for c in range(chunks):
-                s = dot_nt(k_refs[c][...], q_head) * SCALING
+                s = dot_nt(k_refs[c][...], q_head)
                 seg_k = seg_k_ref[c * tokens : (c + 1) * tokens, :]
                 scores.append(jnp.where(seg_k == seg_q, s, NEGATIVE))
             highest = functools.reduce(
                 jnp.maximum, [jnp.max(s, axis=0, keepdims=True) for s in scores]
             )
             powers = [jnp.exp(s - highest) for s in scores]
-            total = functools.reduce(
+            norm = functools.reduce(
                 jnp.add, [jnp.sum(p, axis=0, keepdims=True) for p in powers]
             )
-            inverse = 1.0 / total
             mixed = functools.reduce(
-                jnp.add,
-                [dot_tn(v_refs[c][...], (powers[c] * inverse).astype(BF)) for c in range(chunks)],
+                jnp.add, [dot_tn(v_refs[c][...], powers[c].astype(BF)) for c in range(chunks)]
             )
-            halves.append(mixed[head * HEAD_DIM : (head + 1) * HEAD_DIM, :])
-            lse_ref[0, head : head + 1, q0 : q0 + q_step] = highest + jnp.log(total)
+            halves.append(mixed[head * HEAD_DIM : (head + 1) * HEAD_DIM, :] * (1.0 / norm))
+            lse_ref[0, head : head + 1, q0 : q0 + q_step] = highest + jnp.log(norm)
         both = jnp.concatenate(halves, axis=0)
         o_ref[q0 : q0 + q_step, :] = both.T.astype(BF)
 
@@ -376,9 +413,8 @@
     k_refs = refs[1 : 1 + chunks]
     v_refs = refs[1 + chunks : 1 + 2 * chunks]
     do_ref, lse_ref, seg_q_ref, seg_k_ref = refs[1 + 2 * chunks : 5 + 2 * chunks]
-    dq_ref, own_ref = refs[5 + 2 * chunks : 7 + 2 * chunks]
-    other_refs = refs[7 + 2 * chunks : 6 + 3 * chunks]
-    acc_ref = refs[6 + 3 * chunks]
+    dq_ref, own_ref, *other_refs = refs[-2 - chunks : -1]
+    acc_ref = refs[-1]
     tokens = q_ref.shape[0]
     first = True
     for q0 in range(0, tokens, q_step):
@@ -387,12 +423,12 @@
         seg_q = seg_q_ref[:, q0 : q0 + q_step]
         halves = []
         for head in range(2):
-            q_head = head_only(q, head)
+            q_head = head_only(q, head) * SCALING
             do_head = head_only(do, head)
             lse = lse_ref[0, head : head + 1, q0 : q0 + q_step]
             probs, d_probs = [], []
             for c in range(chunks):
-                s = dot_nt(k_refs[c][...], q_head) * SCALING
+                s = dot_nt(k_refs[c][...], q_head)
                 seg_k = seg_k_ref[c * tokens : (c + 1) * tokens, :]
                 s = jnp.where(seg_k == seg_q, s, NEGATIVE)
                 probs.append(jnp.exp(s - lse))
@@ -404,7 +440,7 @@
             dq_t = None
             for c in range(chunks):
                 ds = (probs[c] * (d_probs[c] - offset)).astype(BF)
-                dk = dot_nn(ds, q_head) * SCALING
+                dk = dot_nn(ds, q_head)
                 dv = dot_nn(probs[c].astype(BF), do_head)
                 term = dot_tn(k_refs[c][...], ds)
                 dq_t = term if dq_t is None else dq_t + term
@@ -423,82 +459,91 @@
         other_refs[c - 1][...] = acc_ref[c].astype(BF)
 
 
-def attention_specs(qkv, others):
-    tokens = qkv.shape[0]
+def attention_specs(qkv, others, first):
+    block = (qkv.shape[0], PAIR)
     pairs = HEADS // 2
-    block = (tokens, PAIR)
-    at = lambda offset: pl.BlockSpec(block, lambda i, offset=offset: (0, offset + i))
+    at = lambda offset: pl.BlockSpec(block, lambda i: (0, offset + first + i))
     operands = [qkv, qkv] + others + [qkv] + others
-    specs = (
-        [at(0), at(pairs)]
-        + [at(0) for _ in others]
-        + [at(2 * pairs)]
-        + [at(pairs) for _ in others]
-    )
-    return operands, specs, tokens, pairs
-
-
-def attend(qkv, others, seg_q, seg_k):
-    operands, specs, tokens, pairs = attention_specs(qkv, others)
-    chunks = 1 + len(others)
-    length = tokens * chunks
-    whole = lambda shape: pl.BlockSpec(shape, lambda i: (0,) * len(shape))
+    specs = [at(0), at(pairs)] + [at(0) for _ in others] + [at(2 * pairs)] + [at(pairs) for _ in others]
+    return operands, specs
+
+
+def whole(shape):
+    return pl.BlockSpec(shape, lambda i: (0,) * len(shape))
+
+
+def attend(qkv, others, seg_q, seg_k, first, count, done=None):
+    operands, specs = attention_specs(qkv, others, first)
+    tokens, length = qkv.shape[0], seg_k.shape[0]
+    operands += [seg_q, seg_k]
+    specs += [whole((1, tokens)), whole((length, 1))]
+    aliases = {}
+    if done is not None:
+        aliases = {len(operands): 0, len(operands) + 1: 1}
+        operands += list(done)
+        specs += [pl.BlockSpec(memory_space=pl.ANY)] * 2
     return pl.pallas_call(
-        functools.partial(attend_kernel, chunks, min(256, tokens)),
-        grid=(pairs,),
-        in_specs=specs + [whole((1, tokens)), whole((length, 1))],
+        functools.partial(attend_kernel, 1 + len(others), min(256, tokens)),
+        grid=(count,),
+        in_specs=specs,
         out_specs=[
-            pl.BlockSpec((tokens, PAIR), lambda i: (0, i)),
-            pl.BlockSpec((1, 2, tokens), lambda i: (i, 0, 0)),
+            pl.BlockSpec((tokens, PAIR), lambda i: (0, first + i)),
+            pl.BlockSpec((1, 2, tokens), lambda i: (first + i, 0, 0)),
         ],
         out_shape=[
             jax.ShapeDtypeStruct((tokens, HEADS * HEAD_DIM), BF),
-            jax.ShapeDtypeStruct((pairs, 2, tokens), F32),
+            jax.ShapeDtypeStruct((HEADS // 2, 2, tokens), F32),
         ],
+        input_output_aliases=aliases,
         compiler_params=pltpu.CompilerParams(vmem_limit_bytes=40 * 2**20),
         cost_estimate=pl.CostEstimate(
-            flops=16 * tokens * length * HEADS * HEAD_DIM,
-            bytes_accessed=8 * length * HEADS * HEAD_DIM,
-            transcendentals=tokens * length * HEADS,
+            flops=16 * tokens * length * count * PAIR,
+            bytes_accessed=8 * length * count * PAIR,
+            transcendentals=2 * tokens * length * count,
         ),
         name="attend",
-    )(*operands, seg_q, seg_k)
-
-
-def attend_back(qkv, others, d_mixture, lse, seg_q, seg_k):
-    operands, specs, tokens, pairs = attention_specs(qkv, others)
+    )(*operands)
+
+
+def attend_back(qkv, others, d_mixture, lse, seg_q, seg_k, first, count, done=None):
+    operands, specs = attention_specs(qkv, others, first)
     chunks = 1 + len(others)
-    length = tokens * chunks
+    tokens, length = qkv.shape[0], seg_k.shape[0]
     width = HEADS * HEAD_DIM
-    whole = lambda shape: pl.BlockSpec(shape, lambda i: (0,) * len(shape))
-    stacked = pl.BlockSpec((2, tokens, PAIR), lambda i: (0, 0, i))
-    out = pl.pallas_call(
+    flat = pl.BlockSpec((tokens, PAIR), lambda i: (0, first + i))
+    stacked = pl.BlockSpec((2, tokens, PAIR), lambda i: (0, 0, first + i))
+    operands += [d_mixture, lse, seg_q, seg_k]
+    specs += [
+        flat,
+        pl.BlockSpec((1, 2, tokens), lambda i: (first + i, 0, 0)),
+        whole((1, tokens)),
+        whole((length, 1)),
+    ]
+    aliases = {}
+    if done is not None:
+        aliases = {len(operands) + n: n for n in range(len(done))}
+        operands += list(done)
+        specs += [pl.BlockSpec(memory_space=pl.ANY)] * len(done)
+    return pl.pallas_call(
         functools.partial(attend_back_kernel, chunks, min(256, tokens)),
-        grid=(pairs,),
-        in_specs=specs
-        + [
-            pl.BlockSpec((tokens, PAIR), lambda i: (0, i)),
-            pl.BlockSpec((1, 2, tokens), lambda i: (i, 0, 0)),
-            whole((1, tokens)),
-            whole((length, 1)),
-        ],
-        out_specs=[pl.BlockSpec((tokens, PAIR), lambda i: (0, i)), stacked]
-        + [stacked for _ in others],
+        grid=(count,),
+        in_specs=specs,
+        out_specs=[flat, stacked] + [stacked for _ in others],
         out_shape=[
             jax.ShapeDtypeStruct((tokens, width), BF),
             jax.ShapeDtypeStruct((2, tokens, width), F32),
         ]
         + [jax.ShapeDtypeStruct((2, tokens, width), BF) for _ in others],
         scratch_shapes=[pltpu.VMEM((chunks, 2, tokens, PAIR), F32)],
+        input_output_aliases=aliases,
         compiler_params=pltpu.CompilerParams(vmem_limit_bytes=40 * 2**20),
         cost_estimate=pl.CostEstimate(
-            flops=40 * tokens * length * width,
-            bytes_accessed=20 * length * width,
-            transcendentals=tokens * length * HEADS,
+            flops=40 * tokens * length * count * PAIR,
+            bytes_accessed=20 * length * count * PAIR,
+            transcendentals=2 * tokens * length * count,
         ),
         name="attend_back",
-    )(*operands, d_mixture, lse, seg_q, seg_k)
-    return out[0], out[1], out[2:]
+    )(*operands)
 
 
 def split_small(small, sizes):
@@ -509,35 +554,41 @@
     return vectors
 
 
-def layer_forward(grid, tag, tick, inputs, weights, seg_q, seg_k):
+def layer_forward(grid, phase, tick, inputs, weights, seg_q, seg_k, result=None):
     width = inputs.shape[1]
     x_low = inputs.astype(BF)
-    qkv_w, attn_w, qv_b, attn_b, attn_g, attn_s, inner_b, outer_b, ffn_g, ffn_s = weights("qkv")
+    qkv_w, attn_w, qv_b, attn_b, attn_g, attn_s, inner_b, outer_b, ffn_g, ffn_s = weights(True)
     bias = jnp.concatenate([qv_b[:width], jnp.zeros((width,), F32), qv_b[width:]])
     qkv = (matrix_product(x_low, qkv_w) + bias).astype(BF)
-    qkv = tick(tag + "qkv", qkv)
+    qkv = tick((phase, AT_QKV), qkv)
     key_value = qkv[:, width:]
     others = [grid.to_member(key_value, shift) for shift in range(1, grid.members)]
-    mixture, lse = attend(qkv, others, seg_q, seg_k)
-    mixture = tick(tag + "attend", mixture)
+    half = HEADS // 4
+    done = attend(qkv, others, seg_q, seg_k, 0, half)
+    done = tick((phase, AT_HALF), done)
+    mixture, lse = attend(qkv, others, seg_q, seg_k, half, HEADS // 2 - half, done)
+    mixture = tick((phase, AT_MIX), mixture)
     branch = matrix_product(mixture, attn_w) + attn_b
     normed, normed_one, inv_one = layer_norm(inputs.astype(F32) + branch, attn_g, attn_s)
-    normed = tick(tag + "normed", normed)
-    inner_w, outer_w = weights("ffn")
+    normed = tick((phase, AT_NORM), normed)
+    normed = tick((phase, AT_FFN), normed)
+    inner_w, outer_w = weights(False)
     normed_low = normed.astype(BF)
     inner = matrix_product(normed_low, inner_w) + inner_b
     active, slope = gelu_both(inner)
-    active = tick(tag + "active", active.astype(BF))
+    active = tick((phase, AT_ACTIVE), active.astype(BF))
     outer = matrix_product(active, outer_w) + outer_b
     output, normed_two, inv_two = layer_norm(normed + outer, ffn_g, ffn_s)
-    output = tick(tag + "out", output)
+    if result is not None:
+        result.append(output)
+    output = tick((phase, AT_OUT), output)
     saved = (x_low, qkv, others, lse, mixture, normed_one, inv_one, normed_low, slope, active, normed_two, inv_two)
     return output, saved
 
 
-def layer_backward(grid, tag, tick, give, upstream, weights, saved, seg_q, seg_k):
-    qkv_w, attn_w, qv_b, attn_b, attn_g, attn_s, inner_b, outer_b, ffn_g, ffn_s = weights("qkv")
-    inner_w, outer_w = weights("ffn")
+def layer_backward(grid, phase, tick, give, upstream, weights, saved, seg_q, seg_k, result=None):
+    qkv_w, attn_w, qv_b, attn_b, attn_g, attn_s, inner_b, outer_b, ffn_g, ffn_s = weights(True)
+    inner_w, outer_w = weights(False)
     (x_low, qkv, others, lse, mixture, normed_one, inv_one, normed_low, slope, active, normed_two, inv_two) = saved
     grad_ffn_g = jnp.sum(upstream * normed_two, axis=0)
     grad_ffn_s = jnp.sum(upstream, axis=0)
@@ -545,15 +596,15 @@
     d_outer = d_second.astype(BF)
     grad_outer_b = column_sum(d_outer)
     grad_outer_w = left_t(active, d_outer).astype(BF)
-    give("outer", grad_outer_w)
+    give(AT_D_OUTER, grad_outer_w)
     d_outer, grad_outer_w = lax.optimization_barrier((d_outer, grad_outer_w))
-    d_outer = tick(tag + "d_outer", d_outer)
+    d_outer = tick((phase, AT_D_OUTER), d_outer)
     d_inner = (right_t(d_outer, outer_w) * slope).astype(BF)
     grad_inner_b = column_sum(d_inner)
     grad_inner_w = left_t(normed_low, d_inner).astype(BF)
-    give("inner", grad_inner_w)
+    give(AT_D_INNER, grad_inner_w)
     d_inner, grad_inner_w = lax.optimization_barrier((d_inner, grad_inner_w))
-    d_inner = tick(tag + "d_inner", d_inner)
+    d_inner = tick((phase, AT_D_INNER), d_inner)
     d_normed = right_t(d_inner, inner_w) + d_second
     grad_attn_g = jnp.sum(d_normed * normed_one, axis=0)
     grad_attn_s = jnp.sum(d_normed, axis=0)
@@ -562,9 +613,14 @@
     grad_attn_b = column_sum(d_branch)
     grad_attn_w = left_t(mixture, d_branch).astype(BF)
     d_mixture = right_t(d_branch, attn_w).astype(BF)
-    d_mixture = tick(tag + "d_mixture", d_mixture)
-    d_queries, own, for_others = attend_back(qkv, others, d_mixture, lse, seg_q, seg_k)
-    d_queries = tick(tag + "d_queries", d_queries)
+    d_mixture = tick((phase, AT_D_MIX), d_mixture)
+    half = HEADS // 4
+    done = attend_back(qkv, others, d_mixture, lse, seg_q, seg_k, 0, half)
+    done = tick((phase, AT_D_HALF), done)
+    d_queries, own, *for_others = attend_back(
+        qkv, others, d_mixture, lse, seg_q, seg_k, half, HEADS // 2 - half, done
+    )
+    d_queries = tick((phase, AT_D_QUERY), d_queries)
     for shift in range(1, grid.members):
         own = own + grid.to_member(for_others[shift - 1], -shift).astype(F32)
     own = own.astype(BF)
@@ -572,11 +628,12 @@
     grad_qv_b = jnp.concatenate([column_sum(d_queries), column_sum(own[1])])
     grad_qkv_w = left_t(x_low, d_qkv).astype(BF)
     small = (grad_qv_b, grad_attn_b, grad_attn_g, grad_attn_s, grad_inner_b, grad_outer_b, grad_ffn_g, grad_ffn_s)
-    give("qkv", grad_qkv_w, grad_attn_w, small)
-    d_qkv = tick(tag + "d_qkv", d_qkv)
+    give(AT_D_QKV, grad_qkv_w, grad_attn_w, small)
+    d_qkv = tick((phase, AT_D_QKV), d_qkv)
     d_input = right_t(d_qkv, qkv_w) + d_first
-    d_input = tick(tag + "d_input", d_input)
-    return d_input
+    if result is not None:
+        result.append(d_input)
+    return tick((phase, AT_D_INPUT), d_input)
 
 
 def contrastive(vectors, positives):
@@ -638,7 +695,6 @@
     is_cls = jnp.any(my_starts[:, None] == q_pos[None, :], axis=0)[:, None]
 
     devices = grid.n_dp * grid.n_f
-    z_up, z_down = list(range(grid.f_bits)), list(range(grid.f_bits))[::-1]
     vectors = (qv_bias, attn_bias, attn_gain, attn_shift, inner_bias, outer_bias, ffn_gain, ffn_shift)
     sizes = [v.shape[1] for v in vectors]
     rows = qkv_weight.shape[1]
@@ -651,136 +707,131 @@
 
     def gather_qkv(*parts):
         out = jnp.concatenate(parts, axis=1)
-        out = yield from grid.gather(out, z_up)
+        out = yield from grid.gather_z(out)
         return (yield from grid.gather_split(out))
 
     def gather_ffn(inner, outer):
         deep = outer.shape[0] // inner.shape[0]
         out = jnp.concatenate([inner, outer.reshape(inner.shape[0], -1)], axis=1)
-        out = yield from grid.gather(out, z_up)
+        out = yield from grid.gather_z(out)
         inner, outer = out[:, : inner.shape[1]], out[:, inner.shape[1] :]
         return (yield from grid.gather_two(inner, outer.reshape(inner.shape[0] * deep, -1)))
 
-    for layer, tag in ((0, "one"), (1, "two")):
-        parts = [qkv_weight[layer], attn_weight[layer]] + ([small_own] if layer == 0 else [])
-        schedule.add("qkv_" + tag, gather_qkv, *parts)
-        schedule.add("ffn_" + tag, gather_ffn, inner_weight[layer], outer_weight[layer])
-    schedule.add("hidden", grid.to_rows, hidden)
-    schedule.add("skip", grid.to_rows, skip_tokens)
-    schedule.add("cots", grid.to_rows, jnp.concatenate([head_cotangent, backbone_cotangent], axis=2))
+    schedule.add(QKV_1, gather_qkv, lambda: (qkv_weight[0], attn_weight[0], small_own))
+    schedule.add(QKV_2, gather_qkv, lambda: (qkv_weight[1], attn_weight[1]))
+    schedule.add(FFN_1, gather_ffn, lambda: (inner_weight[0], outer_weight[0]))
+    schedule.add(FFN_2, gather_ffn, lambda: (inner_weight[1], outer_weight[1]))
+    schedule.add(HIDDEN, grid.to_rows, lambda: (hidden,))
+    schedule.add(
+        SKIP, grid.to_rows, lambda: (jnp.concatenate([skip_tokens, head_cotangent], axis=2),)
+    )
+    schedule.add(COTS, grid.to_rows, lambda: (backbone_cotangent,))
 
     small = []
 
-    def weights_of(layer, tag):
-        def get(which):
-            if which == "ffn":
-                return schedule.get("ffn_" + tag)
+    def weights_of(layer, qkv_name, ffn_name):
+        def get(is_qkv):
+            if not is_qkv:
+                return schedule.get(ffn_name)
             if not small:
-                every = schedule.get("qkv_one")[:, -padded:][:, :small_cols]
+                every = schedule.get(QKV_1)[:, -padded:][:, :small_cols]
                 small.append(every.reshape(devices, 2, -1))
-            pack = schedule.get("qkv_" + tag)
+            pack = schedule.get(qkv_name)
             cut = qkv_weight.shape[2]
             return (pack[:, :cut], pack[:, cut : cut + width], *split_small(small[0][:, layer], sizes))
 
         return get
+
+    backbone, head = weights_of(0, QKV_1, FFN_1), weights_of(1, QKV_2, FFN_2)
 
     def scatter_qkv(*parts):
         out = jnp.concatenate(parts, axis=1)
         out = yield from grid.scatter_split(out)
-        return (yield from grid.scatter(out, z_down))
+        return (yield from grid.scatter_z(out))
 
     core_first = lambda turned: [grid.f_bits] + grid.upper(turned)
 
     def scatter_z(inner, outer):
         deep = outer.shape[0] // inner.shape[0]
         out = jnp.concatenate([inner, outer.reshape(inner.shape[0], -1)], axis=1)
-        out = yield from grid.scatter(out, z_down)
+        out = yield from grid.scatter_z(out)
         return out[:, : inner.shape[1]], out[:, inner.shape[1] :].reshape(out.shape[0] * deep, -1)
 
-    kept_small = {}
-
-    def give_to(tag):
+    kept_small = []
+
+    def give_to(outer_name, inner_name, ffn_name, qkv_name, last):
+        def pack(grad_qkv, grad_attn, vectors):
+            if not last:
+                return grad_qkv, grad_attn
+            cut = [
+                jnp.concatenate([v.reshape(devices, -1) for v in kept], axis=1)
+                for kept in (vectors, kept_small[0])
+            ]
+            flat = jnp.stack(cut, axis=1).reshape(devices * rows, small_cols).astype(BF)
+            return grad_qkv, grad_attn, jnp.pad(flat, ((0, 0), (0, padded - small_cols)))
+
         def give(which, *grads):
-            if which == "qkv":
-                *grads, vectors = grads
-                kept_small[tag] = vectors
-                if tag == "one":
-                    cut = [
-                        jnp.concatenate([v.reshape(devices, -1) for v in kept_small[t]], axis=1)
-                        for t in ("one", "two")
-                    ]
-                    flat = jnp.stack(cut, axis=1).reshape(devices * rows, small_cols).astype(BF)
-                    grads.append(jnp.pad(flat, ((0, 0), (0, padded - small_cols))))
-                schedule.add("back_qkv_" + tag, scatter_qkv, *grads)
+            if which == AT_D_OUTER:
+                schedule.add(outer_name, lambda g: grid.scatter(g, core_first(False)), lambda: grads)
+            elif which == AT_D_INNER:
+                schedule.add(inner_name, lambda g: grid.scatter(g, core_first(True)), lambda: grads)
+                both = lambda: [v.astype(BF) for v in schedule.finish(inner_name, outer_name)]
+                schedule.add(ffn_name, scatter_z, both)
             else:
-                turned = which == "inner"
-                schedule.add(
-                    "back_" + which + "_" + tag,
-                    lambda g: grid.scatter(g, core_first(turned)),
-                    grads[0],
-                )
+                kept_small.append(grads[2])
+                schedule.add(qkv_name, scatter_qkv, lambda: pack(*grads))
 
         return give
-
-    def z_of(tag):
-        schedule.add(
-            "back_z_" + tag,
-            scatter_z,
-            schedule.get("back_inner_" + tag),
-            schedule.get("back_outer_" + tag),
-        )
-
-    mark = jnp.zeros((8, 128), F32) + my_starts[0].astype(F32)
-    for n in range(GATHER_TICKS):
-        mark = tick("g%d" % n, mark)
-    x = schedule.get("hidden")
-    first, saved_one = layer_forward(grid, "f0.", tick, x, weights_of(0, "one"), seg_q, seg_k)
 
     shared = n_bits(grid.chips_per_row)
     cls_bits = list(range(shared, grid.f_bits)) + grid.upper(True)
 
-    def gather_cls(own):
+    def gather_cls(states):
+        own = jnp.dot(cls_hot, states, precision=FULL_PRECISION)[None]
         for bit in [grid.f_bits] + list(range(shared)):
             got = yield grid.swap(own, bit)
             own = own + got
         return (yield from grid.gather(own, cls_bits))
 
-    schedule.add("cls", gather_cls, jnp.dot(cls_hot, first, precision=FULL_PRECISION)[None])
-    for n in range(HEAD_TICKS):
-        first = tick("h%d" % n, first)
-    head_in = jnp.where(is_cls, first, schedule.get("skip").astype(F32))
-    second, saved_two = layer_forward(grid, "f1.", tick, head_in, weights_of(1, "two"), seg_q, seg_k)
-
-    cots = schedule.get("cots")
-    schedule.add(
-        "outs", grid.from_rows, jnp.concatenate([first.astype(BF), second.astype(BF)], axis=1)
-    )
-    head_up = tick("t", cots[:, :width]).astype(F32)
-    d_head_in = layer_backward(
-        grid, "b1.", tick, give_to("two"), head_up, weights_of(1, "two"), saved_two, seg_q, seg_k
-    )
-    [cls_all] = schedule.finish("cls")
-    contrast_loss, d_cls_all = contrastive(cls_all.reshape(-1, width), positives)
+    first_states = []
+    schedule.add(CLS, gather_cls, lambda: (first_states[0],))
+
+    mark = jnp.zeros((8, 128), F32) + my_starts[0].astype(F32)
+    for n in range(START_TICKS):
+        mark = tick((START, n), mark)
+    x = schedule.get(HIDDEN)
+    first, saved_one = layer_forward(grid, F0, tick, x, backbone, seg_q, seg_k, first_states)
+    for n in range(BETWEEN_TICKS):
+        first = tick((BETWEEN, n), first)
+    skip_and_cot = schedule.get(SKIP)
+    head_in = jnp.where(is_cls, first, skip_and_cot[:, :width].astype(F32))
+    second, saved_two = layer_forward(grid, F1, tick, head_in, head, seg_q, seg_k)
+
+    both_out = jnp.concatenate([first.astype(BF), second.astype(BF)], axis=1)
+    schedule.add(OUTS, grid.from_rows, lambda: (both_out,))
+    head_up = tick((TURN, 0), skip_and_cot[:, width:]).astype(F32)
+    give = give_to(OUTER_G2, INNER_G2, FFN_G2, QKV_G2, False)
+    d_head_in = layer_backward(grid, B1, tick, give, head_up, head, saved_two, seg_q, seg_k)
+    skip_grad = jnp.where(is_cls, 0.0, d_head_in).astype(BF)
+    schedule.add(SKIP_BACK, grid.from_rows, lambda: (skip_grad,))
+    contrast_loss, d_cls_all = contrastive(schedule.get(CLS).reshape(-1, width), positives)
     my_row = grid.dp // CORES * (CORES * rows_dev) + grid.row_in_group
     d_cls = lax.dynamic_slice_in_dim(d_cls_all, my_row * SEGS, SEGS, 0)
+    cot = schedule.get(COTS)
     upstream = (
-        cots[:, width:].astype(F32)
+        cot.astype(F32)
         + jnp.where(is_cls, d_head_in, 0.0)
         + lax.dot_general(cls_hot, d_cls, (((0,), (0,)), ((), ())), precision=FULL_PRECISION)
     )
-    schedule.add("skip_back", grid.from_rows, jnp.where(is_cls, 0.0, d_head_in).astype(BF))
-    z_of("two")
-    upstream = tick("u", upstream)
-    d_input = layer_backward(
-        grid, "b0.", tick, give_to("one"), upstream, weights_of(0, "one"), saved_one, seg_q, seg_k
-    )
-    schedule.add("hidden_back", grid.from_rows, d_input.astype(BF))
-    schedule.finish("back_inner_one", "back_outer_one")
-    z_of("one")
+    upstream = tick((UP, 0), upstream)
+    give = give_to(OUTER_G1, INNER_G1, FFN_G1, QKV_G1, True)
+    schedule.add(HIDDEN_BACK, grid.from_rows, lambda: (d_input[0].astype(BF),))
+    d_input = []
+    layer_backward(grid, B0, tick, give, upstream, backbone, saved_one, seg_q, seg_k, d_input)
     mark = jnp.zeros((8, 128), F32)
-    for n in range(TAIL_TICKS):
-        mark = tick("e%d" % n, mark)
-    names = ["hidden_back", "skip_back", "outs", "back_z_one", "back_z_two", "back_qkv_one", "back_qkv_two"]
+    for n in range(END_TICKS):
+        mark = tick((END, n), mark)
+    names = [HIDDEN_BACK, SKIP_BACK, OUTS, FFN_G1, FFN_G2, QKV_G1, QKV_G2]
     hidden_back, skip_back, outs, (inner_1, outer_1), (inner_2, outer_2), qkv_1, qkv_2 = schedule.finish(*names)
 
     cut = qkv_weight.shape[2]

time: 659 us -> 652 us (0.989)
  starting transfers between devices: 96.7 us -> 166 us
  waiting for transfers between devices: 155 us -> 96.7 us
  local copies, waits for them, and re-layouts: 92.9 us -> 85.2 us
  Pallas kernels: 89.5 us -> 81.9 us
    ppermute x18 -> x10, waiting for transfers between devices: 90.8 us -> 9.9 us  [swap(): return lax.ppermute(x, 'fsdp', [(i, i ^ 1 << bit) for i in range(self.n_f)])]
    ppermute x0 -> x16, starting transfers between devices: none -> 28.4 us  [the longest x4 15 us: scatter_z(): inward = (yield lax.ppermute(sent, 'fsdp', [(0, 1), (3, 2)]))]
    ppermute x0 -> x16, waiting for transfers between devices: none -> 27.3 us  [the longest x4 17.3 us: scatter_z(): inward = (yield lax.ppermute(sent, 'fsdp', [(0, 1), (3, 2)]))]
    ppermute x18 -> x10, starting transfers between devices: 18.9 us -> 40.9 us  [swap(): return lax.ppermute(x, 'fsdp', [(i, i ^ 1 << bit) for i in range(self.n_f)])]
    ppermute x4, starting transfers between devices: 0.22 us -> 16.8 us  [to_member(): return lax.ppermute(x, ('dp', 'fsdp'), self.shift_pairs(shift))]
    ppermute x6, starting transfers between devices: 10.8 us -> 23.3 us  [to_rows(): got.append(lax.ppermute(block, ('dp', 'fsdp'), self.source(k)))]
    ppermute x48, starting transfers between devices: 42.2 us -> 33.1 us  [swap(): return lax.ppermute(x, 'dp', [(i, i ^ flip) for i in range(self.n_dp)])]
    ppermute x48, waiting for transfers between devices: 56.3 us -> 47.7 us  [swap(): return lax.ppermute(x, 'dp', [(i, i ^ flip) for i in range(self.n_dp)])]
  transfers between devices with their start and end apart: 82 -> 90, of which waited for: 28 -> 30; matrix products, arithmetic and copies ran while one was open for 36% -> 34% of each run, Pallas kernels for 14% -> 13%
where the time goes in v3:
time: 652 us; the launch traced here: 642 us
  starting transfers between devices  166 us (25%)
  other arithmetic  118 us (18%)
  waiting for transfers between devices  96.7 us (15%)
  matrix products  86.6 us (13%)
  local copies, waits for them, and re-layouts  85.2 us (13%)
  Pallas kernels  81.9 us (13%)
  between operations  6.54 us (1%)
    pallas_call x4, Pallas kernels, attend_back(): pl.pallas_call(functools.partial(attend_back_kernel, chunks, min(256, tok...  49.1 us
    ppermute x48, waiting for transfers between devices, swap(): return lax.ppermute(x, 'dp', [(i, i ^ flip) for i in range(self.n_dp)])  47.7 us
    ppermute x10, starting transfers between devices, swap(): return lax.ppermute(x, 'fsdp', [(i, i ^ 1 << bit) for i in range(self.n_f)])  40.9 us
    another operation x70, other arithmetic, join(): return lax.optimization_barrier(jnp.stack([low, high], axis=place))  37.5 us
    ppermute x48, starting transfers between devices, swap(): return lax.ppermute(x, 'dp', [(i, i ^ flip) for i in range(self.n_dp)])  33.1 us
    pallas_call x4, Pallas kernels, attend(): pl.pallas_call(functools.partial(attend_kernel, 1 + len(others), min(256,...  32.8 us
    dot_general x8, matrix products, right_t(): lax.dot_general(first_op, second_op, (((1,), (1,)), ((), ())), preferred_...  32 us
    unnamed x275, local copies, waits for them, and re-layouts  29.4 us
  transfers between devices with their start and end apart: 90, of which 30 were waited for; matrix products, arithmetic and copies ran while one was open for 34% of the time, Pallas kernels for 13%

profile of v3, /device:TPU:0, one launch (start us, length us, event | category | flops | bytes accessed | tf_op | source)
XLA Modules:
  0.0 641.9 jit_solution(16037001709645022750)
XLA Ops:
  4.1 3.1 collective-permute-start.1
  8.3 2.9 collective-permute-done.1
  12.1 4.6 collective-permute-start.3
  16.7 5.9 collective-permute-done.3
  28.1 8.0 %collective-permute-done.4 = bf16[2,24,3200]{2,1,0:T(8,128)(2,1)S(1)} collective-permute-done((bf16[2,24,3200]{2,1,0:T(8,128)(2,1)S(1)}, bf16[2,24,3200]{2,1,0:T(8,128)(2,1)S(1)}, u32[]{:S(2)}, u32[]{:S(2)}) %collective-permute-start.4) | collective-permute-done | bytes 307232 | tf_op jit(solution)/shard_map/ppermute | solution.py:170
  40.8 4.6 collective-permute-done.6
  52.9 4.5 collective-permute-start.12
  57.4 3.0 collective-permute-start.13
  74.5 2.6 select_bitcast_fusion.1
  82.7 4.0 fusion.18.refs_0_.refs_1_.refs_3_
  99.6 8.2 %attend.4 = (bf16[512,768]{1,0:T(8,128)(2,1)S(1)}, f32[6,2,512]{2,1,0:T(2,128)S(1)}) custom-call(bf16[512,2304]{1,0:T(8,128)(2,1)S(1)} %fusion.18.refs_0_.refs_1_.refs_3_, bf16[512,2304]{1,0:T(8,128)(2,1)S(1)} %fusion.18.refs_0_.refs_1_.refs_3_, bf16[512,1536]{1,0:T(8,128)(2,1)S(1)} %collective-permute-done.17.refs_2_.refs_4_, ...), custom_call_target="tpu_custom_call" | custom-call | flops 3221225472 | bytes 3145728 | tf_op jit(solution)/shard_map/attend/pallas_call | solution.py:485
  122.0 8.1 %attend.5 = (bf16[512,768]{1,0:T(8,128)(2,1)S(1)}, f32[6,2,512]{2,1,0:T(2,128)S(1)}) custom-call(bf16[512,2304]{1,0:T(8,128)(2,1)S(1)} %fusion.18.refs_0_.refs_1_.refs_3_, bf16[512,2304]{1,0:T(8,128)(2,1)S(1)} %fusion.18.refs_0_.refs_1_.refs_3_, bf16[512,1536]{1,0:T(8,128)(2,1)S(1)} %copy-done.16, ...), custom_call_target="tpu_custom_call", output_to_operand_aliasing={{0}: (7, {}), {1}: (8, {})} | custom-call | flops 3221225472 | bytes 3145728 | tf_op jit(solution)/shard_map/attend/pallas_call | solution.py:485
  151.8 5.8 multiply_convert_fusion.1
  157.6 2.7 fusion.162
  164.0 4.1 collective-permute-start.33
  178.8 7.3 %collective-permute-done.33 = bf16[256,1536]{1,0:T(8,128)(2,1)} collective-permute-done((bf16[256,1536]{1,0:T(8,128)(2,1)}, bf16[256,1536]{1,0:T(8,128)(2,1)}, u32[]{:S(2)}, u32[]{:S(2)}) %collective-permute-start.33) | collective-permute-done | bytes 786464 | tf_op jit(solution)/shard_map/ppermute | solution.py:271
  186.0 3.5 select_bitcast_fusion.7
  189.6 2.5 collective-permute-start.37
  200.2 15.8 %collective-permute-start.38 = (bf16[512,1536]{1,0:T(8,128)(2,1)S(1)}, bf16[512,1536]{1,0:T(8,128)(2,1)S(1)}, u32[]{:S(2)}, u32[]{:S(2)}) collective-permute-start(bf16[512,1536]{1,0:T(8,128)(2,1)S(1)} %slice.309), channel_id=1, source_target_pairs={{0,4},{1,5},{2,6},{3,7},{4,0},{5,1},{6,2},{7,3},{8,12},{9,13},{10,... | collective-permute-start | bytes 4718600 | tf_op jit(solution)/shard_map/ppermute | solution.py:311
  219.1 8.2 %attend.6 = (bf16[512,768]{1,0:T(8,128)(2,1)S(1)}, f32[6,2,512]{2,1,0:T(2,128)S(1)}) custom-call(bf16[512,2304]{1,0:T(8,128)(2,1)S(1)} %fusion.19.refs_0_.refs_1_.refs_3_, bf16[512,2304]{1,0:T(8,128)(2,1)S(1)} %fusion.19.refs_0_.refs_1_.refs_3_, bf16[512,1536]{1,0:T(8,128)(2,1)S(1)} %collective-permute-done.38.refs_2_.refs_4_, ...), custom_call_target="tpu_custom_call" | custom-call | flops 3221225472 | bytes 3145728 | tf_op jit(solution)/shard_map/attend/pallas_call | solution.py:485
  227.9 8.3 %attend.7 = (bf16[512,768]{1,0:T(8,128)(2,1)S(1)}, f32[6,2,512]{2,1,0:T(2,128)S(1)}) custom-call(bf16[512,2304]{1,0:T(8,128)(2,1)S(1)} %fusion.19.refs_0_.refs_1_.refs_3_, bf16[512,2304]{1,0:T(8,128)(2,1)S(1)} %fusion.19.refs_0_.refs_1_.refs_3_, ...), custom_call_target="tpu_custom_call", output_to_operand_aliasing={{0}: (7, {}), {1}: (8, {})} | custom-call | flops 3221225472 | bytes 3145728 | tf_op jit(solution)/shard_map/attend/pallas_call | solution.py:485
  236.2 7.9 %collective-permute-done.41 = bf16[2,384,768]{2,1,0:T(8,128)(2,1)S(1)} collective-permute-done((bf16[2,384,768]{2,1,0:T(8,128)(2,1)S(1)}, bf16[2,384,768]{2,1,0:T(8,128)(2,1)S(1)}, u32[]{:S(2)}, u32[]{:S(2)}) %collective-permute-start.41) | collective-permute-done | bytes 1179680 | tf_op jit(solution)/shard_map/ppermute | solution.py:144
  259.4 2.7 select_bitcast_fusion.3
  262.8 2.7 select_bitcast_fusion.5
  266.3 3.2 multiply_convert_fusion
  269.6 2.7 fusion.164
  274.6 3.1 convolution_convert_fusion.5
  280.6 4.6 fusion.165
  285.3 4.5 convolution_convert_fusion.4
  291.0 7.5 %collective-permute-start.47 = (bf16[256,1536]{1,0:T(8,128)(2,1)}, bf16[256,1536]{1,0:T(8,128)(2,1)}, u32[]{:S(2)}, u32[]{:S(2)}) collective-permute-start(bf16[256,1536]{1,0:T(8,128)(2,1)} %get-tuple-element.412), channel_id=1, source_target_pairs={{0,0},{1,1},{4,2},{5,3},{2,4},{3,5},{6,6},{7,7},{8,8},{9,9},{12,10... | collective-permute-start | bytes 2359304 | tf_op jit(solution)/shard_map/ppermute | solution.py:289
  305.7 3.3 dynamic-slice_bitcast_fusion.4
  314.7 5.8 multiply_reduce_fusion
  327.0 3.4 fusion.16
  332.1 12.6 %attend_back.4 = (bf16[512,768]{1,0:T(8,128)(2,1)S(1)}, f32[2,512,768]{2,1,0:T(8,128)S(1)}, bf16[2,512,768]{2,1,0:T(8,128)(2,1)}) custom-call(bf16[512,2304]{1,0:T(8,128)(2,1)S(1)} %copy-done.7, bf16[512,2304]{1,0:T(8,128)(2,1)S(1)} %copy-done.7, bf16[512,1536]{1,0:T(8,128)(2,1)S(1)} %copy-done.19, bf16[512,2304]{1,0:T(8,128)(2,1)S(1)} %copy-done.7, ...), custom_call_target="tpu_custom_call" | custom-call | flops 8053063680 | bytes 7864320 | tf_op jit(solution)/shard_map/attend_back/pallas_call | solution.py:527
  344.6 12.2 %attend_back.5 = (bf16[512,768]{1,0:T(8,128)(2,1)S(1)}, f32[2,512,768]{2,1,0:T(8,128)S(1)}, bf16[2,512,768]{2,1,0:T(8,128)(2,1)}) custom-call(bf16[512,2304]{1,0:T(8,128)(2,1)S(1)} %copy-done.7, bf16[512,2304]{1,0:T(8,128)(2,1)S(1)} %copy-done.7, bf16[512,1536]{1,0:T(8,128)(2,1)S(1)} %copy-done.19, ...), custom_call_target="tpu_custom_call", output_to_operand_aliasing={{0}: (9, {}), {1}: (10, {}), {2}: (11, {})} | custom-call | flops 8053063680 | bytes 7864320 | tf_op jit(solution)/shard_map/attend_back/pallas_call | solution.py:527
  361.1 4.6 collective-permute-start.53
  365.8 4.8 collective-permute-start.54
  381.4 3.9 convolution_convert_fusion.3
  387.1 4.0 collective-permute-done.56
  399.5 4.7 fusion.40
  407.7 4.9 collective-permute-done.57
  412.6 2.6 fusion.15
  422.0 2.9 convolution_convert_fusion.2
  429.7 4.6 fusion.166
  434.4 4.4 convolution_convert_fusion.1
  439.7 4.9 collective-permute-start.68
  445.0 4.6 collective-permute-start.69
  451.1 3.2 fusion.14
  460.3 3.2 multiply_reduce_fusion.2
  475.0 12.2 %attend_back.6 = (bf16[512,768]{1,0:T(8,128)(2,1)S(1)}, f32[2,512,768]{2,1,0:T(8,128)S(1)}, bf16[2,512,768]{2,1,0:T(8,128)(2,1)}) custom-call(bf16[512,2304]{1,0:T(8,128)(2,1)S(1)} %copy-done.5, bf16[512,2304]{1,0:T(8,128)(2,1)S(1)} %copy-done.5, bf16[512,1536]{1,0:T(8,128)(2,1)S(1)} %copy-done.17, bf16[512,2304]{1,0:T(8,128)(2,1)S(1)} %copy-done.5, ...), custom_call_target="tpu_custom_call" | custom-call | flops 8053063680 | bytes 7864320 | tf_op jit(solution)/shard_map/attend_back/pallas_call | solution.py:527
  490.7 2.4 collective-permute-start.71
  493.1 3.3 fusion.13
  498.9 12.2 %attend_back.7 = (bf16[512,768]{1,0:T(8,128)(2,1)S(1)}, f32[2,512,768]{2,1,0:T(8,128)S(1)}, bf16[2,512,768]{2,1,0:T(8,128)(2,1)}) custom-call(bf16[512,2304]{1,0:T(8,128)(2,1)S(1)} %copy-done.5, bf16[512,2304]{1,0:T(8,128)(2,1)S(1)} %copy-done.5, bf16[512,1536]{1,0:T(8,128)(2,1)S(1)} %copy-done.17, ...), custom_call_target="tpu_custom_call", output_to_operand_aliasing={{0}: (9, {}), {1}: (10, {}), {2}: (11, {})} | custom-call | flops 8053063680 | bytes 7864320 | tf_op jit(solution)/shard_map/attend_back/pallas_call | solution.py:527
  519.1 8.4 %collective-permute-done.70 = bf16[2,96,3072]{2,1,0:T(8,128)(2,1)} collective-permute-done((bf16[2,96,3072]{2,1,0:T(8,128)(2,1)}, bf16[2,96,3072]{2,1,0:T(8,128)(2,1)}, u32[]{:S(2)}, u32[]{:S(2)}) %collective-permute-start.70) | collective-permute-done | bytes 1179680 | tf_op jit(solution)/shard_map/ppermute | solution.py:144
  550.2 3.7 collective-permute-start.78
  556.9 2.5 collective-permute-start.76
  559.4 4.7 fusion.37
  564.2 8.2 %collective-permute-done.76 = bf16[2,24,6144]{2,1,0:T(8,128)(2,1)S(1)} collective-permute-done((bf16[2,24,6144]{2,1,0:T(8,128)(2,1)S(1)}, bf16[2,24,6144]{2,1,0:T(8,128)(2,1)S(1)}, u32[]{:S(2)}, u32[]{:S(2)}) %collective-permute-start.76) | collective-permute-done | bytes 589856 | tf_op jit(solution)/shard_map/ppermute | solution.py:180
  578.6 5.9 collective-permute-start.80
  584.6 5.8 collective-permute-done.83
  593.3 15.6 %collective-permute-start.84 = (bf16[24,6144]{1,0:T(8,128)(2,1)S(1)}, bf16[24,6144]{1,0:T(8,128)(2,1)S(1)}, u32[]{:S(2)}, u32[]{:S(2)}) collective-permute-start(bf16[24,6144]{1,0:T(8,128)(2,1)S(1)} %dynamic-slice_bitcast_fusion.33), channel_id=1, source_target_pairs={{0,1},{1,0},{2,3},{3,2},{4,5},{5,4},{6,7},{7,6},{8,9},{9,8},{10,11... | collective-permute-start | bytes 884744 | tf_op jit(solution)/shard_map/ppermute | solution.py:142
  609.1 8.2 %collective-permute-start.87 = (bf16[2,24,3200]{2,1,0:T(8,128)(2,1)S(1)}, bf16[2,24,3200]{2,1,0:T(8,128)(2,1)S(1)}, u32[]{:S(2)}, u32[]{:S(2)}) collective-permute-start(bf16[2,24,3200]{2,1,0:T(8,128)(2,1)S(1)} %dynamic-slice_bitcast_fusion.30), channel_id=1, source_target_pairs={{0,1},{3,2},{4,5},{7,6},{8,9},{11,10},{12,13},{15,14},{16,17},{19,... | collective-permute-start | bytes 921608 | tf_op jit(solution)/shard_map/ppermute | solution.py:180
  617.4 4.3 collective-permute-done.87
  624.0 9.8 %collective-permute-start.89 = (bf16[24,3200]{1,0:T(8,128)(2,1)S(1)}, bf16[24,3200]{1,0:T(8,128)(2,1)S(1)}, u32[]{:S(2)}, u32[]{:S(2)}) collective-permute-start(bf16[24,3200]{1,0:T(8,128)(2,1)S(1)} %dynamic-slice_bitcast_fusion.38), channel_id=1, source_target_pairs={{0,1},{1,0},{2,3},{3,2},{4,5},{5,4},{6,7},{7,6},{8,9},{9,8},{10,11... | collective-permute-start | bytes 460808 | tf_op jit(solution)/shard_map/ppermute | solution.py:142
  (748 shorter events, 276.6 us)
Async XLA Ops:
  24.3 15.1 %collective-permute-start = (s32[2,8]{1,0:T(2,128)S(1)}, s32[2,8]{1,0:T(2,128)S(1)}, u32[]{:S(2)}, u32[]{:S(2)}) collective-permute-start(s32[2,8]{1,0:T(2,128)S(1)} %copy-done.115), channel_id=1, source_target_pairs={{0,4},{4,0},{8,12},{12,8},{16,20},{20,16},{24,28},{28,24},{1,5},{5... | collective-permute-start | bytes 200 | tf_op jit(solution)/shard_map/ppermute | solution.py:144
  39.5 20.9 %collective-permute-start.10 = (bf16[2,24,6144]{2,1,0:T(8,128)(2,1)}, bf16[2,24,6144]{2,1,0:T(8,128)(2,1)}, u32[]{:S(2)}, u32[]{:S(2)}) collective-permute-start(bf16[2,24,6144]{2,1,0:T(8,128)(2,1)} %collective-permute-done.5), channel_id=1, source_target_pairs={{1,0},{2,3},{5,4},{6,7},{9,8},{10,11},{13,12},{14,15},{17,16},{18,... | collective-permute-start | bytes 1769480 | tf_op jit(solution)/shard_map/ppermute | solution.py:170
  46.9 14.6 %collective-permute-start.8 = (bf16[2,48,3200]{2,1,0:T(8,128)(2,1)S(1)}, bf16[2,48,3200]{2,1,0:T(8,128)(2,1)}, u32[]{:S(2)}, u32[]{:S(2)}) collective-permute-start(bf16[2,48,3200]{2,1,0:T(8,128)(2,1)S(1)} %pad_maximum_fusion.32), channel_id=1, source_target_pairs={{0,8},{4,12},{8,0},{12,4},{16,24},{20,28},{24,16},{28,20},{1,9},{5... | collective-permute-start | bytes 1843208 | tf_op jit(solution)/shard_map/ppermute | solution.py:144
  48.6 14.3 %collective-permute-start.9 = (bf16[2,48,3200]{2,1,0:T(8,128)(2,1)S(1)}, bf16[2,48,3200]{2,1,0:T(8,128)(2,1)S(1)}, u32[]{:S(2)}, u32[]{:S(2)}) collective-permute-start(bf16[2,48,3200]{2,1,0:T(8,128)(2,1)S(1)} %pad_maximum_fusion.33), channel_id=1, source_target_pairs={{0,16},{4,20},{8,24},{12,28},{16,0},{20,4},{24,8},{28,12},{1,17},{... | collective-permute-start | bytes 1843208 | tf_op jit(solution)/shard_map/ppermute | solution.py:144
  52.9 19.2 %collective-permute-start.12 = (bf16[256,768]{1,0:T(8,128)(2,1)}, bf16[256,768]{1,0:T(8,128)(2,1)}, u32[]{:S(2)}, u32[]{:S(2)}) collective-permute-start(bf16[256,768]{1,0:T(8,128)(2,1)} %get-tuple-element.455), channel_id=1, source_target_pairs={{0,0},{1,1},{2,4},{3,5},{4,2},{5,3},{6,6},{7,7},{8,8},{9,9},{10,12... | collective-permute-start | bytes 1179656 | tf_op jit(solution)/shard_map/ppermute | solution.py:271
  57.4 16.1 %collective-permute-start.13 = (bf16[256,768]{1,0:T(8,128)(2,1)}, bf16[256,768]{1,0:T(8,128)(2,1)}, u32[]{:S(2)}, u32[]{:S(2)}) collective-permute-start(bf16[256,768]{1,0:T(8,128)(2,1)} %get-tuple-element.454), channel_id=1, source_target_pairs={{0,1},{1,0},{2,5},{3,4},{4,3},{5,2},{6,7},{7,6},{8,9},{9,8},{10,13... | collective-permute-start | bytes 1179656 | tf_op jit(solution)/shard_map/ppermute | solution.py:271
  71.0 15.9 %collective-permute-start.15 = (bf16[384,768]{1,0:T(8,128)(2,1)S(1)}, bf16[384,768]{1,0:T(8,128)(2,1)}, u32[]{:S(2)}, u32[]{:S(2)}) collective-permute-start(bf16[384,768]{1,0:T(8,128)(2,1)S(1)} %reshape.523), channel_id=1, source_target_pairs={{0,8},{4,12},{8,0},{12,4},{16,24},{20,28},{24,16},{28,20},{1,9},{5... | collective-permute-start | bytes 1769480 | tf_op jit(solution)/shard_map/ppermute | solution.py:144
  71.5 15.8 %collective-permute-start.14 = (bf16[96,3072]{1,0:T(8,128)(2,1)}, bf16[96,3072]{1,0:T(8,128)(2,1)}, u32[]{:S(2)}, u32[]{:S(2)}) collective-permute-start(bf16[96,3072]{1,0:T(8,128)(2,1)} %get-tuple-element.434), channel_id=1, source_target_pairs={{0,16},{4,20},{8,24},{12,28},{16,0},{20,4},{24,8},{28,12},{1,17},{... | collective-permute-start | bytes 1769480 | tf_op jit(solution)/shard_map/ppermute | solution.py:144
  89.0 18.8 %collective-permute-start.19 = (bf16[24,6144]{1,0:T(8,128)(2,1)}, bf16[24,6144]{1,0:T(8,128)(2,1)S(1)}, u32[]{:S(2)}, u32[]{:S(2)}) collective-permute-start(bf16[24,6144]{1,0:T(8,128)(2,1)} %constant_dynamic-update-slice_fusion.7), channel_id=1, source_target_pairs={{0,1},{1,0},{2,3},{3,2},{4,5},{5,4},{6,7},{7,6},{8,9},{9,8},{10,11... | collective-permute-start | bytes 884744 | tf_op jit(solution)/shard_map/ppermute | solution.py:142
  92.4 15.4 %collective-permute-start.18 = (bf16[2,24,3072]{2,1,0:T(8,128)(2,1)S(1)}, bf16[2,24,3072]{2,1,0:T(8,128)(2,1)S(1)}, u32[]{:S(2)}, u32[]{:S(2)}) collective-permute-start(bf16[2,24,3072]{2,1,0:T(8,128)(2,1)S(1)} %pad_maximum_fusion.43), channel_id=1, source_target_pairs={{1,2},{2,1},{5,6},{6,5},{9,10},{10,9},{13,14},{14,13},{17,18},{18,... | collective-permute-start | bytes 884744 | tf_op jit(solution)/shard_map/ppermute | solution.py:169
  95.6 34.5 %collective-permute-start.21 = (bf16[2,384,768]{2,1,0:T(8,128)(2,1)}, bf16[2,384,768]{2,1,0:T(8,128)(2,1)}, u32[]{:S(2)}, u32[]{:S(2)}) collective-permute-start(bf16[2,384,768]{2,1,0:T(8,128)(2,1)} %pad_maximum_fusion.22), channel_id=1, source_target_pairs={{0,16},{4,20},{8,24},{12,28},{16,0},{20,4},{24,8},{28,12},{1,17},{... | collective-permute-start | bytes 3538952 | tf_op jit(solution)/shard_map/ppermute | solution.py:144
  99.4 30.8 %collective-permute-start.20 = (bf16[2,96,3072]{2,1,0:T(8,128)(2,1)}, bf16[2,96,3072]{2,1,0:T(8,128)(2,1)}, u32[]{:S(2)}, u32[]{:S(2)}) collective-permute-start(bf16[2,96,3072]{2,1,0:T(8,128)(2,1)} %pad_maximum_fusion.21), channel_id=1, source_target_pairs={{0,8},{4,12},{8,0},{12,4},{16,24},{20,28},{24,16},{28,20},{1,9},{5... | collective-permute-start | bytes 3538952 | tf_op jit(solution)/shard_map/ppermute | solution.py:144
  109.8 22.3 %collective-permute-start.23 = (bf16[2,24,6144]{2,1,0:T(8,128)(2,1)}, bf16[2,24,6144]{2,1,0:T(8,128)(2,1)}, u32[]{:S(2)}, u32[]{:S(2)}) collective-permute-start(bf16[2,24,6144]{2,1,0:T(8,128)(2,1)} %pad_maximum_fusion.36), channel_id=1, source_target_pairs={{1,2},{2,1},{5,6},{6,5},{9,10},{10,9},{13,14},{14,13},{17,18},{18,... | collective-permute-start | bytes 1769480 | tf_op jit(solution)/shard_map/ppermute | solution.py:169
  139.5 29.5 %collective-permute-start.30 = (bf16[2,24,6144]{2,1,0:T(8,128)(2,1)}, bf16[2,24,6144]{2,1,0:T(8,128)(2,1)S(1)}, u32[]{:S(2)}, u32[]{:S(2)}) collective-permute-start(bf16[2,24,6144]{2,1,0:T(8,128)(2,1)} %collective-permute-done.23), channel_id=1, source_target_pairs={{1,0},{2,3},{5,4},{6,7},{9,8},{10,11},{13,12},{14,15},{17,16},{18,... | collective-permute-start | bytes 1769480 | tf_op jit(solution)/shard_map/ppermute | solution.py:170
  147.3 21.8 %collective-permute-start.29 = (bf16[2,48,3072]{2,1,0:T(8,128)(2,1)S(1)}, bf16[2,48,3072]{2,1,0:T(8,128)(2,1)S(1)}, u32[]{:S(2)}, u32[]{:S(2)}) collective-permute-start(bf16[2,48,3072]{2,1,0:T(8,128)(2,1)S(1)} %pad_maximum_fusion.39), channel_id=1, source_target_pairs={{0,16},{4,20},{8,24},{12,28},{16,0},{20,4},{24,8},{28,12},{1,17},{... | collective-permute-start | bytes 1769480 | tf_op jit(solution)/shard_map/ppermute | solution.py:144
  148.7 20.4 %collective-permute-start.28 = (bf16[2,48,3072]{2,1,0:T(8,128)(2,1)S(1)}, bf16[2,48,3072]{2,1,0:T(8,128)(2,1)S(1)}, u32[]{:S(2)}, u32[]{:S(2)}) collective-permute-start(bf16[2,48,3072]{2,1,0:T(8,128)(2,1)S(1)} %pad_maximum_fusion.38), channel_id=1, source_target_pairs={{0,8},{4,12},{8,0},{12,4},{16,24},{20,28},{24,16},{28,20},{1,9},{5... | collective-permute-start | bytes 1769480 | tf_op jit(solution)/shard_map/ppermute | solution.py:144
  161.8 17.0 %collective-permute-start.32 = (bf16[256,1536]{1,0:T(8,128)(2,1)}, bf16[256,1536]{1,0:T(8,128)(2,1)S(1)}, u32[]{:S(2)}, u32[]{:S(2)}) collective-permute-start(bf16[256,1536]{1,0:T(8,128)(2,1)} %get-tuple-element.418), channel_id=1, source_target_pairs={{0,0},{1,1},{2,4},{3,5},{4,2},{5,3},{6,6},{7,7},{8,8},{9,9},{10,12... | collective-permute-start | bytes 2359304 | tf_op jit(solution)/shard_map/ppermute | solution.py:271
  164.0 22.1 %collective-permute-start.33 = (bf16[256,1536]{1,0:T(8,128)(2,1)}, bf16[256,1536]{1,0:T(8,128)(2,1)}, u32[]{:S(2)}, u32[]{:S(2)}) collective-permute-start(bf16[256,1536]{1,0:T(8,128)(2,1)} %get-tuple-element.417), channel_id=1, source_target_pairs={{0,1},{1,0},{2,5},{3,4},{4,3},{5,2},{6,7},{7,6},{8,9},{9,8},{10,13... | collective-permute-start | bytes 2359304 | tf_op jit(solution)/shard_map/ppermute | solution.py:271
  172.1 14.0 %collective-permute-start.31 = (bf16[2,2,96,3072]{3,2,1,0:T(8,128)(2,1)}, bf16[2,2,96,3072]{3,2,1,0:T(8,128)(2,1)}, u32[]{:S(2)}, u32[]{:S(2)}) collective-permute-start(bf16[2,2,96,3072]{3,2,1,0:T(8,128)(2,1)} %pad_maximum_fusion.11), channel_id=1, source_target_pairs={{0,4},{4,0},{8,12},{12,8},{16,20},{20,16},{24,28},{28,24},{1,5},{5... | collective-permute-start | bytes 7077896 | tf_op jit(solution)/shard_map/ppermute | solution.py:144
  177.7 20.8 %collective-permute-start.36 = (bf16[384,768]{1,0:T(8,128)(2,1)}, bf16[384,768]{1,0:T(8,128)(2,1)S(1)}, u32[]{:S(2)}, u32[]{:S(2)}) collective-permute-start(bf16[384,768]{1,0:T(8,128)(2,1)} %reshape.529), channel_id=1, source_target_pairs={{0,8},{4,12},{8,0},{12,4},{16,24},{20,28},{24,16},{28,20},{1,9},{5... | collective-permute-start | bytes 1769480 | tf_op jit(solution)/shard_map/ppermute | solution.py:144
  178.2 20.2 %collective-permute-start.35 = (bf16[96,3072]{1,0:T(8,128)(2,1)}, bf16[96,3072]{1,0:T(8,128)(2,1)S(1)}, u32[]{:S(2)}, u32[]{:S(2)}) collective-permute-start(bf16[96,3072]{1,0:T(8,128)(2,1)} %get-tuple-element.426), channel_id=1, source_target_pairs={{0,16},{4,20},{8,24},{12,28},{16,0},{20,4},{24,8},{28,12},{1,17},{... | collective-permute-start | bytes 1769480 | tf_op jit(solution)/shard_map/ppermute | solution.py:144
  200.2 18.9 %collective-permute-start.38 = (bf16[512,1536]{1,0:T(8,128)(2,1)S(1)}, bf16[512,1536]{1,0:T(8,128)(2,1)S(1)}, u32[]{:S(2)}, u32[]{:S(2)}) collective-permute-start(bf16[512,1536]{1,0:T(8,128)(2,1)S(1)} %slice.309), channel_id=1, source_target_pairs={{0,4},{1,5},{2,6},{3,7},{4,0},{5,1},{6,2},{7,3},{8,12},{9,13},{10,... | collective-permute-start | bytes 4718600 | tf_op jit(solution)/shard_map/ppermute | solution.py:311
  216.2 28.0 %collective-permute-start.41 = (bf16[2,384,768]{2,1,0:T(8,128)(2,1)S(1)}, bf16[2,384,768]{2,1,0:T(8,128)(2,1)S(1)}, u32[]{:S(2)}, u32[]{:S(2)}) collective-permute-start(bf16[2,384,768]{2,1,0:T(8,128)(2,1)S(1)} %pad_maximum_fusion.27), channel_id=1, source_target_pairs={{0,16},{4,20},{8,24},{12,28},{16,0},{20,4},{24,8},{28,12},{1,17},{... | collective-permute-start | bytes 3538952 | tf_op jit(solution)/shard_map/ppermute | solution.py:144
  217.0 28.8 %collective-permute-start.40 = (bf16[2,96,3072]{2,1,0:T(8,128)(2,1)S(1)}, bf16[2,96,3072]{2,1,0:T(8,128)(2,1)S(1)}, u32[]{:S(2)}, u32[]{:S(2)}) collective-permute-start(bf16[2,96,3072]{2,1,0:T(8,128)(2,1)S(1)} %pad_maximum_fusion.26), channel_id=1, source_target_pairs={{0,8},{4,12},{8,0},{12,4},{16,24},{20,28},{24,16},{28,20},{1,9},{5... | collective-permute-start | bytes 3538952 | tf_op jit(solution)/shard_map/ppermute | solution.py:144
  227.3 20.2 %collective-permute-start.42 = (f32[2,2,1,8,768]{4,3,1,0,2:T(8,128)S(1)}, f32[2,2,1,8,768]{4,3,1,0,2:T(8,128)S(1)}, u32[]{:S(2)}, u32[]{:S(2)}) collective-permute-start(f32[2,2,1,8,768]{4,3,1,0,2:T(8,128)S(1)} %bitcast.594), channel_id=1, source_target_pairs={{0,8},{4,12},{8,0},{12,4},{16,24},{20,28},{24,16},{28,20},{1,9},{5... | collective-permute-start | bytes 294920 | tf_op jit(solution)/shard_map/ppermute | solution.py:144
  280.6 25.0 %collective-permute-start.46 = (bf16[2,2,384,768]{3,2,1,0:T(8,128)(2,1)}, bf16[2,2,384,768]{3,2,1,0:T(8,128)(2,1)}, u32[]{:S(2)}, u32[]{:S(2)}) collective-permute-start(bf16[2,2,384,768]{3,2,1,0:T(8,128)(2,1)} %dynamic-slice_bitcast_fusion.5), channel_id=1, source_target_pairs={{0,4},{4,0},{8,12},{12,8},{16,20},{20,16},{24,28},{28,24},{1,5},{5... | collective-permute-start | bytes 7077896 | tf_op jit(solution)/shard_map/ppermute | solution.py:144
  291.0 34.3 %collective-permute-start.47 = (bf16[256,1536]{1,0:T(8,128)(2,1)}, bf16[256,1536]{1,0:T(8,128)(2,1)}, u32[]{:S(2)}, u32[]{:S(2)}) collective-permute-start(bf16[256,1536]{1,0:T(8,128)(2,1)} %get-tuple-element.412), channel_id=1, source_target_pairs={{0,0},{1,1},{4,2},{5,3},{2,4},{3,5},{6,6},{7,7},{8,8},{9,9},{12,10... | collective-permute-start | bytes 2359304 | tf_op jit(solution)/shard_map/ppermute | solution.py:289
  298.6 28.4 %collective-permute-start.48 = (bf16[256,1536]{1,0:T(8,128)(2,1)}, bf16[256,1536]{1,0:T(8,128)(2,1)}, u32[]{:S(2)}, u32[]{:S(2)}) collective-permute-start(bf16[256,1536]{1,0:T(8,128)(2,1)} %get-tuple-element.411), channel_id=1, source_target_pairs={{1,0},{0,1},{5,2},{4,3},{3,4},{2,5},{7,6},{6,7},{9,8},{8,9},{13,10... | collective-permute-start | bytes 2359304 | tf_op jit(solution)/shard_map/ppermute | solution.py:289
  309.0 17.9 %collective-permute-start.49 = (bf16[2,2,96,3072]{3,2,1,0:T(8,128)(2,1)}, bf16[2,2,96,3072]{3,2,1,0:T(8,128)(2,1)}, u32[]{:S(2)}, u32[]{:S(2)}) collective-permute-start(bf16[2,2,96,3072]{3,2,1,0:T(8,128)(2,1)} %dynamic-slice_bitcast_fusion.4), channel_id=1, source_target_pairs={{0,4},{4,0},{8,12},{12,8},{16,20},{20,16},{24,28},{28,24},{1,5},{5... | collective-permute-start | bytes 7077896 | tf_op jit(solution)/shard_map/ppermute | solution.py:144
  314.0 30.6 %collective-permute-start.50 = (bf16[2,384,768]{2,1,0:T(8,128)(2,1)}, bf16[2,384,768]{2,1,0:T(8,128)(2,1)}, u32[]{:S(2)}, u32[]{:S(2)}) collective-permute-start(bf16[2,384,768]{2,1,0:T(8,128)(2,1)} %dynamic-slice_bitcast_fusion.9), channel_id=1, source_target_pairs={{0,16},{4,20},{8,24},{12,28},{16,0},{20,4},{24,8},{28,12},{1,17},{... | collective-permute-start | bytes 3538952 | tf_op jit(solution)/shard_map/ppermute | solution.py:144
  330.5 43.2 %collective-permute-start.51 = (bf16[2,96,3072]{2,1,0:T(8,128)(2,1)S(1)}, bf16[2,96,3072]{2,1,0:T(8,128)(2,1)S(1)}, u32[]{:S(2)}, u32[]{:S(2)}) collective-permute-start(bf16[2,96,3072]{2,1,0:T(8,128)(2,1)S(1)} %dynamic-slice_bitcast_fusion.8), channel_id=1, source_target_pairs={{0,8},{4,12},{8,0},{12,4},{16,24},{20,28},{24,16},{28,20},{1,9},{5... | collective-permute-start | bytes 3538952 | tf_op jit(solution)/shard_map/ppermute | solution.py:144
  356.8 21.3 %collective-permute-start.52 = (bf16[2,512,768]{2,1,0:T(8,128)(2,1)}, bf16[2,512,768]{2,1,0:T(8,128)(2,1)}, u32[]{:S(2)}, u32[]{:S(2)}) collective-permute-start(bf16[2,512,768]{2,1,0:T(8,128)(2,1)} %get-tuple-element.275), channel_id=1, source_target_pairs={{0,4},{1,5},{2,6},{3,7},{4,0},{5,1},{6,2},{7,3},{8,12},{9,13},{10,... | collective-permute-start | bytes 4718600 | tf_op jit(solution)/shard_map/ppermute | solution.py:311
  359.6 27.5 %collective-permute-start.55 = (bf16[384,768]{1,0:T(8,128)(2,1)}, bf16[384,768]{1,0:T(8,128)(2,1)}, u32[]{:S(2)}, u32[]{:S(2)}) collective-permute-start(bf16[384,768]{1,0:T(8,128)(2,1)} %dynamic-slice_bitcast_fusion.21), channel_id=1, source_target_pairs={{0,8},{4,12},{8,0},{12,4},{16,24},{20,28},{24,16},{28,20},{1,9},{5... | collective-permute-start | bytes 1769480 | tf_op jit(solution)/shard_map/ppermute | solution.py:144
  361.1 25.9 %collective-permute-start.53 = (bf16[256,768]{1,0:T(8,128)(2,1)}, bf16[256,768]{1,0:T(8,128)(2,1)}, u32[]{:S(2)}, u32[]{:S(2)}) collective-permute-start(bf16[256,768]{1,0:T(8,128)(2,1)} %get-tuple-element.451), channel_id=1, source_target_pairs={{0,0},{1,1},{2,4},{3,5},{4,2},{5,3},{6,6},{7,7},{8,8},{9,9},{10,12... | collective-permute-start | bytes 1179656 | tf_op jit(solution)/shard_map/ppermute | solution.py:271
  365.8 21.3 %collective-permute-start.54 = (bf16[256,768]{1,0:T(8,128)(2,1)}, bf16[256,768]{1,0:T(8,128)(2,1)}, u32[]{:S(2)}, u32[]{:S(2)}) collective-permute-start(bf16[256,768]{1,0:T(8,128)(2,1)} %get-tuple-element.450), channel_id=1, source_target_pairs={{0,1},{1,0},{2,5},{3,4},{4,3},{5,2},{6,7},{7,6},{8,9},{9,8},{10,13... | collective-permute-start | bytes 1179656 | tf_op jit(solution)/shard_map/ppermute | solution.py:271
  376.0 15.1 %collective-permute-start.56 = (bf16[96,3072]{1,0:T(8,128)(2,1)}, bf16[96,3072]{1,0:T(8,128)(2,1)}, u32[]{:S(2)}, u32[]{:S(2)}) collective-permute-start(bf16[96,3072]{1,0:T(8,128)(2,1)} %dynamic-slice_bitcast_fusion.20), channel_id=1, source_target_pairs={{0,16},{4,20},{8,24},{12,28},{16,0},{20,4},{24,8},{28,12},{1,17},{... | collective-permute-start | bytes 1769480 | tf_op jit(solution)/shard_map/ppermute | solution.py:144
  394.6 18.0 %collective-permute-start.58 = (bf16[2,2,2,48,3072]{4,3,2,1,0:T(8,128)(2,1)}, bf16[2,2,2,48,3072]{4,3,2,1,0:T(8,128)(2,1)}, u32[]{:S(2)}, u32[]{:S(2)}) collective-permute-start(bf16[2,2,2,48,3072]{4,3,2,1,0:T(8,128)(2,1)} %dynamic-slice_bitcast_fusion.3), channel_id=1, source_target_pairs={{0,4},{4,0},{8,12},{12,8},{16,20},{20,16},{24,28},{28,24},{1,5},{5... | collective-permute-start | bytes 7077896 | tf_op jit(solution)/shard_map/ppermute | solution.py:144
  397.7 14.9 %collective-permute-start.57 = (bf16[2,24,6144]{2,1,0:T(8,128)(2,1)S(1)}, bf16[2,24,6144]{2,1,0:T(8,128)(2,1)S(1)}, u32[]{:S(2)}, u32[]{:S(2)}) collective-permute-start(bf16[2,24,6144]{2,1,0:T(8,128)(2,1)S(1)} %fusion.76), channel_id=1, source_target_pairs={{0,1},{3,2},{4,5},{7,6},{8,9},{11,10},{12,13},{15,14},{16,17},{19,... | collective-permute-start | bytes 1769480 | tf_op jit(solution)/shard_map/ppermute | solution.py:180
  416.4 28.6 %collective-permute-start.62 = (bf16[2,48,3072]{2,1,0:T(8,128)(2,1)}, bf16[2,48,3072]{2,1,0:T(8,128)(2,1)}, u32[]{:S(2)}, u32[]{:S(2)}) collective-permute-start(bf16[2,48,3072]{2,1,0:T(8,128)(2,1)} %dynamic-slice_bitcast_fusion.18), channel_id=1, source_target_pairs={{0,16},{4,20},{8,24},{12,28},{16,0},{20,4},{24,8},{28,12},{1,17},{... | collective-permute-start | bytes 1769480 | tf_op jit(solution)/shard_map/ppermute | solution.py:144
  418.0 31.6 %collective-permute-start.61 = (bf16[2,48,3072]{2,1,0:T(8,128)(2,1)}, bf16[2,48,3072]{2,1,0:T(8,128)(2,1)}, u32[]{:S(2)}, u32[]{:S(2)}) collective-permute-start(bf16[2,48,3072]{2,1,0:T(8,128)(2,1)} %dynamic-slice_bitcast_fusion.19), channel_id=1, source_target_pairs={{0,8},{4,12},{8,0},{12,4},{16,24},{20,28},{24,16},{28,20},{1,9},{5... | collective-permute-start | bytes 1769480 | tf_op jit(solution)/shard_map/ppermute | solution.py:144
  427.9 21.6 %collective-permute-start.59 = (bf16[2,2,384,768]{3,2,1,0:T(8,128)(2,1)}, bf16[2,2,384,768]{3,2,1,0:T(8,128)(2,1)}, u32[]{:S(2)}, u32[]{:S(2)}) collective-permute-start(bf16[2,2,384,768]{3,2,1,0:T(8,128)(2,1)} %dynamic-slice_bitcast_fusion.2), channel_id=1, source_target_pairs={{0,4},{4,0},{8,12},{12,8},{16,20},{20,16},{24,28},{28,24},{1,5},{5... | collective-permute-start | bytes 7077896 | tf_op jit(solution)/shard_map/ppermute | solution.py:144
  428.9 20.6 %collective-permute-start.60 = (bf16[2,24,6144]{2,1,0:T(8,128)(2,1)}, bf16[2,24,6144]{2,1,0:T(8,128)(2,1)S(1)}, u32[]{:S(2)}, u32[]{:S(2)}) collective-permute-start(bf16[2,24,6144]{2,1,0:T(8,128)(2,1)} %add_convert_fusion.3), channel_id=1, source_target_pairs={{1,2},{2,1},{5,6},{6,5},{9,10},{10,9},{13,14},{14,13},{17,18},{18,... | collective-permute-start | bytes 1769480 | tf_op jit(solution)/shard_map/ppermute | solution.py:182
  439.7 78.0 %collective-permute-start.68 = (bf16[256,768]{1,0:T(8,128)(2,1)}, bf16[256,768]{1,0:T(8,128)(2,1)}, u32[]{:S(2)}, u32[]{:S(2)}) collective-permute-start(bf16[256,768]{1,0:T(8,128)(2,1)} %get-tuple-element.447), channel_id=1, source_target_pairs={{0,0},{1,1},{4,2},{5,3},{2,4},{3,5},{6,6},{7,7},{8,8},{9,9},{12,10... | collective-permute-start | bytes 1179656 | tf_op jit(solution)/shard_map/ppermute | solution.py:289
  445.0 74.1 %collective-permute-start.69 = (bf16[256,768]{1,0:T(8,128)(2,1)}, bf16[256,768]{1,0:T(8,128)(2,1)}, u32[]{:S(2)}, u32[]{:S(2)}) collective-permute-start(bf16[256,768]{1,0:T(8,128)(2,1)} %get-tuple-element.446), channel_id=1, source_target_pairs={{1,0},{0,1},{5,2},{4,3},{3,4},{2,5},{7,6},{6,7},{9,8},{8,9},{13,10... | collective-permute-start | bytes 1179656 | tf_op jit(solution)/shard_map/ppermute | solution.py:289
  455.5 34.2 %collective-permute-start.65 = (bf16[2,384,768]{2,1,0:T(8,128)(2,1)}, bf16[2,384,768]{2,1,0:T(8,128)(2,1)}, u32[]{:S(2)}, u32[]{:S(2)}) collective-permute-start(bf16[2,384,768]{2,1,0:T(8,128)(2,1)} %dynamic-slice_bitcast_fusion.7), channel_id=1, source_target_pairs={{0,16},{4,20},{8,24},{12,28},{16,0},{20,4},{24,8},{28,12},{1,17},{... | collective-permute-start | bytes 3538952 | tf_op jit(solution)/shard_map/ppermute | solution.py:144
  456.6 15.3 %collective-permute-start.64 = (bf16[24,6144]{1,0:T(8,128)(2,1)S(1)}, bf16[24,6144]{1,0:T(8,128)(2,1)S(1)}, u32[]{:S(2)}, u32[]{:S(2)}) collective-permute-start(bf16[24,6144]{1,0:T(8,128)(2,1)S(1)} %dynamic-slice_bitcast_fusion.37), channel_id=1, source_target_pairs={{0,1},{1,0},{2,3},{3,2},{4,5},{5,4},{6,7},{7,6},{8,9},{9,8},{10,11... | collective-permute-start | bytes 884744 | tf_op jit(solution)/shard_map/ppermute | solution.py:142
  458.4 14.2 %collective-permute-start.63 = (bf16[2,2,96,3072]{3,2,1,0:T(8,128)(2,1)}, bf16[2,2,96,3072]{3,2,1,0:T(8,128)(2,1)}, u32[]{:S(2)}, u32[]{:S(2)}) collective-permute-start(bf16[2,2,96,3072]{3,2,1,0:T(8,128)(2,1)} %dynamic-slice_bitcast_fusion.1), channel_id=1, source_target_pairs={{0,4},{4,0},{8,12},{12,8},{16,20},{20,16},{24,28},{28,24},{1,5},{5... | collective-permute-start | bytes 7077896 | tf_op jit(solution)/shard_map/ppermute | solution.py:144
  472.0 15.2 %collective-permute-start.67 = (bf16[48,3072]{1,0:T(8,128)(2,1)}, bf16[48,3072]{1,0:T(8,128)(2,1)S(1)}, u32[]{:S(2)}, u32[]{:S(2)}) collective-permute-start(bf16[48,3072]{1,0:T(8,128)(2,1)} %dynamic-slice_bitcast_fusion.35), channel_id=1, source_target_pairs={{0,8},{4,12},{8,0},{12,4},{16,24},{20,28},{24,16},{28,20},{1,9},{5... | collective-permute-start | bytes 884744 | tf_op jit(solution)/shard_map/ppermute | solution.py:144
  472.6 17.0 %collective-permute-start.66 = (bf16[48,3072]{1,0:T(8,128)(2,1)}, bf16[48,3072]{1,0:T(8,128)(2,1)S(1)}, u32[]{:S(2)}, u32[]{:S(2)}) collective-permute-start(bf16[48,3072]{1,0:T(8,128)(2,1)} %dynamic-slice_bitcast_fusion.36), channel_id=1, source_target_pairs={{0,16},{4,20},{8,24},{12,28},{16,0},{20,4},{24,8},{28,12},{1,17},{... | collective-permute-start | bytes 884744 | tf_op jit(solution)/shard_map/ppermute | solution.py:144
  490.7 28.4 %collective-permute-start.71 = (bf16[2,24,3072]{2,1,0:T(8,128)(2,1)}, bf16[2,24,3072]{2,1,0:T(8,128)(2,1)}, u32[]{:S(2)}, u32[]{:S(2)}) collective-permute-start(bf16[2,24,3072]{2,1,0:T(8,128)(2,1)} %dynamic-slice_bitcast_fusion.34), channel_id=1, source_target_pairs={{0,1},{3,2},{4,5},{7,6},{8,9},{11,10},{12,13},{15,14},{16,17},{19,... | collective-permute-start | bytes 884744 | tf_op jit(solution)/shard_map/ppermute | solution.py:180
  498.3 29.2 %collective-permute-start.70 = (bf16[2,96,3072]{2,1,0:T(8,128)(2,1)}, bf16[2,96,3072]{2,1,0:T(8,128)(2,1)}, u32[]{:S(2)}, u32[]{:S(2)}) collective-permute-start(bf16[2,96,3072]{2,1,0:T(8,128)(2,1)} %dynamic-slice_bitcast_fusion.6), channel_id=1, source_target_pairs={{0,8},{4,12},{8,0},{12,4},{16,24},{20,28},{24,16},{28,20},{1,9},{5... | collective-permute-start | bytes 3538952 | tf_op jit(solution)/shard_map/ppermute | solution.py:144
  512.0 27.0 %collective-permute-start.72 = (bf16[2,512,768]{2,1,0:T(8,128)(2,1)}, bf16[2,512,768]{2,1,0:T(8,128)(2,1)}, u32[]{:S(2)}, u32[]{:S(2)}) collective-permute-start(bf16[2,512,768]{2,1,0:T(8,128)(2,1)} %get-tuple-element.314), channel_id=1, source_target_pairs={{0,4},{1,5},{2,6},{3,7},{4,0},{5,1},{6,2},{7,3},{8,12},{9,13},{10,... | collective-permute-start | bytes 4718600 | tf_op jit(solution)/shard_map/ppermute | solution.py:311
  517.7 27.9 %collective-permute-start.73 = (bf16[384,768]{1,0:T(8,128)(2,1)}, bf16[384,768]{1,0:T(8,128)(2,1)}, u32[]{:S(2)}, u32[]{:S(2)}) collective-permute-start(bf16[384,768]{1,0:T(8,128)(2,1)} %dynamic-slice_bitcast_fusion.17), channel_id=1, source_target_pairs={{0,8},{4,12},{8,0},{12,4},{16,24},{20,28},{24,16},{28,20},{1,9},{5... | collective-permute-start | bytes 1769480 | tf_op jit(solution)/shard_map/ppermute | solution.py:144
  530.7 14.9 %collective-permute-start.75 = (bf16[2,24,3072]{2,1,0:T(8,128)(2,1)}, bf16[2,24,3072]{2,1,0:T(8,128)(2,1)}, u32[]{:S(2)}, u32[]{:S(2)}) collective-permute-start(bf16[2,24,3072]{2,1,0:T(8,128)(2,1)} %add_convert_fusion.5), channel_id=1, source_target_pairs={{1,2},{2,1},{5,6},{6,5},{9,10},{10,9},{13,14},{14,13},{17,18},{18,... | collective-permute-start | bytes 884744 | tf_op jit(solution)/shard_map/ppermute | solution.py:182
  550.2 22.2 %collective-permute-start.77 = (bf16[2,2,2,48,3200]{4,3,2,1,0:T(8,128)(2,1)}, bf16[2,2,2,48,3200]{4,3,2,1,0:T(8,128)(2,1)}, u32[]{:S(2)}, u32[]{:S(2)}) collective-permute-start(bf16[2,2,2,48,3200]{4,3,2,1,0:T(8,128)(2,1)} %dynamic-slice_bitcast_fusion), channel_id=1, source_target_pairs={{0,4},{4,0},{8,12},{12,8},{16,20},{20,16},{24,28},{28,24},{1,5},{5... | collective-permute-start | bytes 7372808 | tf_op jit(solution)/shard_map/ppermute | solution.py:144
  550.2 14.0 %collective-permute-start.78 = (bf16[24,3072]{1,0:T(8,128)(2,1)S(1)}, bf16[24,3072]{1,0:T(8,128)(2,1)S(1)}, u32[]{:S(2)}, u32[]{:S(2)}) collective-permute-start(bf16[24,3072]{1,0:T(8,128)(2,1)S(1)} %dynamic-slice_bitcast_fusion.39), channel_id=1, source_target_pairs={{0,1},{1,0},{2,3},{3,2},{4,5},{5,4},{6,7},{7,6},{8,9},{9,8},{10,11... | collective-permute-start | bytes 442376 | tf_op jit(solution)/shard_map/ppermute | solution.py:142
  556.9 15.5 %collective-permute-start.76 = (bf16[2,24,6144]{2,1,0:T(8,128)(2,1)S(1)}, bf16[2,24,6144]{2,1,0:T(8,128)(2,1)S(1)}, u32[]{:S(2)}, u32[]{:S(2)}) collective-permute-start(bf16[2,24,6144]{2,1,0:T(8,128)(2,1)S(1)} %fusion.72), channel_id=1, source_target_pairs={{0,1},{3,2},{4,5},{7,6},{8,9},{11,10},{12,13},{15,14},{16,17},{19,... | collective-permute-start | bytes 1769480 | tf_op jit(solution)/shard_map/ppermute | solution.py:180
  574.9 15.5 %collective-permute-start.83 = (bf16[2,48,3200]{2,1,0:T(8,128)(2,1)S(1)}, bf16[2,48,3200]{2,1,0:T(8,128)(2,1)S(1)}, u32[]{:S(2)}, u32[]{:S(2)}) collective-permute-start(bf16[2,48,3200]{2,1,0:T(8,128)(2,1)S(1)} %dynamic-slice_bitcast_fusion.14), channel_id=1, source_target_pairs={{0,16},{4,20},{8,24},{12,28},{16,0},{20,4},{24,8},{28,12},{1,17},{... | collective-permute-start | bytes 1843208 | tf_op jit(solution)/shard_map/ppermute | solution.py:144
  576.8 15.2 %collective-permute-start.82 = (bf16[2,48,3200]{2,1,0:T(8,128)(2,1)S(1)}, bf16[2,48,3200]{2,1,0:T(8,128)(2,1)S(1)}, u32[]{:S(2)}, u32[]{:S(2)}) collective-permute-start(bf16[2,48,3200]{2,1,0:T(8,128)(2,1)S(1)} %dynamic-slice_bitcast_fusion.15), channel_id=1, source_target_pairs={{0,8},{4,12},{8,0},{12,4},{16,24},{20,28},{24,16},{28,20},{1,9},{5... | collective-permute-start | bytes 1843208 | tf_op jit(solution)/shard_map/ppermute | solution.py:144
  577.9 39.4 %collective-permute-start.79 = (bf16[256,768]{1,0:T(8,128)(2,1)S(1)}, bf16[256,768]{1,0:T(8,128)(2,1)S(1)}, u32[]{:S(2)}, u32[]{:S(2)}) collective-permute-start(bf16[256,768]{1,0:T(8,128)(2,1)S(1)} %get-tuple-element.444), channel_id=1, source_target_pairs={{0,0},{1,1},{4,2},{5,3},{2,4},{3,5},{6,6},{7,7},{8,8},{9,9},{12,10... | collective-permute-start | bytes 1179656 | tf_op jit(solution)/shard_map/ppermute | solution.py:289
  578.6 38.8 %collective-permute-start.80 = (bf16[256,768]{1,0:T(8,128)(2,1)S(1)}, bf16[256,768]{1,0:T(8,128)(2,1)S(1)}, u32[]{:S(2)}, u32[]{:S(2)}) collective-permute-start(bf16[256,768]{1,0:T(8,128)(2,1)S(1)} %get-tuple-element.443), channel_id=1, source_target_pairs={{1,0},{0,1},{5,2},{4,3},{3,4},{2,5},{7,6},{6,7},{9,8},{8,9},{13,10... | collective-permute-start | bytes 1179656 | tf_op jit(solution)/shard_map/ppermute | solution.py:289
  592.1 16.7 %collective-permute-start.86 = (bf16[48,3200]{1,0:T(8,128)(2,1)S(1)}, bf16[48,3200]{1,0:T(8,128)(2,1)S(1)}, u32[]{:S(2)}, u32[]{:S(2)}) collective-permute-start(bf16[48,3200]{1,0:T(8,128)(2,1)S(1)} %dynamic-slice_bitcast_fusion.31), channel_id=1, source_target_pairs={{0,8},{4,12},{8,0},{12,4},{16,24},{20,28},{24,16},{28,20},{1,9},{5... | collective-permute-start | bytes 921608 | tf_op jit(solution)/shard_map/ppermute | solution.py:144
  592.7 16.1 %collective-permute-start.85 = (bf16[48,3200]{1,0:T(8,128)(2,1)S(1)}, bf16[48,3200]{1,0:T(8,128)(2,1)S(1)}, u32[]{:S(2)}, u32[]{:S(2)}) collective-permute-start(bf16[48,3200]{1,0:T(8,128)(2,1)S(1)} %dynamic-slice_bitcast_fusion.32), channel_id=1, source_target_pairs={{0,16},{4,20},{8,24},{12,28},{16,0},{20,4},{24,8},{28,12},{1,17},{... | collective-permute-start | bytes 921608 | tf_op jit(solution)/shard_map/ppermute | solution.py:144
  593.3 24.1 %collective-permute-start.84 = (bf16[24,6144]{1,0:T(8,128)(2,1)S(1)}, bf16[24,6144]{1,0:T(8,128)(2,1)S(1)}, u32[]{:S(2)}, u32[]{:S(2)}) collective-permute-start(bf16[24,6144]{1,0:T(8,128)(2,1)S(1)} %dynamic-slice_bitcast_fusion.33), channel_id=1, source_target_pairs={{0,1},{1,0},{2,3},{3,2},{4,5},{5,4},{6,7},{7,6},{8,9},{9,8},{10,11... | collective-permute-start | bytes 884744 | tf_op jit(solution)/shard_map/ppermute | solution.py:142
  (160 other events, 1043.7 us)

commit v4 on v3

--- a/solution.py
+++ b/solution.py
@@ -22,9 +22,9 @@
 F32 = jnp.float32
 
 (
-    QKV_1, FFN_1, QKV_2, FFN_2, HIDDEN, SKIP, COTS, CLS, OUTS, SKIP_BACK, HIDDEN_BACK,
+    QKV_1, FFN_1, QKV_2, FFN_2, HIDDEN, SKIP, COTS, CLS, OUTS, HIDDEN_BACK,
     OUTER_G1, INNER_G1, FFN_G1, QKV_G1, OUTER_G2, INNER_G2, FFN_G2, QKV_G2,
-) = range(19)
+) = range(18)
 START, F0, BETWEEN, F1, TURN, B1, UP, B0, END = range(9)
 AT_QKV, AT_HALF, AT_MIX, AT_NORM, AT_FFN, AT_ACTIVE, AT_OUT = range(7)
 AT_D_OUTER, AT_D_INNER, AT_D_NORM, AT_D_MIX, AT_D_HALF, AT_D_QUERY, AT_D_QKV, AT_D_INPUT = range(8)
@@ -48,25 +48,24 @@
     (F1, AT_HALF): [CLS],
     (F1, AT_MIX): [FFN_2, CLS],
     (F1, AT_NORM): [FFN_2, CLS],
-    (TURN, 0): [OUTS],
     (B1, AT_D_OUTER): [OUTER_G2],
     (B1, AT_D_INNER): [OUTER_G2, INNER_G2],
-    (B1, AT_D_MIX): [INNER_G2, OUTS],
-    (B1, AT_D_HALF): [OUTER_G2, COTS],
-    (B1, AT_D_QUERY): [INNER_G2],
+    (B1, AT_D_MIX): [INNER_G2],
+    (B1, AT_D_HALF): [COTS],
+    (B1, AT_D_QUERY): [OUTER_G2, INNER_G2],
     (B1, AT_D_QKV): [OUTER_G2, INNER_G2, FFN_G2, QKV_G2, COTS],
-    (UP, 0): [FFN_G2, QKV_G2, SKIP_BACK],
-    (B0, AT_D_OUTER): [OUTER_G1],
-    (B0, AT_D_INNER): [FFN_G2, QKV_G2, OUTER_G1, INNER_G1],
+    (UP, 0): [QKV_G2, OUTS],
+    (B0, AT_D_OUTER): [OUTER_G1, FFN_G2],
+    (B0, AT_D_INNER): [QKV_G2, OUTER_G1, INNER_G1],
     (B0, AT_D_MIX): [FFN_G2, INNER_G1],
-    (B0, AT_D_HALF): [QKV_G2, OUTER_G1],
-    (B0, AT_D_QUERY): [INNER_G1, QKV_G2, SKIP_BACK],
-    (B0, AT_D_QKV): [OUTER_G1, INNER_G1, QKV_G1, FFN_G1, QKV_G2],
-    (B0, AT_D_INPUT): [QKV_G1, HIDDEN_BACK, FFN_G1, QKV_G2],
+    (B0, AT_D_HALF): [QKV_G2],
+    (B0, AT_D_QUERY): [OUTER_G1, INNER_G1, QKV_G2, FFN_G2],
+    (B0, AT_D_QKV): [OUTS, OUTER_G1, INNER_G1, QKV_G1, FFN_G1, QKV_G2],
+    (B0, AT_D_INPUT): [QKV_G1, HIDDEN_BACK, QKV_G2],
     (END, 0): [QKV_G1, FFN_G1],
     (END, 1): [QKV_G1],
-    (END, 2): [QKV_G1, HIDDEN_BACK, FFN_G1],
-    (END, 3): [QKV_G1],
+    (END, 2): [QKV_G1, FFN_G1, HIDDEN_BACK],
+    (END, 3): [QKV_G1, FFN_G1],
 }
 
 
@@ -483,7 +482,7 @@
         operands += list(done)
         specs += [pl.BlockSpec(memory_space=pl.ANY)] * 2
     return pl.pallas_call(
-        functools.partial(attend_kernel, 1 + len(others), min(256, tokens)),
+        functools.partial(attend_kernel, 1 + len(others), min(512, tokens)),
         grid=(count,),
         in_specs=specs,
         out_specs=[
@@ -525,7 +524,7 @@
         operands += list(done)
         specs += [pl.BlockSpec(memory_space=pl.ANY)] * len(done)
     return pl.pallas_call(
-        functools.partial(attend_back_kernel, chunks, min(256, tokens)),
+        functools.partial(attend_back_kernel, chunks, min(512, tokens)),
         grid=(count,),
         in_specs=specs,
         out_specs=[flat, stacked] + [stacked for _ in others],
@@ -807,13 +806,12 @@
     head_in = jnp.where(is_cls, first, skip_and_cot[:, :width].astype(F32))
     second, saved_two = layer_forward(grid, F1, tick, head_in, head, seg_q, seg_k)
 
-    both_out = jnp.concatenate([first.astype(BF), second.astype(BF)], axis=1)
-    schedule.add(OUTS, grid.from_rows, lambda: (both_out,))
     head_up = tick((TURN, 0), skip_and_cot[:, width:]).astype(F32)
     give = give_to(OUTER_G2, INNER_G2, FFN_G2, QKV_G2, False)
     d_head_in = layer_backward(grid, B1, tick, give, head_up, head, saved_two, seg_q, seg_k)
     skip_grad = jnp.where(is_cls, 0.0, d_head_in).astype(BF)
-    schedule.add(SKIP_BACK, grid.from_rows, lambda: (skip_grad,))
+    results = jnp.concatenate([first.astype(BF), second.astype(BF), skip_grad], axis=1)
+    schedule.add(OUTS, grid.from_rows, lambda: (results,))
     contrast_loss, d_cls_all = contrastive(schedule.get(CLS).reshape(-1, width), positives)
     my_row = grid.dp // CORES * (CORES * rows_dev) + grid.row_in_group
     d_cls = lax.dynamic_slice_in_dim(d_cls_all, my_row * SEGS, SEGS, 0)
@@ -831,8 +829,8 @@
     mark = jnp.zeros((8, 128), F32)
     for n in range(END_TICKS):
         mark = tick((END, n), mark)
-    names = [HIDDEN_BACK, SKIP_BACK, OUTS, FFN_G1, FFN_G2, QKV_G1, QKV_G2]
-    hidden_back, skip_back, outs, (inner_1, outer_1), (inner_2, outer_2), qkv_1, qkv_2 = schedule.finish(*names)
+    names = [HIDDEN_BACK, OUTS, FFN_G1, FFN_G2, QKV_G1, QKV_G2]
+    hidden_back, outs, (inner_1, outer_1), (inner_2, outer_2), qkv_1, qkv_2 = schedule.finish(*names)
 
     cut = qkv_weight.shape[2]
     pair = lambda a, b: jnp.stack([a, b]).astype(F32)
@@ -844,9 +842,9 @@
     return (
         contrast_loss,
         outs[:, :, :width],
-        outs[:, :, width:],
+        outs[:, :, width : 2 * width],
         hidden_back.astype(F32),
-        skip_back.astype(F32),
+        outs[:, :, 2 * width :].astype(F32),
         pair(qkv_1[:, :cut], qkv_2[:, :cut]),
         cuts[0],
         pair(qkv_1[:, cut : cut + width], qkv_2[:, cut : cut + width]),

time: 652 us -> 620 us (0.951)
  starting transfers between devices: 166 us -> 134 us
  matrix products: 86.6 us -> 109 us
  local copies, waits for them, and re-layouts: 85.2 us -> 77 us
  waiting for transfers between devices: 96.7 us -> 89.4 us
    ppermute x10, starting transfers between devices: 40.9 us -> 23.2 us  [swap(): return lax.ppermute(x, 'fsdp', [(i, i ^ 1 << bit) for i in range(self.n_f)])]
    ppermute x6 -> x4, starting transfers between devices: 23.9 us -> 11.2 us  [from_rows(): got.append(lax.ppermute(block, ('dp', 'fsdp'), back))]
    dot_general x8, matrix products: 32 us -> 43.4 us  [right_t(): lax.dot_general(first_op, second_op, (((1,), (1,)), ((), ())), preferred_...]
    ppermute x4, starting transfers between devices: 16.8 us -> 5.76 us  [to_member(): return lax.ppermute(x, ('dp', 'fsdp'), self.shift_pairs(shift))]
    ppermute x48, waiting for transfers between devices: 47.7 us -> 58.4 us  [swap(): return lax.ppermute(x, 'dp', [(i, i ^ flip) for i in range(self.n_dp)])]
    dot_general x8, matrix products: 24.6 us -> 34.5 us  [left_t(): lax.dot_general(first_op, second_op, (((0,), (0,)), ((), ())), preferred_...]
    ppermute x6, waiting for transfers between devices: 8.65 us -> 0.02 us  [to_rows(): got.append(lax.ppermute(block, ('dp', 'fsdp'), self.source(k)))]
    ppermute x4, waiting for transfers between devices: 17.3 us -> 9.3 us  [scatter_z(): inward = (yield lax.ppermute(sent, 'fsdp', [(0, 1), (3, 2)]))]
  transfers between devices with their start and end apart: 90 -> 88, of which waited for: 30 -> 31; matrix products, arithmetic and copies ran while one was open for 34% -> 36% of each run, Pallas kernels for 13% -> 13%
where the time goes in v4:
time: 620 us; the launch traced here: 608 us
  starting transfers between devices  134 us (22%)
  other arithmetic  114 us (18%)
  matrix products  109 us (18%)
  waiting for transfers between devices  89.4 us (14%)
  Pallas kernels  78.4 us (13%)
  local copies, waits for them, and re-layouts  77 us (12%)
  between operations  6.82 us (1%)
    ppermute x48, waiting for transfers between devices, swap(): return lax.ppermute(x, 'dp', [(i, i ^ flip) for i in range(self.n_dp)])  58.4 us
    pallas_call x4, Pallas kernels, attend_back(): pl.pallas_call(functools.partial(attend_back_kernel, chunks, min(512, tok...  49 us
    dot_general x8, matrix products, right_t(): lax.dot_general(first_op, second_op, (((1,), (1,)), ((), ())), preferred_...  43.4 us
    ppermute x48, starting transfers between devices, swap(): return lax.ppermute(x, 'dp', [(i, i ^ flip) for i in range(self.n_dp)])  40.5 us
    dot_general x8, matrix products, left_t(): lax.dot_general(first_op, second_op, (((0,), (0,)), ((), ())), preferred_...  34.5 us
    another operation x70, other arithmetic, join(): return lax.optimization_barrier(jnp.stack([low, high], axis=place))  33.1 us
    pallas_call x4, Pallas kernels, attend(): pl.pallas_call(functools.partial(attend_kernel, 1 + len(others), min(512,...  29.4 us
    unnamed x285, local copies, waits for them, and re-layouts  26.8 us
  transfers between devices with their start and end apart: 88, of which 31 were waited for; matrix products, arithmetic and copies ran while one was open for 36% of the time, Pallas kernels for 13%

profile of v4, /device:TPU:0, one launch (start us, length us, event | category | flops | bytes accessed | tf_op | source)
XLA Modules:
  0.0 608.3 jit_solution(11740719496173980429)
XLA Ops:
  3.5 3.1 collective-permute-start.1
  11.6 4.6 collective-permute-start.3
  16.2 5.9 collective-permute-done.3
  25.2 2.4 pad_maximum_fusion.17
  27.6 8.0 %collective-permute-done.4 = bf16[2,24,3200]{2,1,0:T(8,128)(2,1)S(1)} collective-permute-done((bf16[2,24,3200]{2,1,0:T(8,128)(2,1)S(1)}, bf16[2,24,3200]{2,1,0:T(8,128)(2,1)S(1)}, u32[]{:S(2)}, u32[]{:S(2)}) %collective-permute-start.4) | collective-permute-done | bytes 307232 | tf_op jit(solution)/shard_map/ppermute | solution.py:169
  40.3 4.6 collective-permute-done.6
  52.3 3.0 collective-permute-start.13
  55.3 4.5 collective-permute-start.12
  70.7 2.6 select_bitcast_fusion.1
  78.8 4.1 fusion.18.refs_0_.refs_1_.refs_3_
  100.1 7.7 %attend.4 = (bf16[512,768]{1,0:T(8,128)(2,1)S(1)}, f32[6,2,512]{2,1,0:T(2,128)S(1)}) custom-call(bf16[512,2304]{1,0:T(8,128)(2,1)S(1)} %fusion.18.refs_0_.refs_1_.refs_3_, bf16[512,2304]{1,0:T(8,128)(2,1)S(1)} %fusion.18.refs_0_.refs_1_.refs_3_, bf16[512,1536]{1,0:T(8,128)(2,1)} %collective-permute-done.17.refs_2_.refs_4_, ...), custom_call_target="tpu_custom_call" | custom-call | flops 3221225472 | bytes 3145728 | tf_op jit(solution)/shard_map/attend/pallas_call | solution.py:484
  118.6 7.7 %attend.5 = (bf16[512,768]{1,0:T(8,128)(2,1)S(1)}, f32[6,2,512]{2,1,0:T(2,128)S(1)}) custom-call(bf16[512,2304]{1,0:T(8,128)(2,1)S(1)} %fusion.18.refs_0_.refs_1_.refs_3_, bf16[512,2304]{1,0:T(8,128)(2,1)S(1)} %fusion.18.refs_0_.refs_1_.refs_3_, ...), custom_call_target="tpu_custom_call", output_to_operand_aliasing={{0}: (7, {}), {1}: (8, {})} | custom-call | flops 3221225472 | bytes 3145728 | tf_op jit(solution)/shard_map/attend/pallas_call | solution.py:484
  147.1 2.4 collective-permute-start.33
  149.5 7.4 %collective-permute-start.32 = (bf16[256,1536]{1,0:T(8,128)(2,1)}, bf16[256,1536]{1,0:T(8,128)(2,1)}, u32[]{:S(2)}, u32[]{:S(2)}) collective-permute-start(bf16[256,1536]{1,0:T(8,128)(2,1)} %get-tuple-element.414), channel_id=1, source_target_pairs={{0,0},{1,1},{2,4},{3,5},{4,2},{5,3},{6,6},{7,7},{8,8},{9,9},{10,12... | collective-permute-start | bytes 2359304 | tf_op jit(solution)/shard_map/ppermute | solution.py:270
  159.8 5.3 multiply_convert_fusion.1
  165.1 2.7 fusion.162
  178.3 3.5 select_bitcast_fusion.7
  192.5 5.0 collective-permute-start.38
  199.2 5.4 collective-permute-start.39
  204.7 7.1 %attend.6 = (bf16[512,768]{1,0:T(8,128)(2,1)S(1)}, f32[6,2,512]{2,1,0:T(2,128)S(1)}) custom-call(bf16[512,2304]{1,0:T(8,128)(2,1)S(1)} %fusion.19.refs_0_.refs_1_.refs_3_, bf16[512,2304]{1,0:T(8,128)(2,1)S(1)} %fusion.19.refs_0_.refs_1_.refs_3_, bf16[512,1536]{1,0:T(8,128)(2,1)S(1)} %collective-permute-done.38.refs_2_.refs_4_, ...), custom_call_target="tpu_custom_call" | custom-call | flops 3221225472 | bytes 3145728 | tf_op jit(solution)/shard_map/attend/pallas_call | solution.py:484
  213.6 6.9 %attend.7 = (bf16[512,768]{1,0:T(8,128)(2,1)S(1)}, f32[6,2,512]{2,1,0:T(2,128)S(1)}) custom-call(bf16[512,2304]{1,0:T(8,128)(2,1)S(1)} %fusion.19.refs_0_.refs_1_.refs_3_, bf16[512,2304]{1,0:T(8,128)(2,1)S(1)} %fusion.19.refs_0_.refs_1_.refs_3_, ...), custom_call_target="tpu_custom_call", output_to_operand_aliasing={{0}: (7, {}), {1}: (8, {})} | custom-call | flops 3221225472 | bytes 3145728 | tf_op jit(solution)/shard_map/attend/pallas_call | solution.py:484
  220.5 5.4 collective-permute-done.41
  243.2 2.7 select_bitcast_fusion.5
  245.9 2.7 select_bitcast_fusion.3
  252.3 5.4 multiply_convert_fusion
  257.7 2.7 fusion.164
  263.7 4.7 convolution_convert_fusion.5
  271.3 10.9 %fusion.165 = (bf16[3072]{0:T(1024)(128)(2,1)S(1)}, bf16[512,3072]{1,0:T(8,128)(2,1)}) fusion(f32[512,3072]{1,0:T(8,128)} %get-tuple-element.517, f32[3072]{0:T(1024)S(1)} %reshape.563, bf16[512,768]{1,0:T(8,128)(2,1)S(1)} %copy-done.94, bf16[3072,768]{1,0:T(8,128)(2,1)} %bitcast.572), kind=kOutput, calls=%fused_computation.536 | convolution fusion | flops 2434790400 | bytes 14960640 | tf_op jit(solution)/shard_map/dot_general | solution.py:106
  282.3 7.3 %convolution_convert_fusion.4 = bf16[768,3072]{1,0:T(8,128)(2,1)} fusion(bf16[512,3072]{1,0:T(8,128)(2,1)} %get-tuple-element.253, f32[512,768]{1,0:T(8,128)} %multiply_add_fusion.1), kind=kOutput, calls=%fused_computation.22 | convolution fusion | flops 2418671616 | bytes 9437184 | tf_op jit(solution)/shard_map/dot_general | solution.py:100
  293.6 3.4 dynamic-slice_bitcast_fusion.4
  297.5 6.6 %multiply_reduce_fusion = (bf16[768]{0:T(1024)(128)(2,1)S(1)}, f32[512]{0:T(512)S(1)}, f32[512]{0:T(512)S(1)}, bf16[768]{0:T(1024)(128)(2,1)S(1)}, f32[512,768]{1,0:T(8,128)S(1)}) fusion(f32[512,768]{1,0:T(8,128)S(1)} %copy-done.22, f32[512]{0:T(512)S(1)} %add_rsqrt_fusion.1, f32[512]{0:T(512)S(1)} %broadcast_multiply_fusion.9, f32[768]{0:T(1024)S(1)} %reshape.561, ...), kind=kOutput, calls=%fused_computation.115 | convolution fusion | flops 2422994432 | bytes 13394944 | tf_op jit(solution)/shard_map/dot_general | solution.py:106
  305.0 3.2 fusion.17
  313.6 2.7 fusion.16
  318.9 12.0 %attend_back.4 = (bf16[512,768]{1,0:T(8,128)(2,1)S(1)}, f32[2,512,768]{2,1,0:T(8,128)S(1)}, bf16[2,512,768]{2,1,0:T(8,128)(2,1)}) custom-call(bf16[512,2304]{1,0:T(8,128)(2,1)S(1)} %copy-done.7, bf16[512,2304]{1,0:T(8,128)(2,1)S(1)} %copy-done.7, bf16[512,1536]{1,0:T(8,128)(2,1)S(1)} %copy-done.16, bf16[512,2304]{1,0:T(8,128)(2,1)S(1)} %copy-done.7, ...), custom_call_target="tpu_custom_call" | custom-call | flops 8053063680 | bytes 7864320 | tf_op jit(solution)/shard_map/attend_back/pallas_call | solution.py:526
  330.9 11.8 %attend_back.5 = (bf16[512,768]{1,0:T(8,128)(2,1)S(1)}, f32[2,512,768]{2,1,0:T(8,128)S(1)}, bf16[2,512,768]{2,1,0:T(8,128)(2,1)}) custom-call(bf16[512,2304]{1,0:T(8,128)(2,1)S(1)} %copy-done.7, bf16[512,2304]{1,0:T(8,128)(2,1)S(1)} %copy-done.7, bf16[512,1536]{1,0:T(8,128)(2,1)S(1)} %copy-done.16, ...), custom_call_target="tpu_custom_call", output_to_operand_aliasing={{0}: (9, {}), {1}: (10, {}), {2}: (11, {})} | custom-call | flops 8053063680 | bytes 7864320 | tf_op jit(solution)/shard_map/attend_back/pallas_call | solution.py:526
  346.2 4.7 collective-permute-start.51
  363.3 3.8 convolution_convert_fusion.3
  368.9 3.3 collective-permute-done.54
  375.7 4.9 fusion.40
  384.7 4.4 collective-permute-start.56
  400.5 4.7 convolution_convert_fusion.2
  405.2 3.1 add_convert_fusion.3
  413.7 10.9 %fusion.166 = (bf16[3072]{0:T(1024)(128)(2,1)S(1)}, bf16[512,3072]{1,0:T(8,128)(2,1)}) fusion(f32[512,3072]{1,0:T(8,128)} %get-tuple-element.511, f32[3072]{0:T(1024)S(1)} %copy-done.121, bf16[512,768]{1,0:T(8,128)(2,1)S(1)} %copy-done.95, bf16[3072,768]{1,0:T(8,128)(2,1)} %bitcast.564), kind=kOutput, calls=%fused_computation.537 | convolution fusion | flops 2434790400 | bytes 14960640 | tf_op jit(solution)/shard_map/dot_general | solution.py:106
  426.4 6.4 %convolution_convert_fusion.1 = bf16[768,3072]{1,0:T(8,128)(2,1)} fusion(bf16[512,3072]{1,0:T(8,128)(2,1)} %get-tuple-element.285, f32[512,768]{1,0:T(8,128)S(1)} %copy-done.81), kind=kOutput, calls=%fused_computation.19 | convolution fusion | flops 2418671616 | bytes 9437184 | tf_op jit(solution)/shard_map/dot_general | solution.py:100
  434.4 3.1 multiply_reduce_fusion.2
  440.5 3.0 collective-permute-start.60
  447.4 2.9 fusion.14
  450.4 2.9 convolution_convert_fusion.8.refs_5_
  460.4 12.7 %attend_back.6 = (bf16[512,768]{1,0:T(8,128)(2,1)S(1)}, f32[2,512,768]{2,1,0:T(8,128)S(1)}, bf16[2,512,768]{2,1,0:T(8,128)(2,1)}) custom-call(bf16[512,2304]{1,0:T(8,128)(2,1)S(1)} %copy-done.5, bf16[512,2304]{1,0:T(8,128)(2,1)S(1)} %copy-done.5, bf16[512,1536]{1,0:T(8,128)(2,1)} %collective-permute-done.17.refs_2_.refs_4_, bf16[512,2304]{1,0:T(8,128)(2,1)S(1)} %copy-done.5, ...), custom_call_target="tpu_custom_call" | custom-call | flops 8053063680 | bytes 7864320 | tf_op jit(solution)/shard_map/attend_back/pallas_call | solution.py:526
  474.4 2.9 collective-permute-start.67
  477.3 12.5 %attend_back.7 = (bf16[512,768]{1,0:T(8,128)(2,1)S(1)}, f32[2,512,768]{2,1,0:T(8,128)S(1)}, bf16[2,512,768]{2,1,0:T(8,128)(2,1)}) custom-call(bf16[512,2304]{1,0:T(8,128)(2,1)S(1)} %copy-done.5, bf16[512,2304]{1,0:T(8,128)(2,1)S(1)} %copy-done.5, ...), custom_call_target="tpu_custom_call", output_to_operand_aliasing={{0}: (9, {}), {1}: (10, {}), {2}: (11, {})} | custom-call | flops 8053063680 | bytes 7864320 | tf_op jit(solution)/shard_map/attend_back/pallas_call | solution.py:526
  490.7 10.4 %collective-permute-start.69 = (bf16[256,2304]{1,0:T(8,128)(2,1)}, bf16[256,2304]{1,0:T(8,128)(2,1)}, u32[]{:S(2)}, u32[]{:S(2)}) collective-permute-start(bf16[256,2304]{1,0:T(8,128)(2,1)} %get-tuple-element.383), channel_id=1, source_target_pairs={{0,0},{1,1},{4,2},{5,3},{2,4},{3,5},{6,6},{7,7},{8,8},{9,9},{12,10... | collective-permute-start | bytes 3538952 | tf_op jit(solution)/shard_map/ppermute | solution.py:288
  517.6 3.9 convolution_convert_fusion
  521.5 4.3 collective-permute-done.72
  535.4 4.0 collective-permute-start.78
  539.5 2.6 fusion.45
  550.3 2.6 collective-permute-done.78
  552.9 10.6 %collective-permute-done.79 = bf16[2,48,3200]{2,1,0:T(8,128)(2,1)S(1)} collective-permute-done((bf16[2,48,3200]{2,1,0:T(8,128)(2,1)S(1)}, bf16[2,48,3200]{2,1,0:T(8,128)(2,1)S(1)}, u32[]{:S(2)}, u32[]{:S(2)}) %collective-permute-start.79) | collective-permute-done | bytes 614432 | tf_op jit(solution)/shard_map/ppermute | solution.py:143
  568.4 6.8 %collective-permute-done.83 = bf16[48,3200]{1,0:T(8,128)(2,1)S(1)} collective-permute-done((bf16[48,3200]{1,0:T(8,128)(2,1)S(1)}, bf16[48,3200]{1,0:T(8,128)(2,1)S(1)}, u32[]{:S(2)}, u32[]{:S(2)}) %collective-permute-start.83) | collective-permute-done | bytes 307232 | tf_op jit(solution)/shard_map/ppermute | solution.py:143
  576.1 3.9 collective-permute-start.84
  580.0 6.7 %collective-permute-done.84 = bf16[2,24,3200]{2,1,0:T(8,128)(2,1)S(1)} collective-permute-done((bf16[2,24,3200]{2,1,0:T(8,128)(2,1)S(1)}, bf16[2,24,3200]{2,1,0:T(8,128)(2,1)S(1)}, u32[]{:S(2)}, u32[]{:S(2)}) %collective-permute-start.84) | collective-permute-done | bytes 307232 | tf_op jit(solution)/shard_map/ppermute | solution.py:179
  586.9 2.5 collective-permute-start.85
  591.8 4.0 collective-permute-done.85
  596.0 4.1 collective-permute-start.87
  (748 shorter events, 263.4 us)
Async XLA Ops:
  22.2 13.4 %collective-permute-start.5 = (bf16[2,24,6144]{2,1,0:T(8,128)(2,1)S(1)}, bf16[2,24,6144]{2,1,0:T(8,128)(2,1)}, u32[]{:S(2)}, u32[]{:S(2)}) collective-permute-start(bf16[2,24,6144]{2,1,0:T(8,128)(2,1)S(1)} %pad_maximum_fusion.35), channel_id=1, source_target_pairs={{1,2},{2,1},{5,6},{6,5},{9,10},{10,9},{13,14},{14,13},{17,18},{18,... | collective-permute-start | bytes 1769480 | tf_op jit(solution)/shard_map/ppermute | solution.py:168
  23.8 15.1 %collective-permute-start = (s32[2,8]{1,0:T(2,128)S(1)}, s32[2,8]{1,0:T(2,128)S(1)}, u32[]{:S(2)}, u32[]{:S(2)}) collective-permute-start(s32[2,8]{1,0:T(2,128)S(1)} %copy-done.127), channel_id=1, source_target_pairs={{0,4},{4,0},{8,12},{12,8},{16,20},{20,16},{24,28},{28,24},{1,5},{5... | collective-permute-start | bytes 200 | tf_op jit(solution)/shard_map/ppermute | solution.py:143
  39.0 20.7 %collective-permute-start.10 = (bf16[2,24,6144]{2,1,0:T(8,128)(2,1)}, bf16[2,24,6144]{2,1,0:T(8,128)(2,1)}, u32[]{:S(2)}, u32[]{:S(2)}) collective-permute-start(bf16[2,24,6144]{2,1,0:T(8,128)(2,1)} %collective-permute-done.5), channel_id=1, source_target_pairs={{1,0},{2,3},{5,4},{6,7},{9,8},{10,11},{13,12},{14,15},{17,16},{18,... | collective-permute-start | bytes 1769480 | tf_op jit(solution)/shard_map/ppermute | solution.py:169
  46.5 14.5 %collective-permute-start.8 = (bf16[2,48,3200]{2,1,0:T(8,128)(2,1)S(1)}, bf16[2,48,3200]{2,1,0:T(8,128)(2,1)S(1)}, u32[]{:S(2)}, u32[]{:S(2)}) collective-permute-start(bf16[2,48,3200]{2,1,0:T(8,128)(2,1)S(1)} %pad_maximum_fusion.32), channel_id=1, source_target_pairs={{0,8},{4,12},{8,0},{12,4},{16,24},{20,28},{24,16},{28,20},{1,9},{5... | collective-permute-start | bytes 1843208 | tf_op jit(solution)/shard_map/ppermute | solution.py:143
  48.1 14.3 %collective-permute-start.9 = (bf16[2,48,3200]{2,1,0:T(8,128)(2,1)S(1)}, bf16[2,48,3200]{2,1,0:T(8,128)(2,1)S(1)}, u32[]{:S(2)}, u32[]{:S(2)}) collective-permute-start(bf16[2,48,3200]{2,1,0:T(8,128)(2,1)S(1)} %pad_maximum_fusion.33), channel_id=1, source_target_pairs={{0,16},{4,20},{8,24},{12,28},{16,0},{20,4},{24,8},{28,12},{1,17},{... | collective-permute-start | bytes 1843208 | tf_op jit(solution)/shard_map/ppermute | solution.py:143
  52.3 18.2 %collective-permute-start.13 = (bf16[256,768]{1,0:T(8,128)(2,1)}, bf16[256,768]{1,0:T(8,128)(2,1)}, u32[]{:S(2)}, u32[]{:S(2)}) collective-permute-start(bf16[256,768]{1,0:T(8,128)(2,1)} %get-tuple-element.446), channel_id=1, source_target_pairs={{0,1},{1,0},{2,5},{3,4},{4,3},{5,2},{6,7},{7,6},{8,9},{9,8},{10,13... | collective-permute-start | bytes 1179656 | tf_op jit(solution)/shard_map/ppermute | solution.py:270
  55.3 15.2 %collective-permute-start.12 = (bf16[256,768]{1,0:T(8,128)(2,1)}, bf16[256,768]{1,0:T(8,128)(2,1)}, u32[]{:S(2)}, u32[]{:S(2)}) collective-permute-start(bf16[256,768]{1,0:T(8,128)(2,1)} %get-tuple-element.447), channel_id=1, source_target_pairs={{0,0},{1,1},{2,4},{3,5},{4,2},{5,3},{6,6},{7,7},{8,8},{9,9},{10,12... | collective-permute-start | bytes 1179656 | tf_op jit(solution)/shard_map/ppermute | solution.py:270
  69.4 15.9 %collective-permute-start.15 = (bf16[384,768]{1,0:T(8,128)(2,1)S(1)}, bf16[384,768]{1,0:T(8,128)(2,1)}, u32[]{:S(2)}, u32[]{:S(2)}) collective-permute-start(bf16[384,768]{1,0:T(8,128)(2,1)S(1)} %reshape.520), channel_id=1, source_target_pairs={{0,8},{4,12},{8,0},{12,4},{16,24},{20,28},{24,16},{28,20},{1,9},{5... | collective-permute-start | bytes 1769480 | tf_op jit(solution)/shard_map/ppermute | solution.py:143
  69.9 15.8 %collective-permute-start.14 = (bf16[96,3072]{1,0:T(8,128)(2,1)}, bf16[96,3072]{1,0:T(8,128)(2,1)}, u32[]{:S(2)}, u32[]{:S(2)}) collective-permute-start(bf16[96,3072]{1,0:T(8,128)(2,1)} %get-tuple-element.430), channel_id=1, source_target_pairs={{0,16},{4,20},{8,24},{12,28},{16,0},{20,4},{24,8},{28,12},{1,17},{... | collective-permute-start | bytes 1769480 | tf_op jit(solution)/shard_map/ppermute | solution.py:143
  70.6 15.1 %collective-permute-start.16 = (bf16[24,3072]{1,0:T(8,128)(2,1)S(1)}, bf16[24,3072]{1,0:T(8,128)(2,1)S(1)}, u32[]{:S(2)}, u32[]{:S(2)}) collective-permute-start(bf16[24,3072]{1,0:T(8,128)(2,1)S(1)} %constant_dynamic-update-slice_fusion.5), channel_id=1, source_target_pairs={{0,1},{1,0},{2,3},{3,2},{4,5},{5,4},{6,7},{7,6},{8,9},{9,8},{10,11... | collective-permute-start | bytes 442376 | tf_op jit(solution)/shard_map/ppermute | solution.py:141
  88.2 12.0 %collective-permute-start.17 = (bf16[512,1536]{1,0:T(8,128)(2,1)}, bf16[512,1536]{1,0:T(8,128)(2,1)}, u32[]{:S(2)}, u32[]{:S(2)}) collective-permute-start(bf16[512,1536]{1,0:T(8,128)(2,1)} %slice.289), channel_id=1, source_target_pairs={{0,4},{1,5},{2,6},{3,7},{4,0},{5,1},{6,2},{7,3},{8,12},{9,13},{10,... | collective-permute-start | bytes 4718600 | tf_op jit(solution)/shard_map/ppermute | solution.py:310
  93.6 14.2 %collective-permute-start.19 = (bf16[24,6144]{1,0:T(8,128)(2,1)S(1)}, bf16[24,6144]{1,0:T(8,128)(2,1)S(1)}, u32[]{:S(2)}, u32[]{:S(2)}) collective-permute-start(bf16[24,6144]{1,0:T(8,128)(2,1)S(1)} %constant_dynamic-update-slice_fusion.7), channel_id=1, source_target_pairs={{0,1},{1,0},{2,3},{3,2},{4,5},{5,4},{6,7},{7,6},{8,9},{9,8},{10,11... | collective-permute-start | bytes 884744 | tf_op jit(solution)/shard_map/ppermute | solution.py:141
  95.4 12.4 %collective-permute-start.18 = (bf16[2,24,3072]{2,1,0:T(8,128)(2,1)S(1)}, bf16[2,24,3072]{2,1,0:T(8,128)(2,1)S(1)}, u32[]{:S(2)}, u32[]{:S(2)}) collective-permute-start(bf16[2,24,3072]{2,1,0:T(8,128)(2,1)S(1)} %pad_maximum_fusion.43), channel_id=1, source_target_pairs={{1,2},{2,1},{5,6},{6,5},{9,10},{10,9},{13,14},{14,13},{17,18},{18,... | collective-permute-start | bytes 884744 | tf_op jit(solution)/shard_map/ppermute | solution.py:168
  98.4 27.9 %collective-permute-start.21 = (bf16[2,384,768]{2,1,0:T(8,128)(2,1)}, bf16[2,384,768]{2,1,0:T(8,128)(2,1)}, u32[]{:S(2)}, u32[]{:S(2)}) collective-permute-start(bf16[2,384,768]{2,1,0:T(8,128)(2,1)} %pad_maximum_fusion.22), channel_id=1, source_target_pairs={{0,16},{4,20},{8,24},{12,28},{16,0},{20,4},{24,8},{28,12},{1,17},{... | collective-permute-start | bytes 3538952 | tf_op jit(solution)/shard_map/ppermute | solution.py:143
  99.8 27.6 %collective-permute-start.20 = (bf16[2,96,3072]{2,1,0:T(8,128)(2,1)}, bf16[2,96,3072]{2,1,0:T(8,128)(2,1)}, u32[]{:S(2)}, u32[]{:S(2)}) collective-permute-start(bf16[2,96,3072]{2,1,0:T(8,128)(2,1)} %pad_maximum_fusion.21), channel_id=1, source_target_pairs={{0,8},{4,12},{8,0},{12,4},{16,24},{20,28},{24,16},{28,20},{1,9},{5... | collective-permute-start | bytes 3538952 | tf_op jit(solution)/shard_map/ppermute | solution.py:143
  108.8 19.3 %collective-permute-start.23 = (bf16[2,24,6144]{2,1,0:T(8,128)(2,1)}, bf16[2,24,6144]{2,1,0:T(8,128)(2,1)}, u32[]{:S(2)}, u32[]{:S(2)}) collective-permute-start(bf16[2,24,6144]{2,1,0:T(8,128)(2,1)} %pad_maximum_fusion.36), channel_id=1, source_target_pairs={{1,2},{2,1},{5,6},{6,5},{9,10},{10,9},{13,14},{14,13},{17,18},{18,... | collective-permute-start | bytes 1769480 | tf_op jit(solution)/shard_map/ppermute | solution.py:168
  116.2 11.9 %collective-permute-start.22 = (bf16[2,24,3072]{2,1,0:T(8,128)(2,1)}, bf16[2,24,3072]{2,1,0:T(8,128)(2,1)S(1)}, u32[]{:S(2)}, u32[]{:S(2)}) collective-permute-start(bf16[2,24,3072]{2,1,0:T(8,128)(2,1)} %copy-done.102), channel_id=1, source_target_pairs={{1,0},{2,3},{5,4},{6,7},{9,8},{10,11},{13,12},{14,15},{17,16},{18,... | collective-permute-start | bytes 884744 | tf_op jit(solution)/shard_map/ppermute | solution.py:169
  135.7 33.3 %collective-permute-start.30 = (bf16[2,24,6144]{2,1,0:T(8,128)(2,1)}, bf16[2,24,6144]{2,1,0:T(8,128)(2,1)S(1)}, u32[]{:S(2)}, u32[]{:S(2)}) collective-permute-start(bf16[2,24,6144]{2,1,0:T(8,128)(2,1)} %collective-permute-done.23), channel_id=1, source_target_pairs={{1,0},{2,3},{5,4},{6,7},{9,8},{10,11},{13,12},{14,15},{17,16},{18,... | collective-permute-start | bytes 1769480 | tf_op jit(solution)/shard_map/ppermute | solution.py:169
  143.0 26.0 %collective-permute-start.29 = (bf16[2,48,3072]{2,1,0:T(8,128)(2,1)S(1)}, bf16[2,48,3072]{2,1,0:T(8,128)(2,1)S(1)}, u32[]{:S(2)}, u32[]{:S(2)}) collective-permute-start(bf16[2,48,3072]{2,1,0:T(8,128)(2,1)S(1)} %pad_maximum_fusion.39), channel_id=1, source_target_pairs={{0,16},{4,20},{8,24},{12,28},{16,0},{20,4},{24,8},{28,12},{1,17},{... | collective-permute-start | bytes 1769480 | tf_op jit(solution)/shard_map/ppermute | solution.py:143
  144.1 24.8 %collective-permute-start.28 = (bf16[2,48,3072]{2,1,0:T(8,128)(2,1)S(1)}, bf16[2,48,3072]{2,1,0:T(8,128)(2,1)S(1)}, u32[]{:S(2)}, u32[]{:S(2)}) collective-permute-start(bf16[2,48,3072]{2,1,0:T(8,128)(2,1)S(1)} %pad_maximum_fusion.38), channel_id=1, source_target_pairs={{0,8},{4,12},{8,0},{12,4},{16,24},{20,28},{24,16},{28,20},{1,9},{5... | collective-permute-start | bytes 1769480 | tf_op jit(solution)/shard_map/ppermute | solution.py:143
  147.1 30.9 %collective-permute-start.33 = (bf16[256,1536]{1,0:T(8,128)(2,1)}, bf16[256,1536]{1,0:T(8,128)(2,1)}, u32[]{:S(2)}, u32[]{:S(2)}) collective-permute-start(bf16[256,1536]{1,0:T(8,128)(2,1)} %get-tuple-element.413), channel_id=1, source_target_pairs={{0,1},{1,0},{2,5},{3,4},{4,3},{5,2},{6,7},{7,6},{8,9},{9,8},{10,13... | collective-permute-start | bytes 2359304 | tf_op jit(solution)/shard_map/ppermute | solution.py:270
  149.5 28.6 %collective-permute-start.32 = (bf16[256,1536]{1,0:T(8,128)(2,1)}, bf16[256,1536]{1,0:T(8,128)(2,1)}, u32[]{:S(2)}, u32[]{:S(2)}) collective-permute-start(bf16[256,1536]{1,0:T(8,128)(2,1)} %get-tuple-element.414), channel_id=1, source_target_pairs={{0,0},{1,1},{2,4},{3,5},{4,2},{5,3},{6,6},{7,7},{8,8},{9,9},{10,12... | collective-permute-start | bytes 2359304 | tf_op jit(solution)/shard_map/ppermute | solution.py:270
  176.2 15.3 %collective-permute-start.36 = (bf16[384,768]{1,0:T(8,128)(2,1)S(1)}, bf16[384,768]{1,0:T(8,128)(2,1)S(1)}, u32[]{:S(2)}, u32[]{:S(2)}) collective-permute-start(bf16[384,768]{1,0:T(8,128)(2,1)S(1)} %reshape.526), channel_id=1, source_target_pairs={{0,8},{4,12},{8,0},{12,4},{16,24},{20,28},{24,16},{28,20},{1,9},{5... | collective-permute-start | bytes 1769480 | tf_op jit(solution)/shard_map/ppermute | solution.py:143
  177.2 15.2 %collective-permute-start.35 = (bf16[96,3072]{1,0:T(8,128)(2,1)}, bf16[96,3072]{1,0:T(8,128)(2,1)S(1)}, u32[]{:S(2)}, u32[]{:S(2)}) collective-permute-start(bf16[96,3072]{1,0:T(8,128)(2,1)} %get-tuple-element.422), channel_id=1, source_target_pairs={{0,16},{4,20},{8,24},{12,28},{16,0},{20,4},{24,8},{28,12},{1,17},{... | collective-permute-start | bytes 1769480 | tf_op jit(solution)/shard_map/ppermute | solution.py:143
  178.0 14.3 %collective-permute-start.37 = (f32[1,8,768]{2,1,0:T(8,128)S(1)}, f32[1,8,768]{2,1,0:T(8,128)S(1)}, u32[]{:S(2)}, u32[]{:S(2)}) collective-permute-start(f32[1,8,768]{2,1,0:T(8,128)S(1)} %add.586), channel_id=1, source_target_pairs={{0,1},{1,0},{2,3},{3,2},{4,5},{5,4},{6,7},{7,6},{8,9},{9,8},{10,11... | collective-permute-start | bytes 73736 | tf_op jit(solution)/shard_map/ppermute | solution.py:141
  192.5 12.2 %collective-permute-start.38 = (bf16[512,1536]{1,0:T(8,128)(2,1)S(1)}, bf16[512,1536]{1,0:T(8,128)(2,1)S(1)}, u32[]{:S(2)}, u32[]{:S(2)}) collective-permute-start(bf16[512,1536]{1,0:T(8,128)(2,1)S(1)} %slice.312), channel_id=1, source_target_pairs={{0,4},{1,5},{2,6},{3,7},{4,0},{5,1},{6,2},{7,3},{8,12},{9,13},{10,... | collective-permute-start | bytes 4718600 | tf_op jit(solution)/shard_map/ppermute | solution.py:310
  197.9 28.0 %collective-permute-start.41 = (bf16[2,384,768]{2,1,0:T(8,128)(2,1)S(1)}, bf16[2,384,768]{2,1,0:T(8,128)(2,1)S(1)}, u32[]{:S(2)}, u32[]{:S(2)}) collective-permute-start(bf16[2,384,768]{2,1,0:T(8,128)(2,1)S(1)} %pad_maximum_fusion.27), channel_id=1, source_target_pairs={{0,16},{4,20},{8,24},{12,28},{16,0},{20,4},{24,8},{28,12},{1,17},{... | collective-permute-start | bytes 3538952 | tf_op jit(solution)/shard_map/ppermute | solution.py:143
  198.8 28.3 %collective-permute-start.40 = (bf16[2,96,3072]{2,1,0:T(8,128)(2,1)S(1)}, bf16[2,96,3072]{2,1,0:T(8,128)(2,1)S(1)}, u32[]{:S(2)}, u32[]{:S(2)}) collective-permute-start(bf16[2,96,3072]{2,1,0:T(8,128)(2,1)S(1)} %pad_maximum_fusion.26), channel_id=1, source_target_pairs={{0,8},{4,12},{8,0},{12,4},{16,24},{20,28},{24,16},{28,20},{1,9},{5... | collective-permute-start | bytes 3538952 | tf_op jit(solution)/shard_map/ppermute | solution.py:143
  199.2 12.6 %collective-permute-start.39 = (f32[2,1,8,768]{3,2,0,1:T(8,128)S(1)}, f32[2,1,8,768]{3,2,0,1:T(8,128)S(1)}, u32[]{:S(2)}, u32[]{:S(2)}) collective-permute-start(f32[2,1,8,768]{3,2,0,1:T(8,128)S(1)} %bitcast.586), channel_id=1, source_target_pairs={{0,2},{1,3},{2,0},{3,1},{4,6},{5,7},{6,4},{7,5},{8,10},{9,11},{10,... | collective-permute-start | bytes 147464 | tf_op jit(solution)/shard_map/ppermute | solution.py:141
  211.8 17.3 %collective-permute-start.42 = (f32[2,2,1,8,768]{4,3,1,0,2:T(8,128)S(1)}, f32[2,2,1,8,768]{4,3,1,0,2:T(8,128)S(1)}, u32[]{:S(2)}, u32[]{:S(2)}) collective-permute-start(f32[2,2,1,8,768]{4,3,1,0,2:T(8,128)S(1)} %bitcast.584), channel_id=1, source_target_pairs={{0,8},{4,12},{8,0},{12,4},{16,24},{20,28},{24,16},{28,20},{1,9},{5... | collective-permute-start | bytes 294920 | tf_op jit(solution)/shard_map/ppermute | solution.py:143
  271.3 22.3 %collective-permute-start.46 = (bf16[2,2,384,768]{3,2,1,0:T(8,128)(2,1)}, bf16[2,2,384,768]{3,2,1,0:T(8,128)(2,1)}, u32[]{:S(2)}, u32[]{:S(2)}) collective-permute-start(bf16[2,2,384,768]{3,2,1,0:T(8,128)(2,1)} %dynamic-slice_bitcast_fusion.5), channel_id=1, source_target_pairs={{0,4},{4,0},{8,12},{12,8},{16,20},{20,16},{24,28},{28,24},{1,5},{5... | collective-permute-start | bytes 7077896 | tf_op jit(solution)/shard_map/ppermute | solution.py:143
  297.0 16.5 %collective-permute-start.47 = (bf16[2,2,96,3072]{3,2,1,0:T(8,128)(2,1)}, bf16[2,2,96,3072]{3,2,1,0:T(8,128)(2,1)}, u32[]{:S(2)}, u32[]{:S(2)}) collective-permute-start(bf16[2,2,96,3072]{3,2,1,0:T(8,128)(2,1)} %dynamic-slice_bitcast_fusion.4), channel_id=1, source_target_pairs={{0,4},{4,0},{8,12},{12,8},{16,20},{20,16},{24,28},{28,24},{1,5},{5... | collective-permute-start | bytes 7077896 | tf_op jit(solution)/shard_map/ppermute | solution.py:143
  308.3 42.6 %collective-permute-start.48 = (bf16[2,384,768]{2,1,0:T(8,128)(2,1)S(1)}, bf16[2,384,768]{2,1,0:T(8,128)(2,1)S(1)}, u32[]{:S(2)}, u32[]{:S(2)}) collective-permute-start(bf16[2,384,768]{2,1,0:T(8,128)(2,1)S(1)} %dynamic-slice_bitcast_fusion.11), channel_id=1, source_target_pairs={{0,16},{4,20},{8,24},{12,28},{16,0},{20,4},{24,8},{28,12},{1,17},{... | collective-permute-start | bytes 3538952 | tf_op jit(solution)/shard_map/ppermute | solution.py:143
  316.5 34.5 %collective-permute-start.49 = (bf16[2,96,3072]{2,1,0:T(8,128)(2,1)S(1)}, bf16[2,96,3072]{2,1,0:T(8,128)(2,1)S(1)}, u32[]{:S(2)}, u32[]{:S(2)}) collective-permute-start(bf16[2,96,3072]{2,1,0:T(8,128)(2,1)S(1)} %dynamic-slice_bitcast_fusion.10), channel_id=1, source_target_pairs={{0,8},{4,12},{8,0},{12,4},{16,24},{20,28},{24,16},{28,20},{1,9},{5... | collective-permute-start | bytes 3538952 | tf_op jit(solution)/shard_map/ppermute | solution.py:143
  343.6 16.5 %collective-permute-start.50 = (bf16[2,512,768]{2,1,0:T(8,128)(2,1)}, bf16[2,512,768]{2,1,0:T(8,128)(2,1)}, u32[]{:S(2)}, u32[]{:S(2)}) collective-permute-start(bf16[2,512,768]{2,1,0:T(8,128)(2,1)} %get-tuple-element.268), channel_id=1, source_target_pairs={{0,4},{1,5},{2,6},{3,7},{4,0},{5,1},{6,2},{7,3},{8,12},{9,13},{10,... | collective-permute-start | bytes 4718600 | tf_op jit(solution)/shard_map/ppermute | solution.py:310
  344.5 24.4 %collective-permute-start.52 = (bf16[256,768]{1,0:T(8,128)(2,1)}, bf16[256,768]{1,0:T(8,128)(2,1)}, u32[]{:S(2)}, u32[]{:S(2)}) collective-permute-start(bf16[256,768]{1,0:T(8,128)(2,1)} %get-tuple-element.442), channel_id=1, source_target_pairs={{0,1},{1,0},{2,5},{3,4},{4,3},{5,2},{6,7},{7,6},{8,9},{9,8},{10,13... | collective-permute-start | bytes 1179656 | tf_op jit(solution)/shard_map/ppermute | solution.py:270
  346.2 22.7 %collective-permute-start.51 = (bf16[256,768]{1,0:T(8,128)(2,1)}, bf16[256,768]{1,0:T(8,128)(2,1)}, u32[]{:S(2)}, u32[]{:S(2)}) collective-permute-start(bf16[256,768]{1,0:T(8,128)(2,1)} %get-tuple-element.443), channel_id=1, source_target_pairs={{0,0},{1,1},{2,4},{3,5},{4,2},{5,3},{6,6},{7,7},{8,8},{9,9},{10,12... | collective-permute-start | bytes 1179656 | tf_op jit(solution)/shard_map/ppermute | solution.py:270
  357.6 14.7 %collective-permute-start.54 = (bf16[96,3072]{1,0:T(8,128)(2,1)}, bf16[96,3072]{1,0:T(8,128)(2,1)}, u32[]{:S(2)}, u32[]{:S(2)}) collective-permute-start(bf16[96,3072]{1,0:T(8,128)(2,1)} %dynamic-slice_bitcast_fusion.20), channel_id=1, source_target_pairs={{0,16},{4,20},{8,24},{12,28},{16,0},{20,4},{24,8},{28,12},{1,17},{... | collective-permute-start | bytes 1769480 | tf_op jit(solution)/shard_map/ppermute | solution.py:143
  359.7 14.4 %collective-permute-start.53 = (bf16[384,768]{1,0:T(8,128)(2,1)}, bf16[384,768]{1,0:T(8,128)(2,1)}, u32[]{:S(2)}, u32[]{:S(2)}) collective-permute-start(bf16[384,768]{1,0:T(8,128)(2,1)} %dynamic-slice_bitcast_fusion.21), channel_id=1, source_target_pairs={{0,8},{4,12},{8,0},{12,4},{16,24},{20,28},{24,16},{28,20},{1,9},{5... | collective-permute-start | bytes 1769480 | tf_op jit(solution)/shard_map/ppermute | solution.py:143
  384.7 20.6 %collective-permute-start.56 = (bf16[2,24,6144]{2,1,0:T(8,128)(2,1)}, bf16[2,24,6144]{2,1,0:T(8,128)(2,1)}, u32[]{:S(2)}, u32[]{:S(2)}) collective-permute-start(bf16[2,24,6144]{2,1,0:T(8,128)(2,1)} %fusion.78), channel_id=1, source_target_pairs={{0,1},{3,2},{4,5},{7,6},{8,9},{11,10},{12,13},{15,14},{16,17},{19,... | collective-permute-start | bytes 1769480 | tf_op jit(solution)/shard_map/ppermute | solution.py:179
  400.0 32.8 %collective-permute-start.58 = (bf16[2,48,3072]{2,1,0:T(8,128)(2,1)}, bf16[2,48,3072]{2,1,0:T(8,128)(2,1)}, u32[]{:S(2)}, u32[]{:S(2)}) collective-permute-start(bf16[2,48,3072]{2,1,0:T(8,128)(2,1)} %dynamic-slice_bitcast_fusion.19), channel_id=1, source_target_pairs={{0,8},{4,12},{8,0},{12,4},{16,24},{20,28},{24,16},{28,20},{1,9},{5... | collective-permute-start | bytes 1769480 | tf_op jit(solution)/shard_map/ppermute | solution.py:143
  410.0 22.9 %collective-permute-start.57 = (bf16[2,2,384,768]{3,2,1,0:T(8,128)(2,1)}, bf16[2,2,384,768]{3,2,1,0:T(8,128)(2,1)}, u32[]{:S(2)}, u32[]{:S(2)}) collective-permute-start(bf16[2,2,384,768]{3,2,1,0:T(8,128)(2,1)} %dynamic-slice_bitcast_fusion.2), channel_id=1, source_target_pairs={{0,4},{4,0},{8,12},{12,8},{16,20},{20,16},{24,28},{28,24},{1,5},{5... | collective-permute-start | bytes 7077896 | tf_op jit(solution)/shard_map/ppermute | solution.py:143
  410.9 21.9 %collective-permute-start.59 = (bf16[2,48,3072]{2,1,0:T(8,128)(2,1)}, bf16[2,48,3072]{2,1,0:T(8,128)(2,1)}, u32[]{:S(2)}, u32[]{:S(2)}) collective-permute-start(bf16[2,48,3072]{2,1,0:T(8,128)(2,1)} %dynamic-slice_bitcast_fusion.18), channel_id=1, source_target_pairs={{0,16},{4,20},{8,24},{12,28},{16,0},{20,4},{24,8},{28,12},{1,17},{... | collective-permute-start | bytes 1769480 | tf_op jit(solution)/shard_map/ppermute | solution.py:143
  413.7 107.8 %collective-permute-start.70 = (bf16[256,2304]{1,0:T(8,128)(2,1)}, bf16[256,2304]{1,0:T(8,128)(2,1)}, u32[]{:S(2)}, u32[]{:S(2)}) collective-permute-start(bf16[256,2304]{1,0:T(8,128)(2,1)} %get-tuple-element.382), channel_id=1, source_target_pairs={{1,0},{0,1},{5,2},{4,3},{3,4},{2,5},{7,6},{6,7},{9,8},{8,9},{13,10... | collective-permute-start | bytes 3538952 | tf_op jit(solution)/shard_map/ppermute | solution.py:288
  424.7 30.5 %collective-permute-start.61 = (bf16[2,24,6144]{2,1,0:T(8,128)(2,1)}, bf16[2,24,6144]{2,1,0:T(8,128)(2,1)}, u32[]{:S(2)}, u32[]{:S(2)}) collective-permute-start(bf16[2,24,6144]{2,1,0:T(8,128)(2,1)} %add_convert_fusion.3), channel_id=1, source_target_pairs={{1,2},{2,1},{5,6},{6,5},{9,10},{10,9},{13,14},{14,13},{17,18},{18,... | collective-permute-start | bytes 1769480 | tf_op jit(solution)/shard_map/ppermute | solution.py:181
  440.5 15.9 %collective-permute-start.60 = (bf16[2,2,96,3072]{3,2,1,0:T(8,128)(2,1)S(1)}, bf16[2,2,96,3072]{3,2,1,0:T(8,128)(2,1)S(1)}, u32[]{:S(2)}, u32[]{:S(2)}) collective-permute-start(bf16[2,2,96,3072]{3,2,1,0:T(8,128)(2,1)S(1)} %dynamic-slice_bitcast_fusion.1), channel_id=1, source_target_pairs={{0,4},{4,0},{8,12},{12,8},{16,20},{20,16},{24,28},{28,24},{1,5},{5... | collective-permute-start | bytes 7077896 | tf_op jit(solution)/shard_map/ppermute | solution.py:143
  443.5 29.6 %collective-permute-start.63 = (bf16[48,3072]{1,0:T(8,128)(2,1)S(1)}, bf16[48,3072]{1,0:T(8,128)(2,1)S(1)}, u32[]{:S(2)}, u32[]{:S(2)}) collective-permute-start(bf16[48,3072]{1,0:T(8,128)(2,1)S(1)} %dynamic-slice_bitcast_fusion.34), channel_id=1, source_target_pairs={{0,8},{4,12},{8,0},{12,4},{16,24},{20,28},{24,16},{28,20},{1,9},{5... | collective-permute-start | bytes 884744 | tf_op jit(solution)/shard_map/ppermute | solution.py:143
  446.5 27.3 %collective-permute-start.62 = (bf16[48,3072]{1,0:T(8,128)(2,1)S(1)}, bf16[48,3072]{1,0:T(8,128)(2,1)S(1)}, u32[]{:S(2)}, u32[]{:S(2)}) collective-permute-start(bf16[48,3072]{1,0:T(8,128)(2,1)S(1)} %dynamic-slice_bitcast_fusion.35), channel_id=1, source_target_pairs={{0,16},{4,20},{8,24},{12,28},{16,0},{20,4},{24,8},{28,12},{1,17},{... | collective-permute-start | bytes 884744 | tf_op jit(solution)/shard_map/ppermute | solution.py:143
  455.2 35.5 %collective-permute-start.64 = (bf16[2,384,768]{2,1,0:T(8,128)(2,1)S(1)}, bf16[2,384,768]{2,1,0:T(8,128)(2,1)S(1)}, u32[]{:S(2)}, u32[]{:S(2)}) collective-permute-start(bf16[2,384,768]{2,1,0:T(8,128)(2,1)S(1)} %dynamic-slice_bitcast_fusion.9), channel_id=1, source_target_pairs={{0,16},{4,20},{8,24},{12,28},{16,0},{20,4},{24,8},{28,12},{1,17},{... | collective-permute-start | bytes 3538952 | tf_op jit(solution)/shard_map/ppermute | solution.py:143
  459.3 41.8 %collective-permute-start.66 = (bf16[24,6144]{1,0:T(8,128)(2,1)S(1)}, bf16[24,6144]{1,0:T(8,128)(2,1)S(1)}, u32[]{:S(2)}, u32[]{:S(2)}) collective-permute-start(bf16[24,6144]{1,0:T(8,128)(2,1)S(1)} %dynamic-slice_bitcast_fusion.33), channel_id=1, source_target_pairs={{0,1},{1,0},{2,3},{3,2},{4,5},{5,4},{6,7},{7,6},{8,9},{9,8},{10,11... | collective-permute-start | bytes 884744 | tf_op jit(solution)/shard_map/ppermute | solution.py:141
  473.2 28.0 %collective-permute-start.65 = (bf16[2,96,3072]{2,1,0:T(8,128)(2,1)S(1)}, bf16[2,96,3072]{2,1,0:T(8,128)(2,1)S(1)}, u32[]{:S(2)}, u32[]{:S(2)}) collective-permute-start(bf16[2,96,3072]{2,1,0:T(8,128)(2,1)S(1)} %dynamic-slice_bitcast_fusion.8), channel_id=1, source_target_pairs={{0,8},{4,12},{8,0},{12,4},{16,24},{20,28},{24,16},{28,20},{1,9},{5... | collective-permute-start | bytes 3538952 | tf_op jit(solution)/shard_map/ppermute | solution.py:143
  474.4 26.7 %collective-permute-start.67 = (bf16[2,24,3072]{2,1,0:T(8,128)(2,1)S(1)}, bf16[2,24,3072]{2,1,0:T(8,128)(2,1)S(1)}, u32[]{:S(2)}, u32[]{:S(2)}) collective-permute-start(bf16[2,24,3072]{2,1,0:T(8,128)(2,1)S(1)} %dynamic-slice_bitcast_fusion.32), channel_id=1, source_target_pairs={{0,1},{3,2},{4,5},{7,6},{8,9},{11,10},{12,13},{15,14},{16,17},{19,... | collective-permute-start | bytes 884744 | tf_op jit(solution)/shard_map/ppermute | solution.py:179
  490.7 30.8 %collective-permute-start.69 = (bf16[256,2304]{1,0:T(8,128)(2,1)}, bf16[256,2304]{1,0:T(8,128)(2,1)}, u32[]{:S(2)}, u32[]{:S(2)}) collective-permute-start(bf16[256,2304]{1,0:T(8,128)(2,1)} %get-tuple-element.383), channel_id=1, source_target_pairs={{0,0},{1,1},{4,2},{5,3},{2,4},{3,5},{6,6},{7,7},{8,8},{9,9},{12,10... | collective-permute-start | bytes 3538952 | tf_op jit(solution)/shard_map/ppermute | solution.py:288
  505.2 16.3 %collective-permute-start.73 = (bf16[2,24,3072]{2,1,0:T(8,128)(2,1)}, bf16[2,24,3072]{2,1,0:T(8,128)(2,1)}, u32[]{:S(2)}, u32[]{:S(2)}) collective-permute-start(bf16[2,24,3072]{2,1,0:T(8,128)(2,1)} %add_convert_fusion.5), channel_id=1, source_target_pairs={{1,2},{2,1},{5,6},{6,5},{9,10},{10,9},{13,14},{14,13},{17,18},{18,... | collective-permute-start | bytes 884744 | tf_op jit(solution)/shard_map/ppermute | solution.py:181
  509.7 16.0 %collective-permute-start.72 = (bf16[96,3072]{1,0:T(8,128)(2,1)}, bf16[96,3072]{1,0:T(8,128)(2,1)}, u32[]{:S(2)}, u32[]{:S(2)}) collective-permute-start(bf16[96,3072]{1,0:T(8,128)(2,1)} %dynamic-slice_bitcast_fusion.16), channel_id=1, source_target_pairs={{0,16},{4,20},{8,24},{12,28},{16,0},{20,4},{24,8},{28,12},{1,17},{... | collective-permute-start | bytes 1769480 | tf_op jit(solution)/shard_map/ppermute | solution.py:143
  511.8 15.8 %collective-permute-start.71 = (bf16[384,768]{1,0:T(8,128)(2,1)}, bf16[384,768]{1,0:T(8,128)(2,1)}, u32[]{:S(2)}, u32[]{:S(2)}) collective-permute-start(bf16[384,768]{1,0:T(8,128)(2,1)} %dynamic-slice_bitcast_fusion.17), channel_id=1, source_target_pairs={{0,8},{4,12},{8,0},{12,4},{16,24},{20,28},{24,16},{28,20},{1,9},{5... | collective-permute-start | bytes 1769480 | tf_op jit(solution)/shard_map/ppermute | solution.py:143
  530.2 15.8 %collective-permute-start.75 = (bf16[24,3072]{1,0:T(8,128)(2,1)S(1)}, bf16[24,3072]{1,0:T(8,128)(2,1)S(1)}, u32[]{:S(2)}, u32[]{:S(2)}) collective-permute-start(bf16[24,3072]{1,0:T(8,128)(2,1)S(1)} %dynamic-slice_bitcast_fusion.37), channel_id=1, source_target_pairs={{0,1},{1,0},{2,3},{3,2},{4,5},{5,4},{6,7},{7,6},{8,9},{9,8},{10,11... | collective-permute-start | bytes 442376 | tf_op jit(solution)/shard_map/ppermute | solution.py:141
  533.1 13.0 %collective-permute-start.74 = (bf16[2,2,2,48,3200]{4,3,2,1,0:T(8,128)(2,1)S(1)}, bf16[2,2,2,48,3200]{4,3,2,1,0:T(8,128)(2,1)S(1)}, u32[]{:S(2)}, u32[]{:S(2)}) collective-permute-start(bf16[2,2,2,48,3200]{4,3,2,1,0:T(8,128)(2,1)S(1)} %dynamic-slice_bitcast_fusion), channel_id=1, source_target_pairs={{0,4},{4,0},{8,12},{12,8},{16,20},{20,16},{24,28},{28,24},{1,5},{5... | collective-permute-start | bytes 7372808 | tf_op jit(solution)/shard_map/ppermute | solution.py:143
  535.4 17.5 %collective-permute-start.78 = (bf16[2,24,6144]{2,1,0:T(8,128)(2,1)S(1)}, bf16[2,24,6144]{2,1,0:T(8,128)(2,1)S(1)}, u32[]{:S(2)}, u32[]{:S(2)}) collective-permute-start(bf16[2,24,6144]{2,1,0:T(8,128)(2,1)S(1)} %fusion.74), channel_id=1, source_target_pairs={{0,1},{3,2},{4,5},{7,6},{8,9},{11,10},{12,13},{15,14},{16,17},{19,... | collective-permute-start | bytes 1769480 | tf_op jit(solution)/shard_map/ppermute | solution.py:179
  546.9 33.1 %collective-permute-start.77 = (bf16[256,768]{1,0:T(8,128)(2,1)S(1)}, bf16[256,768]{1,0:T(8,128)(2,1)S(1)}, u32[]{:S(2)}, u32[]{:S(2)}) collective-permute-start(bf16[256,768]{1,0:T(8,128)(2,1)S(1)} %get-tuple-element.438), channel_id=1, source_target_pairs={{1,0},{0,1},{5,2},{4,3},{3,4},{2,5},{7,6},{6,7},{9,8},{8,9},{13,10... | collective-permute-start | bytes 1179656 | tf_op jit(solution)/shard_map/ppermute | solution.py:288
  547.0 33.0 %collective-permute-start.76 = (bf16[256,768]{1,0:T(8,128)(2,1)S(1)}, bf16[256,768]{1,0:T(8,128)(2,1)S(1)}, u32[]{:S(2)}, u32[]{:S(2)}) collective-permute-start(bf16[256,768]{1,0:T(8,128)(2,1)S(1)} %get-tuple-element.439), channel_id=1, source_target_pairs={{0,0},{1,1},{4,2},{5,3},{2,4},{3,5},{6,6},{7,7},{8,8},{9,9},{12,10... | collective-permute-start | bytes 1179656 | tf_op jit(solution)/shard_map/ppermute | solution.py:288
  547.8 15.7 %collective-permute-start.79 = (bf16[2,48,3200]{2,1,0:T(8,128)(2,1)S(1)}, bf16[2,48,3200]{2,1,0:T(8,128)(2,1)S(1)}, u32[]{:S(2)}, u32[]{:S(2)}) collective-permute-start(bf16[2,48,3200]{2,1,0:T(8,128)(2,1)S(1)} %dynamic-slice_bitcast_fusion.15), channel_id=1, source_target_pairs={{0,8},{4,12},{8,0},{12,4},{16,24},{20,28},{24,16},{28,20},{1,9},{5... | collective-permute-start | bytes 1843208 | tf_op jit(solution)/shard_map/ppermute | solution.py:143
  549.0 16.0 %collective-permute-start.80 = (bf16[2,48,3200]{2,1,0:T(8,128)(2,1)S(1)}, bf16[2,48,3200]{2,1,0:T(8,128)(2,1)S(1)}, u32[]{:S(2)}, u32[]{:S(2)}) collective-permute-start(bf16[2,48,3200]{2,1,0:T(8,128)(2,1)S(1)} %dynamic-slice_bitcast_fusion.14), channel_id=1, source_target_pairs={{0,16},{4,20},{8,24},{12,28},{16,0},{20,4},{24,8},{28,12},{1,17},{... | collective-permute-start | bytes 1843208 | tf_op jit(solution)/shard_map/ppermute | solution.py:143
  567.7 12.3 %collective-permute-start.81 = (bf16[2,24,6144]{2,1,0:T(8,128)(2,1)S(1)}, bf16[2,24,6144]{2,1,0:T(8,128)(2,1)S(1)}, u32[]{:S(2)}, u32[]{:S(2)}) collective-permute-start(bf16[2,24,6144]{2,1,0:T(8,128)(2,1)S(1)} %add_convert_fusion.2), channel_id=1, source_target_pairs={{1,2},{2,1},{5,6},{6,5},{9,10},{10,9},{13,14},{14,13},{17,18},{18,... | collective-permute-start | bytes 1769480 | tf_op jit(solution)/shard_map/ppermute | solution.py:181
  (163 other events, 975.9 us)

commit v5 on v4

--- a/solution.py
+++ b/solution.py
@@ -40,8 +40,8 @@
     (START, 6): [QKV_1, HIDDEN, QKV_2],
     (F0, AT_QKV): [FFN_1, QKV_2, FFN_2],
     (F0, AT_HALF): [QKV_2, FFN_2],
-    (F0, AT_MIX): [FFN_1, QKV_2, FFN_2],
-    (F0, AT_NORM): [FFN_1, QKV_2, SKIP],
+    (F0, AT_MIX): [FFN_1, QKV_2, FFN_2, SKIP],
+    (F0, AT_NORM): [FFN_1, QKV_2],
     (F0, AT_OUT): [QKV_2, FFN_2, CLS],
     (BETWEEN, 0): [QKV_2, SKIP, CLS],
     (F1, AT_QKV): [FFN_2, CLS],

time: 620 us -> 617 us (level)
  transfers between devices with their start and end apart: 88 -> 88, of which waited for: 31 -> 29; matrix products, arithmetic and copies ran while one was open for 36% -> 36% of each run, Pallas kernels for 13% -> 13%
where the time goes in v5:
time: 617 us; the launch traced here: 605 us
  starting transfers between devices  131 us (21%)
  other arithmetic  114 us (18%)
  matrix products  109 us (18%)
  waiting for transfers between devices  88.2 us (14%)
  Pallas kernels  78.4 us (13%)
  local copies, waits for them, and re-layouts  78.1 us (13%)
  between operations  6.83 us (1%)
    ppermute x48, waiting for transfers between devices, swap(): return lax.ppermute(x, 'dp', [(i, i ^ flip) for i in range(self.n_dp)])  56.8 us
    pallas_call x4, Pallas kernels, attend_back(): pl.pallas_call(functools.partial(attend_back_kernel, chunks, min(512, tok...  48.9 us
    dot_general x8, matrix products, right_t(): lax.dot_general(first_op, second_op, (((1,), (1,)), ((), ())), preferred_...  43.4 us
    ppermute x48, starting transfers between devices, swap(): return lax.ppermute(x, 'dp', [(i, i ^ flip) for i in range(self.n_dp)])  39.7 us
    dot_general x8, matrix products, left_t(): lax.dot_general(first_op, second_op, (((0,), (0,)), ((), ())), preferred_...  34.5 us
    another operation x70, other arithmetic, join(): return lax.optimization_barrier(jnp.stack([low, high], axis=place))  33.1 us
    pallas_call x4, Pallas kernels, attend(): pl.pallas_call(functools.partial(attend_kernel, 1 + len(others), min(512,...  29.4 us
    unnamed x285, local copies, waits for them, and re-layouts  27.9 us
  transfers between devices with their start and end apart: 88, of which 29 were waited for; matrix products, arithmetic and copies ran while one was open for 36% of the time, Pallas kernels for 13%

profile of v5, /device:TPU:0, one launch (start us, length us, event | category | flops | bytes accessed | tf_op | source)
XLA Modules:
  0.0 605.2 jit_solution(2717213423497630891)
XLA Ops:
  3.5 3.1 collective-permute-start.1
  11.6 4.6 collective-permute-start.3
  16.2 5.9 collective-permute-done.3
  25.2 2.4 pad_maximum_fusion.17
  27.6 8.0 %collective-permute-done.4 = bf16[2,24,3200]{2,1,0:T(8,128)(2,1)S(1)} collective-permute-done((bf16[2,24,3200]{2,1,0:T(8,128)(2,1)S(1)}, bf16[2,24,3200]{2,1,0:T(8,128)(2,1)S(1)}, u32[]{:S(2)}, u32[]{:S(2)}) %collective-permute-start.4) | collective-permute-done | bytes 307232 | tf_op jit(solution)/shard_map/ppermute | solution.py:169
  40.3 4.6 collective-permute-done.6
  52.3 3.0 collective-permute-start.13
  55.3 4.5 collective-permute-start.12
  70.7 2.6 select_bitcast_fusion.1
  78.8 4.1 fusion.18.refs_0_.refs_1_.refs_3_
  100.1 7.7 %attend.4 = (bf16[512,768]{1,0:T(8,128)(2,1)S(1)}, f32[6,2,512]{2,1,0:T(2,128)S(1)}) custom-call(bf16[512,2304]{1,0:T(8,128)(2,1)S(1)} %fusion.18.refs_0_.refs_1_.refs_3_, bf16[512,2304]{1,0:T(8,128)(2,1)S(1)} %fusion.18.refs_0_.refs_1_.refs_3_, bf16[512,1536]{1,0:T(8,128)(2,1)} %collective-permute-done.17.refs_2_.refs_4_, ...), custom_call_target="tpu_custom_call" | custom-call | flops 3221225472 | bytes 3145728 | tf_op jit(solution)/shard_map/attend/pallas_call | solution.py:484
  118.6 7.7 %attend.5 = (bf16[512,768]{1,0:T(8,128)(2,1)S(1)}, f32[6,2,512]{2,1,0:T(2,128)S(1)}) custom-call(bf16[512,2304]{1,0:T(8,128)(2,1)S(1)} %fusion.18.refs_0_.refs_1_.refs_3_, bf16[512,2304]{1,0:T(8,128)(2,1)S(1)} %fusion.18.refs_0_.refs_1_.refs_3_, ...), custom_call_target="tpu_custom_call", output_to_operand_aliasing={{0}: (7, {}), {1}: (8, {})} | custom-call | flops 3221225472 | bytes 3145728 | tf_op jit(solution)/shard_map/attend/pallas_call | solution.py:484
  143.4 2.7 collective-permute-start.33
  146.1 7.4 %collective-permute-start.32 = (bf16[256,1536]{1,0:T(8,128)(2,1)}, bf16[256,1536]{1,0:T(8,128)(2,1)}, u32[]{:S(2)}, u32[]{:S(2)}) collective-permute-start(bf16[256,1536]{1,0:T(8,128)(2,1)} %get-tuple-element.414), channel_id=1, source_target_pairs={{0,0},{1,1},{2,4},{3,5},{4,2},{5,3},{6,6},{7,7},{8,8},{9,9},{10,12... | collective-permute-start | bytes 2359304 | tf_op jit(solution)/shard_map/ppermute | solution.py:270
  158.7 5.3 multiply_convert_fusion.1
  164.0 2.7 fusion.162
  177.8 3.5 select_bitcast_fusion.7
  196.1 5.6 collective-permute-start.39
  201.7 7.1 %attend.6 = (bf16[512,768]{1,0:T(8,128)(2,1)S(1)}, f32[6,2,512]{2,1,0:T(2,128)S(1)}) custom-call(bf16[512,2304]{1,0:T(8,128)(2,1)S(1)} %fusion.19.refs_0_.refs_1_.refs_3_, bf16[512,2304]{1,0:T(8,128)(2,1)S(1)} %fusion.19.refs_0_.refs_1_.refs_3_, bf16[512,1536]{1,0:T(8,128)(2,1)S(1)} %collective-permute-done.38.refs_2_.refs_4_, ...), custom_call_target="tpu_custom_call" | custom-call | flops 3221225472 | bytes 3145728 | tf_op jit(solution)/shard_map/attend/pallas_call | solution.py:484
  210.4 6.9 %attend.7 = (bf16[512,768]{1,0:T(8,128)(2,1)S(1)}, f32[6,2,512]{2,1,0:T(2,128)S(1)}) custom-call(bf16[512,2304]{1,0:T(8,128)(2,1)S(1)} %fusion.19.refs_0_.refs_1_.refs_3_, bf16[512,2304]{1,0:T(8,128)(2,1)S(1)} %fusion.19.refs_0_.refs_1_.refs_3_, ...), custom_call_target="tpu_custom_call", output_to_operand_aliasing={{0}: (7, {}), {1}: (8, {})} | custom-call | flops 3221225472 | bytes 3145728 | tf_op jit(solution)/shard_map/attend/pallas_call | solution.py:484
  217.3 5.1 collective-permute-done.41
  236.9 2.4 collective-permute-done.45
  240.0 2.7 select_bitcast_fusion.5
  242.7 2.7 select_bitcast_fusion.3
  249.1 5.4 multiply_convert_fusion
  254.6 2.7 fusion.164
  260.5 4.7 convolution_convert_fusion.5
  268.2 10.9 %fusion.165 = (bf16[3072]{0:T(1024)(128)(2,1)S(1)}, bf16[512,3072]{1,0:T(8,128)(2,1)}) fusion(f32[512,3072]{1,0:T(8,128)} %get-tuple-element.517, f32[3072]{0:T(1024)S(1)} %reshape.563, bf16[512,768]{1,0:T(8,128)(2,1)S(1)} %copy-done.94, bf16[3072,768]{1,0:T(8,128)(2,1)} %bitcast.572), kind=kOutput, calls=%fused_computation.536 | convolution fusion | flops 2434790400 | bytes 14960640 | tf_op jit(solution)/shard_map/dot_general | solution.py:106
  279.2 7.3 %convolution_convert_fusion.4 = bf16[768,3072]{1,0:T(8,128)(2,1)} fusion(bf16[512,3072]{1,0:T(8,128)(2,1)} %get-tuple-element.253, f32[512,768]{1,0:T(8,128)} %multiply_add_fusion.1), kind=kOutput, calls=%fused_computation.22 | convolution fusion | flops 2418671616 | bytes 9437184 | tf_op jit(solution)/shard_map/dot_general | solution.py:100
  290.5 3.4 dynamic-slice_bitcast_fusion.4
  294.4 6.6 %multiply_reduce_fusion = (bf16[768]{0:T(1024)(128)(2,1)S(1)}, f32[512]{0:T(512)S(1)}, f32[512]{0:T(512)S(1)}, bf16[768]{0:T(1024)(128)(2,1)S(1)}, f32[512,768]{1,0:T(8,128)S(1)}) fusion(f32[512,768]{1,0:T(8,128)S(1)} %copy-done.22, f32[512]{0:T(512)S(1)} %add_rsqrt_fusion.1, f32[512]{0:T(512)S(1)} %broadcast_multiply_fusion.9, f32[768]{0:T(1024)S(1)} %reshape.561, ...), kind=kOutput, calls=%fused_computation.115 | convolution fusion | flops 2422994432 | bytes 13394944 | tf_op jit(solution)/shard_map/dot_general | solution.py:106
  301.8 3.2 fusion.17
  310.1 2.7 fusion.16
  315.3 12.0 %attend_back.4 = (bf16[512,768]{1,0:T(8,128)(2,1)S(1)}, f32[2,512,768]{2,1,0:T(8,128)S(1)}, bf16[2,512,768]{2,1,0:T(8,128)(2,1)}) custom-call(bf16[512,2304]{1,0:T(8,128)(2,1)S(1)} %copy-done.7, bf16[512,2304]{1,0:T(8,128)(2,1)S(1)} %copy-done.7, bf16[512,1536]{1,0:T(8,128)(2,1)S(1)} %copy-done.16, bf16[512,2304]{1,0:T(8,128)(2,1)S(1)} %copy-done.7, ...), custom_call_target="tpu_custom_call" | custom-call | flops 8053063680 | bytes 7864320 | tf_op jit(solution)/shard_map/attend_back/pallas_call | solution.py:526
  327.3 11.8 %attend_back.5 = (bf16[512,768]{1,0:T(8,128)(2,1)S(1)}, f32[2,512,768]{2,1,0:T(8,128)S(1)}, bf16[2,512,768]{2,1,0:T(8,128)(2,1)}) custom-call(bf16[512,2304]{1,0:T(8,128)(2,1)S(1)} %copy-done.7, bf16[512,2304]{1,0:T(8,128)(2,1)S(1)} %copy-done.7, bf16[512,1536]{1,0:T(8,128)(2,1)S(1)} %copy-done.16, ...), custom_call_target="tpu_custom_call", output_to_operand_aliasing={{0}: (9, {}), {1}: (10, {}), {2}: (11, {})} | custom-call | flops 8053063680 | bytes 7864320 | tf_op jit(solution)/shard_map/attend_back/pallas_call | solution.py:526
  342.7 4.7 collective-permute-start.51
  360.0 3.8 convolution_convert_fusion.3
  365.6 3.1 collective-permute-done.54
  372.5 4.9 fusion.40
  381.5 4.4 collective-permute-start.56
  397.4 4.7 convolution_convert_fusion.2
  402.2 3.1 add_convert_fusion.3
  410.6 10.9 %fusion.166 = (bf16[3072]{0:T(1024)(128)(2,1)S(1)}, bf16[512,3072]{1,0:T(8,128)(2,1)}) fusion(f32[512,3072]{1,0:T(8,128)} %get-tuple-element.511, f32[3072]{0:T(1024)S(1)} %copy-done.121, bf16[512,768]{1,0:T(8,128)(2,1)S(1)} %copy-done.95, bf16[3072,768]{1,0:T(8,128)(2,1)} %bitcast.564), kind=kOutput, calls=%fused_computation.537 | convolution fusion | flops 2434790400 | bytes 14960640 | tf_op jit(solution)/shard_map/dot_general | solution.py:106
  423.3 6.4 %convolution_convert_fusion.1 = bf16[768,3072]{1,0:T(8,128)(2,1)} fusion(bf16[512,3072]{1,0:T(8,128)(2,1)} %get-tuple-element.285, f32[512,768]{1,0:T(8,128)S(1)} %copy-done.81), kind=kOutput, calls=%fused_computation.19 | convolution fusion | flops 2418671616 | bytes 9437184 | tf_op jit(solution)/shard_map/dot_general | solution.py:100
  431.3 3.1 multiply_reduce_fusion.2
  437.4 3.1 collective-permute-start.60
  444.2 2.9 fusion.14
  447.2 2.9 convolution_convert_fusion.8.refs_5_
  456.9 12.7 %attend_back.6 = (bf16[512,768]{1,0:T(8,128)(2,1)S(1)}, f32[2,512,768]{2,1,0:T(8,128)S(1)}, bf16[2,512,768]{2,1,0:T(8,128)(2,1)}) custom-call(bf16[512,2304]{1,0:T(8,128)(2,1)S(1)} %copy-done.5, bf16[512,2304]{1,0:T(8,128)(2,1)S(1)} %copy-done.5, bf16[512,1536]{1,0:T(8,128)(2,1)} %collective-permute-done.17.refs_2_.refs_4_, bf16[512,2304]{1,0:T(8,128)(2,1)S(1)} %copy-done.5, ...), custom_call_target="tpu_custom_call" | custom-call | flops 8053063680 | bytes 7864320 | tf_op jit(solution)/shard_map/attend_back/pallas_call | solution.py:526
  471.0 2.9 collective-permute-start.67
  474.0 12.5 %attend_back.7 = (bf16[512,768]{1,0:T(8,128)(2,1)S(1)}, f32[2,512,768]{2,1,0:T(8,128)S(1)}, bf16[2,512,768]{2,1,0:T(8,128)(2,1)}) custom-call(bf16[512,2304]{1,0:T(8,128)(2,1)S(1)} %copy-done.5, bf16[512,2304]{1,0:T(8,128)(2,1)S(1)} %copy-done.5, ...), custom_call_target="tpu_custom_call", output_to_operand_aliasing={{0}: (9, {}), {1}: (10, {}), {2}: (11, {})} | custom-call | flops 8053063680 | bytes 7864320 | tf_op jit(solution)/shard_map/attend_back/pallas_call | solution.py:526
  487.4 10.4 %collective-permute-start.69 = (bf16[256,2304]{1,0:T(8,128)(2,1)}, bf16[256,2304]{1,0:T(8,128)(2,1)}, u32[]{:S(2)}, u32[]{:S(2)}) collective-permute-start(bf16[256,2304]{1,0:T(8,128)(2,1)} %get-tuple-element.383), channel_id=1, source_target_pairs={{0,0},{1,1},{4,2},{5,3},{2,4},{3,5},{6,6},{7,7},{8,8},{9,9},{12,10... | collective-permute-start | bytes 3538952 | tf_op jit(solution)/shard_map/ppermute | solution.py:288
  514.4 3.9 convolution_convert_fusion
  518.3 4.1 collective-permute-done.72
  532.2 4.2 collective-permute-start.78
  536.3 2.6 fusion.45
  546.8 3.0 collective-permute-done.78
  549.8 10.6 %collective-permute-done.79 = bf16[2,48,3200]{2,1,0:T(8,128)(2,1)S(1)} collective-permute-done((bf16[2,48,3200]{2,1,0:T(8,128)(2,1)S(1)}, bf16[2,48,3200]{2,1,0:T(8,128)(2,1)S(1)}, u32[]{:S(2)}, u32[]{:S(2)}) %collective-permute-start.79) | collective-permute-done | bytes 614432 | tf_op jit(solution)/shard_map/ppermute | solution.py:143
  565.1 6.9 %collective-permute-done.83 = bf16[48,3200]{1,0:T(8,128)(2,1)S(1)} collective-permute-done((bf16[48,3200]{1,0:T(8,128)(2,1)S(1)}, bf16[48,3200]{1,0:T(8,128)(2,1)S(1)}, u32[]{:S(2)}, u32[]{:S(2)}) %collective-permute-start.83) | collective-permute-done | bytes 307232 | tf_op jit(solution)/shard_map/ppermute | solution.py:143
  572.9 3.9 collective-permute-start.84
  576.9 6.7 %collective-permute-done.84 = bf16[2,24,3200]{2,1,0:T(8,128)(2,1)S(1)} collective-permute-done((bf16[2,24,3200]{2,1,0:T(8,128)(2,1)S(1)}, bf16[2,24,3200]{2,1,0:T(8,128)(2,1)S(1)}, u32[]{:S(2)}, u32[]{:S(2)}) %collective-permute-start.84) | collective-permute-done | bytes 307232 | tf_op jit(solution)/shard_map/ppermute | solution.py:179
  583.8 2.5 collective-permute-start.85
  588.7 4.0 collective-permute-done.85
  592.9 4.1 collective-permute-start.87
  (748 shorter events, 262.3 us)
Async XLA Ops:
  22.2 13.4 %collective-permute-start.5 = (bf16[2,24,6144]{2,1,0:T(8,128)(2,1)S(1)}, bf16[2,24,6144]{2,1,0:T(8,128)(2,1)}, u32[]{:S(2)}, u32[]{:S(2)}) collective-permute-start(bf16[2,24,6144]{2,1,0:T(8,128)(2,1)S(1)} %pad_maximum_fusion.35), channel_id=1, source_target_pairs={{1,2},{2,1},{5,6},{6,5},{9,10},{10,9},{13,14},{14,13},{17,18},{18,... | collective-permute-start | bytes 1769480 | tf_op jit(solution)/shard_map/ppermute | solution.py:168
  23.8 15.1 %collective-permute-start = (s32[2,8]{1,0:T(2,128)S(1)}, s32[2,8]{1,0:T(2,128)S(1)}, u32[]{:S(2)}, u32[]{:S(2)}) collective-permute-start(s32[2,8]{1,0:T(2,128)S(1)} %copy-done.127), channel_id=1, source_target_pairs={{0,4},{4,0},{8,12},{12,8},{16,20},{20,16},{24,28},{28,24},{1,5},{5... | collective-permute-start | bytes 200 | tf_op jit(solution)/shard_map/ppermute | solution.py:143
  39.0 20.7 %collective-permute-start.10 = (bf16[2,24,6144]{2,1,0:T(8,128)(2,1)}, bf16[2,24,6144]{2,1,0:T(8,128)(2,1)}, u32[]{:S(2)}, u32[]{:S(2)}) collective-permute-start(bf16[2,24,6144]{2,1,0:T(8,128)(2,1)} %collective-permute-done.5), channel_id=1, source_target_pairs={{1,0},{2,3},{5,4},{6,7},{9,8},{10,11},{13,12},{14,15},{17,16},{18,... | collective-permute-start | bytes 1769480 | tf_op jit(solution)/shard_map/ppermute | solution.py:169
  46.5 14.5 %collective-permute-start.8 = (bf16[2,48,3200]{2,1,0:T(8,128)(2,1)S(1)}, bf16[2,48,3200]{2,1,0:T(8,128)(2,1)S(1)}, u32[]{:S(2)}, u32[]{:S(2)}) collective-permute-start(bf16[2,48,3200]{2,1,0:T(8,128)(2,1)S(1)} %pad_maximum_fusion.32), channel_id=1, source_target_pairs={{0,8},{4,12},{8,0},{12,4},{16,24},{20,28},{24,16},{28,20},{1,9},{5... | collective-permute-start | bytes 1843208 | tf_op jit(solution)/shard_map/ppermute | solution.py:143
  48.1 14.3 %collective-permute-start.9 = (bf16[2,48,3200]{2,1,0:T(8,128)(2,1)S(1)}, bf16[2,48,3200]{2,1,0:T(8,128)(2,1)S(1)}, u32[]{:S(2)}, u32[]{:S(2)}) collective-permute-start(bf16[2,48,3200]{2,1,0:T(8,128)(2,1)S(1)} %pad_maximum_fusion.33), channel_id=1, source_target_pairs={{0,16},{4,20},{8,24},{12,28},{16,0},{20,4},{24,8},{28,12},{1,17},{... | collective-permute-start | bytes 1843208 | tf_op jit(solution)/shard_map/ppermute | solution.py:143
  52.3 18.2 %collective-permute-start.13 = (bf16[256,768]{1,0:T(8,128)(2,1)}, bf16[256,768]{1,0:T(8,128)(2,1)}, u32[]{:S(2)}, u32[]{:S(2)}) collective-permute-start(bf16[256,768]{1,0:T(8,128)(2,1)} %get-tuple-element.446), channel_id=1, source_target_pairs={{0,1},{1,0},{2,5},{3,4},{4,3},{5,2},{6,7},{7,6},{8,9},{9,8},{10,13... | collective-permute-start | bytes 1179656 | tf_op jit(solution)/shard_map/ppermute | solution.py:270
  55.3 15.2 %collective-permute-start.12 = (bf16[256,768]{1,0:T(8,128)(2,1)}, bf16[256,768]{1,0:T(8,128)(2,1)}, u32[]{:S(2)}, u32[]{:S(2)}) collective-permute-start(bf16[256,768]{1,0:T(8,128)(2,1)} %get-tuple-element.447), channel_id=1, source_target_pairs={{0,0},{1,1},{2,4},{3,5},{4,2},{5,3},{6,6},{7,7},{8,8},{9,9},{10,12... | collective-permute-start | bytes 1179656 | tf_op jit(solution)/shard_map/ppermute | solution.py:270
  69.4 15.9 %collective-permute-start.15 = (bf16[384,768]{1,0:T(8,128)(2,1)S(1)}, bf16[384,768]{1,0:T(8,128)(2,1)}, u32[]{:S(2)}, u32[]{:S(2)}) collective-permute-start(bf16[384,768]{1,0:T(8,128)(2,1)S(1)} %reshape.520), channel_id=1, source_target_pairs={{0,8},{4,12},{8,0},{12,4},{16,24},{20,28},{24,16},{28,20},{1,9},{5... | collective-permute-start | bytes 1769480 | tf_op jit(solution)/shard_map/ppermute | solution.py:143
  69.9 15.8 %collective-permute-start.14 = (bf16[96,3072]{1,0:T(8,128)(2,1)}, bf16[96,3072]{1,0:T(8,128)(2,1)}, u32[]{:S(2)}, u32[]{:S(2)}) collective-permute-start(bf16[96,3072]{1,0:T(8,128)(2,1)} %get-tuple-element.430), channel_id=1, source_target_pairs={{0,16},{4,20},{8,24},{12,28},{16,0},{20,4},{24,8},{28,12},{1,17},{... | collective-permute-start | bytes 1769480 | tf_op jit(solution)/shard_map/ppermute | solution.py:143
  70.6 15.1 %collective-permute-start.16 = (bf16[24,3072]{1,0:T(8,128)(2,1)S(1)}, bf16[24,3072]{1,0:T(8,128)(2,1)S(1)}, u32[]{:S(2)}, u32[]{:S(2)}) collective-permute-start(bf16[24,3072]{1,0:T(8,128)(2,1)S(1)} %constant_dynamic-update-slice_fusion.5), channel_id=1, source_target_pairs={{0,1},{1,0},{2,3},{3,2},{4,5},{5,4},{6,7},{7,6},{8,9},{9,8},{10,11... | collective-permute-start | bytes 442376 | tf_op jit(solution)/shard_map/ppermute | solution.py:141
  88.2 12.0 %collective-permute-start.17 = (bf16[512,1536]{1,0:T(8,128)(2,1)}, bf16[512,1536]{1,0:T(8,128)(2,1)}, u32[]{:S(2)}, u32[]{:S(2)}) collective-permute-start(bf16[512,1536]{1,0:T(8,128)(2,1)} %slice.289), channel_id=1, source_target_pairs={{0,4},{1,5},{2,6},{3,7},{4,0},{5,1},{6,2},{7,3},{8,12},{9,13},{10,... | collective-permute-start | bytes 4718600 | tf_op jit(solution)/shard_map/ppermute | solution.py:310
  93.6 14.2 %collective-permute-start.19 = (bf16[24,6144]{1,0:T(8,128)(2,1)S(1)}, bf16[24,6144]{1,0:T(8,128)(2,1)S(1)}, u32[]{:S(2)}, u32[]{:S(2)}) collective-permute-start(bf16[24,6144]{1,0:T(8,128)(2,1)S(1)} %constant_dynamic-update-slice_fusion.7), channel_id=1, source_target_pairs={{0,1},{1,0},{2,3},{3,2},{4,5},{5,4},{6,7},{7,6},{8,9},{9,8},{10,11... | collective-permute-start | bytes 884744 | tf_op jit(solution)/shard_map/ppermute | solution.py:141
  95.4 12.4 %collective-permute-start.18 = (bf16[2,24,3072]{2,1,0:T(8,128)(2,1)S(1)}, bf16[2,24,3072]{2,1,0:T(8,128)(2,1)S(1)}, u32[]{:S(2)}, u32[]{:S(2)}) collective-permute-start(bf16[2,24,3072]{2,1,0:T(8,128)(2,1)S(1)} %pad_maximum_fusion.43), channel_id=1, source_target_pairs={{1,2},{2,1},{5,6},{6,5},{9,10},{10,9},{13,14},{14,13},{17,18},{18,... | collective-permute-start | bytes 884744 | tf_op jit(solution)/shard_map/ppermute | solution.py:168
  98.4 27.9 %collective-permute-start.21 = (bf16[2,384,768]{2,1,0:T(8,128)(2,1)}, bf16[2,384,768]{2,1,0:T(8,128)(2,1)}, u32[]{:S(2)}, u32[]{:S(2)}) collective-permute-start(bf16[2,384,768]{2,1,0:T(8,128)(2,1)} %pad_maximum_fusion.22), channel_id=1, source_target_pairs={{0,16},{4,20},{8,24},{12,28},{16,0},{20,4},{24,8},{28,12},{1,17},{... | collective-permute-start | bytes 3538952 | tf_op jit(solution)/shard_map/ppermute | solution.py:143
  99.8 27.6 %collective-permute-start.20 = (bf16[2,96,3072]{2,1,0:T(8,128)(2,1)}, bf16[2,96,3072]{2,1,0:T(8,128)(2,1)}, u32[]{:S(2)}, u32[]{:S(2)}) collective-permute-start(bf16[2,96,3072]{2,1,0:T(8,128)(2,1)} %pad_maximum_fusion.21), channel_id=1, source_target_pairs={{0,8},{4,12},{8,0},{12,4},{16,24},{20,28},{24,16},{28,20},{1,9},{5... | collective-permute-start | bytes 3538952 | tf_op jit(solution)/shard_map/ppermute | solution.py:143
  108.8 19.3 %collective-permute-start.23 = (bf16[2,24,6144]{2,1,0:T(8,128)(2,1)}, bf16[2,24,6144]{2,1,0:T(8,128)(2,1)}, u32[]{:S(2)}, u32[]{:S(2)}) collective-permute-start(bf16[2,24,6144]{2,1,0:T(8,128)(2,1)} %pad_maximum_fusion.36), channel_id=1, source_target_pairs={{1,2},{2,1},{5,6},{6,5},{9,10},{10,9},{13,14},{14,13},{17,18},{18,... | collective-permute-start | bytes 1769480 | tf_op jit(solution)/shard_map/ppermute | solution.py:168
  133.0 20.6 %collective-permute-start.25 = (bf16[2,2,384,768]{3,2,1,0:T(8,128)(2,1)S(1)}, bf16[2,2,384,768]{3,2,1,0:T(8,128)(2,1)S(1)}, u32[]{:S(2)}, u32[]{:S(2)}) collective-permute-start(bf16[2,2,384,768]{3,2,1,0:T(8,128)(2,1)S(1)} %pad_maximum_fusion.10), channel_id=1, source_target_pairs={{0,4},{4,0},{8,12},{12,8},{16,20},{20,16},{24,28},{28,24},{1,5},{5... | collective-permute-start | bytes 7077896 | tf_op jit(solution)/shard_map/ppermute | solution.py:143
  133.1 20.5 %collective-permute-start.24 = (bf16[2,2,96,3072]{3,2,1,0:T(8,128)(2,1)S(1)}, bf16[2,2,96,3072]{3,2,1,0:T(8,128)(2,1)S(1)}, u32[]{:S(2)}, u32[]{:S(2)}) collective-permute-start(bf16[2,2,96,3072]{3,2,1,0:T(8,128)(2,1)S(1)} %pad_maximum_fusion.9), channel_id=1, source_target_pairs={{0,4},{4,0},{8,12},{12,8},{16,20},{20,16},{24,28},{28,24},{1,5},{5... | collective-permute-start | bytes 7077896 | tf_op jit(solution)/shard_map/ppermute | solution.py:143
  136.3 31.6 %collective-permute-start.30 = (bf16[2,24,6144]{2,1,0:T(8,128)(2,1)}, bf16[2,24,6144]{2,1,0:T(8,128)(2,1)S(1)}, u32[]{:S(2)}, u32[]{:S(2)}) collective-permute-start(bf16[2,24,6144]{2,1,0:T(8,128)(2,1)} %collective-permute-done.23), channel_id=1, source_target_pairs={{1,0},{2,3},{5,4},{6,7},{9,8},{10,11},{13,12},{14,15},{17,16},{18,... | collective-permute-start | bytes 1769480 | tf_op jit(solution)/shard_map/ppermute | solution.py:169
  143.4 33.2 %collective-permute-start.33 = (bf16[256,1536]{1,0:T(8,128)(2,1)}, bf16[256,1536]{1,0:T(8,128)(2,1)}, u32[]{:S(2)}, u32[]{:S(2)}) collective-permute-start(bf16[256,1536]{1,0:T(8,128)(2,1)} %get-tuple-element.413), channel_id=1, source_target_pairs={{0,1},{1,0},{2,5},{3,4},{4,3},{5,2},{6,7},{7,6},{8,9},{9,8},{10,13... | collective-permute-start | bytes 2359304 | tf_op jit(solution)/shard_map/ppermute | solution.py:270
  146.1 31.2 %collective-permute-start.32 = (bf16[256,1536]{1,0:T(8,128)(2,1)}, bf16[256,1536]{1,0:T(8,128)(2,1)}, u32[]{:S(2)}, u32[]{:S(2)}) collective-permute-start(bf16[256,1536]{1,0:T(8,128)(2,1)} %get-tuple-element.414), channel_id=1, source_target_pairs={{0,0},{1,1},{2,4},{3,5},{4,2},{5,3},{6,6},{7,7},{8,8},{9,9},{10,12... | collective-permute-start | bytes 2359304 | tf_op jit(solution)/shard_map/ppermute | solution.py:270
  153.8 14.0 %collective-permute-start.29 = (bf16[2,48,3072]{2,1,0:T(8,128)(2,1)S(1)}, bf16[2,48,3072]{2,1,0:T(8,128)(2,1)S(1)}, u32[]{:S(2)}, u32[]{:S(2)}) collective-permute-start(bf16[2,48,3072]{2,1,0:T(8,128)(2,1)S(1)} %pad_maximum_fusion.39), channel_id=1, source_target_pairs={{0,16},{4,20},{8,24},{12,28},{16,0},{20,4},{24,8},{28,12},{1,17},{... | collective-permute-start | bytes 1769480 | tf_op jit(solution)/shard_map/ppermute | solution.py:143
  155.1 12.8 %collective-permute-start.28 = (bf16[2,48,3072]{2,1,0:T(8,128)(2,1)S(1)}, bf16[2,48,3072]{2,1,0:T(8,128)(2,1)S(1)}, u32[]{:S(2)}, u32[]{:S(2)}) collective-permute-start(bf16[2,48,3072]{2,1,0:T(8,128)(2,1)S(1)} %pad_maximum_fusion.38), channel_id=1, source_target_pairs={{0,8},{4,12},{8,0},{12,4},{16,24},{20,28},{24,16},{28,20},{1,9},{5... | collective-permute-start | bytes 1769480 | tf_op jit(solution)/shard_map/ppermute | solution.py:143
  175.1 15.3 %collective-permute-start.36 = (bf16[384,768]{1,0:T(8,128)(2,1)S(1)}, bf16[384,768]{1,0:T(8,128)(2,1)S(1)}, u32[]{:S(2)}, u32[]{:S(2)}) collective-permute-start(bf16[384,768]{1,0:T(8,128)(2,1)S(1)} %reshape.526), channel_id=1, source_target_pairs={{0,8},{4,12},{8,0},{12,4},{16,24},{20,28},{24,16},{28,20},{1,9},{5... | collective-permute-start | bytes 1769480 | tf_op jit(solution)/shard_map/ppermute | solution.py:143
  176.5 15.2 %collective-permute-start.35 = (bf16[96,3072]{1,0:T(8,128)(2,1)}, bf16[96,3072]{1,0:T(8,128)(2,1)S(1)}, u32[]{:S(2)}, u32[]{:S(2)}) collective-permute-start(bf16[96,3072]{1,0:T(8,128)(2,1)} %get-tuple-element.422), channel_id=1, source_target_pairs={{0,16},{4,20},{8,24},{12,28},{16,0},{20,4},{24,8},{28,12},{1,17},{... | collective-permute-start | bytes 1769480 | tf_op jit(solution)/shard_map/ppermute | solution.py:143
  177.4 14.3 %collective-permute-start.37 = (f32[1,8,768]{2,1,0:T(8,128)S(1)}, f32[1,8,768]{2,1,0:T(8,128)S(1)}, u32[]{:S(2)}, u32[]{:S(2)}) collective-permute-start(f32[1,8,768]{2,1,0:T(8,128)S(1)} %add.586), channel_id=1, source_target_pairs={{0,1},{1,0},{2,3},{3,2},{4,5},{5,4},{6,7},{7,6},{8,9},{9,8},{10,11... | collective-permute-start | bytes 73736 | tf_op jit(solution)/shard_map/ppermute | solution.py:141
  194.3 28.0 %collective-permute-start.41 = (bf16[2,384,768]{2,1,0:T(8,128)(2,1)S(1)}, bf16[2,384,768]{2,1,0:T(8,128)(2,1)S(1)}, u32[]{:S(2)}, u32[]{:S(2)}) collective-permute-start(bf16[2,384,768]{2,1,0:T(8,128)(2,1)S(1)} %pad_maximum_fusion.27), channel_id=1, source_target_pairs={{0,16},{4,20},{8,24},{12,28},{16,0},{20,4},{24,8},{28,12},{1,17},{... | collective-permute-start | bytes 3538952 | tf_op jit(solution)/shard_map/ppermute | solution.py:143
  195.6 28.3 %collective-permute-start.40 = (bf16[2,96,3072]{2,1,0:T(8,128)(2,1)S(1)}, bf16[2,96,3072]{2,1,0:T(8,128)(2,1)S(1)}, u32[]{:S(2)}, u32[]{:S(2)}) collective-permute-start(bf16[2,96,3072]{2,1,0:T(8,128)(2,1)S(1)} %pad_maximum_fusion.26), channel_id=1, source_target_pairs={{0,8},{4,12},{8,0},{12,4},{16,24},{20,28},{24,16},{28,20},{1,9},{5... | collective-permute-start | bytes 3538952 | tf_op jit(solution)/shard_map/ppermute | solution.py:143
  196.1 12.7 %collective-permute-start.39 = (f32[2,1,8,768]{3,2,0,1:T(8,128)S(1)}, f32[2,1,8,768]{3,2,0,1:T(8,128)S(1)}, u32[]{:S(2)}, u32[]{:S(2)}) collective-permute-start(f32[2,1,8,768]{3,2,0,1:T(8,128)S(1)} %bitcast.586), channel_id=1, source_target_pairs={{0,2},{1,3},{2,0},{3,1},{4,6},{5,7},{6,4},{7,5},{8,10},{9,11},{10,... | collective-permute-start | bytes 147464 | tf_op jit(solution)/shard_map/ppermute | solution.py:141
  208.9 17.1 %collective-permute-start.42 = (f32[2,2,1,8,768]{4,3,1,0,2:T(8,128)S(1)}, f32[2,2,1,8,768]{4,3,1,0,2:T(8,128)S(1)}, u32[]{:S(2)}, u32[]{:S(2)}) collective-permute-start(f32[2,2,1,8,768]{4,3,1,0,2:T(8,128)S(1)} %bitcast.584), channel_id=1, source_target_pairs={{0,8},{4,12},{8,0},{12,4},{16,24},{20,28},{24,16},{28,20},{1,9},{5... | collective-permute-start | bytes 294920 | tf_op jit(solution)/shard_map/ppermute | solution.py:143
  268.2 22.3 %collective-permute-start.46 = (bf16[2,2,384,768]{3,2,1,0:T(8,128)(2,1)}, bf16[2,2,384,768]{3,2,1,0:T(8,128)(2,1)}, u32[]{:S(2)}, u32[]{:S(2)}) collective-permute-start(bf16[2,2,384,768]{3,2,1,0:T(8,128)(2,1)} %dynamic-slice_bitcast_fusion.5), channel_id=1, source_target_pairs={{0,4},{4,0},{8,12},{12,8},{16,20},{20,16},{24,28},{28,24},{1,5},{5... | collective-permute-start | bytes 7077896 | tf_op jit(solution)/shard_map/ppermute | solution.py:143
  293.9 16.1 %collective-permute-start.47 = (bf16[2,2,96,3072]{3,2,1,0:T(8,128)(2,1)}, bf16[2,2,96,3072]{3,2,1,0:T(8,128)(2,1)}, u32[]{:S(2)}, u32[]{:S(2)}) collective-permute-start(bf16[2,2,96,3072]{3,2,1,0:T(8,128)(2,1)} %dynamic-slice_bitcast_fusion.4), channel_id=1, source_target_pairs={{0,4},{4,0},{8,12},{12,8},{16,20},{20,16},{24,28},{28,24},{1,5},{5... | collective-permute-start | bytes 7077896 | tf_op jit(solution)/shard_map/ppermute | solution.py:143
  305.2 42.2 %collective-permute-start.48 = (bf16[2,384,768]{2,1,0:T(8,128)(2,1)S(1)}, bf16[2,384,768]{2,1,0:T(8,128)(2,1)S(1)}, u32[]{:S(2)}, u32[]{:S(2)}) collective-permute-start(bf16[2,384,768]{2,1,0:T(8,128)(2,1)S(1)} %dynamic-slice_bitcast_fusion.11), channel_id=1, source_target_pairs={{0,16},{4,20},{8,24},{12,28},{16,0},{20,4},{24,8},{28,12},{1,17},{... | collective-permute-start | bytes 3538952 | tf_op jit(solution)/shard_map/ppermute | solution.py:143
  312.9 34.5 %collective-permute-start.49 = (bf16[2,96,3072]{2,1,0:T(8,128)(2,1)S(1)}, bf16[2,96,3072]{2,1,0:T(8,128)(2,1)S(1)}, u32[]{:S(2)}, u32[]{:S(2)}) collective-permute-start(bf16[2,96,3072]{2,1,0:T(8,128)(2,1)S(1)} %dynamic-slice_bitcast_fusion.10), channel_id=1, source_target_pairs={{0,8},{4,12},{8,0},{12,4},{16,24},{20,28},{24,16},{28,20},{1,9},{5... | collective-permute-start | bytes 3538952 | tf_op jit(solution)/shard_map/ppermute | solution.py:143
  340.0 16.7 %collective-permute-start.50 = (bf16[2,512,768]{2,1,0:T(8,128)(2,1)}, bf16[2,512,768]{2,1,0:T(8,128)(2,1)}, u32[]{:S(2)}, u32[]{:S(2)}) collective-permute-start(bf16[2,512,768]{2,1,0:T(8,128)(2,1)} %get-tuple-element.268), channel_id=1, source_target_pairs={{0,4},{1,5},{2,6},{3,7},{4,0},{5,1},{6,2},{7,3},{8,12},{9,13},{10,... | collective-permute-start | bytes 4718600 | tf_op jit(solution)/shard_map/ppermute | solution.py:310
  341.0 24.7 %collective-permute-start.52 = (bf16[256,768]{1,0:T(8,128)(2,1)}, bf16[256,768]{1,0:T(8,128)(2,1)}, u32[]{:S(2)}, u32[]{:S(2)}) collective-permute-start(bf16[256,768]{1,0:T(8,128)(2,1)} %get-tuple-element.442), channel_id=1, source_target_pairs={{0,1},{1,0},{2,5},{3,4},{4,3},{5,2},{6,7},{7,6},{8,9},{9,8},{10,13... | collective-permute-start | bytes 1179656 | tf_op jit(solution)/shard_map/ppermute | solution.py:270
  342.7 22.9 %collective-permute-start.51 = (bf16[256,768]{1,0:T(8,128)(2,1)}, bf16[256,768]{1,0:T(8,128)(2,1)}, u32[]{:S(2)}, u32[]{:S(2)}) collective-permute-start(bf16[256,768]{1,0:T(8,128)(2,1)} %get-tuple-element.443), channel_id=1, source_target_pairs={{0,0},{1,1},{2,4},{3,5},{4,2},{5,3},{6,6},{7,7},{8,8},{9,9},{10,12... | collective-permute-start | bytes 1179656 | tf_op jit(solution)/shard_map/ppermute | solution.py:270
  354.0 14.7 %collective-permute-start.54 = (bf16[96,3072]{1,0:T(8,128)(2,1)}, bf16[96,3072]{1,0:T(8,128)(2,1)}, u32[]{:S(2)}, u32[]{:S(2)}) collective-permute-start(bf16[96,3072]{1,0:T(8,128)(2,1)} %dynamic-slice_bitcast_fusion.20), channel_id=1, source_target_pairs={{0,16},{4,20},{8,24},{12,28},{16,0},{20,4},{24,8},{28,12},{1,17},{... | collective-permute-start | bytes 1769480 | tf_op jit(solution)/shard_map/ppermute | solution.py:143
  356.5 14.4 %collective-permute-start.53 = (bf16[384,768]{1,0:T(8,128)(2,1)}, bf16[384,768]{1,0:T(8,128)(2,1)}, u32[]{:S(2)}, u32[]{:S(2)}) collective-permute-start(bf16[384,768]{1,0:T(8,128)(2,1)} %dynamic-slice_bitcast_fusion.21), channel_id=1, source_target_pairs={{0,8},{4,12},{8,0},{12,4},{16,24},{20,28},{24,16},{28,20},{1,9},{5... | collective-permute-start | bytes 1769480 | tf_op jit(solution)/shard_map/ppermute | solution.py:143
  381.5 20.7 %collective-permute-start.56 = (bf16[2,24,6144]{2,1,0:T(8,128)(2,1)}, bf16[2,24,6144]{2,1,0:T(8,128)(2,1)}, u32[]{:S(2)}, u32[]{:S(2)}) collective-permute-start(bf16[2,24,6144]{2,1,0:T(8,128)(2,1)} %fusion.78), channel_id=1, source_target_pairs={{0,1},{3,2},{4,5},{7,6},{8,9},{11,10},{12,13},{15,14},{16,17},{19,... | collective-permute-start | bytes 1769480 | tf_op jit(solution)/shard_map/ppermute | solution.py:179
  396.8 32.9 %collective-permute-start.58 = (bf16[2,48,3072]{2,1,0:T(8,128)(2,1)}, bf16[2,48,3072]{2,1,0:T(8,128)(2,1)}, u32[]{:S(2)}, u32[]{:S(2)}) collective-permute-start(bf16[2,48,3072]{2,1,0:T(8,128)(2,1)} %dynamic-slice_bitcast_fusion.19), channel_id=1, source_target_pairs={{0,8},{4,12},{8,0},{12,4},{16,24},{20,28},{24,16},{28,20},{1,9},{5... | collective-permute-start | bytes 1769480 | tf_op jit(solution)/shard_map/ppermute | solution.py:143
  406.9 22.8 %collective-permute-start.57 = (bf16[2,2,384,768]{3,2,1,0:T(8,128)(2,1)}, bf16[2,2,384,768]{3,2,1,0:T(8,128)(2,1)}, u32[]{:S(2)}, u32[]{:S(2)}) collective-permute-start(bf16[2,2,384,768]{3,2,1,0:T(8,128)(2,1)} %dynamic-slice_bitcast_fusion.2), channel_id=1, source_target_pairs={{0,4},{4,0},{8,12},{12,8},{16,20},{20,16},{24,28},{28,24},{1,5},{5... | collective-permute-start | bytes 7077896 | tf_op jit(solution)/shard_map/ppermute | solution.py:143
  407.9 21.9 %collective-permute-start.59 = (bf16[2,48,3072]{2,1,0:T(8,128)(2,1)}, bf16[2,48,3072]{2,1,0:T(8,128)(2,1)}, u32[]{:S(2)}, u32[]{:S(2)}) collective-permute-start(bf16[2,48,3072]{2,1,0:T(8,128)(2,1)} %dynamic-slice_bitcast_fusion.18), channel_id=1, source_target_pairs={{0,16},{4,20},{8,24},{12,28},{16,0},{20,4},{24,8},{28,12},{1,17},{... | collective-permute-start | bytes 1769480 | tf_op jit(solution)/shard_map/ppermute | solution.py:143
  410.6 107.7 %collective-permute-start.70 = (bf16[256,2304]{1,0:T(8,128)(2,1)}, bf16[256,2304]{1,0:T(8,128)(2,1)}, u32[]{:S(2)}, u32[]{:S(2)}) collective-permute-start(bf16[256,2304]{1,0:T(8,128)(2,1)} %get-tuple-element.382), channel_id=1, source_target_pairs={{1,0},{0,1},{5,2},{4,3},{3,4},{2,5},{7,6},{6,7},{9,8},{8,9},{13,10... | collective-permute-start | bytes 3538952 | tf_op jit(solution)/shard_map/ppermute | solution.py:288
  421.6 30.4 %collective-permute-start.61 = (bf16[2,24,6144]{2,1,0:T(8,128)(2,1)}, bf16[2,24,6144]{2,1,0:T(8,128)(2,1)}, u32[]{:S(2)}, u32[]{:S(2)}) collective-permute-start(bf16[2,24,6144]{2,1,0:T(8,128)(2,1)} %add_convert_fusion.3), channel_id=1, source_target_pairs={{1,2},{2,1},{5,6},{6,5},{9,10},{10,9},{13,14},{14,13},{17,18},{18,... | collective-permute-start | bytes 1769480 | tf_op jit(solution)/shard_map/ppermute | solution.py:181
  437.4 15.5 %collective-permute-start.60 = (bf16[2,2,96,3072]{3,2,1,0:T(8,128)(2,1)S(1)}, bf16[2,2,96,3072]{3,2,1,0:T(8,128)(2,1)S(1)}, u32[]{:S(2)}, u32[]{:S(2)}) collective-permute-start(bf16[2,2,96,3072]{3,2,1,0:T(8,128)(2,1)S(1)} %dynamic-slice_bitcast_fusion.1), channel_id=1, source_target_pairs={{0,4},{4,0},{8,12},{12,8},{16,20},{20,16},{24,28},{28,24},{1,5},{5... | collective-permute-start | bytes 7077896 | tf_op jit(solution)/shard_map/ppermute | solution.py:143
  440.5 29.1 %collective-permute-start.63 = (bf16[48,3072]{1,0:T(8,128)(2,1)S(1)}, bf16[48,3072]{1,0:T(8,128)(2,1)S(1)}, u32[]{:S(2)}, u32[]{:S(2)}) collective-permute-start(bf16[48,3072]{1,0:T(8,128)(2,1)S(1)} %dynamic-slice_bitcast_fusion.34), channel_id=1, source_target_pairs={{0,8},{4,12},{8,0},{12,4},{16,24},{20,28},{24,16},{28,20},{1,9},{5... | collective-permute-start | bytes 884744 | tf_op jit(solution)/shard_map/ppermute | solution.py:143
  443.0 27.8 %collective-permute-start.62 = (bf16[48,3072]{1,0:T(8,128)(2,1)S(1)}, bf16[48,3072]{1,0:T(8,128)(2,1)S(1)}, u32[]{:S(2)}, u32[]{:S(2)}) collective-permute-start(bf16[48,3072]{1,0:T(8,128)(2,1)S(1)} %dynamic-slice_bitcast_fusion.35), channel_id=1, source_target_pairs={{0,16},{4,20},{8,24},{12,28},{16,0},{20,4},{24,8},{28,12},{1,17},{... | collective-permute-start | bytes 884744 | tf_op jit(solution)/shard_map/ppermute | solution.py:143
  452.0 35.4 %collective-permute-start.64 = (bf16[2,384,768]{2,1,0:T(8,128)(2,1)S(1)}, bf16[2,384,768]{2,1,0:T(8,128)(2,1)S(1)}, u32[]{:S(2)}, u32[]{:S(2)}) collective-permute-start(bf16[2,384,768]{2,1,0:T(8,128)(2,1)S(1)} %dynamic-slice_bitcast_fusion.9), channel_id=1, source_target_pairs={{0,16},{4,20},{8,24},{12,28},{16,0},{20,4},{24,8},{28,12},{1,17},{... | collective-permute-start | bytes 3538952 | tf_op jit(solution)/shard_map/ppermute | solution.py:143
  455.8 42.0 %collective-permute-start.66 = (bf16[24,6144]{1,0:T(8,128)(2,1)S(1)}, bf16[24,6144]{1,0:T(8,128)(2,1)S(1)}, u32[]{:S(2)}, u32[]{:S(2)}) collective-permute-start(bf16[24,6144]{1,0:T(8,128)(2,1)S(1)} %dynamic-slice_bitcast_fusion.33), channel_id=1, source_target_pairs={{0,1},{1,0},{2,3},{3,2},{4,5},{5,4},{6,7},{7,6},{8,9},{9,8},{10,11... | collective-permute-start | bytes 884744 | tf_op jit(solution)/shard_map/ppermute | solution.py:141
  469.7 28.1 %collective-permute-start.65 = (bf16[2,96,3072]{2,1,0:T(8,128)(2,1)S(1)}, bf16[2,96,3072]{2,1,0:T(8,128)(2,1)S(1)}, u32[]{:S(2)}, u32[]{:S(2)}) collective-permute-start(bf16[2,96,3072]{2,1,0:T(8,128)(2,1)S(1)} %dynamic-slice_bitcast_fusion.8), channel_id=1, source_target_pairs={{0,8},{4,12},{8,0},{12,4},{16,24},{20,28},{24,16},{28,20},{1,9},{5... | collective-permute-start | bytes 3538952 | tf_op jit(solution)/shard_map/ppermute | solution.py:143
  471.0 26.7 %collective-permute-start.67 = (bf16[2,24,3072]{2,1,0:T(8,128)(2,1)S(1)}, bf16[2,24,3072]{2,1,0:T(8,128)(2,1)S(1)}, u32[]{:S(2)}, u32[]{:S(2)}) collective-permute-start(bf16[2,24,3072]{2,1,0:T(8,128)(2,1)S(1)} %dynamic-slice_bitcast_fusion.32), channel_id=1, source_target_pairs={{0,1},{3,2},{4,5},{7,6},{8,9},{11,10},{12,13},{15,14},{16,17},{19,... | collective-permute-start | bytes 884744 | tf_op jit(solution)/shard_map/ppermute | solution.py:179
  487.4 30.9 %collective-permute-start.69 = (bf16[256,2304]{1,0:T(8,128)(2,1)}, bf16[256,2304]{1,0:T(8,128)(2,1)}, u32[]{:S(2)}, u32[]{:S(2)}) collective-permute-start(bf16[256,2304]{1,0:T(8,128)(2,1)} %get-tuple-element.383), channel_id=1, source_target_pairs={{0,0},{1,1},{4,2},{5,3},{2,4},{3,5},{6,6},{7,7},{8,8},{9,9},{12,10... | collective-permute-start | bytes 3538952 | tf_op jit(solution)/shard_map/ppermute | solution.py:288
  501.9 16.4 %collective-permute-start.73 = (bf16[2,24,3072]{2,1,0:T(8,128)(2,1)}, bf16[2,24,3072]{2,1,0:T(8,128)(2,1)}, u32[]{:S(2)}, u32[]{:S(2)}) collective-permute-start(bf16[2,24,3072]{2,1,0:T(8,128)(2,1)} %add_convert_fusion.5), channel_id=1, source_target_pairs={{1,2},{2,1},{5,6},{6,5},{9,10},{10,9},{13,14},{14,13},{17,18},{18,... | collective-permute-start | bytes 884744 | tf_op jit(solution)/shard_map/ppermute | solution.py:181
  506.4 16.0 %collective-permute-start.72 = (bf16[96,3072]{1,0:T(8,128)(2,1)}, bf16[96,3072]{1,0:T(8,128)(2,1)}, u32[]{:S(2)}, u32[]{:S(2)}) collective-permute-start(bf16[96,3072]{1,0:T(8,128)(2,1)} %dynamic-slice_bitcast_fusion.16), channel_id=1, source_target_pairs={{0,16},{4,20},{8,24},{12,28},{16,0},{20,4},{24,8},{28,12},{1,17},{... | collective-permute-start | bytes 1769480 | tf_op jit(solution)/shard_map/ppermute | solution.py:143
  508.7 15.8 %collective-permute-start.71 = (bf16[384,768]{1,0:T(8,128)(2,1)}, bf16[384,768]{1,0:T(8,128)(2,1)}, u32[]{:S(2)}, u32[]{:S(2)}) collective-permute-start(bf16[384,768]{1,0:T(8,128)(2,1)} %dynamic-slice_bitcast_fusion.17), channel_id=1, source_target_pairs={{0,8},{4,12},{8,0},{12,4},{16,24},{20,28},{24,16},{28,20},{1,9},{5... | collective-permute-start | bytes 1769480 | tf_op jit(solution)/shard_map/ppermute | solution.py:143
  527.1 15.8 %collective-permute-start.75 = (bf16[24,3072]{1,0:T(8,128)(2,1)S(1)}, bf16[24,3072]{1,0:T(8,128)(2,1)S(1)}, u32[]{:S(2)}, u32[]{:S(2)}) collective-permute-start(bf16[24,3072]{1,0:T(8,128)(2,1)S(1)} %dynamic-slice_bitcast_fusion.37), channel_id=1, source_target_pairs={{0,1},{1,0},{2,3},{3,2},{4,5},{5,4},{6,7},{7,6},{8,9},{9,8},{10,11... | collective-permute-start | bytes 442376 | tf_op jit(solution)/shard_map/ppermute | solution.py:141
  529.8 13.1 %collective-permute-start.74 = (bf16[2,2,2,48,3200]{4,3,2,1,0:T(8,128)(2,1)S(1)}, bf16[2,2,2,48,3200]{4,3,2,1,0:T(8,128)(2,1)S(1)}, u32[]{:S(2)}, u32[]{:S(2)}) collective-permute-start(bf16[2,2,2,48,3200]{4,3,2,1,0:T(8,128)(2,1)S(1)} %dynamic-slice_bitcast_fusion), channel_id=1, source_target_pairs={{0,4},{4,0},{8,12},{12,8},{16,20},{20,16},{24,28},{28,24},{1,5},{5... | collective-permute-start | bytes 7372808 | tf_op jit(solution)/shard_map/ppermute | solution.py:143
  532.2 17.6 %collective-permute-start.78 = (bf16[2,24,6144]{2,1,0:T(8,128)(2,1)S(1)}, bf16[2,24,6144]{2,1,0:T(8,128)(2,1)S(1)}, u32[]{:S(2)}, u32[]{:S(2)}) collective-permute-start(bf16[2,24,6144]{2,1,0:T(8,128)(2,1)S(1)} %fusion.74), channel_id=1, source_target_pairs={{0,1},{3,2},{4,5},{7,6},{8,9},{11,10},{12,13},{15,14},{16,17},{19,... | collective-permute-start | bytes 1769480 | tf_op jit(solution)/shard_map/ppermute | solution.py:179
  543.8 33.1 %collective-permute-start.77 = (bf16[256,768]{1,0:T(8,128)(2,1)S(1)}, bf16[256,768]{1,0:T(8,128)(2,1)S(1)}, u32[]{:S(2)}, u32[]{:S(2)}) collective-permute-start(bf16[256,768]{1,0:T(8,128)(2,1)S(1)} %get-tuple-element.438), channel_id=1, source_target_pairs={{1,0},{0,1},{5,2},{4,3},{3,4},{2,5},{7,6},{6,7},{9,8},{8,9},{13,10... | collective-permute-start | bytes 1179656 | tf_op jit(solution)/shard_map/ppermute | solution.py:288
  543.9 33.0 %collective-permute-start.76 = (bf16[256,768]{1,0:T(8,128)(2,1)S(1)}, bf16[256,768]{1,0:T(8,128)(2,1)S(1)}, u32[]{:S(2)}, u32[]{:S(2)}) collective-permute-start(bf16[256,768]{1,0:T(8,128)(2,1)S(1)} %get-tuple-element.439), channel_id=1, source_target_pairs={{0,0},{1,1},{4,2},{5,3},{2,4},{3,5},{6,6},{7,7},{8,8},{9,9},{12,10... | collective-permute-start | bytes 1179656 | tf_op jit(solution)/shard_map/ppermute | solution.py:288
  544.7 15.7 %collective-permute-start.79 = (bf16[2,48,3200]{2,1,0:T(8,128)(2,1)S(1)}, bf16[2,48,3200]{2,1,0:T(8,128)(2,1)S(1)}, u32[]{:S(2)}, u32[]{:S(2)}) collective-permute-start(bf16[2,48,3200]{2,1,0:T(8,128)(2,1)S(1)} %dynamic-slice_bitcast_fusion.15), channel_id=1, source_target_pairs={{0,8},{4,12},{8,0},{12,4},{16,24},{20,28},{24,16},{28,20},{1,9},{5... | collective-permute-start | bytes 1843208 | tf_op jit(solution)/shard_map/ppermute | solution.py:143
  545.8 16.0 %collective-permute-start.80 = (bf16[2,48,3200]{2,1,0:T(8,128)(2,1)S(1)}, bf16[2,48,3200]{2,1,0:T(8,128)(2,1)S(1)}, u32[]{:S(2)}, u32[]{:S(2)}) collective-permute-start(bf16[2,48,3200]{2,1,0:T(8,128)(2,1)S(1)} %dynamic-slice_bitcast_fusion.14), channel_id=1, source_target_pairs={{0,16},{4,20},{8,24},{12,28},{16,0},{20,4},{24,8},{28,12},{1,17},{... | collective-permute-start | bytes 1843208 | tf_op jit(solution)/shard_map/ppermute | solution.py:143
  564.4 12.5 %collective-permute-start.81 = (bf16[2,24,6144]{2,1,0:T(8,128)(2,1)S(1)}, bf16[2,24,6144]{2,1,0:T(8,128)(2,1)S(1)}, u32[]{:S(2)}, u32[]{:S(2)}) collective-permute-start(bf16[2,24,6144]{2,1,0:T(8,128)(2,1)S(1)} %add_convert_fusion.2), channel_id=1, source_target_pairs={{1,2},{2,1},{5,6},{6,5},{9,10},{10,9},{13,14},{14,13},{17,18},{18,... | collective-permute-start | bytes 1769480 | tf_op jit(solution)/shard_map/ppermute | solution.py:181
  (163 other events, 977.7 us)
